TPU v7x, 32 devices: a whole 2x2x4 slice. The times are simulated.
32 devices in a mesh: kz: 4 (over z), pen: 8 (over y, x, core).
Axes of the slice: x: 2, y: 2, z: 4, core: 2. Of those that a mesh axis runs over, the one named last changes fastest.
Arguments:
- spectrum: bfloat16 [64, 2, 64, 4096], P('kz', None, None, 'pen'), may hold values from -6 to 6
- depth_weights: bfloat16 [64, 16, 64], P('kz'), may hold values from -0.125 to 0.125
- pair_tilt: int32 [64, 16], P('kz'), may hold values from 0 to 15
- pair_tile_within: int32 [64, 16], P('kz'), may hold values from 0 to 1
- tilt_pos: int32 [16], replicated, may hold values from 0 to 15, each once
- owner: int32 [64], P('kz'), may hold values from 0 to 7, as said below
- measured: bfloat16 [32, 2, 4096], P(('kz', 'pen')), may hold values from -6 to 6
Outputs:
- updated: bfloat16 [64, 2, 64, 4096], P(('kz', 'pen'))
- residual: bfloat16 [32, 2, 4096], P(('kz', 'pen'))
Inputs may be any that keep to these rules, and one draw needn't show every extreme that they name: Within every group of 16 consecutive blocks each owner value is taken by exactly 2 blocks.
All inputs are finite; a program needn't handle non-finite values.
Results may differ from a plain program's by a relative error of at most 0.004.
Values may be sent and summed in bfloat16 or wider, within the bound.
No kernel may reach another device: no remote copies, remote signals or barrier semaphores. Data moves between devices by JAX's collectives and lax.ppermute only.
A program may use at most 64 MiB of HBM per device.

v0:
```python
import jax
import jax.numpy as jnp
from jax import lax
from jax.sharding import PartitionSpec as P


def body(spectrum, depth_weights, pair_tilt, pair_tile_within, tilt_pos, owner, measured):
    n_pen = lax.axis_size("pen")
    n_kz = lax.axis_size("kz")
    group_blocks = spectrum.shape[0]
    per_owner = group_blocks // n_pen
    depth = spectrum.shape[2]
    columns = spectrum.shape[3]
    tile_dev = measured.shape[0]
    tile_cell_grid = measured.shape[2]
    all_tiles = tile_dev * n_kz * n_pen
    tiles_per_tilt = all_tiles // tilt_pos.shape[0]
    pairs = depth_weights.shape[1]
    ids = jnp.arange(group_blocks, dtype=jnp.int32)
    same = owner[:, None] == owner[None, :]
    earlier = ids[None, :] < ids[:, None]
    rank = jnp.sum(same & earlier, axis=1)
    position = owner * per_owner + rank
    inverse_map = jnp.sum(jnp.where(position[None, :] == ids[:, None], ids[None, :], 0), axis=1)
    outgoing = jnp.take(spectrum, inverse_map, axis=0).reshape(n_pen, per_owner, 2, depth, columns)
    incoming = lax.all_to_all(outgoing, "pen", split_axis=0, concat_axis=4, tiled=True)
    block_list = incoming.reshape(per_owner, 2, depth, tile_cell_grid)
    mine = lax.dynamic_slice_in_dim(inverse_map, lax.axis_index("pen") * per_owner, per_owner)
    weight_table = jnp.take(depth_weights, mine, axis=0)
    slot = jnp.take(tilt_pos, jnp.take(pair_tilt, mine, axis=0)) * tiles_per_tilt + jnp.take(
        pair_tile_within, mine, axis=0
    )
    flat_slot = slot.reshape(-1)
    partial_value = jnp.einsum(
        "yso,ynop->ysnp", weight_table, block_list, preferred_element_type=jnp.float32
    )
    local_tiles = jax.ops.segment_sum(
        partial_value.reshape(per_owner * pairs, 2 * tile_cell_grid),
        flat_slot,
        num_segments=all_tiles,
    )
    slices = lax.psum_scatter(local_tiles, ("kz", "pen"), scatter_dimension=0, tiled=True)
    residual = (slices.reshape(tile_dev, 2, tile_cell_grid) - measured.astype(jnp.float32)).astype(
        jnp.bfloat16
    )
    every_tile = lax.all_gather(residual, ("kz", "pen"), axis=0, tiled=True)
    used_flags = jnp.take(every_tile, flat_slot, axis=0).reshape(
        per_owner, pairs, 2, tile_cell_grid
    )
    gradient_volume = jnp.einsum(
        "egi,egah->eaih", weight_table, used_flags, preferred_element_type=jnp.float32
    )
    updated = (block_list.astype(jnp.float32) - 8.0 * gradient_volume).astype(jnp.bfloat16)
    return (updated, residual)


def solution(mesh):
    return jax.shard_map(
        body,
        mesh=mesh,
        in_specs=(
            P("kz", None, None, "pen"),
            P("kz", None, None),
            P("kz", None),
            P("kz", None),
            P(),
            P("kz"),
            P(("kz", "pen"), None, None),
        ),
        out_specs=(P(("kz", "pen"), None, None, None), P(("kz", "pen"), None, None)),
        check_vma=False,
    )
```

profile of v0, /device:TPU:0, one launch (start us, length us, event | category | flops | bytes accessed | tf_op | source)
XLA Modules:
  0.0 245.1 jit_solution(12438724191073512914)
XLA Ops:
  7.2 0.0 copy-start
  7.2 1.0 convert_reduce_fusion
  8.2 0.7 multiply_add_fusion
  8.8 0.1 select_reduce_fusion
  9.0 0.1 reduce_sum.24
  9.1 0.0 copy-done
  9.1 2.0 gather_fusion
  11.1 3.2 %broadcast_select_fusion = bf16[8,2,2,64,512]{4,3,2,1,0:T(8,128)(2,1)} fusion(bf16[8,2,2,64,512]{4,3,2,1,0:T(8,128)(2,1)} %bitcast.30, pred[8,2]{1,0:T(8,128)(4,1)S(1)} %compare_and_fusion), kind=kLoop, calls=%fused_computation.11 | loop fusion | flops 1048576 | bytes 4194320 | tf_op jit(solution)/shard_map/jit(_take)/select_n | solution.py:25
  14.3 0.0 copy-start.4
  14.3 0.0 copy-start.5
  14.3 0.0 copy-start.1
  14.3 5.3 %all-to-all-start = ((bf16[8,2,2,64,512]{4,3,2,1,0:T(8,128)(2,1)}), bf16[8,2,2,64,512]{4,3,2,1,0:T(8,128)(2,1)}, u32[]{:S(2)}, u32[]{:S(2)}) async-start(bf16[8,2,2,64,512]{4,3,2,1,0:T(8,128)(2,1)} %broadcast_select_fusion), calls=%async_computation | async-start | bytes 4194304 | tf_op jit(solution)/shard_map/all_to_all | solution.py:26
  19.6 0.0 all-reduce.3.cloned.1.call-start
  19.6 0.1 compare_and_fusion.1
  19.7 0.0 copy-done.4
  19.7 0.6 gather_fusion.5
  20.3 0.0 copy-done.5
  20.3 0.6 gather_fusion.4
  20.8 0.1 compare_select_fusion.2
  20.9 0.1 reshape.121
  21.0 0.0 copy-done.1
  21.0 0.7 gather_fusion.1
  21.7 0.1 reshape.120
  21.8 0.1 compare_and_fusion.2
  21.9 0.1 reshape.145
  22.0 1.4 gather_fusion.2
  23.4 23.0 %all-to-all-done = bf16[8,2,2,64,512]{4,3,2,1,0:T(8,128)(2,1)} async-done(((bf16[8,2,2,64,512]{4,3,2,1,0:T(8,128)(2,1)}), bf16[8,2,2,64,512]{4,3,2,1,0:T(8,128)(2,1)}, u32[]{:S(2)}, u32[]{:S(2)}) %all-to-all-start) | async-done | bytes 2097184 | tf_op jit(solution)/shard_map/all_to_all | solution.py:26
  46.3 4.1 %copy.19 = bf16[1,2,2,64,8,512]{5,4,3,2,1,0:T(8,128)(2,1)} copy(bf16[1,2,2,64,8,512]{5,3,2,1,4,0:T(8,128)(2,1)} %bitcast.4) | data formatting | bytes 4194304 | tf_op jit(solution)/shard_map/all_to_all | solution.py:26
  50.4 4.2 %reshape.92 = bf16[2,2,64,4096]{3,2,1,0:T(8,128)(2,1)} reshape(bf16[1,2,2,64,8,512]{5,4,3,2,1,0:T(8,128)(2,1)} %copy.19) | data formatting | bytes 4194304 | tf_op jit(solution)/shard_map/reshape | solution.py:27
  54.6 2.0 fusion.8
  56.6 0.8 copy.20
  57.5 0.0 copy-start.3
  57.5 0.6 copy.23
  58.1 2.8 %scatter_custom_fusion = f32[32,8192]{1,0:T(8,128)} fusion(s32[32]{0:T(128)S(1)} %reshape.145, f32[32,8192]{1,0:T(8,128)S(1)} %bitcast.33, f32[]{:T(128)} %constant.62.clone.1), kind=kCustom, calls=%fused_computation.13 | custom fusion | flops 262144 | bytes 1048580 | tf_op jit(solution)/shard_map/scatter-add | solution.py:37
  60.9 0.0 all-reduce.3.cloned.1.call-update
  60.9 0.1 broadcast_in_dim_reshape.3
  61.0 129.7 %all-reduce.3.cloned.1.call-done = f32[32,8192]{1,0:T(8,128)} async-done(((f32[32,8192]{1,0:T(8,128)}), f32[32,8192]{1,0:T(8,128)}) %all-reduce.3.cloned.1.call-update) | async-done | bytes 1048592
  190.7 1.0 dynamic-slice_reduce_fusion
  191.8 0.0 copy-done.3
  191.8 0.0 copy-start.2
  191.9 40.9 %all_gather.3 = bf16[32,2,4096]{2,1,0:T(2,128)(2,1)S(1)} all-gather(bf16[1,2,4096]{2,1,0:T(2,128)(2,1)S(1)} %subtract_convert_fusion), channel_id=1, replica_groups=mesh['kz'=4,'pen'=8] {'kz','pen'}, dimensions={0}, use_global_device_ids=true | all-gather | bytes 540672 | tf_op jit(solution)/shard_map/all_gather | solution.py:46
  232.8 1.6 gather_fusion.3
  234.4 3.8 %fusion.2 = bf16[2,2,64,4096]{3,2,1,0:T(8,128)(2,1)} fusion(bf16[2,2,64,4096]{3,2,1,0:T(8,128)(2,1)} %reshape.92, bf16[2,16,2,4096]{3,2,1,0:T(2,128)(2,1)S(1)} %bitcast.32, pred[2,16]{1,0:T(4,128)(4,1)S(1)} %get-tuple-element.3, bf16[2,16,64]{2,1,0:T(8,128)(2,1)S(1)} %gather_fusion.2, pred[2]{0:T(512)(128)(4,1)S(1)} %get-tuple-element.5), kind=kOutput, calls=%fused_computation.10 | convolution fusion | flops 38012928 | bytes 4722722 | tf_op jit(solution)/shard_map/egi,egah->eaih/dot_general | solution.py:50
  238.2 0.0 copy-done.2
  (9 shorter events, 0.1 us)
Async XLA Ops:
  7.2 1.9 copy-start
  14.3 5.4 %copy-start.4 = (s32[16,16]{1,0:T(8,128)S(1)}, s32[16,16]{1,0:T(8,128)}, u32[]{:S(2)}) copy-start(s32[16,16]{1,0:T(8,128)} %param.12) | copy-start | bytes 3076
  14.3 6.0 %copy-start.5 = (s32[16,16]{1,0:T(8,128)S(1)}, s32[16,16]{1,0:T(8,128)}, u32[]{:S(2)}) copy-start(s32[16,16]{1,0:T(8,128)} %param.11) | copy-start | bytes 3076
  14.3 6.8 %copy-start.1 = (s32[16]{0:T(128)S(1)}, s32[16]{0:T(128)}, u32[]{:S(2)}) copy-start(s32[16]{0:T(128)} %param.13) | copy-start | bytes 196
  14.3 32.1 %all-to-all-start = ((bf16[8,2,2,64,512]{4,3,2,1,0:T(8,128)(2,1)}), bf16[8,2,2,64,512]{4,3,2,1,0:T(8,128)(2,1)}, u32[]{:S(2)}, u32[]{:S(2)}) async-start(bf16[8,2,2,64,512]{4,3,2,1,0:T(8,128)(2,1)} %broadcast_select_fusion), calls=%async_computation | async-start | bytes 4194304 | tf_op jit(solution)/shard_map/all_to_all | solution.py:26
  19.6 171.2 %all-reduce.3.cloned.1.call-start = ((), (), s32[]{:S(2)}) async-start(), calls=%async_computation.1 | async-start | bytes 2097152
  57.5 134.4 %copy-start.3 = (bf16[1,2,4096]{2,1,0:T(2,128)(2,1)S(1)}, bf16[1,2,4096]{2,1,0:T(2,128)(2,1)}, u32[]{:S(2)}) copy-start(bf16[1,2,4096]{2,1,0:T(2,128)(2,1)} %param.15) | copy-start | bytes 49156
  191.8 46.4 %copy-start.2 = (bf16[1,2,4096]{2,1,0:T(2,128)(2,1)}, bf16[1,2,4096]{2,1,0:T(2,128)(2,1)S(1)}, u32[]{:S(2)}) copy-start(bf16[1,2,4096]{2,1,0:T(2,128)(2,1)S(1)} %subtract_convert_fusion) | copy-start | bytes 49156
Sparse Core Ops, SparseCore 0:
  61.0 129.6 all-reduce.2
where the time goes:
time: 246 us; the launch traced here: 245 us
  waiting for transfers between devices  153 us (62%)
  blocking collectives  40.9 us (17%)
  local copies, waits for them, and re-layouts  18 us (7%)
  between operations  14.2 us (6%)
  other arithmetic  8.04 us (3%)
  matrix products  5.89 us (2%)
  starting transfers between devices  5.34 us (2%)
    unnamed x2, waiting for transfers between devices  130 us
    all_gather x1, blocking collectives, body(): every_tile = lax.all_gather(residual, ('kz', 'pen'), axis=0, tiled=True)  40.9 us
    all_to_all x1, waiting for transfers between devices, body(): lax.all_to_all(outgoing, 'pen', split_axis=0, concat_axis=4, tiled=True)  23 us
    all_to_all x1, starting transfers between devices, body(): lax.all_to_all(outgoing, 'pen', split_axis=0, concat_axis=4, tiled=True)  5.3 us
  transfers between devices with their start and end apart: 2, of which 2 were waited for; matrix products, arithmetic and copies ran while one was open for 2% of the time, Pallas kernels for 0%

commit v1 on v0

v1 whole, which is shorter than its diff:
```python
import jax
import jax.numpy as jnp
from jax import lax
from jax.experimental import pallas as pl
from jax.experimental.pallas import tpu as pltpu
from jax.sharding import PartitionSpec as P

BF16 = jnp.bfloat16
F32 = jnp.float32
I32 = jnp.int32
SMEM = pl.BlockSpec(memory_space=pltpu.SMEM)
VMEM = pl.BlockSpec(memory_space=pltpu.VMEM)
ANY = pl.BlockSpec(memory_space=pl.ANY)


def split_hi_lo(value):
    hi = value.astype(BF16)
    return hi, (value - hi.astype(F32)).astype(BF16)


def order_blocks(n_pen, per_owner, owner_ref, spectrum_ref, out_ref, count_ref, sems):
    blocks = spectrum_ref.shape[0]
    for o in range(n_pen):
        count_ref[o] = 0
    copies = []
    for b in range(blocks):
        o = owner_ref[b]
        r = count_ref[o]
        count_ref[o] = r + 1
        copy = pltpu.make_async_copy(spectrum_ref.at[b], out_ref.at[o * per_owner + r], sems.at[b])
        copy.start()
        copies.append(copy)
    for copy in copies:
        copy.wait()


def slots(tilt_pos_ref, tilt, within, tiles_per_tilt, flip):
    place = jnp.zeros_like(tilt)
    for t in range(tilt_pos_ref.shape[0]):
        place = jnp.where(tilt == t, tilt_pos_ref[t], place)
    return (place * tiles_per_tilt + within) ^ flip


def forward(n_kz, chunk, tiles_per_tilt, where_ref, tilt_pos_ref, tilt_ref, within_ref,
            weights_ref, spectrum_ref, *rest):
    outs, table = rest[:n_kz], rest[n_kz]
    blocks, pairs, depth = weights_ref.shape
    columns = spectrum_ref.shape[3]
    tiles = n_kz * chunk
    slot = slots(tilt_pos_ref, tilt_ref[...], within_ref[...], tiles_per_tilt, where_ref[0] * chunk)
    rows = lax.broadcasted_iota(I32, (tiles, pairs), 0)
    for b in range(blocks):
        hot = jnp.where(slot[b : b + 1, :] == rows, 1.0, 0.0).astype(BF16)
        hi, lo = split_hi_lo(jnp.dot(hot, weights_ref[b], preferred_element_type=F32))
        table[:tiles, b * depth : (b + 1) * depth] = hi
        table[tiles:, b * depth : (b + 1) * depth] = lo
    for c in range(2):
        both = jnp.dot(
            table[...],
            spectrum_ref[:, c].reshape(blocks * depth, columns),
            preferred_element_type=F32,
        )
        total = both[:tiles] + both[tiles:]
        for k in range(n_kz):
            outs[k][c * chunk : (c + 1) * chunk, :] = total[k * chunk : (k + 1) * chunk]


def adjoint_table(n_kz, chunk, n_pen, per_owner, tiles_per_tilt, where_ref, tilt_pos_ref, owner_ref,
                  tilt_ref, within_ref, weights_ref, out_ref, mine_ref, slot_ref):
    blocks, pairs, depth = weights_ref.shape
    rows_all = n_kz * 2 * chunk
    pen = where_ref[1]
    seen = jnp.int32(0)
    for b in range(blocks):
        hit = owner_ref[b] == pen

        @pl.when(hit)
        def _(b=b, seen=seen):
            mine_ref[seen] = b

        seen = seen + hit.astype(I32)
    slot = slots(tilt_pos_ref, tilt_ref[...], within_ref[...], tiles_per_tilt, where_ref[0] * chunk)
    slot_ref[...] = slot
    rows = lax.broadcasted_iota(I32, (rows_all, pairs), 0)
    for r in range(per_owner):
        b = mine_ref[r]
        at = slot_ref[pl.ds(b, 1), :]
        low = at & (chunk - 1)
        for c in range(2):
            place = (at - low) * 2 + c * chunk + low
            hot = jnp.where(place == rows, -8.0, 0.0).astype(BF16)
            hi, lo = split_hi_lo(jnp.dot(hot, weights_ref[b], preferred_element_type=F32))
            first = (c * per_owner + r) * depth
            out_ref[:rows_all, first : first + depth] = hi
            out_ref[rows_all:, first : first + depth] = lo


def residual_chunk(n_kz, *refs):
    parts, measured_ref, out_ref = refs[:n_kz], refs[n_kz], refs[n_kz + 1]
    total = parts[0][...]
    for part in parts[1:]:
        total = total + part[...]
    out_ref[...] = (total - measured_ref[...].astype(F32)).astype(BF16)


def adjoint(chunk, per_owner, where_ref, table_ref, tiles_ref, blocks_ref, out_ref, residual_ref):
    depth = blocks_ref.shape[3]
    r_tiles = tiles_ref[0]
    rows = r_tiles.shape[0]
    both = jnp.concatenate([r_tiles, r_tiles], axis=0)
    step = lax.dot_general(
        table_ref[...], both, (((0,), (0,)), ((), ())), preferred_element_type=F32
    )
    for r in range(per_owner):
        for c in range(2):
            first = (c * per_owner + r) * depth
            out_ref[r, c] = (blocks_ref[0, r, c].astype(F32) + step[first : first + depth]).astype(BF16)
    pick_row = lax.broadcasted_iota(I32, (16, rows), 0)
    pick_at = lax.broadcasted_iota(I32, (16, rows), 1)
    pick = jnp.where(pick_at == pick_row * chunk + where_ref[1], 1.0, 0.0)
    pick = jnp.where(pick_row < 2, pick, 0.0).astype(BF16)
    own = jnp.dot(pick, r_tiles, preferred_element_type=F32)
    residual_ref[0] = own[:2].astype(BF16)


def body(spectrum, depth_weights, pair_tilt, pair_tile_within, tilt_pos, owner, measured):
    n_pen = lax.axis_size("pen")
    n_kz = lax.axis_size("kz")
    blocks, _, depth, columns = spectrum.shape
    per_owner = blocks // n_pen
    pairs = depth_weights.shape[1]
    tile_dev, _, cells = measured.shape
    chunk = tile_dev * n_pen
    tiles = chunk * n_kz
    tiles_per_tilt = tiles // tilt_pos.shape[0]
    where = jnp.stack([lax.axis_index("kz"), lax.axis_index("pen")]).astype(I32)

    def call(kernel, *static):
        def bound(*refs):
            return kernel(*static, *refs)
        return bound

    outgoing = pl.pallas_call(
        call(order_blocks, n_pen, per_owner),
        out_shape=jax.ShapeDtypeStruct(spectrum.shape, BF16),
        in_specs=[SMEM, ANY],
        out_specs=ANY,
        scratch_shapes=[pltpu.SMEM((n_pen,), I32), pltpu.SemaphoreType.DMA((blocks,))],
    )(owner, spectrum)
    outgoing = outgoing.reshape(n_pen, per_owner, 2, depth, columns)
    incoming = lax.all_to_all(outgoing, "pen", split_axis=0, concat_axis=0, tiled=True)

    sent = measured.reshape(2, n_pen, columns).transpose(1, 0, 2)
    got = lax.all_to_all(sent, "pen", split_axis=0, concat_axis=0, tiled=True)
    measured_rows = got.transpose(1, 0, 2).reshape(2 * chunk, columns)

    parts = pl.pallas_call(
        call(forward, n_kz, chunk, tiles_per_tilt),
        out_shape=[jax.ShapeDtypeStruct((2 * chunk, columns), F32)] * n_kz,
        in_specs=[SMEM, SMEM, VMEM, VMEM, VMEM, VMEM],
        out_specs=[VMEM] * n_kz,
        scratch_shapes=[pltpu.VMEM((2 * tiles, blocks * depth), BF16)],
        compiler_params=pltpu.CompilerParams(vmem_limit_bytes=48 << 20),
    )(where, tilt_pos, pair_tilt, pair_tile_within, depth_weights, spectrum)

    def across(value, k):
        return lax.ppermute(value, "kz", [(i, i ^ k) for i in range(n_kz)])

    summed = [parts[0]] + [across(parts[k], k) for k in range(1, n_kz)]
    table = pl.pallas_call(
        call(adjoint_table, n_kz, chunk, n_pen, per_owner, tiles_per_tilt),
        out_shape=jax.ShapeDtypeStruct((4 * tiles, 2 * per_owner * depth), BF16),
        in_specs=[SMEM, SMEM, SMEM, VMEM, VMEM, VMEM],
        out_specs=VMEM,
        scratch_shapes=[pltpu.SMEM((per_owner,), I32), pltpu.VMEM((blocks, pairs), I32)],
    )(where, tilt_pos, owner, pair_tilt, pair_tile_within, depth_weights)

    own = pl.pallas_call(
        call(residual_chunk, n_kz),
        out_shape=jax.ShapeDtypeStruct((2 * chunk, columns), BF16),
        in_specs=[VMEM] * (n_kz + 1),
        out_specs=VMEM,
    )(*summed, measured_rows)

    held = jnp.concatenate([own] + [across(own, k) for k in range(1, n_kz)], axis=0)
    every = lax.all_gather(held, "pen", axis=0, tiled=False)

    updated, residual = pl.pallas_call(
        call(adjoint, chunk, per_owner),
        grid=(n_pen,),
        out_shape=[
            jax.ShapeDtypeStruct((per_owner, 2, depth, cells), BF16),
            jax.ShapeDtypeStruct((tile_dev, 2, cells), BF16),
        ],
        in_specs=[
            SMEM,
            pl.BlockSpec((4 * tiles, 2 * per_owner * depth), lambda p: (0, 0)),
            pl.BlockSpec((1, 2 * tiles, columns), lambda p: (p, 0, 0)),
            pl.BlockSpec((1, per_owner, 2, depth, columns), lambda p: (p, 0, 0, 0, 0)),
        ],
        out_specs=[
            pl.BlockSpec((per_owner, 2, depth, columns), lambda p: (0, 0, 0, p)),
            pl.BlockSpec((tile_dev, 2, columns), lambda p: (0, 0, p)),
        ],
        compiler_params=pltpu.CompilerParams(vmem_limit_bytes=48 << 20),
    )(where, table, every, incoming)
    return (updated, residual)


def solution(mesh):
    return jax.shard_map(
        body,
        mesh=mesh,
        in_specs=(
            P("kz", None, None, "pen"),
            P("kz", None, None),
            P("kz", None),
            P("kz", None),
            P(),
            P("kz"),
            P(("kz", "pen"), None, None),
        ),
        out_specs=(P(("kz", "pen"), None, None, None), P(("kz", "pen"), None, None)),
        check_vma=False,
    )
```

time: 246 us -> 116 us (0.47)
  waiting for transfers between devices: 153 us -> 5.04 us
  Pallas kernels: 0 us -> 76.4 us
  blocking collectives: 40.9 us -> 10.3 us
  local copies, waits for them, and re-layouts: 18 us -> 3.33 us
  between operations: 14.2 us -> 0.75 us
  starting transfers between devices: 5.34 us -> 18.4 us
  other arithmetic: 8.04 us -> 0.8 us
  matrix products: 5.89 us -> 0 us
    unnamed x2 -> x0, waiting for transfers between devices: 130 us -> none
    pallas_call x0 -> x5, Pallas kernels: none -> 76.4 us  [the longest x1 65.4 us: body(): pl.pallas_call(call(order_blocks, n_pen, per_owner), out_shape=jax.ShapeD...]
    all_gather x1, blocking collectives: 40.9 us -> 10.3 us  [body(): every = lax.all_gather(held, 'pen', axis=0, tiled=False)]
    all_to_all x1 -> x2, waiting for transfers between devices: 23 us -> 0.01 us  [the longest x1 0.01 us: body(): got = lax.all_to_all(sent, 'pen', split_axis=0, concat_axis=0, tiled=True)]
    ppermute x0 -> x6, starting transfers between devices: none -> 8.77 us  [across(): return lax.ppermute(value, 'kz', [(i, i ^ k) for i in range(n_kz)])]
    gather x7 -> x0, local copies, waits for them, and re-layouts: 6.9 us -> none  [the longest x1 2 us: body(): jnp.take(spectrum, inverse_map, axis=0)]
    dot_general x2 -> x0, matrix products: 5.89 us -> none  [the longest x1 3.85 us: body(): jnp.einsum('egi,egah->eaih', weight_table, used_flags, preferred_element_...]
    ppermute x0 -> x6, waiting for transfers between devices: none -> 5.03 us  [across(): return lax.ppermute(value, 'kz', [(i, i ^ k) for i in range(n_kz)])]
  transfers between devices with their start and end apart: 2 -> 8, of which waited for: 2 -> 3; matrix products, arithmetic and copies ran while one was open for 2% -> 1% of each run, Pallas kernels for 0% -> 61%
where the time goes in v1:
time: 116 us; the launch traced here: 115 us
  Pallas kernels  76.4 us (66%)
  starting transfers between devices  18.4 us (16%)
  blocking collectives  10.3 us (9%)
  waiting for transfers between devices  5.04 us (4%)
  local copies, waits for them, and re-layouts  3.33 us (3%)
    pallas_call x1, Pallas kernels, body(): pl.pallas_call(call(order_blocks, n_pen, per_owner), out_shape=jax.ShapeD...  65.4 us
    all_gather x1, blocking collectives, body(): every = lax.all_gather(held, 'pen', axis=0, tiled=False)  10.3 us
    ppermute x6, starting transfers between devices, across(): return lax.ppermute(value, 'kz', [(i, i ^ k) for i in range(n_kz)])  8.77 us
    pallas_call x1, Pallas kernels, body(): pl.pallas_call(call(adjoint, chunk, per_owner), grid=(n_pen,), out_shape=...  6.52 us
    all_to_all x1, starting transfers between devices, body(): got = lax.all_to_all(sent, 'pen', split_axis=0, concat_axis=0, tiled=True)  5.18 us
    ppermute x6, waiting for transfers between devices, across(): return lax.ppermute(value, 'kz', [(i, i ^ k) for i in range(n_kz)])  5.03 us
    all_to_all x1, starting transfers between devices, body(): lax.all_to_all(outgoing, 'pen', split_axis=0, concat_axis=0, tiled=True)  4.49 us
    unnamed x24, local copies, waits for them, and re-layouts  2.73 us
  transfers between devices with their start and end apart: 8, of which 3 were waited for; matrix products, arithmetic and copies ran while one was open for 1% of the time, Pallas kernels for 61%

profile of v1, /device:TPU:0, one launch (start us, length us, event | category | flops | bytes accessed | tf_op | source)
XLA Modules:
  0.0 115.1 jit_solution(13985954696523675157)
XLA Ops:
  0.6 5.2 %all-to-all-start = ((bf16[8,2,512]{2,1,0:T(2,128)(2,1)}), bf16[8,2,512]{2,1,0:T(2,128)(2,1)S(1)}, u32[]{:S(2)}, u32[]{:S(2)}) async-start(bf16[8,2,512]{2,1,0:T(2,128)(2,1)} %bitcast.15), calls=%async_computation | async-start | bytes 32768 | tf_op jit(solution)/shard_map/all_to_all | solution.py:154
  5.8 65.4 %shard_map.89 = bf16[16,2,64,512]{3,2,1,0:T(8,128)(2,1)} custom-call(s32[16]{0:T(128)} %refs_0_.1, bf16[16,2,64,512]{3,2,1,0:T(8,128)(2,1)} %refs_1_.5), custom_call_target="tpu_custom_call" | custom-call | tf_op jit(solution)/shard_map/pallas_call | solution.py:143
  71.3 0.0 all-to-all-done
  71.3 0.0 copy-start
  71.3 0.0 copy-start.1
  71.3 0.0 copy-start.3
  71.3 0.0 copy-start.4
  71.3 0.0 copy-start.8
  71.3 4.5 %all-to-all-start.1 = ((bf16[8,2,2,64,512]{4,3,2,1,0:T(8,128)(2,1)}), bf16[8,2,2,64,512]{4,3,2,1,0:T(8,128)(2,1)}, u32[]{:S(2)}, u32[]{:S(2)}) async-start(bf16[8,2,2,64,512]{4,3,2,1,0:T(8,128)(2,1)} %bitcast.12), calls=%async_computation.1 | async-start | bytes 4194304 | tf_op jit(solution)/shard_map/all_to_all | solution.py:151
  75.8 0.1 pad_add_fusion.refs_0_
  75.9 0.0 copy-done
  75.9 0.0 copy-done.1
  75.9 0.0 copy-done.3
  75.9 0.0 copy-done.4
  75.9 0.0 copy-done.8
  75.9 0.0 copy-start.6
  75.9 1.2 %shard_map.87 = (f32[16,512]{1,0:T(8,128)S(1)}, f32[16,512]{1,0:T(8,128)S(1)}, f32[16,512]{1,0:T(8,128)S(1)}, f32[16,512]{1,0:T(8,128)S(1)}) custom-call(s32[2]{0:T(128)S(1)} %pad_add_fusion.refs_0_, s32[16]{0:T(128)S(1)} %copy-done.8, s32[16,16]{1,0:T(8,128)S(1)} %copy-done.3, s32[16,16]{1,0:T(8,128)S(1)} %copy-done.4, bf16[16,16,64]{2,1,0:T(8,128)(2,1)S(1)} %copy-done.1, ...), custom_call_target="tpu_custom_call" | custom-call | tf_op jit(solution)/shard_map/pallas_call | solution.py:157
  77.2 0.0 copy-start.5
  77.2 0.6 copy-done.5
  77.8 1.6 %collective-permute-start = (f32[16,512]{1,0:T(8,128)S(1)}, f32[16,512]{1,0:T(8,128)S(1)}, u32[]{:S(2)}, u32[]{:S(2)}) collective-permute-start(f32[16,512]{1,0:T(8,128)S(1)} %get-tuple-element.7), channel_id=1, source_target_pairs={{0,8},{8,0},{16,24},{24,16},{1,9},{9,1},{17,25},{25,17},{2,10},{10... | collective-permute-start | bytes 98312 | tf_op jit(solution)/shard_map/ppermute | solution.py:167
  79.4 2.6 %collective-permute-start.1 = (f32[16,512]{1,0:T(8,128)S(1)}, f32[16,512]{1,0:T(8,128)S(1)}, u32[]{:S(2)}, u32[]{:S(2)}) collective-permute-start(f32[16,512]{1,0:T(8,128)S(1)} %get-tuple-element.8), channel_id=1, source_target_pairs={{0,16},{8,24},{16,0},{24,8},{1,17},{9,25},{17,1},{25,9},{2,18},{10... | collective-permute-start | bytes 98312 | tf_op jit(solution)/shard_map/ppermute | solution.py:167
  82.0 0.2 collective-permute-start.2
  82.2 0.6 copy.11
  82.8 0.0 collective-permute-done.refs_1_
  82.8 0.0 copy-start.9
  82.8 1.9 %collective-permute-done.1.refs_2_ = f32[16,512]{1,0:T(8,128)S(1)} collective-permute-done((f32[16,512]{1,0:T(8,128)S(1)}, f32[16,512]{1,0:T(8,128)S(1)}, u32[]{:S(2)}, u32[]{:S(2)}) %collective-permute-start.1) | collective-permute-done | bytes 32800 | tf_op jit(solution)/shard_map/ppermute | solution.py:167
  84.7 0.0 copy-start.10
  84.7 2.9 %collective-permute-done.2.refs_3_ = f32[16,512]{1,0:T(8,128)S(1)} collective-permute-done((f32[16,512]{1,0:T(8,128)S(1)}, f32[16,512]{1,0:T(8,128)S(1)}, u32[]{:S(2)}, u32[]{:S(2)}) %collective-permute-start.2) | collective-permute-done | bytes 32800 | tf_op jit(solution)/shard_map/ppermute | solution.py:167
  87.7 0.0 copy-start.11
  87.7 0.0 copy-done.9
  87.7 0.0 copy-done.10
  87.7 0.6 copy-done.11
  88.3 1.4 %shard_map.88 = bf16[16,512]{1,0:T(8,128)(2,1)} custom-call(f32[16,512]{1,0:T(8,128)} %copy-done.5, f32[16,512]{1,0:T(8,128)} %copy-done.9, f32[16,512]{1,0:T(8,128)} %copy-done.10, f32[16,512]{1,0:T(8,128)} %copy-done.11, bf16[16,512]{1,0:T(8,128)(2,1)} %bitcast.13), custom_call_target="tpu_custom_call" | custom-call | tf_op jit(solution)/shard_map/pallas_call | solution.py:178
  89.7 0.4 collective-permute-start.5
  90.1 0.0 collective-permute-start.4
  90.1 4.0 %collective-permute-start.3 = (bf16[16,512]{1,0:T(8,128)(2,1)}, bf16[16,512]{1,0:T(8,128)(2,1)S(1)}, u32[]{:S(2)}, u32[]{:S(2)}) collective-permute-start(bf16[16,512]{1,0:T(8,128)(2,1)} %shard_map.88), channel_id=1, source_target_pairs={{0,8},{8,0},{16,24},{24,16},{1,9},{9,1},{17,25},{25,17},{2,10},{10... | collective-permute-start | bytes 49160 | tf_op jit(solution)/shard_map/ppermute | solution.py:167
  94.1 0.0 copy-done.6
  94.1 1.8 %shard_map.86.refs_1_ = bf16[128,256]{1,0:T(8,128)(2,1)} custom-call(s32[2]{0:T(128)} %copy-done.6, s32[16]{0:T(128)} %refs_1_.4, s32[16]{0:T(128)} %refs_0_.1, s32[16,16]{1,0:T(8,128)} %refs_2_.3, s32[16,16]{1,0:T(8,128)} %refs_3_.3, bf16[16,16,64]{2,1,0:T(8,128)(2,1)} %refs_4_.3), custom_call_target="tpu_custom_call" | custom-call | tf_op jit(solution)/shard_map/pallas_call | solution.py:170
  95.9 0.0 collective-permute-done.5
  95.9 0.0 collective-permute-done.4
  95.9 0.2 collective-permute-done.3
  96.1 0.7 pad_maximum_fusion
  96.8 10.3 %all-gather = bf16[512,512]{1,0:T(8,128)(2,1)S(1)} all-gather(bf16[64,512]{1,0:T(8,128)(2,1)S(1)} %pad_maximum_fusion), channel_id=2, replica_groups=mesh['kz'=4,'pen'=8] {'pen'}, dimensions={0}, use_global_device_ids=true | all-gather | bytes 589824 | tf_op jit(solution)/shard_map/all_gather | solution.py:186
  107.1 0.0 all-to-all-done.1.refs_3_
  107.1 0.0 copy-start.2
  107.1 0.8 copy-done.2
  107.9 0.6 copy-done.7
  108.5 6.5 %shard_map.90 = (bf16[2,2,64,4096]{3,2,1,0:T(8,128)(2,1)}, bf16[1,2,4096]{2,1,0:T(2,128)(2,1)}) custom-call(s32[2]{0:T(128)S(1)} %copy-done.7, bf16[128,256]{1,0:T(8,128)(2,1)S(1)} %copy-done.2, bf16[8,64,512]{2,1,0:T(8,128)(2,1)S(1)} %bitcast.11, bf16[8,2,2,64,512]{4,3,2,1,0:T(8,128)(2,1)} %all-to-all-done.1.refs_3_), custom_call_target="tpu_custom_call" | custom-call | tf_op jit(solution)/shard_map/pallas_call | solution.py:188
  (1 shorter events, 0.0 us)
Async XLA Ops:
  0.6 70.6 %all-to-all-start = ((bf16[8,2,512]{2,1,0:T(2,128)(2,1)}), bf16[8,2,512]{2,1,0:T(2,128)(2,1)S(1)}, u32[]{:S(2)}, u32[]{:S(2)}) async-start(bf16[8,2,512]{2,1,0:T(2,128)(2,1)} %bitcast.15), calls=%async_computation | async-start | bytes 32768 | tf_op jit(solution)/shard_map/all_to_all | solution.py:154
  71.3 4.6 %copy-start = (bf16[16,2,64,512]{3,2,1,0:T(8,128)(2,1)S(1)}, bf16[16,2,64,512]{3,2,1,0:T(8,128)(2,1)}, u32[]{:S(2)}) copy-start(bf16[16,2,64,512]{3,2,1,0:T(8,128)(2,1)} %refs_1_.5) | copy-start | bytes 6291460
  71.3 4.6 %copy-start.1 = (bf16[16,16,64]{2,1,0:T(8,128)(2,1)S(1)}, bf16[16,16,64]{2,1,0:T(8,128)(2,1)}, u32[]{:S(2)}) copy-start(bf16[16,16,64]{2,1,0:T(8,128)(2,1)} %refs_4_.3) | copy-start | bytes 98308
  71.3 4.6 %copy-start.3 = (s32[16,16]{1,0:T(8,128)S(1)}, s32[16,16]{1,0:T(8,128)}, u32[]{:S(2)}) copy-start(s32[16,16]{1,0:T(8,128)} %refs_2_.3) | copy-start | bytes 3076
  71.3 4.6 %copy-start.4 = (s32[16,16]{1,0:T(8,128)S(1)}, s32[16,16]{1,0:T(8,128)}, u32[]{:S(2)}) copy-start(s32[16,16]{1,0:T(8,128)} %refs_3_.3) | copy-start | bytes 3076
  71.3 4.6 %copy-start.8 = (s32[16]{0:T(128)S(1)}, s32[16]{0:T(128)}, u32[]{:S(2)}) copy-start(s32[16]{0:T(128)} %refs_1_.4) | copy-start | bytes 196
  71.3 35.8 %all-to-all-start.1 = ((bf16[8,2,2,64,512]{4,3,2,1,0:T(8,128)(2,1)}), bf16[8,2,2,64,512]{4,3,2,1,0:T(8,128)(2,1)}, u32[]{:S(2)}, u32[]{:S(2)}) async-start(bf16[8,2,2,64,512]{4,3,2,1,0:T(8,128)(2,1)} %bitcast.12), calls=%async_computation.1 | async-start | bytes 4194304 | tf_op jit(solution)/shard_map/all_to_all | solution.py:151
  75.9 18.2 %copy-start.6 = (s32[2]{0:T(128)}, s32[2]{0:T(128)S(1)}, u32[]{:S(2)}) copy-start(s32[2]{0:T(128)S(1)} %pad_add_fusion.refs_0_) | copy-start | bytes 28
  77.2 0.6 copy-start.5
  77.8 5.0 %collective-permute-start = (f32[16,512]{1,0:T(8,128)S(1)}, f32[16,512]{1,0:T(8,128)S(1)}, u32[]{:S(2)}, u32[]{:S(2)}) collective-permute-start(f32[16,512]{1,0:T(8,128)S(1)} %get-tuple-element.7), channel_id=1, source_target_pairs={{0,8},{8,0},{16,24},{24,16},{1,9},{9,1},{17,25},{25,17},{2,10},{10... | collective-permute-start | bytes 98312 | tf_op jit(solution)/shard_map/ppermute | solution.py:167
  79.4 5.4 %collective-permute-start.1 = (f32[16,512]{1,0:T(8,128)S(1)}, f32[16,512]{1,0:T(8,128)S(1)}, u32[]{:S(2)}, u32[]{:S(2)}) collective-permute-start(f32[16,512]{1,0:T(8,128)S(1)} %get-tuple-element.8), channel_id=1, source_target_pairs={{0,16},{8,24},{16,0},{24,8},{1,17},{9,25},{17,1},{25,9},{2,18},{10... | collective-permute-start | bytes 98312 | tf_op jit(solution)/shard_map/ppermute | solution.py:167
  82.0 5.7 %collective-permute-start.2 = (f32[16,512]{1,0:T(8,128)S(1)}, f32[16,512]{1,0:T(8,128)S(1)}, u32[]{:S(2)}, u32[]{:S(2)}) collective-permute-start(f32[16,512]{1,0:T(8,128)S(1)} %get-tuple-element.9), channel_id=1, source_target_pairs={{0,24},{8,16},{16,8},{24,0},{1,25},{9,17},{17,9},{25,1},{2,26},{10... | collective-permute-start | bytes 98312 | tf_op jit(solution)/shard_map/ppermute | solution.py:167
  82.8 4.9 %copy-start.9 = (f32[16,512]{1,0:T(8,128)}, f32[16,512]{1,0:T(8,128)S(1)}, u32[]{:S(2)}) copy-start(f32[16,512]{1,0:T(8,128)S(1)} %collective-permute-done.refs_1_) | copy-start | bytes 98308
  84.7 3.0 %copy-start.10 = (f32[16,512]{1,0:T(8,128)}, f32[16,512]{1,0:T(8,128)S(1)}, u32[]{:S(2)}) copy-start(f32[16,512]{1,0:T(8,128)S(1)} %collective-permute-done.1.refs_2_) | copy-start | bytes 98308
  87.7 0.6 copy-start.11
  89.7 6.2 %collective-permute-start.5 = (bf16[16,512]{1,0:T(8,128)(2,1)}, bf16[16,512]{1,0:T(8,128)(2,1)S(1)}, u32[]{:S(2)}, u32[]{:S(2)}) collective-permute-start(bf16[16,512]{1,0:T(8,128)(2,1)} %shard_map.88), channel_id=1, source_target_pairs={{0,24},{8,16},{16,8},{24,0},{1,25},{9,17},{17,9},{25,1},{2,26},{10... | collective-permute-start | bytes 49160 | tf_op jit(solution)/shard_map/ppermute | solution.py:167
  90.1 5.8 %collective-permute-start.4 = (bf16[16,512]{1,0:T(8,128)(2,1)}, bf16[16,512]{1,0:T(8,128)(2,1)S(1)}, u32[]{:S(2)}, u32[]{:S(2)}) collective-permute-start(bf16[16,512]{1,0:T(8,128)(2,1)} %shard_map.88), channel_id=1, source_target_pairs={{0,16},{8,24},{16,0},{24,8},{1,17},{9,25},{17,1},{25,9},{2,18},{10... | collective-permute-start | bytes 49160 | tf_op jit(solution)/shard_map/ppermute | solution.py:167
  90.1 5.9 %collective-permute-start.3 = (bf16[16,512]{1,0:T(8,128)(2,1)}, bf16[16,512]{1,0:T(8,128)(2,1)S(1)}, u32[]{:S(2)}, u32[]{:S(2)}) collective-permute-start(bf16[16,512]{1,0:T(8,128)(2,1)} %shard_map.88), channel_id=1, source_target_pairs={{0,8},{8,0},{16,24},{24,16},{1,9},{9,1},{17,25},{25,17},{2,10},{10... | collective-permute-start | bytes 49160 | tf_op jit(solution)/shard_map/ppermute | solution.py:167
  107.1 0.8 copy-start.2
  107.9 0.6 copy-start.7

commit v2 on v1

--- a/solution.py
+++ b/solution.py
@@ -41,13 +41,14 @@
     return (place * tiles_per_tilt + within) ^ flip
 
 
-def forward(n_kz, chunk, tiles_per_tilt, where_ref, tilt_pos_ref, tilt_ref, within_ref,
-            weights_ref, spectrum_ref, *rest):
+def forward(n_kz, chunk, tiles_per_tilt, tilt_pos_ref, tilt_ref, within_ref, weights_ref,
+            spectrum_ref, *rest):
     outs, table = rest[:n_kz], rest[n_kz]
     blocks, pairs, depth = weights_ref.shape
     columns = spectrum_ref.shape[3]
     tiles = n_kz * chunk
-    slot = slots(tilt_pos_ref, tilt_ref[...], within_ref[...], tiles_per_tilt, where_ref[0] * chunk)
+    flip = lax.axis_index("kz") * chunk
+    slot = slots(tilt_pos_ref, tilt_ref[...], within_ref[...], tiles_per_tilt, flip)
     rows = lax.broadcasted_iota(I32, (tiles, pairs), 0)
     for b in range(blocks):
         hot = jnp.where(slot[b : b + 1, :] == rows, 1.0, 0.0).astype(BF16)
@@ -65,11 +66,11 @@
             outs[k][c * chunk : (c + 1) * chunk, :] = total[k * chunk : (k + 1) * chunk]
 
 
-def adjoint_table(n_kz, chunk, n_pen, per_owner, tiles_per_tilt, where_ref, tilt_pos_ref, owner_ref,
+def adjoint_table(n_kz, chunk, n_pen, per_owner, tiles_per_tilt, tilt_pos_ref, owner_ref,
                   tilt_ref, within_ref, weights_ref, out_ref, mine_ref, slot_ref):
     blocks, pairs, depth = weights_ref.shape
     rows_all = n_kz * 2 * chunk
-    pen = where_ref[1]
+    pen = lax.axis_index("pen")
     seen = jnp.int32(0)
     for b in range(blocks):
         hit = owner_ref[b] == pen
@@ -79,8 +80,8 @@
             mine_ref[seen] = b
 
         seen = seen + hit.astype(I32)
-    slot = slots(tilt_pos_ref, tilt_ref[...], within_ref[...], tiles_per_tilt, where_ref[0] * chunk)
-    slot_ref[...] = slot
+    flip = lax.axis_index("kz") * chunk
+    slot_ref[...] = slots(tilt_pos_ref, tilt_ref[...], within_ref[...], tiles_per_tilt, flip)
     rows = lax.broadcasted_iota(I32, (rows_all, pairs), 0)
     for r in range(per_owner):
         b = mine_ref[r]
@@ -95,32 +96,48 @@
             out_ref[rows_all:, first : first + depth] = lo
 
 
-def residual_chunk(n_kz, *refs):
-    parts, measured_ref, out_ref = refs[:n_kz], refs[n_kz], refs[n_kz + 1]
-    total = parts[0][...]
-    for part in parts[1:]:
-        total = total + part[...]
-    out_ref[...] = (total - measured_ref[...].astype(F32)).astype(BF16)
-
-
-def adjoint(chunk, per_owner, where_ref, table_ref, tiles_ref, blocks_ref, out_ref, residual_ref):
-    depth = blocks_ref.shape[3]
-    r_tiles = tiles_ref[0]
-    rows = r_tiles.shape[0]
-    both = jnp.concatenate([r_tiles, r_tiles], axis=0)
-    step = lax.dot_general(
-        table_ref[...], both, (((0,), (0,)), ((), ())), preferred_element_type=F32
-    )
-    for r in range(per_owner):
-        for c in range(2):
-            first = (c * per_owner + r) * depth
-            out_ref[r, c] = (blocks_ref[0, r, c].astype(F32) + step[first : first + depth]).astype(BF16)
+def adjoint(n_pen, chunk, per_owner, table_ref, tiles_ref, blocks_ref, out_ref, residual_ref,
+            table, tiles, held, made, table_sem, tile_sems, in_sems, out_sems):
+    depth, columns = blocks_ref.shape[3:]
+    rows = tiles_ref.shape[1]
+    get_table = pltpu.make_async_copy(table_ref, table, table_sem)
+    get_table.start()
+    gets, puts = [], []
+    for p in range(n_pen):
+        gets.append(
+            (
+                pltpu.make_async_copy(tiles_ref.at[p], tiles.at[p], tile_sems.at[p]),
+                pltpu.make_async_copy(blocks_ref.at[p], held.at[p], in_sems.at[p]),
+            )
+        )
+        for get in gets[p]:
+            get.start()
     pick_row = lax.broadcasted_iota(I32, (16, rows), 0)
     pick_at = lax.broadcasted_iota(I32, (16, rows), 1)
-    pick = jnp.where(pick_at == pick_row * chunk + where_ref[1], 1.0, 0.0)
+    pick = jnp.where(pick_at == pick_row * chunk + lax.axis_index("pen"), 1.0, 0.0)
     pick = jnp.where(pick_row < 2, pick, 0.0).astype(BF16)
-    own = jnp.dot(pick, r_tiles, preferred_element_type=F32)
-    residual_ref[0] = own[:2].astype(BF16)
+    get_table.wait()
+    for p in range(n_pen):
+        gets[p][0].wait()
+        here = tiles[p]
+        own = jnp.dot(pick, here, preferred_element_type=F32)
+        residual_ref[0, :, p * columns : (p + 1) * columns] = own[:2].astype(BF16)
+        step = lax.dot_general(
+            table[...],
+            jnp.concatenate([here, here], axis=0),
+            (((0,), (0,)), ((), ())),
+            preferred_element_type=F32,
+        )
+        gets[p][1].wait()
+        for r in range(per_owner):
+            for c in range(2):
+                first = (c * per_owner + r) * depth
+                made[p, r, c] = (held[p, r, c].astype(F32) + step[first : first + depth]).astype(BF16)
+        to = out_ref.at[:, :, :, pl.ds(p * columns, columns)]
+        puts.append(pltpu.make_async_copy(made.at[p], to, out_sems.at[p]))
+        puts[p].start()
+    for put in puts:
+        put.wait()
 
 
 def body(spectrum, depth_weights, pair_tilt, pair_tile_within, tilt_pos, owner, measured):
@@ -133,7 +150,6 @@
     chunk = tile_dev * n_pen
     tiles = chunk * n_kz
     tiles_per_tilt = tiles // tilt_pos.shape[0]
-    where = jnp.stack([lax.axis_index("kz"), lax.axis_index("pen")]).astype(I32)
 
     def call(kernel, *static):
         def bound(*refs):
@@ -144,7 +160,7 @@
         call(order_blocks, n_pen, per_owner),
         out_shape=jax.ShapeDtypeStruct(spectrum.shape, BF16),
         in_specs=[SMEM, ANY],
-        out_specs=ANY,
+        out_specs=VMEM,
         scratch_shapes=[pltpu.SMEM((n_pen,), I32), pltpu.SemaphoreType.DMA((blocks,))],
     )(owner, spectrum)
     outgoing = outgoing.reshape(n_pen, per_owner, 2, depth, columns)
@@ -157,11 +173,11 @@
     parts = pl.pallas_call(
         call(forward, n_kz, chunk, tiles_per_tilt),
         out_shape=[jax.ShapeDtypeStruct((2 * chunk, columns), F32)] * n_kz,
-        in_specs=[SMEM, SMEM, VMEM, VMEM, VMEM, VMEM],
+        in_specs=[SMEM, VMEM, VMEM, VMEM, VMEM],
         out_specs=[VMEM] * n_kz,
         scratch_shapes=[pltpu.VMEM((2 * tiles, blocks * depth), BF16)],
         compiler_params=pltpu.CompilerParams(vmem_limit_bytes=48 << 20),
-    )(where, tilt_pos, pair_tilt, pair_tile_within, depth_weights, spectrum)
+    )(tilt_pos, pair_tilt, pair_tile_within, depth_weights, spectrum)
 
     def across(value, k):
         return lax.ppermute(value, "kz", [(i, i ^ k) for i in range(n_kz)])
@@ -170,40 +186,40 @@
     table = pl.pallas_call(
         call(adjoint_table, n_kz, chunk, n_pen, per_owner, tiles_per_tilt),
         out_shape=jax.ShapeDtypeStruct((4 * tiles, 2 * per_owner * depth), BF16),
-        in_specs=[SMEM, SMEM, SMEM, VMEM, VMEM, VMEM],
+        in_specs=[SMEM, SMEM, VMEM, VMEM, VMEM],
         out_specs=VMEM,
         scratch_shapes=[pltpu.SMEM((per_owner,), I32), pltpu.VMEM((blocks, pairs), I32)],
-    )(where, tilt_pos, owner, pair_tilt, pair_tile_within, depth_weights)
-
-    own = pl.pallas_call(
-        call(residual_chunk, n_kz),
-        out_shape=jax.ShapeDtypeStruct((2 * chunk, columns), BF16),
-        in_specs=[VMEM] * (n_kz + 1),
-        out_specs=VMEM,
-    )(*summed, measured_rows)
+    )(tilt_pos, owner, pair_tilt, pair_tile_within, depth_weights)
+
+    total = summed[0]
+    for part in summed[1:]:
+        total = total + part
+    own = (total - measured_rows.astype(F32)).astype(BF16)
 
     held = jnp.concatenate([own] + [across(own, k) for k in range(1, n_kz)], axis=0)
     every = lax.all_gather(held, "pen", axis=0, tiled=False)
 
+    piece = (n_pen, per_owner, 2, depth, columns)
     updated, residual = pl.pallas_call(
-        call(adjoint, chunk, per_owner),
-        grid=(n_pen,),
+        call(adjoint, n_pen, chunk, per_owner),
         out_shape=[
             jax.ShapeDtypeStruct((per_owner, 2, depth, cells), BF16),
             jax.ShapeDtypeStruct((tile_dev, 2, cells), BF16),
         ],
-        in_specs=[
-            SMEM,
-            pl.BlockSpec((4 * tiles, 2 * per_owner * depth), lambda p: (0, 0)),
-            pl.BlockSpec((1, 2 * tiles, columns), lambda p: (p, 0, 0)),
-            pl.BlockSpec((1, per_owner, 2, depth, columns), lambda p: (p, 0, 0, 0, 0)),
+        in_specs=[ANY, ANY, ANY],
+        out_specs=[ANY, VMEM],
+        scratch_shapes=[
+            pltpu.VMEM(table.shape, BF16),
+            pltpu.VMEM(every.shape, BF16),
+            pltpu.VMEM(piece, BF16),
+            pltpu.VMEM(piece, BF16),
+            pltpu.SemaphoreType.DMA,
+            pltpu.SemaphoreType.DMA((n_pen,)),
+            pltpu.SemaphoreType.DMA((n_pen,)),
+            pltpu.SemaphoreType.DMA((n_pen,)),
         ],
-        out_specs=[
-            pl.BlockSpec((per_owner, 2, depth, columns), lambda p: (0, 0, 0, p)),
-            pl.BlockSpec((tile_dev, 2, columns), lambda p: (0, 0, p)),
-        ],
-        compiler_params=pltpu.CompilerParams(vmem_limit_bytes=48 << 20),
-    )(where, table, every, incoming)
+        compiler_params=pltpu.CompilerParams(vmem_limit_bytes=60 << 20),
+    )(table, every, incoming)
     return (updated, residual)
 
 

time: 116 us -> 52.7 us (0.45)
  Pallas kernels: 76.4 us -> 12.2 us
  blocking collectives: 10.3 us -> 14.2 us
  local copies, waits for them, and re-layouts: 3.33 us -> 0.02 us
  waiting for transfers between devices: 5.04 us -> 6.49 us
    pallas_call x1, Pallas kernels: 65.4 us -> 3.74 us  [body(): pl.pallas_call(call(order_blocks, n_pen, per_owner), out_shape=jax.ShapeD...]
    all_gather x1, blocking collectives: 10.3 us -> 14.2 us  [body(): every = lax.all_gather(held, 'pen', axis=0, tiled=False)]
    unnamed x24 -> x10, local copies, waits for them, and re-layouts: 2.73 us -> 0.02 us
    pallas_call x2 -> x1, Pallas kernels: 7.94 us -> 5.44 us  [body(): pl.pallas_call(call(adjoint, n_pen, chunk, per_owner), out_shape=[jax.Sha...]
  transfers between devices with their start and end apart: 8 -> 8, of which waited for: 3 -> 3; matrix products, arithmetic and copies ran while one was open for 1% -> 0% of each run, Pallas kernels for 61% -> 13%
where the time goes in v2:
time: 52.7 us; the launch traced here: 52.3 us
  starting transfers between devices  18.6 us (35%)
  blocking collectives  14.2 us (27%)
  Pallas kernels  12.2 us (23%)
  waiting for transfers between devices  6.49 us (12%)
  between operations  0.74 us (1%)
    all_gather x1, blocking collectives, body(): every = lax.all_gather(held, 'pen', axis=0, tiled=False)  14.2 us
    ppermute x6, starting transfers between devices, across(): return lax.ppermute(value, 'kz', [(i, i ^ k) for i in range(n_kz)])  8.88 us
    ppermute x6, waiting for transfers between devices, across(): return lax.ppermute(value, 'kz', [(i, i ^ k) for i in range(n_kz)])  5.47 us
    pallas_call x1, Pallas kernels, body(): pl.pallas_call(call(adjoint, n_pen, chunk, per_owner), out_shape=[jax.Sha...  5.44 us
    all_to_all x1, starting transfers between devices, body(): got = lax.all_to_all(sent, 'pen', split_axis=0, concat_axis=0, tiled=True)  5.18 us
    all_to_all x1, starting transfers between devices, body(): lax.all_to_all(outgoing, 'pen', split_axis=0, concat_axis=0, tiled=True)  4.49 us
    pallas_call x1, Pallas kernels, body(): pl.pallas_call(call(order_blocks, n_pen, per_owner), out_shape=jax.ShapeD...  3.74 us
    pallas_call x1, Pallas kernels, body(): pl.pallas_call(call(adjoint_table, n_kz, chunk, n_pen, per_owner, tiles_p...  1.79 us
  transfers between devices with their start and end apart: 8, of which 3 were waited for; matrix products, arithmetic and copies ran while one was open for 0% of the time, Pallas kernels for 13%

profile of v2, /device:TPU:0, one launch (start us, length us, event | category | flops | bytes accessed | tf_op | source)
XLA Modules:
  0.0 52.3 jit_solution(10417046134242267362)
XLA Ops:
  0.6 5.2 %all-to-all-start = ((bf16[8,2,512]{2,1,0:T(2,128)(2,1)}), bf16[8,2,512]{2,1,0:T(2,128)(2,1)S(1)}, u32[]{:S(2)}, u32[]{:S(2)}) async-start(bf16[8,2,512]{2,1,0:T(2,128)(2,1)} %bitcast.13), calls=%async_computation | async-start | bytes 32768 | tf_op jit(solution)/shard_map/all_to_all | solution.py:170
  5.8 3.7 %shard_map.88 = bf16[16,2,64,512]{3,2,1,0:T(8,128)(2,1)} custom-call(s32[16]{0:T(128)} %refs_0_.5, bf16[16,2,64,512]{3,2,1,0:T(8,128)(2,1)} %refs_1_.5), custom_call_target="tpu_custom_call" | custom-call | tf_op jit(solution)/shard_map/pallas_call | solution.py:159
  9.6 1.0 %all-to-all-done = bf16[8,2,512]{2,1,0:T(2,128)(2,1)S(1)} async-done(((bf16[8,2,512]{2,1,0:T(2,128)(2,1)}), bf16[8,2,512]{2,1,0:T(2,128)(2,1)S(1)}, u32[]{:S(2)}, u32[]{:S(2)}) %all-to-all-start) | async-done | bytes 16416 | tf_op jit(solution)/shard_map/all_to_all | solution.py:170
  10.6 0.0 copy-start
  10.6 0.0 copy-start.1
  10.6 0.0 copy-start.2
  10.6 0.0 copy-start.3
  10.6 0.0 copy-start.4
  10.6 4.5 %all-to-all-start.1 = ((bf16[8,2,2,64,512]{4,3,2,1,0:T(8,128)(2,1)}), bf16[8,2,2,64,512]{4,3,2,1,0:T(8,128)(2,1)}, u32[]{:S(2)}, u32[]{:S(2)}) async-start(bf16[8,2,2,64,512]{4,3,2,1,0:T(8,128)(2,1)} %bitcast.11), calls=%async_computation.1 | async-start | bytes 4194304 | tf_op jit(solution)/shard_map/all_to_all | solution.py:167
  15.1 0.0 copy-done
  15.1 0.0 copy-done.1
  15.1 0.0 copy-done.2
  15.1 0.0 copy-done.3
  15.1 0.0 copy-done.4
  15.1 1.2 %shard_map.87 = (f32[16,512]{1,0:T(8,128)S(1)}, f32[16,512]{1,0:T(8,128)S(1)}, f32[16,512]{1,0:T(8,128)S(1)}, f32[16,512]{1,0:T(8,128)S(1)}) custom-call(s32[16]{0:T(128)S(1)} %copy-done.4, s32[16,16]{1,0:T(8,128)S(1)} %copy-done.2, s32[16,16]{1,0:T(8,128)S(1)} %copy-done.3, bf16[16,16,64]{2,1,0:T(8,128)(2,1)S(1)} %copy-done.1, ...), custom_call_target="tpu_custom_call" | custom-call | tf_op jit(solution)/shard_map/pallas_call | solution.py:173
  16.4 1.6 %collective-permute-start = (f32[16,512]{1,0:T(8,128)S(1)}, f32[16,512]{1,0:T(8,128)S(1)}, u32[]{:S(2)}, u32[]{:S(2)}) collective-permute-start(f32[16,512]{1,0:T(8,128)S(1)} %get-tuple-element.7), channel_id=1, source_target_pairs={{0,8},{8,0},{16,24},{24,16},{1,9},{9,1},{17,25},{25,17},{2,10},{10... | collective-permute-start | bytes 98312 | tf_op jit(solution)/shard_map/ppermute | solution.py:183
  18.0 2.6 %collective-permute-start.1 = (f32[16,512]{1,0:T(8,128)S(1)}, f32[16,512]{1,0:T(8,128)S(1)}, u32[]{:S(2)}, u32[]{:S(2)}) collective-permute-start(f32[16,512]{1,0:T(8,128)S(1)} %get-tuple-element.8), channel_id=1, source_target_pairs={{0,16},{8,24},{16,0},{24,8},{1,17},{9,25},{17,1},{25,9},{2,18},{10... | collective-permute-start | bytes 98312 | tf_op jit(solution)/shard_map/ppermute | solution.py:183
  20.6 0.2 collective-permute-start.2
  20.8 0.0 collective-permute-done
  20.8 2.6 %collective-permute-done.1 = f32[16,512]{1,0:T(8,128)S(1)} collective-permute-done((f32[16,512]{1,0:T(8,128)S(1)}, f32[16,512]{1,0:T(8,128)S(1)}, u32[]{:S(2)}, u32[]{:S(2)}) %collective-permute-start.1) | collective-permute-done | bytes 32800 | tf_op jit(solution)/shard_map/ppermute | solution.py:183
  23.4 2.9 %collective-permute-done.2 = f32[16,512]{1,0:T(8,128)S(1)} collective-permute-done((f32[16,512]{1,0:T(8,128)S(1)}, f32[16,512]{1,0:T(8,128)S(1)}, u32[]{:S(2)}, u32[]{:S(2)}) %collective-permute-start.2) | collective-permute-done | bytes 32800 | tf_op jit(solution)/shard_map/ppermute | solution.py:183
  26.3 0.5 collective-permute-start.5
  26.8 0.0 collective-permute-start.4
  26.8 4.0 %collective-permute-start.3 = (bf16[16,512]{1,0:T(8,128)(2,1)S(1)}, bf16[16,512]{1,0:T(8,128)(2,1)S(1)}, u32[]{:S(2)}, u32[]{:S(2)}) collective-permute-start(bf16[16,512]{1,0:T(8,128)(2,1)S(1)} %fusion), channel_id=1, source_target_pairs={{0,8},{8,0},{16,24},{24,16},{1,9},{9,1},{17,25},{25,17},{2,10},{10... | collective-permute-start | bytes 49160 | tf_op jit(solution)/shard_map/ppermute | solution.py:183
  30.7 1.8 %shard_map.86.refs_0_ = bf16[128,256]{1,0:T(8,128)(2,1)} custom-call(s32[16]{0:T(128)} %refs_0_.4, s32[16]{0:T(128)} %refs_0_.5, s32[16,16]{1,0:T(8,128)} %refs_1_.4, s32[16,16]{1,0:T(8,128)} %refs_2_.3, bf16[16,16,64]{2,1,0:T(8,128)(2,1)} %refs_3_.3), custom_call_target="tpu_custom_call" | custom-call | tf_op jit(solution)/shard_map/pallas_call | solution.py:186
  32.5 0.0 collective-permute-done.5
  32.5 0.0 collective-permute-done.4
  32.5 0.0 collective-permute-done.3
  32.6 14.2 %all-gather = bf16[512,512]{1,0:T(8,128)(2,1)} all-gather(bf16[64,512]{1,0:T(8,128)(2,1)S(1)} %pad_maximum_fusion), channel_id=2, replica_groups=mesh['kz'=4,'pen'=8] {'pen'}, dimensions={0}, use_global_device_ids=true | all-gather | bytes 589824 | tf_op jit(solution)/shard_map/all_gather | solution.py:200
  46.8 0.0 all-to-all-done.1.refs_2_
  46.8 5.4 %shard_map.89 = (bf16[2,2,64,4096]{3,2,1,0:T(8,128)(2,1)}, bf16[1,2,4096]{2,1,0:T(2,128)(2,1)}) custom-call(bf16[128,256]{1,0:T(8,128)(2,1)} %shard_map.86.refs_0_, bf16[8,64,512]{2,1,0:T(8,128)(2,1)} %bitcast.12, bf16[8,2,2,64,512]{4,3,2,1,0:T(8,128)(2,1)} %all-to-all-done.1.refs_2_), custom_call_target="tpu_custom_call" | custom-call | tf_op jit(solution)/shard_map/pallas_call | solution.py:203
  (3 shorter events, 0.0 us)
Async XLA Ops:
  0.6 9.9 %all-to-all-start = ((bf16[8,2,512]{2,1,0:T(2,128)(2,1)}), bf16[8,2,512]{2,1,0:T(2,128)(2,1)S(1)}, u32[]{:S(2)}, u32[]{:S(2)}) async-start(bf16[8,2,512]{2,1,0:T(2,128)(2,1)} %bitcast.13), calls=%async_computation | async-start | bytes 32768 | tf_op jit(solution)/shard_map/all_to_all | solution.py:170
  10.6 4.5 %copy-start = (bf16[16,2,64,512]{3,2,1,0:T(8,128)(2,1)S(1)}, bf16[16,2,64,512]{3,2,1,0:T(8,128)(2,1)}, u32[]{:S(2)}) copy-start(bf16[16,2,64,512]{3,2,1,0:T(8,128)(2,1)} %refs_1_.5) | copy-start | bytes 6291460
  10.6 4.5 %copy-start.1 = (bf16[16,16,64]{2,1,0:T(8,128)(2,1)S(1)}, bf16[16,16,64]{2,1,0:T(8,128)(2,1)}, u32[]{:S(2)}) copy-start(bf16[16,16,64]{2,1,0:T(8,128)(2,1)} %refs_3_.3) | copy-start | bytes 98308
  10.6 4.5 %copy-start.2 = (s32[16,16]{1,0:T(8,128)S(1)}, s32[16,16]{1,0:T(8,128)}, u32[]{:S(2)}) copy-start(s32[16,16]{1,0:T(8,128)} %refs_1_.4) | copy-start | bytes 3076
  10.6 4.5 %copy-start.3 = (s32[16,16]{1,0:T(8,128)S(1)}, s32[16,16]{1,0:T(8,128)}, u32[]{:S(2)}) copy-start(s32[16,16]{1,0:T(8,128)} %refs_2_.3) | copy-start | bytes 3076
  10.6 4.6 %copy-start.4 = (s32[16]{0:T(128)S(1)}, s32[16]{0:T(128)}, u32[]{:S(2)}) copy-start(s32[16]{0:T(128)} %refs_0_.4) | copy-start | bytes 196
  10.6 36.2 %all-to-all-start.1 = ((bf16[8,2,2,64,512]{4,3,2,1,0:T(8,128)(2,1)}), bf16[8,2,2,64,512]{4,3,2,1,0:T(8,128)(2,1)}, u32[]{:S(2)}, u32[]{:S(2)}) async-start(bf16[8,2,2,64,512]{4,3,2,1,0:T(8,128)(2,1)} %bitcast.11), calls=%async_computation.1 | async-start | bytes 4194304 | tf_op jit(solution)/shard_map/all_to_all | solution.py:167
  16.4 4.4 %collective-permute-start = (f32[16,512]{1,0:T(8,128)S(1)}, f32[16,512]{1,0:T(8,128)S(1)}, u32[]{:S(2)}, u32[]{:S(2)}) collective-permute-start(f32[16,512]{1,0:T(8,128)S(1)} %get-tuple-element.7), channel_id=1, source_target_pairs={{0,8},{8,0},{16,24},{24,16},{1,9},{9,1},{17,25},{25,17},{2,10},{10... | collective-permute-start | bytes 98312 | tf_op jit(solution)/shard_map/ppermute | solution.py:183
  18.0 5.4 %collective-permute-start.1 = (f32[16,512]{1,0:T(8,128)S(1)}, f32[16,512]{1,0:T(8,128)S(1)}, u32[]{:S(2)}, u32[]{:S(2)}) collective-permute-start(f32[16,512]{1,0:T(8,128)S(1)} %get-tuple-element.8), channel_id=1, source_target_pairs={{0,16},{8,24},{16,0},{24,8},{1,17},{9,25},{17,1},{25,9},{2,18},{10... | collective-permute-start | bytes 98312 | tf_op jit(solution)/shard_map/ppermute | solution.py:183
  20.6 5.7 %collective-permute-start.2 = (f32[16,512]{1,0:T(8,128)S(1)}, f32[16,512]{1,0:T(8,128)S(1)}, u32[]{:S(2)}, u32[]{:S(2)}) collective-permute-start(f32[16,512]{1,0:T(8,128)S(1)} %get-tuple-element.9), channel_id=1, source_target_pairs={{0,24},{8,16},{16,8},{24,0},{1,25},{9,17},{17,9},{25,1},{2,26},{10... | collective-permute-start | bytes 98312 | tf_op jit(solution)/shard_map/ppermute | solution.py:183
  26.3 6.2 %collective-permute-start.5 = (bf16[16,512]{1,0:T(8,128)(2,1)S(1)}, bf16[16,512]{1,0:T(8,128)(2,1)S(1)}, u32[]{:S(2)}, u32[]{:S(2)}) collective-permute-start(bf16[16,512]{1,0:T(8,128)(2,1)S(1)} %fusion), channel_id=1, source_target_pairs={{0,24},{8,16},{16,8},{24,0},{1,25},{9,17},{17,9},{25,1},{2,26},{10... | collective-permute-start | bytes 49160 | tf_op jit(solution)/shard_map/ppermute | solution.py:183
  26.8 5.8 %collective-permute-start.4 = (bf16[16,512]{1,0:T(8,128)(2,1)S(1)}, bf16[16,512]{1,0:T(8,128)(2,1)S(1)}, u32[]{:S(2)}, u32[]{:S(2)}) collective-permute-start(bf16[16,512]{1,0:T(8,128)(2,1)S(1)} %fusion), channel_id=1, source_target_pairs={{0,16},{8,24},{16,0},{24,8},{1,17},{9,25},{17,1},{25,9},{2,18},{10... | collective-permute-start | bytes 49160 | tf_op jit(solution)/shard_map/ppermute | solution.py:183
  26.8 5.8 %collective-permute-start.3 = (bf16[16,512]{1,0:T(8,128)(2,1)S(1)}, bf16[16,512]{1,0:T(8,128)(2,1)S(1)}, u32[]{:S(2)}, u32[]{:S(2)}) collective-permute-start(bf16[16,512]{1,0:T(8,128)(2,1)S(1)} %fusion), channel_id=1, source_target_pairs={{0,8},{8,0},{16,24},{24,16},{1,9},{9,1},{17,25},{25,17},{2,10},{10... | collective-permute-start | bytes 49160 | tf_op jit(solution)/shard_map/ppermute | solution.py:183

commit v3 on v2

v3 whole, which is shorter than its diff:
```python
import jax
import jax.numpy as jnp
from jax import lax
from jax.experimental import pallas as pl
from jax.experimental.pallas import tpu as pltpu
from jax.sharding import PartitionSpec as P

BF16 = jnp.bfloat16
F32 = jnp.float32
I32 = jnp.int32
SMEM = pl.BlockSpec(memory_space=pltpu.SMEM)
VMEM = pl.BlockSpec(memory_space=pltpu.VMEM)
ANY = pl.BlockSpec(memory_space=pl.ANY)


def split_hi_lo(value):
    hi = value.astype(BF16)
    return hi, (value - hi.astype(F32)).astype(BF16)


def order_blocks(per_owner, owner_ref, spectrum_ref, out_ref, inverse_ref, count_ref, sems):
    blocks = spectrum_ref.shape[0]
    for o in range(blocks // per_owner):
        count_ref[o] = 0
    gets = []
    for b in range(blocks):
        o = owner_ref[b]
        r = count_ref[o]
        count_ref[o] = r + 1
        at = o * per_owner + r
        inverse_ref[at] = b
        gets.append(pltpu.make_async_copy(spectrum_ref.at[b], out_ref.at[at], sems.at[b]))
        gets[b].start()
    for get in gets:
        get.wait()


def slots(tilt_pos_ref, tilt, within, tiles_per_tilt, flip):
    place = jnp.zeros_like(tilt)
    for t in range(tilt_pos_ref.shape[0]):
        place = jnp.where(tilt == t, tilt_pos_ref[t], place)
    return (place * tiles_per_tilt + within) ^ flip


def forward(n_kz, chunk, tiles_per_tilt, inverse_ref, tilt_pos_ref, tilt_ref, within_ref,
            weights_ref, spectrum_ref, *rest):
    outs, table, slot_ref = rest[:n_kz], rest[n_kz], rest[n_kz + 1]
    blocks, pairs, depth = weights_ref.shape
    columns = spectrum_ref.shape[3]
    tiles = n_kz * chunk
    flip = lax.axis_index("kz") * chunk
    slot_ref[...] = slots(tilt_pos_ref, tilt_ref[...], within_ref[...], tiles_per_tilt, flip)
    rows = lax.broadcasted_iota(I32, (tiles, pairs), 0)
    for at in range(blocks):
        b = inverse_ref[at]
        hot = jnp.where(slot_ref[pl.ds(b, 1), :] == rows, 1.0, 0.0).astype(BF16)
        hi, lo = split_hi_lo(jnp.dot(hot, weights_ref[b], preferred_element_type=F32))
        table[:tiles, at * depth : (at + 1) * depth] = hi
        table[tiles:, at * depth : (at + 1) * depth] = lo
    for c in range(2):
        both = jnp.dot(
            table[...],
            spectrum_ref[:, c].reshape(blocks * depth, columns),
            preferred_element_type=F32,
        )
        total = both[:tiles] + both[tiles:]
        for k in range(n_kz):
            outs[k][c * chunk : (c + 1) * chunk, :] = total[k * chunk : (k + 1) * chunk]


def adjoint_table(n_kz, chunk, per_owner, tiles_per_tilt, inverse_ref, tilt_pos_ref, tilt_ref,
                  within_ref, weights_ref, out_ref, slot_ref):
    depth = weights_ref.shape[2]
    pairs = weights_ref.shape[1]
    rows_all = n_kz * 2 * chunk
    flip = lax.axis_index("kz") * chunk
    slot_ref[...] = slots(tilt_pos_ref, tilt_ref[...], within_ref[...], tiles_per_tilt, flip)
    rows = lax.broadcasted_iota(I32, (rows_all, pairs), 0)
    for r in range(per_owner):
        b = inverse_ref[lax.axis_index("pen") * per_owner + r]
        at = slot_ref[pl.ds(b, 1), :]
        low = at & (chunk - 1)
        for c in range(2):
            place = (at - low) * 2 + c * chunk + low
            hot = jnp.where(place == rows, -8.0, 0.0).astype(BF16)
            hi, lo = split_hi_lo(jnp.dot(hot, weights_ref[b], preferred_element_type=F32))
            first = (c * per_owner + r) * depth
            out_ref[:rows_all, first : first + depth] = hi
            out_ref[rows_all:, first : first + depth] = lo


def adjoint(n_pen, chunk, per_owner, table_ref, blocks_ref, *rest):
    tile_refs, rest = rest[:n_pen], rest[n_pen:]
    out_ref, residual_ref, made, out_sems = rest
    depth, columns = blocks_ref.shape[3:]
    rows = tile_refs[0].shape[0]
    pen = lax.axis_index("pen")
    puts = []
    pick_row = lax.broadcasted_iota(I32, (16, rows), 0)
    pick_at = lax.broadcasted_iota(I32, (16, rows), 1)
    pick = jnp.where(pick_at == pick_row * chunk + pen, 1.0, 0.0)
    pick = jnp.where(pick_row < 2, pick, 0.0).astype(BF16)
    for j in range(n_pen):
        first_column = pl.multiple_of((pen ^ j) * columns, columns)
        here = tile_refs[j][...]
        own = jnp.dot(pick, here, preferred_element_type=F32)
        residual_ref[0, :, pl.ds(first_column, columns)] = own[:2].astype(BF16)
        step = lax.dot_general(
            table_ref[...],
            jnp.concatenate([here, here], axis=0),
            (((0,), (0,)), ((), ())),
            preferred_element_type=F32,
        )
        for r in range(per_owner):
            for c in range(2):
                first = (c * per_owner + r) * depth
                held = blocks_ref[pen ^ j, r, c].astype(F32)
                made[j, r, c] = (held + step[first : first + depth]).astype(BF16)
        to = out_ref.at[:, :, :, pl.ds(first_column, columns)]
        puts.append(pltpu.make_async_copy(made.at[j], to, out_sems.at[j]))
        puts[j].start()
    for put in puts:
        put.wait()


def body(spectrum, depth_weights, pair_tilt, pair_tile_within, tilt_pos, owner, measured):
    n_pen = lax.axis_size("pen")
    n_kz = lax.axis_size("kz")
    blocks, _, depth, columns = spectrum.shape
    per_owner = blocks // n_pen
    pairs = depth_weights.shape[1]
    tile_dev, _, cells = measured.shape
    chunk = tile_dev * n_pen
    tiles = chunk * n_kz
    tiles_per_tilt = tiles // tilt_pos.shape[0]

    def call(kernel, *static):
        def bound(*refs):
            return kernel(*static, *refs)
        return bound

    ordered, inverse = pl.pallas_call(
        call(order_blocks, per_owner),
        out_shape=[
            jax.ShapeDtypeStruct(spectrum.shape, BF16),
            jax.ShapeDtypeStruct((blocks,), I32),
        ],
        in_specs=[SMEM, ANY],
        out_specs=[VMEM, SMEM],
        scratch_shapes=[pltpu.SMEM((n_pen,), I32), pltpu.SemaphoreType.DMA((blocks,))],
        compiler_params=pltpu.CompilerParams(vmem_limit_bytes=8 << 20),
    )(owner, spectrum)
    outgoing = ordered.reshape(n_pen, per_owner, 2, depth, columns)
    incoming = lax.all_to_all(outgoing, "pen", split_axis=0, concat_axis=0, tiled=True)

    parts = pl.pallas_call(
        call(forward, n_kz, chunk, tiles_per_tilt),
        out_shape=[jax.ShapeDtypeStruct((2 * chunk, columns), F32)] * n_kz,
        in_specs=[SMEM, SMEM, VMEM, VMEM, VMEM, VMEM],
        out_specs=[VMEM] * n_kz,
        scratch_shapes=[
            pltpu.VMEM((2 * tiles, blocks * depth), BF16),
            pltpu.VMEM((blocks, pairs), I32),
        ],
        compiler_params=pltpu.CompilerParams(vmem_limit_bytes=16 << 20),
    )(inverse, tilt_pos, pair_tilt, pair_tile_within, depth_weights, ordered)

    def across(value, k):
        return lax.ppermute(value, "kz", [(i, i ^ k) for i in range(n_kz)])

    summed = [parts[0]] + [across(parts[k], k) for k in range(1, n_kz)]
    table = pl.pallas_call(
        call(adjoint_table, n_kz, chunk, per_owner, tiles_per_tilt),
        out_shape=jax.ShapeDtypeStruct((4 * tiles, 2 * per_owner * depth), BF16),
        in_specs=[SMEM, SMEM, VMEM, VMEM, VMEM],
        out_specs=VMEM,
        scratch_shapes=[pltpu.VMEM((blocks, pairs), I32)],
        compiler_params=pltpu.CompilerParams(vmem_limit_bytes=8 << 20),
    )(inverse, tilt_pos, pair_tilt, pair_tile_within, depth_weights)

    sent = measured.reshape(2, n_pen, columns).transpose(1, 0, 2)
    got = lax.all_to_all(sent, "pen", split_axis=0, concat_axis=0, tiled=True)
    measured_rows = got.transpose(1, 0, 2).reshape(2 * chunk, columns)
    total = summed[0]
    for part in summed[1:]:
        total = total + part
    own = (total - measured_rows.astype(F32)).astype(BF16)

    def between(value, k):
        return lax.ppermute(value, "pen", [(i, i ^ k) for i in range(n_pen)])

    held = jnp.concatenate([own] + [across(own, k) for k in range(1, n_kz)], axis=0)
    every = [held] + [between(held, k) for k in range(2, n_pen, 2)]
    every = [tile for kept in every for tile in (kept, between(kept, 1))]

    updated, residual = pl.pallas_call(
        call(adjoint, n_pen, chunk, per_owner),
        out_shape=[
            jax.ShapeDtypeStruct((per_owner, 2, depth, cells), BF16),
            jax.ShapeDtypeStruct((tile_dev, 2, cells), BF16),
        ],
        in_specs=[VMEM] * (n_pen + 2),
        out_specs=[ANY, VMEM],
        scratch_shapes=[
            pltpu.VMEM((n_pen, per_owner, 2, depth, columns), BF16),
            pltpu.SemaphoreType.DMA((n_pen,)),
        ],
        compiler_params=pltpu.CompilerParams(vmem_limit_bytes=16 << 20),
    )(table, incoming, *every)
    return (updated, residual)


def solution(mesh):
    return jax.shard_map(
        body,
        mesh=mesh,
        in_specs=(
            P("kz", None, None, "pen"),
            P("kz", None, None),
            P("kz", None),
            P("kz", None),
            P(),
            P("kz"),
            P(("kz", "pen"), None, None),
        ),
        out_specs=(P(("kz", "pen"), None, None, None), P(("kz", "pen"), None, None)),
        check_vma=False,
    )
```

time: 52.7 us -> 51.4 us (0.975)
  blocking collectives: 14.2 us -> 0 us
  waiting for transfers between devices: 6.49 us -> 14.2 us
  local copies, waits for them, and re-layouts: 0.02 us -> 5.19 us
  starting transfers between devices: 18.6 us -> 22.4 us
  Pallas kernels: 12.2 us -> 8.45 us
    all_gather x1 -> x0, blocking collectives: 14.2 us -> none  [body(): every = lax.all_gather(held, 'pen', axis=0, tiled=False)]
    ppermute x0 -> x7, waiting for transfers between devices: none -> 7 us  [between(): return lax.ppermute(value, 'pen', [(i, i ^ k) for i in range(n_pen)])]
    unnamed x10 -> x16, local copies, waits for them, and re-layouts: 0.02 us -> 5.19 us
    ppermute x0 -> x7, starting transfers between devices: none -> 4.02 us  [between(): return lax.ppermute(value, 'pen', [(i, i ^ k) for i in range(n_pen)])]
    pallas_call x1, Pallas kernels: 5.44 us -> 2.3 us  [body(): pl.pallas_call(call(adjoint, n_pen, chunk, per_owner), out_shape=[jax.Sha...]
    ppermute x6, waiting for transfers between devices: 5.47 us -> 7.21 us  [across(): return lax.ppermute(value, 'kz', [(i, i ^ k) for i in range(n_kz)])]
    all_to_all x1, waiting for transfers between devices: 1.01 us -> 0.01 us  [body(): got = lax.all_to_all(sent, 'pen', split_axis=0, concat_axis=0, tiled=True)]
    pallas_call x2, Pallas kernels: 5.52 us -> 4.92 us  [the longest x1 4.12 us: body(): pl.pallas_call(call(order_blocks, per_owner), out_shape=[jax.ShapeDtypeSt...]
  transfers between devices with their start and end apart: 8 -> 15, of which waited for: 3 -> 7; matrix products, arithmetic and copies ran while one was open for 0% -> 0% of each run, Pallas kernels for 13% -> 12%
where the time goes in v3:
time: 51.4 us; the launch traced here: 51.1 us
  starting transfers between devices  22.4 us (44%)
  waiting for transfers between devices  14.2 us (28%)
  Pallas kernels  8.45 us (16%)
  local copies, waits for them, and re-layouts  5.19 us (10%)
  between operations  0.76 us (1%)
    ppermute x6, starting transfers between devices, across(): return lax.ppermute(value, 'kz', [(i, i ^ k) for i in range(n_kz)])  8.86 us
    ppermute x6, waiting for transfers between devices, across(): return lax.ppermute(value, 'kz', [(i, i ^ k) for i in range(n_kz)])  7.21 us
    ppermute x7, waiting for transfers between devices, between(): return lax.ppermute(value, 'pen', [(i, i ^ k) for i in range(n_pen)])  7 us
    unnamed x16, local copies, waits for them, and re-layouts  5.19 us
    all_to_all x1, starting transfers between devices, body(): got = lax.all_to_all(sent, 'pen', split_axis=0, concat_axis=0, tiled=True)  5.18 us
    all_to_all x1, starting transfers between devices, body(): lax.all_to_all(outgoing, 'pen', split_axis=0, concat_axis=0, tiled=True)  4.34 us
    pallas_call x1, Pallas kernels, body(): pl.pallas_call(call(order_blocks, per_owner), out_shape=[jax.ShapeDtypeSt...  4.12 us
    ppermute x7, starting transfers between devices, between(): return lax.ppermute(value, 'pen', [(i, i ^ k) for i in range(n_pen)])  4.02 us
  transfers between devices with their start and end apart: 15, of which 7 were waited for; matrix products, arithmetic and copies ran while one was open for 0% of the time, Pallas kernels for 12%

profile of v3, /device:TPU:0, one launch (start us, length us, event | category | flops | bytes accessed | tf_op | source)
XLA Modules:
  0.0 51.1 jit_solution(5581320157184288968)
XLA Ops:
  0.6 5.2 %all-to-all-start.1 = ((bf16[8,2,512]{2,1,0:T(2,128)(2,1)}), bf16[8,2,512]{2,1,0:T(2,128)(2,1)S(1)}, u32[]{:S(2)}, u32[]{:S(2)}) async-start(bf16[8,2,512]{2,1,0:T(2,128)(2,1)} %bitcast.11), calls=%async_computation.1 | async-start | bytes 32768 | tf_op jit(solution)/shard_map/all_to_all | solution.py:182
  5.8 0.0 copy-start.2
  5.8 1.6 %copy-done.2 = bf16[16,2,64,512]{3,2,1,0:T(8,128)(2,1)S(1)} copy-done((bf16[16,2,64,512]{3,2,1,0:T(8,128)(2,1)S(1)}, bf16[16,2,64,512]{3,2,1,0:T(8,128)(2,1)}, u32[]{:S(2)}) %copy-start.2) | copy-done | bytes 2097176
  7.4 0.0 copy-start.7
  7.4 0.7 %copy-done.7 = s32[16]{0:T(128)S(1)} copy-done((s32[16]{0:T(128)S(1)}, s32[16]{0:T(128)}, u32[]{:S(2)}) %copy-start.7) | copy-done | bytes 88
  8.1 4.1 %shard_map.86 = (bf16[16,2,64,512]{3,2,1,0:T(8,128)(2,1)S(1)}, s32[16]{0:T(128)S(1)}) custom-call(s32[16]{0:T(128)S(1)} %copy-done.7, bf16[16,2,64,512]{3,2,1,0:T(8,128)(2,1)S(1)} %copy-done.2), custom_call_target="tpu_custom_call" | custom-call | tf_op jit(solution)/shard_map/pallas_call | solution.py:142
  12.2 0.0 copy-start
  12.2 1.3 %copy-done = bf16[16,2,64,512]{3,2,1,0:T(8,128)(2,1)} copy-done((bf16[16,2,64,512]{3,2,1,0:T(8,128)(2,1)}, bf16[16,2,64,512]{3,2,1,0:T(8,128)(2,1)S(1)}, u32[]{:S(2)}) %copy-start) | copy-done | bytes 2097176
  13.5 0.0 all-to-all-done.1
  13.5 0.0 copy-start.3
  13.5 0.0 copy-start.6
  13.5 4.3 %all-to-all-start = ((bf16[8,2,2,64,512]{4,3,2,1,0:T(8,128)(2,1)}), bf16[8,2,2,64,512]{4,3,2,1,0:T(8,128)(2,1)S(1)}, u32[]{:S(2)}, u32[]{:S(2)}) async-start(bf16[8,2,2,64,512]{4,3,2,1,0:T(8,128)(2,1)} %bitcast.10), calls=%async_computation | async-start | bytes 4194304 | tf_op jit(solution)/shard_map/all_to_all | solution.py:154
  17.9 0.0 copy-done.3
  17.9 0.0 copy-done.4
  17.9 0.0 copy-done.5
  17.9 0.0 copy-done.6
  17.9 0.0 copy-start.1
  17.9 1.6 %copy-done.1 = bf16[16,2,64,512]{3,2,1,0:T(8,128)(2,1)S(1)} copy-done((bf16[16,2,64,512]{3,2,1,0:T(8,128)(2,1)S(1)}, bf16[16,2,64,512]{3,2,1,0:T(8,128)(2,1)}, u32[]{:S(2)}) %copy-start.1) | copy-done | bytes 2097176
  19.5 1.2 %shard_map.88 = (f32[16,512]{1,0:T(8,128)S(1)}, f32[16,512]{1,0:T(8,128)S(1)}, f32[16,512]{1,0:T(8,128)S(1)}, f32[16,512]{1,0:T(8,128)S(1)}) custom-call(s32[16]{0:T(128)S(1)} %get-tuple-element.8.refs_0_, s32[16]{0:T(128)S(1)} %copy-done.6, s32[16,16]{1,0:T(8,128)S(1)} %copy-done.4, s32[16,16]{1,0:T(8,128)S(1)} %copy-done.5, ...), custom_call_target="tpu_custom_call" | custom-call | tf_op jit(solution)/shard_map/pallas_call | solution.py:156
  20.8 1.6 %collective-permute-start = (f32[16,512]{1,0:T(8,128)S(1)}, f32[16,512]{1,0:T(8,128)S(1)}, u32[]{:S(2)}, u32[]{:S(2)}) collective-permute-start(f32[16,512]{1,0:T(8,128)S(1)} %get-tuple-element.11), channel_id=1, source_target_pairs={{0,8},{8,0},{16,24},{24,16},{1,9},{9,1},{17,25},{25,17},{2,10},{10... | collective-permute-start | bytes 98312 | tf_op jit(solution)/shard_map/ppermute | solution.py:169
  22.4 2.6 %collective-permute-start.1 = (f32[16,512]{1,0:T(8,128)S(1)}, f32[16,512]{1,0:T(8,128)S(1)}, u32[]{:S(2)}, u32[]{:S(2)}) collective-permute-start(f32[16,512]{1,0:T(8,128)S(1)} %get-tuple-element.12), channel_id=1, source_target_pairs={{0,16},{8,24},{16,0},{24,8},{1,17},{9,25},{17,1},{25,9},{2,18},{10... | collective-permute-start | bytes 98312 | tf_op jit(solution)/shard_map/ppermute | solution.py:169
  25.0 0.2 collective-permute-start.2
  25.2 0.0 collective-permute-done
  25.2 2.5 %collective-permute-done.1 = f32[16,512]{1,0:T(8,128)S(1)} collective-permute-done((f32[16,512]{1,0:T(8,128)S(1)}, f32[16,512]{1,0:T(8,128)S(1)}, u32[]{:S(2)}, u32[]{:S(2)}) %collective-permute-start.1) | collective-permute-done | bytes 32800 | tf_op jit(solution)/shard_map/ppermute | solution.py:169
  27.7 3.0 %collective-permute-done.2 = f32[16,512]{1,0:T(8,128)S(1)} collective-permute-done((f32[16,512]{1,0:T(8,128)S(1)}, f32[16,512]{1,0:T(8,128)S(1)}, u32[]{:S(2)}, u32[]{:S(2)}) %collective-permute-start.2) | collective-permute-done | bytes 32800 | tf_op jit(solution)/shard_map/ppermute | solution.py:169
  30.7 0.4 collective-permute-start.5
  31.2 0.0 collective-permute-start.4
  31.2 4.0 %collective-permute-start.3 = (bf16[16,512]{1,0:T(8,128)(2,1)S(1)}, bf16[16,512]{1,0:T(8,128)(2,1)S(1)}, u32[]{:S(2)}, u32[]{:S(2)}) collective-permute-start(bf16[16,512]{1,0:T(8,128)(2,1)S(1)} %fusion), channel_id=1, source_target_pairs={{0,8},{8,0},{16,24},{24,16},{1,9},{9,1},{17,25},{25,17},{2,10},{10... | collective-permute-start | bytes 49160 | tf_op jit(solution)/shard_map/ppermute | solution.py:169
  35.2 1.1 %collective-permute-done.5 = bf16[16,512]{1,0:T(8,128)(2,1)S(1)} collective-permute-done((bf16[16,512]{1,0:T(8,128)(2,1)S(1)}, bf16[16,512]{1,0:T(8,128)(2,1)S(1)}, u32[]{:S(2)}, u32[]{:S(2)}) %collective-permute-start.5) | collective-permute-done | bytes 16416 | tf_op jit(solution)/shard_map/ppermute | solution.py:169
  36.3 0.0 collective-permute-done.4
  36.3 0.6 %collective-permute-done.3 = bf16[16,512]{1,0:T(8,128)(2,1)S(1)} collective-permute-done((bf16[16,512]{1,0:T(8,128)(2,1)S(1)}, bf16[16,512]{1,0:T(8,128)(2,1)S(1)}, u32[]{:S(2)}, u32[]{:S(2)}) %collective-permute-start.3) | collective-permute-done | bytes 16416 | tf_op jit(solution)/shard_map/ppermute | solution.py:169
  36.9 2.9 %collective-permute-start.11 = (bf16[64,512]{1,0:T(8,128)(2,1)S(1)}, bf16[64,512]{1,0:T(8,128)(2,1)S(1)}, u32[]{:S(2)}, u32[]{:S(2)}) collective-permute-start(bf16[64,512]{1,0:T(8,128)(2,1)S(1)} %pad_maximum_fusion.refs_2_), channel_id=1, source_target_pairs={{0,6},{1,7},{2,4},{3,5},{4,2},{5,3},{6,0},{7,1},{8,14},{9,15},{10,... | collective-permute-start | bytes 196616 | tf_op jit(solution)/shard_map/ppermute | solution.py:190
  39.8 0.6 %collective-permute-start.9 = (bf16[64,512]{1,0:T(8,128)(2,1)S(1)}, bf16[64,512]{1,0:T(8,128)(2,1)S(1)}, u32[]{:S(2)}, u32[]{:S(2)}) collective-permute-start(bf16[64,512]{1,0:T(8,128)(2,1)S(1)} %pad_maximum_fusion.refs_2_), channel_id=1, source_target_pairs={{0,4},{1,5},{2,6},{3,7},{4,0},{5,1},{6,2},{7,3},{8,12},{9,13},{10,... | collective-permute-start | bytes 196616 | tf_op jit(solution)/shard_map/ppermute | solution.py:190
  40.3 0.1 collective-permute-start.7
  40.4 0.0 collective-permute-start.6
  40.4 6.1 %collective-permute-done.11.refs_8_ = bf16[64,512]{1,0:T(8,128)(2,1)S(1)} collective-permute-done((bf16[64,512]{1,0:T(8,128)(2,1)S(1)}, bf16[64,512]{1,0:T(8,128)(2,1)S(1)}, u32[]{:S(2)}, u32[]{:S(2)}) %collective-permute-start.11) | collective-permute-done | bytes 65568 | tf_op jit(solution)/shard_map/ppermute | solution.py:190
  46.5 0.0 collective-permute-start.12
  46.5 0.9 %collective-permute-done.9.refs_6_ = bf16[64,512]{1,0:T(8,128)(2,1)S(1)} collective-permute-done((bf16[64,512]{1,0:T(8,128)(2,1)S(1)}, bf16[64,512]{1,0:T(8,128)(2,1)S(1)}, u32[]{:S(2)}, u32[]{:S(2)}) %collective-permute-start.9) | collective-permute-done | bytes 65568 | tf_op jit(solution)/shard_map/ppermute | solution.py:190
  47.3 0.0 collective-permute-start.10
  47.3 0.0 collective-permute-done.7.refs_4_
  47.3 0.5 collective-permute-start.8
  47.8 0.8 %shard_map.87.refs_0_ = bf16[128,256]{1,0:T(8,128)(2,1)S(1)} custom-call(s32[16]{0:T(128)S(1)} %get-tuple-element.8.refs_0_, s32[16]{0:T(128)S(1)} %copy-done.6, s32[16,16]{1,0:T(8,128)S(1)} %copy-done.4, s32[16,16]{1,0:T(8,128)S(1)} %copy-done.5, bf16[16,16,64]{2,1,0:T(8,128)(2,1)S(1)} %copy-done.3), custom_call_target="tpu_custom_call" | custom-call | tf_op jit(solution)/shard_map/pallas_call | solution.py:172
  48.7 0.0 collective-permute-done.6.refs_3_
  48.7 0.0 collective-permute-done.12.refs_9_
  48.7 0.0 collective-permute-done.10.refs_7_
  48.7 0.1 collective-permute-done.8.refs_5_
  48.7 0.0 all-to-all-done.refs_1_
  48.7 2.3 %shard_map.89 = (bf16[2,2,64,4096]{3,2,1,0:T(8,128)(2,1)}, bf16[1,2,4096]{2,1,0:T(2,128)(2,1)}) custom-call(bf16[128,256]{1,0:T(8,128)(2,1)S(1)} %shard_map.87.refs_0_, bf16[8,2,2,64,512]{4,3,2,1,0:T(8,128)(2,1)S(1)} %all-to-all-done.refs_1_, bf16[64,512]{1,0:T(8,128)(2,1)S(1)} %pad_maximum_fusion.refs_2_, ...), custom_call_target="tpu_custom_call" | custom-call | tf_op jit(solution)/shard_map/pallas_call | solution.py:196
  (5 shorter events, 0.0 us)
Async XLA Ops:
  0.6 12.9 %all-to-all-start.1 = ((bf16[8,2,512]{2,1,0:T(2,128)(2,1)}), bf16[8,2,512]{2,1,0:T(2,128)(2,1)S(1)}, u32[]{:S(2)}, u32[]{:S(2)}) async-start(bf16[8,2,512]{2,1,0:T(2,128)(2,1)} %bitcast.11), calls=%async_computation.1 | async-start | bytes 32768 | tf_op jit(solution)/shard_map/all_to_all | solution.py:182
  5.8 1.6 %copy-start.2 = (bf16[16,2,64,512]{3,2,1,0:T(8,128)(2,1)S(1)}, bf16[16,2,64,512]{3,2,1,0:T(8,128)(2,1)}, u32[]{:S(2)}) copy-start(bf16[16,2,64,512]{3,2,1,0:T(8,128)(2,1)} %refs_1_.3) | copy-start | bytes 6291460
  7.4 0.7 %copy-start.7 = (s32[16]{0:T(128)S(1)}, s32[16]{0:T(128)}, u32[]{:S(2)}) copy-start(s32[16]{0:T(128)} %refs_0_.1) | copy-start | bytes 196
  12.2 1.3 %copy-start = (bf16[16,2,64,512]{3,2,1,0:T(8,128)(2,1)}, bf16[16,2,64,512]{3,2,1,0:T(8,128)(2,1)S(1)}, u32[]{:S(2)}) copy-start(bf16[16,2,64,512]{3,2,1,0:T(8,128)(2,1)S(1)} %get-tuple-element.9.refs_5_) | copy-start | bytes 6291460
  13.5 4.4 %copy-start.3 = (bf16[16,16,64]{2,1,0:T(8,128)(2,1)S(1)}, bf16[16,16,64]{2,1,0:T(8,128)(2,1)}, u32[]{:S(2)}) copy-start(bf16[16,16,64]{2,1,0:T(8,128)(2,1)} %refs_4_.3) | copy-start | bytes 98308
  13.5 4.4 %copy-start.4 = (s32[16,16]{1,0:T(8,128)S(1)}, s32[16,16]{1,0:T(8,128)}, u32[]{:S(2)}) copy-start(s32[16,16]{1,0:T(8,128)} %refs_2_.3) | copy-start | bytes 3076
  13.5 4.4 %copy-start.5 = (s32[16,16]{1,0:T(8,128)S(1)}, s32[16,16]{1,0:T(8,128)}, u32[]{:S(2)}) copy-start(s32[16,16]{1,0:T(8,128)} %refs_3_.3) | copy-start | bytes 3076
  13.5 4.4 %copy-start.6 = (s32[16]{0:T(128)S(1)}, s32[16]{0:T(128)}, u32[]{:S(2)}) copy-start(s32[16]{0:T(128)} %refs_1_.5) | copy-start | bytes 196
  13.5 35.2 %all-to-all-start = ((bf16[8,2,2,64,512]{4,3,2,1,0:T(8,128)(2,1)}), bf16[8,2,2,64,512]{4,3,2,1,0:T(8,128)(2,1)S(1)}, u32[]{:S(2)}, u32[]{:S(2)}) async-start(bf16[8,2,2,64,512]{4,3,2,1,0:T(8,128)(2,1)} %bitcast.10), calls=%async_computation | async-start | bytes 4194304 | tf_op jit(solution)/shard_map/all_to_all | solution.py:154
  17.9 1.6 %copy-start.1 = (bf16[16,2,64,512]{3,2,1,0:T(8,128)(2,1)S(1)}, bf16[16,2,64,512]{3,2,1,0:T(8,128)(2,1)}, u32[]{:S(2)}) copy-start(bf16[16,2,64,512]{3,2,1,0:T(8,128)(2,1)} %copy-done) | copy-start | bytes 6291460
  20.8 4.4 %collective-permute-start = (f32[16,512]{1,0:T(8,128)S(1)}, f32[16,512]{1,0:T(8,128)S(1)}, u32[]{:S(2)}, u32[]{:S(2)}) collective-permute-start(f32[16,512]{1,0:T(8,128)S(1)} %get-tuple-element.11), channel_id=1, source_target_pairs={{0,8},{8,0},{16,24},{24,16},{1,9},{9,1},{17,25},{25,17},{2,10},{10... | collective-permute-start | bytes 98312 | tf_op jit(solution)/shard_map/ppermute | solution.py:169
  22.4 5.4 %collective-permute-start.1 = (f32[16,512]{1,0:T(8,128)S(1)}, f32[16,512]{1,0:T(8,128)S(1)}, u32[]{:S(2)}, u32[]{:S(2)}) collective-permute-start(f32[16,512]{1,0:T(8,128)S(1)} %get-tuple-element.12), channel_id=1, source_target_pairs={{0,16},{8,24},{16,0},{24,8},{1,17},{9,25},{17,1},{25,9},{2,18},{10... | collective-permute-start | bytes 98312 | tf_op jit(solution)/shard_map/ppermute | solution.py:169
  25.0 5.7 %collective-permute-start.2 = (f32[16,512]{1,0:T(8,128)S(1)}, f32[16,512]{1,0:T(8,128)S(1)}, u32[]{:S(2)}, u32[]{:S(2)}) collective-permute-start(f32[16,512]{1,0:T(8,128)S(1)} %get-tuple-element.13), channel_id=1, source_target_pairs={{0,24},{8,16},{16,8},{24,0},{1,25},{9,17},{17,9},{25,1},{2,26},{10... | collective-permute-start | bytes 98312 | tf_op jit(solution)/shard_map/ppermute | solution.py:169
  30.7 5.6 %collective-permute-start.5 = (bf16[16,512]{1,0:T(8,128)(2,1)S(1)}, bf16[16,512]{1,0:T(8,128)(2,1)S(1)}, u32[]{:S(2)}, u32[]{:S(2)}) collective-permute-start(bf16[16,512]{1,0:T(8,128)(2,1)S(1)} %fusion), channel_id=1, source_target_pairs={{0,24},{8,16},{16,8},{24,0},{1,25},{9,17},{17,9},{25,1},{2,26},{10... | collective-permute-start | bytes 49160 | tf_op jit(solution)/shard_map/ppermute | solution.py:169
  31.2 5.2 %collective-permute-start.4 = (bf16[16,512]{1,0:T(8,128)(2,1)S(1)}, bf16[16,512]{1,0:T(8,128)(2,1)S(1)}, u32[]{:S(2)}, u32[]{:S(2)}) collective-permute-start(bf16[16,512]{1,0:T(8,128)(2,1)S(1)} %fusion), channel_id=1, source_target_pairs={{0,16},{8,24},{16,0},{24,8},{1,17},{9,25},{17,1},{25,9},{2,18},{10... | collective-permute-start | bytes 49160 | tf_op jit(solution)/shard_map/ppermute | solution.py:169
  31.2 5.7 %collective-permute-start.3 = (bf16[16,512]{1,0:T(8,128)(2,1)S(1)}, bf16[16,512]{1,0:T(8,128)(2,1)S(1)}, u32[]{:S(2)}, u32[]{:S(2)}) collective-permute-start(bf16[16,512]{1,0:T(8,128)(2,1)S(1)} %fusion), channel_id=1, source_target_pairs={{0,8},{8,0},{16,24},{24,16},{1,9},{9,1},{17,25},{25,17},{2,10},{10... | collective-permute-start | bytes 49160 | tf_op jit(solution)/shard_map/ppermute | solution.py:169
  36.9 9.6 %collective-permute-start.11 = (bf16[64,512]{1,0:T(8,128)(2,1)S(1)}, bf16[64,512]{1,0:T(8,128)(2,1)S(1)}, u32[]{:S(2)}, u32[]{:S(2)}) collective-permute-start(bf16[64,512]{1,0:T(8,128)(2,1)S(1)} %pad_maximum_fusion.refs_2_), channel_id=1, source_target_pairs={{0,6},{1,7},{2,4},{3,5},{4,2},{5,3},{6,0},{7,1},{8,14},{9,15},{10,... | collective-permute-start | bytes 196616 | tf_op jit(solution)/shard_map/ppermute | solution.py:190
  39.8 7.6 %collective-permute-start.9 = (bf16[64,512]{1,0:T(8,128)(2,1)S(1)}, bf16[64,512]{1,0:T(8,128)(2,1)S(1)}, u32[]{:S(2)}, u32[]{:S(2)}) collective-permute-start(bf16[64,512]{1,0:T(8,128)(2,1)S(1)} %pad_maximum_fusion.refs_2_), channel_id=1, source_target_pairs={{0,4},{1,5},{2,6},{3,7},{4,0},{5,1},{6,2},{7,3},{8,12},{9,13},{10,... | collective-permute-start | bytes 196616 | tf_op jit(solution)/shard_map/ppermute | solution.py:190
  40.3 7.0 %collective-permute-start.7 = (bf16[64,512]{1,0:T(8,128)(2,1)S(1)}, bf16[64,512]{1,0:T(8,128)(2,1)S(1)}, u32[]{:S(2)}, u32[]{:S(2)}) collective-permute-start(bf16[64,512]{1,0:T(8,128)(2,1)S(1)} %pad_maximum_fusion.refs_2_), channel_id=1, source_target_pairs={{0,2},{1,3},{2,0},{3,1},{4,6},{5,7},{6,4},{7,5},{8,10},{9,11},{10,... | collective-permute-start | bytes 196616 | tf_op jit(solution)/shard_map/ppermute | solution.py:190
  40.4 8.3 %collective-permute-start.6 = (bf16[64,512]{1,0:T(8,128)(2,1)S(1)}, bf16[64,512]{1,0:T(8,128)(2,1)S(1)}, u32[]{:S(2)}, u32[]{:S(2)}) collective-permute-start(bf16[64,512]{1,0:T(8,128)(2,1)S(1)} %pad_maximum_fusion.refs_2_), channel_id=1, source_target_pairs={{0,1},{1,0},{2,3},{3,2},{4,5},{5,4},{6,7},{7,6},{8,9},{9,8},{10,11... | collective-permute-start | bytes 196616 | tf_op jit(solution)/shard_map/ppermute | solution.py:190
  46.5 2.2 %collective-permute-start.12 = (bf16[64,512]{1,0:T(8,128)(2,1)S(1)}, bf16[64,512]{1,0:T(8,128)(2,1)S(1)}, u32[]{:S(2)}, u32[]{:S(2)}) collective-permute-start(bf16[64,512]{1,0:T(8,128)(2,1)S(1)} %collective-permute-done.11.refs_8_), channel_id=1, source_target_pairs={{0,1},{1,0},{2,3},{3,2},{4,5},{5,4},{6,7},{7,6},{8,9},{9,8},{10,11... | collective-permute-start | bytes 196616 | tf_op jit(solution)/shard_map/ppermute | solution.py:190
  47.3 1.3 %collective-permute-start.10 = (bf16[64,512]{1,0:T(8,128)(2,1)S(1)}, bf16[64,512]{1,0:T(8,128)(2,1)S(1)}, u32[]{:S(2)}, u32[]{:S(2)}) collective-permute-start(bf16[64,512]{1,0:T(8,128)(2,1)S(1)} %collective-permute-done.9.refs_6_), channel_id=1, source_target_pairs={{0,1},{1,0},{2,3},{3,2},{4,5},{5,4},{6,7},{7,6},{8,9},{9,8},{10,11... | collective-permute-start | bytes 196616 | tf_op jit(solution)/shard_map/ppermute | solution.py:190
  47.3 1.4 %collective-permute-start.8 = (bf16[64,512]{1,0:T(8,128)(2,1)S(1)}, bf16[64,512]{1,0:T(8,128)(2,1)S(1)}, u32[]{:S(2)}, u32[]{:S(2)}) collective-permute-start(bf16[64,512]{1,0:T(8,128)(2,1)S(1)} %collective-permute-done.7.refs_4_), channel_id=1, source_target_pairs={{0,1},{1,0},{2,3},{3,2},{4,5},{5,4},{6,7},{7,6},{8,9},{9,8},{10,11... | collective-permute-start | bytes 196616 | tf_op jit(solution)/shard_map/ppermute | solution.py:190

commit v4 on v3

--- a/solution.py
+++ b/solution.py
@@ -18,21 +18,29 @@
     return hi, (value - hi.astype(F32)).astype(BF16)
 
 
-def order_blocks(per_owner, owner_ref, spectrum_ref, out_ref, inverse_ref, count_ref, sems):
+def order_blocks(per_owner, owner_ref, spectrum_ref, out_ref, inverse_ref, held, owner, count,
+                 owner_sem, in_sems, out_sems):
     blocks = spectrum_ref.shape[0]
+    get_owner = pltpu.make_async_copy(owner_ref, owner, owner_sem)
+    get_owner.start()
+    gets, puts = [], []
+    for b in range(blocks):
+        gets.append(pltpu.make_async_copy(spectrum_ref.at[b], held.at[b], in_sems.at[b]))
+        gets[b].start()
     for o in range(blocks // per_owner):
-        count_ref[o] = 0
-    gets = []
+        count[o] = 0
+    get_owner.wait()
     for b in range(blocks):
-        o = owner_ref[b]
-        r = count_ref[o]
-        count_ref[o] = r + 1
+        o = owner[b]
+        r = count[o]
+        count[o] = r + 1
         at = o * per_owner + r
         inverse_ref[at] = b
-        gets.append(pltpu.make_async_copy(spectrum_ref.at[b], out_ref.at[at], sems.at[b]))
-        gets[b].start()
-    for get in gets:
-        get.wait()
+        gets[b].wait()
+        puts.append(pltpu.make_async_copy(held.at[b], out_ref.at[at], out_sems.at[b]))
+        puts[b].start()
+    for put in puts:
+        put.wait()
 
 
 def slots(tilt_pos_ref, tilt, within, tiles_per_tilt, flip):
@@ -42,21 +50,21 @@
     return (place * tiles_per_tilt + within) ^ flip
 
 
-def forward(n_kz, chunk, tiles_per_tilt, inverse_ref, tilt_pos_ref, tilt_ref, within_ref,
-            weights_ref, spectrum_ref, *rest):
-    outs, table, slot_ref = rest[:n_kz], rest[n_kz], rest[n_kz + 1]
+def forward(n_kz, chunk, tiles_per_tilt, tilt_pos_ref, tilt_ref, within_ref, weights_ref,
+            spectrum_ref, after_ref, *rest):
+    del after_ref
+    outs, table = rest[:n_kz], rest[n_kz]
     blocks, pairs, depth = weights_ref.shape
     columns = spectrum_ref.shape[3]
     tiles = n_kz * chunk
     flip = lax.axis_index("kz") * chunk
-    slot_ref[...] = slots(tilt_pos_ref, tilt_ref[...], within_ref[...], tiles_per_tilt, flip)
+    slot = slots(tilt_pos_ref, tilt_ref[...], within_ref[...], tiles_per_tilt, flip)
     rows = lax.broadcasted_iota(I32, (tiles, pairs), 0)
-    for at in range(blocks):
-        b = inverse_ref[at]
-        hot = jnp.where(slot_ref[pl.ds(b, 1), :] == rows, 1.0, 0.0).astype(BF16)
+    for b in range(blocks):
+        hot = jnp.where(slot[b : b + 1, :] == rows, 1.0, 0.0).astype(BF16)
         hi, lo = split_hi_lo(jnp.dot(hot, weights_ref[b], preferred_element_type=F32))
-        table[:tiles, at * depth : (at + 1) * depth] = hi
-        table[tiles:, at * depth : (at + 1) * depth] = lo
+        table[:tiles, b * depth : (b + 1) * depth] = hi
+        table[tiles:, b * depth : (b + 1) * depth] = lo
     for c in range(2):
         both = jnp.dot(
             table[...],
@@ -145,10 +153,17 @@
             jax.ShapeDtypeStruct(spectrum.shape, BF16),
             jax.ShapeDtypeStruct((blocks,), I32),
         ],
-        in_specs=[SMEM, ANY],
-        out_specs=[VMEM, SMEM],
-        scratch_shapes=[pltpu.SMEM((n_pen,), I32), pltpu.SemaphoreType.DMA((blocks,))],
-        compiler_params=pltpu.CompilerParams(vmem_limit_bytes=8 << 20),
+        in_specs=[ANY, ANY],
+        out_specs=[ANY, SMEM],
+        scratch_shapes=[
+            pltpu.VMEM(spectrum.shape, BF16),
+            pltpu.SMEM((blocks,), I32),
+            pltpu.SMEM((n_pen,), I32),
+            pltpu.SemaphoreType.DMA,
+            pltpu.SemaphoreType.DMA((blocks,)),
+            pltpu.SemaphoreType.DMA((blocks,)),
+        ],
+        compiler_params=pltpu.CompilerParams(vmem_limit_bytes=62 << 20),
     )(owner, spectrum)
     outgoing = ordered.reshape(n_pen, per_owner, 2, depth, columns)
     incoming = lax.all_to_all(outgoing, "pen", split_axis=0, concat_axis=0, tiled=True)
@@ -156,14 +171,11 @@
     parts = pl.pallas_call(
         call(forward, n_kz, chunk, tiles_per_tilt),
         out_shape=[jax.ShapeDtypeStruct((2 * chunk, columns), F32)] * n_kz,
-        in_specs=[SMEM, SMEM, VMEM, VMEM, VMEM, VMEM],
+        in_specs=[SMEM, VMEM, VMEM, VMEM, VMEM, ANY],
         out_specs=[VMEM] * n_kz,
-        scratch_shapes=[
-            pltpu.VMEM((2 * tiles, blocks * depth), BF16),
-            pltpu.VMEM((blocks, pairs), I32),
-        ],
+        scratch_shapes=[pltpu.VMEM((2 * tiles, blocks * depth), BF16)],
         compiler_params=pltpu.CompilerParams(vmem_limit_bytes=16 << 20),
-    )(inverse, tilt_pos, pair_tilt, pair_tile_within, depth_weights, ordered)
+    )(tilt_pos, pair_tilt, pair_tile_within, depth_weights, spectrum, inverse)
 
     def across(value, k):
         return lax.ppermute(value, "kz", [(i, i ^ k) for i in range(n_kz)])

time: 51.4 us -> 49.6 us (0.965)
  local copies, waits for them, and re-layouts: 5.19 us -> 0.03 us
  waiting for transfers between devices: 14.2 us -> 16.9 us
  Pallas kernels: 8.45 us -> 9.05 us
    unnamed x16 -> x12, local copies, waits for them, and re-layouts: 5.19 us -> 0.03 us
    all_to_all x1, waiting for transfers between devices: 0.01 us -> 1.65 us  [body(): got = lax.all_to_all(sent, 'pen', split_axis=0, concat_axis=0, tiled=True)]
    pallas_call x1, Pallas kernels: 2.3 us -> 3.94 us  [body(): pl.pallas_call(call(adjoint, n_pen, chunk, per_owner), out_shape=[jax.Sha...]
    pallas_call x1, Pallas kernels: 4.12 us -> 3.09 us  [body(): pl.pallas_call(call(order_blocks, per_owner), out_shape=[jax.ShapeDtypeSt...]
    ppermute x7, waiting for transfers between devices: 7 us -> 8.02 us  [between(): return lax.ppermute(value, 'pen', [(i, i ^ k) for i in range(n_pen)])]
  transfers between devices with their start and end apart: 15 -> 15, of which waited for: 7 -> 8; matrix products, arithmetic and copies ran while one was open for 0% -> 0% of each run, Pallas kernels for 12% -> 10%
where the time goes in v4:
time: 49.6 us; the launch traced here: 49.3 us
  starting transfers between devices  22.6 us (46%)
  waiting for transfers between devices  16.9 us (34%)
  Pallas kernels  9.05 us (18%)
  between operations  0.77 us (2%)
    ppermute x6, starting transfers between devices, across(): return lax.ppermute(value, 'kz', [(i, i ^ k) for i in range(n_kz)])  8.88 us
    ppermute x7, waiting for transfers between devices, between(): return lax.ppermute(value, 'pen', [(i, i ^ k) for i in range(n_pen)])  8.02 us
    ppermute x6, waiting for transfers between devices, across(): return lax.ppermute(value, 'kz', [(i, i ^ k) for i in range(n_kz)])  7.18 us
    all_to_all x1, starting transfers between devices, body(): got = lax.all_to_all(sent, 'pen', split_axis=0, concat_axis=0, tiled=True)  5.18 us
    all_to_all x1, starting transfers between devices, body(): lax.all_to_all(outgoing, 'pen', split_axis=0, concat_axis=0, tiled=True)  4.51 us
    ppermute x7, starting transfers between devices, between(): return lax.ppermute(value, 'pen', [(i, i ^ k) for i in range(n_pen)])  4 us
    pallas_call x1, Pallas kernels, body(): pl.pallas_call(call(adjoint, n_pen, chunk, per_owner), out_shape=[jax.Sha...  3.94 us
    pallas_call x1, Pallas kernels, body(): pl.pallas_call(call(order_blocks, per_owner), out_shape=[jax.ShapeDtypeSt...  3.09 us
  transfers between devices with their start and end apart: 15, of which 8 were waited for; matrix products, arithmetic and copies ran while one was open for 0% of the time, Pallas kernels for 10%

profile of v4, /device:TPU:0, one launch (start us, length us, event | category | flops | bytes accessed | tf_op | source)
XLA Modules:
  0.0 49.3 jit_solution(10760785512280616612)
XLA Ops:
  0.6 5.2 %all-to-all-start.1 = ((bf16[8,2,512]{2,1,0:T(2,128)(2,1)}), bf16[8,2,512]{2,1,0:T(2,128)(2,1)S(1)}, u32[]{:S(2)}, u32[]{:S(2)}) async-start(bf16[8,2,512]{2,1,0:T(2,128)(2,1)} %bitcast.11), calls=%async_computation.1 | async-start | bytes 32768 | tf_op jit(solution)/shard_map/all_to_all | solution.py:194
  5.8 3.1 %shard_map.86 = (bf16[16,2,64,512]{3,2,1,0:T(8,128)(2,1)}, s32[16]{0:T(128)}) custom-call(s32[16]{0:T(128)} %refs_0_.2, bf16[16,2,64,512]{3,2,1,0:T(8,128)(2,1)} %refs_4_.3), custom_call_target="tpu_custom_call" | custom-call | tf_op jit(solution)/shard_map/pallas_call | solution.py:150
  8.9 1.7 %all-to-all-done.1 = bf16[8,2,512]{2,1,0:T(2,128)(2,1)S(1)} async-done(((bf16[8,2,512]{2,1,0:T(2,128)(2,1)}), bf16[8,2,512]{2,1,0:T(2,128)(2,1)S(1)}, u32[]{:S(2)}, u32[]{:S(2)}) %all-to-all-start.1) | async-done | bytes 16416 | tf_op jit(solution)/shard_map/all_to_all | solution.py:194
  10.6 0.0 copy-start
  10.6 0.0 copy-start.1
  10.6 0.0 copy-start.2
  10.6 0.0 copy-start.3
  10.6 0.0 copy-start.4
  10.6 0.0 copy-start.5
  10.6 4.5 %all-to-all-start = ((bf16[8,2,2,64,512]{4,3,2,1,0:T(8,128)(2,1)}), bf16[8,2,2,64,512]{4,3,2,1,0:T(8,128)(2,1)}, u32[]{:S(2)}, u32[]{:S(2)}) async-start(bf16[8,2,2,64,512]{4,3,2,1,0:T(8,128)(2,1)} %bitcast.10), calls=%async_computation | async-start | bytes 4194304 | tf_op jit(solution)/shard_map/all_to_all | solution.py:169
  15.1 0.0 copy-done
  15.1 0.0 copy-done.1
  15.1 0.0 copy-done.2
  15.1 0.0 copy-done.3
  15.2 0.0 copy-done.4
  15.2 0.0 copy-done.5
  15.2 1.2 %shard_map.88 = (f32[16,512]{1,0:T(8,128)S(1)}, f32[16,512]{1,0:T(8,128)S(1)}, f32[16,512]{1,0:T(8,128)S(1)}, f32[16,512]{1,0:T(8,128)S(1)}) custom-call(s32[16]{0:T(128)S(1)} %copy-done.4, s32[16,16]{1,0:T(8,128)S(1)} %copy-done.2, s32[16,16]{1,0:T(8,128)S(1)} %copy-done.3, bf16[16,16,64]{2,1,0:T(8,128)(2,1)S(1)} %copy-done.1, ...), custom_call_target="tpu_custom_call" | custom-call | tf_op jit(solution)/shard_map/pallas_call | solution.py:171
  16.4 1.6 %collective-permute-start = (f32[16,512]{1,0:T(8,128)S(1)}, f32[16,512]{1,0:T(8,128)S(1)}, u32[]{:S(2)}, u32[]{:S(2)}) collective-permute-start(f32[16,512]{1,0:T(8,128)S(1)} %get-tuple-element.11), channel_id=1, source_target_pairs={{0,8},{8,0},{16,24},{24,16},{1,9},{9,1},{17,25},{25,17},{2,10},{10... | collective-permute-start | bytes 98312 | tf_op jit(solution)/shard_map/ppermute | solution.py:181
  18.0 2.6 %collective-permute-start.1 = (f32[16,512]{1,0:T(8,128)S(1)}, f32[16,512]{1,0:T(8,128)S(1)}, u32[]{:S(2)}, u32[]{:S(2)}) collective-permute-start(f32[16,512]{1,0:T(8,128)S(1)} %get-tuple-element.12), channel_id=1, source_target_pairs={{0,16},{8,24},{16,0},{24,8},{1,17},{9,25},{17,1},{25,9},{2,18},{10... | collective-permute-start | bytes 98312 | tf_op jit(solution)/shard_map/ppermute | solution.py:181
  20.6 0.2 collective-permute-start.2
  20.8 0.0 collective-permute-done
  20.8 2.6 %collective-permute-done.1 = f32[16,512]{1,0:T(8,128)S(1)} collective-permute-done((f32[16,512]{1,0:T(8,128)S(1)}, f32[16,512]{1,0:T(8,128)S(1)}, u32[]{:S(2)}, u32[]{:S(2)}) %collective-permute-start.1) | collective-permute-done | bytes 32800 | tf_op jit(solution)/shard_map/ppermute | solution.py:181
  23.4 2.9 %collective-permute-done.2 = f32[16,512]{1,0:T(8,128)S(1)} collective-permute-done((f32[16,512]{1,0:T(8,128)S(1)}, f32[16,512]{1,0:T(8,128)S(1)}, u32[]{:S(2)}, u32[]{:S(2)}) %collective-permute-start.2) | collective-permute-done | bytes 32800 | tf_op jit(solution)/shard_map/ppermute | solution.py:181
  26.3 0.5 collective-permute-start.5
  26.8 0.0 collective-permute-start.4
  26.8 4.0 %collective-permute-start.3 = (bf16[16,512]{1,0:T(8,128)(2,1)S(1)}, bf16[16,512]{1,0:T(8,128)(2,1)S(1)}, u32[]{:S(2)}, u32[]{:S(2)}) collective-permute-start(bf16[16,512]{1,0:T(8,128)(2,1)S(1)} %fusion), channel_id=1, source_target_pairs={{0,8},{8,0},{16,24},{24,16},{1,9},{9,1},{17,25},{25,17},{2,10},{10... | collective-permute-start | bytes 49160 | tf_op jit(solution)/shard_map/ppermute | solution.py:181
  30.8 1.1 %collective-permute-done.5 = bf16[16,512]{1,0:T(8,128)(2,1)S(1)} collective-permute-done((bf16[16,512]{1,0:T(8,128)(2,1)S(1)}, bf16[16,512]{1,0:T(8,128)(2,1)S(1)}, u32[]{:S(2)}, u32[]{:S(2)}) %collective-permute-start.5) | collective-permute-done | bytes 16416 | tf_op jit(solution)/shard_map/ppermute | solution.py:181
  31.9 0.0 collective-permute-done.4
  31.9 0.6 %collective-permute-done.3 = bf16[16,512]{1,0:T(8,128)(2,1)S(1)} collective-permute-done((bf16[16,512]{1,0:T(8,128)(2,1)S(1)}, bf16[16,512]{1,0:T(8,128)(2,1)S(1)}, u32[]{:S(2)}, u32[]{:S(2)}) %collective-permute-start.3) | collective-permute-done | bytes 16416 | tf_op jit(solution)/shard_map/ppermute | solution.py:181
  32.5 2.8 %collective-permute-start.11 = (bf16[64,512]{1,0:T(8,128)(2,1)S(1)}, bf16[64,512]{1,0:T(8,128)(2,1)S(1)}, u32[]{:S(2)}, u32[]{:S(2)}) collective-permute-start(bf16[64,512]{1,0:T(8,128)(2,1)S(1)} %pad_maximum_fusion.refs_2_), channel_id=1, source_target_pairs={{0,6},{1,7},{2,4},{3,5},{4,2},{5,3},{6,0},{7,1},{8,14},{9,15},{10,... | collective-permute-start | bytes 196616 | tf_op jit(solution)/shard_map/ppermute | solution.py:202
  35.3 0.5 %collective-permute-start.9 = (bf16[64,512]{1,0:T(8,128)(2,1)S(1)}, bf16[64,512]{1,0:T(8,128)(2,1)S(1)}, u32[]{:S(2)}, u32[]{:S(2)}) collective-permute-start(bf16[64,512]{1,0:T(8,128)(2,1)S(1)} %pad_maximum_fusion.refs_2_), channel_id=1, source_target_pairs={{0,4},{1,5},{2,6},{3,7},{4,0},{5,1},{6,2},{7,3},{8,12},{9,13},{10,... | collective-permute-start | bytes 196616 | tf_op jit(solution)/shard_map/ppermute | solution.py:202
  35.8 0.2 collective-permute-start.7
  36.0 0.0 collective-permute-start.6
  36.0 7.6 %collective-permute-done.11.refs_8_ = bf16[64,512]{1,0:T(8,128)(2,1)S(1)} collective-permute-done((bf16[64,512]{1,0:T(8,128)(2,1)S(1)}, bf16[64,512]{1,0:T(8,128)(2,1)S(1)}, u32[]{:S(2)}, u32[]{:S(2)}) %collective-permute-start.11) | collective-permute-done | bytes 65568 | tf_op jit(solution)/shard_map/ppermute | solution.py:202
  43.6 0.0 collective-permute-start.12
  43.6 0.2 collective-permute-done.9.refs_6_
  43.8 0.3 collective-permute-start.10
  44.1 0.0 collective-permute-done.7.refs_4_
  44.1 0.2 collective-permute-start.8
  44.3 0.8 %shard_map.87.refs_0_ = bf16[128,256]{1,0:T(8,128)(2,1)S(1)} custom-call(s32[16]{0:T(128)S(1)} %copy-done.5, s32[16]{0:T(128)S(1)} %copy-done.4, s32[16,16]{1,0:T(8,128)S(1)} %copy-done.2, s32[16,16]{1,0:T(8,128)S(1)} %copy-done.3, bf16[16,16,64]{2,1,0:T(8,128)(2,1)S(1)} %copy-done.1), custom_call_target="tpu_custom_call" | custom-call | tf_op jit(solution)/shard_map/pallas_call | solution.py:184
  45.1 0.0 collective-permute-done.6.refs_3_
  45.1 0.0 collective-permute-done.12.refs_9_
  45.1 0.0 collective-permute-done.10.refs_7_
  45.1 0.2 collective-permute-done.8.refs_5_
  45.4 0.0 all-to-all-done.refs_1_
  45.4 3.9 %shard_map.89 = (bf16[2,2,64,4096]{3,2,1,0:T(8,128)(2,1)}, bf16[1,2,4096]{2,1,0:T(2,128)(2,1)}) custom-call(bf16[128,256]{1,0:T(8,128)(2,1)S(1)} %shard_map.87.refs_0_, bf16[8,2,2,64,512]{4,3,2,1,0:T(8,128)(2,1)} %all-to-all-done.refs_1_, bf16[64,512]{1,0:T(8,128)(2,1)S(1)} %pad_maximum_fusion.refs_2_, bf16[64,512]{1,0:T(8,128)(2,1)S(1)} %collective-permute-done.6.refs_3_, ...), custom_call_target="tpu_custom_call" | custom-call | tf_op jit(solution)/shard_map/pallas_call | solution.py:208
  (3 shorter events, 0.0 us)
Async XLA Ops:
  0.6 9.9 %all-to-all-start.1 = ((bf16[8,2,512]{2,1,0:T(2,128)(2,1)}), bf16[8,2,512]{2,1,0:T(2,128)(2,1)S(1)}, u32[]{:S(2)}, u32[]{:S(2)}) async-start(bf16[8,2,512]{2,1,0:T(2,128)(2,1)} %bitcast.11), calls=%async_computation.1 | async-start | bytes 32768 | tf_op jit(solution)/shard_map/all_to_all | solution.py:194
  10.6 4.6 %copy-start = (bf16[16,2,64,512]{3,2,1,0:T(8,128)(2,1)S(1)}, bf16[16,2,64,512]{3,2,1,0:T(8,128)(2,1)}, u32[]{:S(2)}) copy-start(bf16[16,2,64,512]{3,2,1,0:T(8,128)(2,1)} %refs_4_.3) | copy-start | bytes 6291460
  10.6 4.6 %copy-start.1 = (bf16[16,16,64]{2,1,0:T(8,128)(2,1)S(1)}, bf16[16,16,64]{2,1,0:T(8,128)(2,1)}, u32[]{:S(2)}) copy-start(bf16[16,16,64]{2,1,0:T(8,128)(2,1)} %refs_3_.3) | copy-start | bytes 98308
  10.6 4.6 %copy-start.2 = (s32[16,16]{1,0:T(8,128)S(1)}, s32[16,16]{1,0:T(8,128)}, u32[]{:S(2)}) copy-start(s32[16,16]{1,0:T(8,128)} %refs_1_.5) | copy-start | bytes 3076
  10.6 4.6 %copy-start.3 = (s32[16,16]{1,0:T(8,128)S(1)}, s32[16,16]{1,0:T(8,128)}, u32[]{:S(2)}) copy-start(s32[16,16]{1,0:T(8,128)} %refs_2_.3) | copy-start | bytes 3076
  10.6 4.6 %copy-start.4 = (s32[16]{0:T(128)S(1)}, s32[16]{0:T(128)}, u32[]{:S(2)}) copy-start(s32[16]{0:T(128)} %refs_0_.3) | copy-start | bytes 196
  10.6 4.6 %copy-start.5 = (s32[16]{0:T(128)S(1)}, s32[16]{0:T(128)}, u32[]{:S(2)}) copy-start(s32[16]{0:T(128)} %get-tuple-element.8.refs_0_.refs_5_) | copy-start | bytes 196
  10.6 34.8 %all-to-all-start = ((bf16[8,2,2,64,512]{4,3,2,1,0:T(8,128)(2,1)}), bf16[8,2,2,64,512]{4,3,2,1,0:T(8,128)(2,1)}, u32[]{:S(2)}, u32[]{:S(2)}) async-start(bf16[8,2,2,64,512]{4,3,2,1,0:T(8,128)(2,1)} %bitcast.10), calls=%async_computation | async-start | bytes 4194304 | tf_op jit(solution)/shard_map/all_to_all | solution.py:169
  16.4 4.4 %collective-permute-start = (f32[16,512]{1,0:T(8,128)S(1)}, f32[16,512]{1,0:T(8,128)S(1)}, u32[]{:S(2)}, u32[]{:S(2)}) collective-permute-start(f32[16,512]{1,0:T(8,128)S(1)} %get-tuple-element.11), channel_id=1, source_target_pairs={{0,8},{8,0},{16,24},{24,16},{1,9},{9,1},{17,25},{25,17},{2,10},{10... | collective-permute-start | bytes 98312 | tf_op jit(solution)/shard_map/ppermute | solution.py:181
  18.0 5.4 %collective-permute-start.1 = (f32[16,512]{1,0:T(8,128)S(1)}, f32[16,512]{1,0:T(8,128)S(1)}, u32[]{:S(2)}, u32[]{:S(2)}) collective-permute-start(f32[16,512]{1,0:T(8,128)S(1)} %get-tuple-element.12), channel_id=1, source_target_pairs={{0,16},{8,24},{16,0},{24,8},{1,17},{9,25},{17,1},{25,9},{2,18},{10... | collective-permute-start | bytes 98312 | tf_op jit(solution)/shard_map/ppermute | solution.py:181
  20.6 5.7 %collective-permute-start.2 = (f32[16,512]{1,0:T(8,128)S(1)}, f32[16,512]{1,0:T(8,128)S(1)}, u32[]{:S(2)}, u32[]{:S(2)}) collective-permute-start(f32[16,512]{1,0:T(8,128)S(1)} %get-tuple-element.13), channel_id=1, source_target_pairs={{0,24},{8,16},{16,8},{24,0},{1,25},{9,17},{17,9},{25,1},{2,26},{10... | collective-permute-start | bytes 98312 | tf_op jit(solution)/shard_map/ppermute | solution.py:181
  26.3 5.6 %collective-permute-start.5 = (bf16[16,512]{1,0:T(8,128)(2,1)S(1)}, bf16[16,512]{1,0:T(8,128)(2,1)S(1)}, u32[]{:S(2)}, u32[]{:S(2)}) collective-permute-start(bf16[16,512]{1,0:T(8,128)(2,1)S(1)} %fusion), channel_id=1, source_target_pairs={{0,24},{8,16},{16,8},{24,0},{1,25},{9,17},{17,9},{25,1},{2,26},{10... | collective-permute-start | bytes 49160 | tf_op jit(solution)/shard_map/ppermute | solution.py:181
  26.8 5.1 %collective-permute-start.4 = (bf16[16,512]{1,0:T(8,128)(2,1)S(1)}, bf16[16,512]{1,0:T(8,128)(2,1)S(1)}, u32[]{:S(2)}, u32[]{:S(2)}) collective-permute-start(bf16[16,512]{1,0:T(8,128)(2,1)S(1)} %fusion), channel_id=1, source_target_pairs={{0,16},{8,24},{16,0},{24,8},{1,17},{9,25},{17,1},{25,9},{2,18},{10... | collective-permute-start | bytes 49160 | tf_op jit(solution)/shard_map/ppermute | solution.py:181
  26.8 5.7 %collective-permute-start.3 = (bf16[16,512]{1,0:T(8,128)(2,1)S(1)}, bf16[16,512]{1,0:T(8,128)(2,1)S(1)}, u32[]{:S(2)}, u32[]{:S(2)}) collective-permute-start(bf16[16,512]{1,0:T(8,128)(2,1)S(1)} %fusion), channel_id=1, source_target_pairs={{0,8},{8,0},{16,24},{24,16},{1,9},{9,1},{17,25},{25,17},{2,10},{10... | collective-permute-start | bytes 49160 | tf_op jit(solution)/shard_map/ppermute | solution.py:181
  32.5 11.1 %collective-permute-start.11 = (bf16[64,512]{1,0:T(8,128)(2,1)S(1)}, bf16[64,512]{1,0:T(8,128)(2,1)S(1)}, u32[]{:S(2)}, u32[]{:S(2)}) collective-permute-start(bf16[64,512]{1,0:T(8,128)(2,1)S(1)} %pad_maximum_fusion.refs_2_), channel_id=1, source_target_pairs={{0,6},{1,7},{2,4},{3,5},{4,2},{5,3},{6,0},{7,1},{8,14},{9,15},{10,... | collective-permute-start | bytes 196616 | tf_op jit(solution)/shard_map/ppermute | solution.py:202
  35.3 8.5 %collective-permute-start.9 = (bf16[64,512]{1,0:T(8,128)(2,1)S(1)}, bf16[64,512]{1,0:T(8,128)(2,1)S(1)}, u32[]{:S(2)}, u32[]{:S(2)}) collective-permute-start(bf16[64,512]{1,0:T(8,128)(2,1)S(1)} %pad_maximum_fusion.refs_2_), channel_id=1, source_target_pairs={{0,4},{1,5},{2,6},{3,7},{4,0},{5,1},{6,2},{7,3},{8,12},{9,13},{10,... | collective-permute-start | bytes 196616 | tf_op jit(solution)/shard_map/ppermute | solution.py:202
  35.8 8.3 %collective-permute-start.7 = (bf16[64,512]{1,0:T(8,128)(2,1)S(1)}, bf16[64,512]{1,0:T(8,128)(2,1)S(1)}, u32[]{:S(2)}, u32[]{:S(2)}) collective-permute-start(bf16[64,512]{1,0:T(8,128)(2,1)S(1)} %pad_maximum_fusion.refs_2_), channel_id=1, source_target_pairs={{0,2},{1,3},{2,0},{3,1},{4,6},{5,7},{6,4},{7,5},{8,10},{9,11},{10,... | collective-permute-start | bytes 196616 | tf_op jit(solution)/shard_map/ppermute | solution.py:202
  36.0 9.1 %collective-permute-start.6 = (bf16[64,512]{1,0:T(8,128)(2,1)S(1)}, bf16[64,512]{1,0:T(8,128)(2,1)S(1)}, u32[]{:S(2)}, u32[]{:S(2)}) collective-permute-start(bf16[64,512]{1,0:T(8,128)(2,1)S(1)} %pad_maximum_fusion.refs_2_), channel_id=1, source_target_pairs={{0,1},{1,0},{2,3},{3,2},{4,5},{5,4},{6,7},{7,6},{8,9},{9,8},{10,11... | collective-permute-start | bytes 196616 | tf_op jit(solution)/shard_map/ppermute | solution.py:202
  43.6 1.5 %collective-permute-start.12 = (bf16[64,512]{1,0:T(8,128)(2,1)S(1)}, bf16[64,512]{1,0:T(8,128)(2,1)S(1)}, u32[]{:S(2)}, u32[]{:S(2)}) collective-permute-start(bf16[64,512]{1,0:T(8,128)(2,1)S(1)} %collective-permute-done.11.refs_8_), channel_id=1, source_target_pairs={{0,1},{1,0},{2,3},{3,2},{4,5},{5,4},{6,7},{7,6},{8,9},{9,8},{10,11... | collective-permute-start | bytes 196616 | tf_op jit(solution)/shard_map/ppermute | solution.py:202
  43.8 1.3 %collective-permute-start.10 = (bf16[64,512]{1,0:T(8,128)(2,1)S(1)}, bf16[64,512]{1,0:T(8,128)(2,1)S(1)}, u32[]{:S(2)}, u32[]{:S(2)}) collective-permute-start(bf16[64,512]{1,0:T(8,128)(2,1)S(1)} %collective-permute-done.9.refs_6_), channel_id=1, source_target_pairs={{0,1},{1,0},{2,3},{3,2},{4,5},{5,4},{6,7},{7,6},{8,9},{9,8},{10,11... | collective-permute-start | bytes 196616 | tf_op jit(solution)/shard_map/ppermute | solution.py:202
  44.1 1.3 %collective-permute-start.8 = (bf16[64,512]{1,0:T(8,128)(2,1)S(1)}, bf16[64,512]{1,0:T(8,128)(2,1)S(1)}, u32[]{:S(2)}, u32[]{:S(2)}) collective-permute-start(bf16[64,512]{1,0:T(8,128)(2,1)S(1)} %collective-permute-done.7.refs_4_), channel_id=1, source_target_pairs={{0,1},{1,0},{2,3},{3,2},{4,5},{5,4},{6,7},{7,6},{8,9},{9,8},{10,11... | collective-permute-start | bytes 196616 | tf_op jit(solution)/shard_map/ppermute | solution.py:202

commit v5 on v4

--- a/solution.py
+++ b/solution.py
@@ -18,27 +18,45 @@
     return hi, (value - hi.astype(F32)).astype(BF16)
 
 
-def order_blocks(per_owner, owner_ref, spectrum_ref, out_ref, inverse_ref, held, owner, count,
-                 owner_sem, in_sems, out_sems):
-    blocks = spectrum_ref.shape[0]
+def order_blocks(n_pen, per_owner, owner_ref, spectrum_ref, measured_ref, *rest):
+    chips = n_pen // 2
+    first_ref, outs, inverse_ref, rest = rest[0], rest[1 : 1 + chips], rest[1 + chips], rest[2 + chips :]
+    held, tile, below, owner, count, owner_sem, tile_sem, in_sems, out_sems, below_sems = rest
+    blocks, rows, columns = spectrum_ref.shape
+    pen = lax.axis_index("pen")
     get_owner = pltpu.make_async_copy(owner_ref, owner, owner_sem)
     get_owner.start()
+    get_tile = pltpu.make_async_copy(measured_ref, tile, tile_sem)
+    get_tile.start()
     gets, puts = [], []
     for b in range(blocks):
         gets.append(pltpu.make_async_copy(spectrum_ref.at[b], held.at[b], in_sems.at[b]))
         gets[b].start()
-    for o in range(blocks // per_owner):
+    for o in range(n_pen):
         count[o] = 0
     get_owner.wait()
     for b in range(blocks):
         o = owner[b]
         r = count[o]
         count[o] = r + 1
-        at = o * per_owner + r
-        inverse_ref[at] = b
-        gets[b].wait()
-        puts.append(pltpu.make_async_copy(held.at[b], out_ref.at[at], out_sems.at[b]))
-        puts[b].start()
+        inverse_ref[o * per_owner + r] = b
+    get_tile.wait()
+    for o in range(n_pen):
+        part = tile[0, :, o * columns : (o + 1) * columns].astype(F32)
+        below[o] = jnp.concatenate([part, jnp.zeros((14, columns), F32)], axis=0).astype(BF16)
+        puts.append(pltpu.make_async_copy(below.at[o], first_ref.at[o, pl.ds(rows, 16)], below_sems.at[o]))
+        puts[-1].start()
+    for get in gets:
+        get.wait()
+    for o in range(n_pen):
+        from_ref = held.at[inverse_ref[o * per_owner]]
+        puts.append(pltpu.make_async_copy(from_ref, first_ref.at[o, pl.ds(0, rows)], out_sems.at[o, 0]))
+        puts[-1].start()
+    for q in range(n_pen):
+        for r in range(1, per_owner):
+            from_ref = held.at[inverse_ref[(pen ^ q) * per_owner + r]]
+            puts.append(pltpu.make_async_copy(from_ref, outs[q // 2].at[q % 2, r - 1], out_sems.at[q, r]))
+            puts[-1].start()
     for put in puts:
         put.wait()
 
@@ -92,15 +110,38 @@
             place = (at - low) * 2 + c * chunk + low
             hot = jnp.where(place == rows, -8.0, 0.0).astype(BF16)
             hi, lo = split_hi_lo(jnp.dot(hot, weights_ref[b], preferred_element_type=F32))
-            first = (c * per_owner + r) * depth
+            first = (r * 2 + c) * depth
             out_ref[:rows_all, first : first + depth] = hi
             out_ref[rows_all:, first : first + depth] = lo
 
 
-def adjoint(n_pen, chunk, per_owner, table_ref, blocks_ref, *rest):
-    tile_refs, rest = rest[:n_pen], rest[n_pen:]
+def residual_chunk(n_kz, n_pen, *refs):
+    parts, first_ref = refs[:n_kz], refs[n_kz]
+    out_ref, below, sems = refs[n_kz + 1 + n_pen // 2], *refs[-2:]
+    skip = first_ref.shape[1] - 16
+    gets = []
+    for p in range(n_pen):
+        from_ref = first_ref.at[p, pl.ds(skip, 16)]
+        gets.append(pltpu.make_async_copy(from_ref, below.at[pl.ds(16 * p, 16)], sems.at[p]))
+        gets[p].start()
+    total = parts[0][...]
+    for part in parts[1:]:
+        total = total + part[...]
+    to = lax.broadcasted_iota(I32, (2 * n_pen, 16 * n_pen), 0)
+    at = lax.broadcasted_iota(I32, (2 * n_pen, 16 * n_pen), 1)
+    from_row = jnp.where(to >= n_pen, (to - n_pen) * 16 + 1, to * 16)
+    pick = jnp.where(at == from_row, 1.0, 0.0).astype(BF16)
+    for get in gets:
+        get.wait()
+    measured = jnp.dot(pick, below[...], preferred_element_type=F32)
+    out_ref[...] = (total - measured).astype(BF16)
+
+
+def adjoint(n_pen, chunk, per_owner, table_ref, first_ref, *rest):
+    chips = n_pen // 2
+    kept, swapped, tile_refs, rest = rest[:chips], rest[chips:n_pen], rest[n_pen : 2 * n_pen], rest[2 * n_pen :]
     out_ref, residual_ref, made, out_sems = rest
-    depth, columns = blocks_ref.shape[3:]
+    span, columns = swapped[0].shape[1:]
     rows = tile_refs[0].shape[0]
     pen = lax.axis_index("pen")
     puts = []
@@ -108,9 +149,10 @@
     pick_at = lax.broadcasted_iota(I32, (16, rows), 1)
     pick = jnp.where(pick_at == pick_row * chunk + pen, 1.0, 0.0)
     pick = jnp.where(pick_row < 2, pick, 0.0).astype(BF16)
-    for j in range(n_pen):
-        first_column = pl.multiple_of((pen ^ j) * columns, columns)
-        here = tile_refs[j][...]
+    for q in range(n_pen):
+        first_column = pl.multiple_of((pen ^ q) * columns, columns)
+        later = swapped[q // 2] if q % 2 else kept[q // 2].at[0]
+        here = tile_refs[q][...]
         own = jnp.dot(pick, here, preferred_element_type=F32)
         residual_ref[0, :, pl.ds(first_column, columns)] = own[:2].astype(BF16)
         step = lax.dot_general(
@@ -120,13 +162,11 @@
             preferred_element_type=F32,
         )
         for r in range(per_owner):
-            for c in range(2):
-                first = (c * per_owner + r) * depth
-                held = blocks_ref[pen ^ j, r, c].astype(F32)
-                made[j, r, c] = (held + step[first : first + depth]).astype(BF16)
-        to = out_ref.at[:, :, :, pl.ds(first_column, columns)]
-        puts.append(pltpu.make_async_copy(made.at[j], to, out_sems.at[j]))
-        puts[j].start()
+            held = later[r - 1] if r else first_ref[pen ^ q, :span]
+            made[q, r] = (held.astype(F32) + step[r * span : (r + 1) * span]).astype(BF16)
+        to = out_ref.at[:, :, pl.ds(first_column, columns)]
+        puts.append(pltpu.make_async_copy(made.at[q], to, out_sems.at[q]))
+        puts[-1].start()
     for put in puts:
         put.wait()
 
@@ -141,32 +181,42 @@
     chunk = tile_dev * n_pen
     tiles = chunk * n_kz
     tiles_per_tilt = tiles // tilt_pos.shape[0]
+    chips = n_pen // 2
 
     def call(kernel, *static):
         def bound(*refs):
             return kernel(*static, *refs)
         return bound
 
-    ordered, inverse = pl.pallas_call(
-        call(order_blocks, per_owner),
-        out_shape=[
-            jax.ShapeDtypeStruct(spectrum.shape, BF16),
-            jax.ShapeDtypeStruct((blocks,), I32),
-        ],
-        in_specs=[ANY, ANY],
-        out_specs=[ANY, SMEM],
+    def across(value, k):
+        return lax.ppermute(value, "kz", [(i, i ^ k) for i in range(n_kz)])
+
+    def between(value, k):
+        return lax.ppermute(value, "pen", [(i, i ^ k) for i in range(n_pen)])
+
+    span = 2 * depth
+    first, *outs, inverse = pl.pallas_call(
+        call(order_blocks, n_pen, per_owner),
+        out_shape=[jax.ShapeDtypeStruct((n_pen, span + 16, columns), BF16)]
+        + [jax.ShapeDtypeStruct((2, per_owner - 1, span, columns), BF16)] * chips
+        + [jax.ShapeDtypeStruct((blocks,), I32)],
+        in_specs=[ANY, ANY, ANY],
+        out_specs=[ANY] * (chips + 1) + [SMEM],
         scratch_shapes=[
-            pltpu.VMEM(spectrum.shape, BF16),
+            pltpu.VMEM((blocks, span, columns), BF16),
+            pltpu.VMEM(measured.shape, BF16),
+            pltpu.VMEM((n_pen, 16, columns), BF16),
             pltpu.SMEM((blocks,), I32),
             pltpu.SMEM((n_pen,), I32),
             pltpu.SemaphoreType.DMA,
+            pltpu.SemaphoreType.DMA,
             pltpu.SemaphoreType.DMA((blocks,)),
-            pltpu.SemaphoreType.DMA((blocks,)),
+            pltpu.SemaphoreType.DMA((n_pen, per_owner)),
+            pltpu.SemaphoreType.DMA((n_pen,)),
         ],
         compiler_params=pltpu.CompilerParams(vmem_limit_bytes=62 << 20),
-    )(owner, spectrum)
-    outgoing = ordered.reshape(n_pen, per_owner, 2, depth, columns)
-    incoming = lax.all_to_all(outgoing, "pen", split_axis=0, concat_axis=0, tiled=True)
+    )(owner, spectrum.reshape(blocks, span, columns), measured)
+    first = lax.all_to_all(first, "pen", split_axis=0, concat_axis=0, tiled=True)
 
     parts = pl.pallas_call(
         call(forward, n_kz, chunk, tiles_per_tilt),
@@ -176,9 +226,6 @@
         scratch_shapes=[pltpu.VMEM((2 * tiles, blocks * depth), BF16)],
         compiler_params=pltpu.CompilerParams(vmem_limit_bytes=16 << 20),
     )(tilt_pos, pair_tilt, pair_tile_within, depth_weights, spectrum, inverse)
-
-    def across(value, k):
-        return lax.ppermute(value, "kz", [(i, i ^ k) for i in range(n_kz)])
 
     summed = [parts[0]] + [across(parts[k], k) for k in range(1, n_kz)]
     table = pl.pallas_call(
@@ -190,35 +237,45 @@
         compiler_params=pltpu.CompilerParams(vmem_limit_bytes=8 << 20),
     )(inverse, tilt_pos, pair_tilt, pair_tile_within, depth_weights)
 
-    sent = measured.reshape(2, n_pen, columns).transpose(1, 0, 2)
-    got = lax.all_to_all(sent, "pen", split_axis=0, concat_axis=0, tiled=True)
-    measured_rows = got.transpose(1, 0, 2).reshape(2 * chunk, columns)
-    total = summed[0]
-    for part in summed[1:]:
-        total = total + part
-    own = (total - measured_rows.astype(F32)).astype(BF16)
-
-    def between(value, k):
-        return lax.ppermute(value, "pen", [(i, i ^ k) for i in range(n_pen)])
-
-    held = jnp.concatenate([own] + [across(own, k) for k in range(1, n_kz)], axis=0)
+    own, *outs = pl.pallas_call(
+        call(residual_chunk, n_kz, n_pen),
+        out_shape=[jax.ShapeDtypeStruct((2 * chunk, columns), BF16)]
+        + [jax.ShapeDtypeStruct(out.shape, BF16) for out in outs],
+        in_specs=[VMEM] * n_kz + [ANY] * (chips + 1),
+        out_specs=[VMEM] + [ANY] * chips,
+        scratch_shapes=[
+            pltpu.VMEM((16 * n_pen, columns), BF16),
+            pltpu.SemaphoreType.DMA((n_pen,)),
+        ],
+        input_output_aliases={n_kz + 1 + i: 1 + i for i in range(chips)},
+        compiler_params=pltpu.CompilerParams(vmem_limit_bytes=56 << 20),
+    )(*summed, first, *outs)
+    kept = [outs[0]] + [between(outs[i], 2 * i) for i in range(1, chips)]
+
+    held = own
+    step = 1
+    while step < n_kz:
+        held = jnp.concatenate([held, across(held, step)], axis=0)
+        step *= 2
     every = [held] + [between(held, k) for k in range(2, n_pen, 2)]
-    every = [tile for kept in every for tile in (kept, between(kept, 1))]
+    every = [tile for one in every for tile in (one, between(one, 1))]
+    swapped = [between(one[1], 1) for one in kept]
 
     updated, residual = pl.pallas_call(
         call(adjoint, n_pen, chunk, per_owner),
         out_shape=[
-            jax.ShapeDtypeStruct((per_owner, 2, depth, cells), BF16),
+            jax.ShapeDtypeStruct((per_owner, span, cells), BF16),
             jax.ShapeDtypeStruct((tile_dev, 2, cells), BF16),
         ],
-        in_specs=[VMEM] * (n_pen + 2),
+        in_specs=[VMEM] * (2 * n_pen + 2),
         out_specs=[ANY, VMEM],
         scratch_shapes=[
-            pltpu.VMEM((n_pen, per_owner, 2, depth, columns), BF16),
+            pltpu.VMEM((n_pen, per_owner, span, columns), BF16),
             pltpu.SemaphoreType.DMA((n_pen,)),
         ],
         compiler_params=pltpu.CompilerParams(vmem_limit_bytes=16 << 20),
-    )(table, incoming, *every)
+    )(table, first, *kept, *swapped, *every)
+    updated = updated.reshape(per_owner, 2, depth, cells)
     return (updated, residual)
 
 

time: 49.6 us -> 59.9 us (1.21)
  local copies, waits for them, and re-layouts: 0.03 us -> 4.29 us
  waiting for transfers between devices: 16.9 us -> 19.5 us
  Pallas kernels: 9.05 us -> 10.6 us
  starting transfers between devices: 22.6 us -> 23.4 us
  other arithmetic: 0.03 us -> 0.72 us
    ppermute x7 -> x14, starting transfers between devices: 4 us -> 9.45 us  [between(): return lax.ppermute(value, 'pen', [(i, i ^ k) for i in range(n_pen)])]
    all_to_all x2 -> x1, starting transfers between devices: 9.69 us -> 5.31 us  [body(): lax.all_to_all(first, 'pen', split_axis=0, concat_axis=0, tiled=True)]
    all_to_all x2 -> x1, waiting for transfers between devices: 1.66 us -> 5.03 us  [body(): lax.all_to_all(first, 'pen', split_axis=0, concat_axis=0, tiled=True)]
    unnamed x12 -> x28, local copies, waits for them, and re-layouts: 0.03 us -> 3.34 us
    pallas_call x1 -> x2, Pallas kernels: 3.09 us -> 6.25 us  [the longest x1 3.8 us: body(): pl.pallas_call(call(order_blocks, n_pen, per_owner), out_shape=[jax.Shape...]
    pallas_call x1, Pallas kernels: 3.94 us -> 2.36 us  [body(): pl.pallas_call(call(adjoint, n_pen, chunk, per_owner), out_shape=[jax.Sha...]
    ppermute x7 -> x14, waiting for transfers between devices: 8.02 us -> 6.48 us  [between(): return lax.ppermute(value, 'pen', [(i, i ^ k) for i in range(n_pen)])]
    squeeze x0 -> x4, local copies, waits for them, and re-layouts: none -> 0.94 us  [body(): swapped = [between(one[1], 1) for one in kept]]
  transfers between devices with their start and end apart: 15 -> 20, of which waited for: 8 -> 7; matrix products, arithmetic and copies ran while one was open for 0% -> 4% of each run, Pallas kernels for 10% -> 3%
where the time goes in v5:
time: 59.9 us; the launch traced here: 59.3 us
  starting transfers between devices  23.4 us (39%)
  waiting for transfers between devices  19.5 us (33%)
  Pallas kernels  10.6 us (18%)
  local copies, waits for them, and re-layouts  4.29 us (7%)
  between operations  0.85 us (1%)
  other arithmetic  0.72 us (1%)
    ppermute x14, starting transfers between devices, between(): return lax.ppermute(value, 'pen', [(i, i ^ k) for i in range(n_pen)])  9.45 us
    ppermute x5, starting transfers between devices, across(): return lax.ppermute(value, 'kz', [(i, i ^ k) for i in range(n_kz)])  8.62 us
    ppermute x5, waiting for transfers between devices, across(): return lax.ppermute(value, 'kz', [(i, i ^ k) for i in range(n_kz)])  7.95 us
    ppermute x14, waiting for transfers between devices, between(): return lax.ppermute(value, 'pen', [(i, i ^ k) for i in range(n_pen)])  6.48 us
    all_to_all x1, starting transfers between devices, body(): lax.all_to_all(first, 'pen', split_axis=0, concat_axis=0, tiled=True)  5.31 us
    all_to_all x1, waiting for transfers between devices, body(): lax.all_to_all(first, 'pen', split_axis=0, concat_axis=0, tiled=True)  5.03 us
    pallas_call x1, Pallas kernels, body(): pl.pallas_call(call(order_blocks, n_pen, per_owner), out_shape=[jax.Shape...  3.8 us
    unnamed x28, local copies, waits for them, and re-layouts  3.34 us
  transfers between devices with their start and end apart: 20, of which 7 were waited for; matrix products, arithmetic and copies ran while one was open for 4% of the time, Pallas kernels for 3%

profile of v5, /device:TPU:0, one launch (start us, length us, event | category | flops | bytes accessed | tf_op | source)
XLA Modules:
  0.0 59.3 jit_solution(3646106751698390249)
XLA Ops:
  0.7 3.8 %shard_map.86 = (bf16[8,144,512]{2,1,0:T(8,128)(2,1)}, bf16[2,1,128,512]{3,2,1,0:T(8,128)(2,1)}, bf16[2,1,128,512]{3,2,1,0:T(8,128)(2,1)}, bf16[2,1,128,512]{3,2...) custom-call(s32[16]{0:T(128)} %refs_0_.2, bf16[16,128,512]{2,1,0:T(8,128)(2,1)} %bitcast.10, ...), custom_call_target="tpu_custom_call" | custom-call | tf_op jit(solution)/shard_map/pallas_call | solution.py:198
  4.5 0.0 copy-start.2
  4.5 0.0 copy-start.9
  4.5 5.3 %all-to-all-start = ((bf16[8,144,512]{2,1,0:T(8,128)(2,1)}), bf16[8,144,512]{2,1,0:T(8,128)(2,1)S(1)}, u32[]{:S(2)}, u32[]{:S(2)}) async-start(bf16[8,144,512]{2,1,0:T(8,128)(2,1)} %get-tuple-element.20), calls=%async_computation | async-start | bytes 2359296 | tf_op jit(solution)/shard_map/all_to_all | solution.py:219
  9.9 1.2 %shard_map.88 = (f32[16,512]{1,0:T(8,128)S(1)}, f32[16,512]{1,0:T(8,128)S(1)}, f32[16,512]{1,0:T(8,128)S(1)}, f32[16,512]{1,0:T(8,128)S(1)}) custom-call(s32[16]{0:T(128)S(1)} %copy-done.8, s32[16,16]{1,0:T(8,128)S(1)} %copy-done.6, s32[16,16]{1,0:T(8,128)S(1)} %copy-done.7, bf16[16,16,64]{2,1,0:T(8,128)(2,1)S(1)} %copy-done.4, ...), custom_call_target="tpu_custom_call" | custom-call | tf_op jit(solution)/shard_map/pallas_call | solution.py:221
  11.1 0.6 %copy-done.5 = f32[16,512]{1,0:T(8,128)} copy-done((f32[16,512]{1,0:T(8,128)}, f32[16,512]{1,0:T(8,128)S(1)}, u32[]{:S(2)}) %copy-start.5) | copy-done | bytes 32792
  11.7 1.6 %collective-permute-start = (f32[16,512]{1,0:T(8,128)S(1)}, f32[16,512]{1,0:T(8,128)S(1)}, u32[]{:S(2)}, u32[]{:S(2)}) collective-permute-start(f32[16,512]{1,0:T(8,128)S(1)} %get-tuple-element.22), channel_id=1, source_target_pairs={{0,8},{8,0},{16,24},{24,16},{1,9},{9,1},{17,25},{25,17},{2,10},{10... | collective-permute-start | bytes 98312 | tf_op jit(solution)/shard_map/ppermute | solution.py:192
  13.3 2.6 %collective-permute-start.1 = (f32[16,512]{1,0:T(8,128)S(1)}, f32[16,512]{1,0:T(8,128)S(1)}, u32[]{:S(2)}, u32[]{:S(2)}) collective-permute-start(f32[16,512]{1,0:T(8,128)S(1)} %get-tuple-element.23), channel_id=1, source_target_pairs={{0,16},{8,24},{16,0},{24,8},{1,17},{9,25},{17,1},{25,9},{2,18},{10... | collective-permute-start | bytes 98312 | tf_op jit(solution)/shard_map/ppermute | solution.py:192
  15.9 0.2 collective-permute-start.2
  16.1 0.0 collective-permute-done.refs_1_
  16.1 2.6 %collective-permute-done.1.refs_2_ = f32[16,512]{1,0:T(8,128)S(1)} collective-permute-done((f32[16,512]{1,0:T(8,128)S(1)}, f32[16,512]{1,0:T(8,128)S(1)}, u32[]{:S(2)}, u32[]{:S(2)}) %collective-permute-start.1) | collective-permute-done | bytes 32800 | tf_op jit(solution)/shard_map/ppermute | solution.py:192
  18.7 2.9 %collective-permute-done.2.refs_3_ = f32[16,512]{1,0:T(8,128)S(1)} collective-permute-done((f32[16,512]{1,0:T(8,128)S(1)}, f32[16,512]{1,0:T(8,128)S(1)}, u32[]{:S(2)}, u32[]{:S(2)}) %collective-permute-start.2) | collective-permute-done | bytes 32800 | tf_op jit(solution)/shard_map/ppermute | solution.py:192
  21.6 5.0 %all-to-all-done.refs_4_.refs_1_ = bf16[8,144,512]{2,1,0:T(8,128)(2,1)S(1)} async-done(((bf16[8,144,512]{2,1,0:T(8,128)(2,1)}), bf16[8,144,512]{2,1,0:T(8,128)(2,1)S(1)}, u32[]{:S(2)}, u32[]{:S(2)}) %all-to-all-start) | async-done | bytes 1179680 | tf_op jit(solution)/shard_map/all_to_all | solution.py:219
  26.6 1.0 %copy-done = bf16[8,144,512]{2,1,0:T(8,128)(2,1)} copy-done((bf16[8,144,512]{2,1,0:T(8,128)(2,1)}, bf16[8,144,512]{2,1,0:T(8,128)(2,1)S(1)}, u32[]{:S(2)}) %copy-start) | copy-done | bytes 1179672
  27.6 2.5 %shard_map.89 = (bf16[16,512]{1,0:T(8,128)(2,1)}, bf16[2,1,128,512]{3,2,1,0:T(8,128)(2,1)}, bf16[2,1,128,512]{3,2,1,0:T(8,128)(2,1)}, bf16[2,1,128,512]{3,2,1,0:T(8,128)(2,1)}, bf16[2,1,128,512]{3,2,1,0:T(8,128)(2,1)}) custom-call(f32[16,512]{1,0:T(8,128)} %copy-done.5, ...), custom_call_target="tpu_custom_call", output_to_operand_aliasing={{1}: (5, {}), {2}: (6, {}), {3}: (7, {}), {4}: (8, {})} | custom-call | tf_op jit(solution)/shard_map/pallas_call | solution.py:240
  30.1 0.0 copy-start.1
  30.1 1.6 %collective-permute-start.10 = (bf16[16,512]{1,0:T(8,128)(2,1)}, bf16[16,512]{1,0:T(8,128)(2,1)S(1)}, u32[]{:S(2)}, u32[]{:S(2)}) collective-permute-start(bf16[16,512]{1,0:T(8,128)(2,1)} %get-tuple-element.33), channel_id=1, source_target_pairs={{0,8},{8,0},{16,24},{24,16},{1,9},{9,1},{17,25},{25,17},{2,10},{10... | collective-permute-start | bytes 49160 | tf_op jit(solution)/shard_map/ppermute | solution.py:192
  31.8 0.9 %slice_bitcast_fusion.3 = bf16[1,128,512]{2,1,0:T(8,128)(2,1)S(1)} fusion(bf16[2,1,128,512]{3,2,1,0:T(8,128)(2,1)} %get-tuple-element.29.refs_2_), kind=kLoop, calls=%fused_computation.3 | loop fusion | bytes 262144 | tf_op jit(solution)/shard_map/squeeze | solution.py:262
  32.7 0.7 %constant_dynamic-update-slice_fusion.2 = bf16[64,512]{1,0:T(8,128)(2,1)S(1)} fusion(bf16[16,512]{1,0:T(8,128)(2,1)} %get-tuple-element.33), kind=kLoop, calls=%fused_computation.7 | loop fusion | bytes 32768
  33.4 0.5 collective-permute-start.3
  33.9 0.7 %collective-permute-start.4 = (bf16[2,1,128,512]{3,2,1,0:T(8,128)(2,1)}, bf16[2,1,128,512]{3,2,1,0:T(8,128)(2,1)S(1)}, u32[]{:S(2)}, u32[]{:S(2)}) collective-permute-start(bf16[2,1,128,512]{3,2,1,0:T(8,128)(2,1)} %get-tuple-element.31), channel_id=1, source_target_pairs={{0,4},{1,5},{2,6},{3,7},{4,0},{5,1},{6,2},{7,3},{8,12},{9,13},{10,... | collective-permute-start | bytes 786440 | tf_op jit(solution)/shard_map/ppermute | solution.py:195
  34.6 2.3 %collective-permute-start.5 = (bf16[2,1,128,512]{3,2,1,0:T(8,128)(2,1)}, bf16[2,1,128,512]{3,2,1,0:T(8,128)(2,1)S(1)}, u32[]{:S(2)}, u32[]{:S(2)}) collective-permute-start(bf16[2,1,128,512]{3,2,1,0:T(8,128)(2,1)} %get-tuple-element.32), channel_id=1, source_target_pairs={{0,6},{1,7},{2,4},{3,5},{4,2},{5,3},{6,0},{7,1},{8,14},{9,15},{10,... | collective-permute-start | bytes 786440 | tf_op jit(solution)/shard_map/ppermute | solution.py:195
  36.9 0.0 collective-permute-done.10
  36.9 0.7 %pad_maximum_fusion = bf16[32,512]{1,0:T(8,128)(2,1)S(1)} fusion(bf16[16,512]{1,0:T(8,128)(2,1)S(1)} %collective-permute-done.10, bf16[16,512]{1,0:T(8,128)(2,1)} %get-tuple-element.33), kind=kLoop, calls=%fused_computation.4 | loop fusion | flops 65536 | bytes 65536 | tf_op jit(solution)/shard_map/concatenate | solution.py:258
  37.6 2.6 %collective-permute-start.11 = (bf16[32,512]{1,0:T(8,128)(2,1)S(1)}, bf16[32,512]{1,0:T(8,128)(2,1)S(1)}, u32[]{:S(2)}, u32[]{:S(2)}) collective-permute-start(bf16[32,512]{1,0:T(8,128)(2,1)S(1)} %pad_maximum_fusion), channel_id=1, source_target_pairs={{0,16},{8,24},{16,0},{24,8},{1,17},{9,25},{17,1},{25,9},{2,18},{10... | collective-permute-start | bytes 98312 | tf_op jit(solution)/shard_map/ppermute | solution.py:192
  40.2 2.5 %collective-permute-done.11 = bf16[32,512]{1,0:T(8,128)(2,1)S(1)} collective-permute-done((bf16[32,512]{1,0:T(8,128)(2,1)S(1)}, bf16[32,512]{1,0:T(8,128)(2,1)S(1)}, u32[]{:S(2)}, u32[]{:S(2)}) %collective-permute-start.11) | collective-permute-done | bytes 32800 | tf_op jit(solution)/shard_map/ppermute | solution.py:192
  42.7 0.6 %collective-permute-start.17 = (bf16[64,512]{1,0:T(8,128)(2,1)S(1)}, bf16[64,512]{1,0:T(8,128)(2,1)S(1)}, u32[]{:S(2)}, u32[]{:S(2)}) collective-permute-start(bf16[64,512]{1,0:T(8,128)(2,1)S(1)} %constant_dynamic-update-slice_fusion.refs_10_), channel_id=1, source_target_pairs={{0,6},{1,7},{2,4},{3,5},{4,2},{5,3},{6,0},{7,1},{8,14},{9,15},{10,... | collective-permute-start | bytes 196616 | tf_op jit(solution)/shard_map/ppermute | solution.py:195
  43.3 0.0 collective-permute-done.3.refs_3_
  43.3 1.4 %collective-permute-start.15 = (bf16[64,512]{1,0:T(8,128)(2,1)S(1)}, bf16[64,512]{1,0:T(8,128)(2,1)S(1)}, u32[]{:S(2)}, u32[]{:S(2)}) collective-permute-start(bf16[64,512]{1,0:T(8,128)(2,1)S(1)} %constant_dynamic-update-slice_fusion.refs_10_), channel_id=1, source_target_pairs={{0,4},{1,5},{2,6},{3,7},{4,0},{5,1},{6,2},{7,3},{8,12},{9,13},{10,... | collective-permute-start | bytes 196616 | tf_op jit(solution)/shard_map/ppermute | solution.py:195
  44.7 4.9 %collective-permute-done.4.refs_4_ = bf16[2,1,128,512]{3,2,1,0:T(8,128)(2,1)S(1)} collective-permute-done((bf16[2,1,128,512]{3,2,1,0:T(8,128)(2,1)}, bf16[2,1,128,512]{3,2,1,0:T(8,128)(2,1)S(1)}, u32[]{:S(2)}, u32[]{:S(2)}) %collective-permute-start.4) | collective-permute-done | bytes 262176 | tf_op jit(solution)/shard_map/ppermute | solution.py:195
  49.5 2.3 %collective-permute-start.13 = (bf16[64,512]{1,0:T(8,128)(2,1)S(1)}, bf16[64,512]{1,0:T(8,128)(2,1)S(1)}, u32[]{:S(2)}, u32[]{:S(2)}) collective-permute-start(bf16[64,512]{1,0:T(8,128)(2,1)S(1)} %constant_dynamic-update-slice_fusion.refs_10_), channel_id=1, source_target_pairs={{0,2},{1,3},{2,0},{3,1},{4,6},{5,7},{6,4},{7,5},{8,10},{9,11},{10,... | collective-permute-start | bytes 196616 | tf_op jit(solution)/shard_map/ppermute | solution.py:195
  51.8 0.1 collective-permute-start.12
  51.9 0.0 collective-permute-done.5.refs_5_
  51.9 0.5 collective-permute-start.18
  52.4 0.2 collective-permute-start.7
  52.6 1.5 %collective-permute-done.13.refs_12_ = bf16[64,512]{1,0:T(8,128)(2,1)S(1)} collective-permute-done((bf16[64,512]{1,0:T(8,128)(2,1)S(1)}, bf16[64,512]{1,0:T(8,128)(2,1)S(1)}, u32[]{:S(2)}, u32[]{:S(2)}) %collective-permute-start.13) | collective-permute-done | bytes 65568 | tf_op jit(solution)/shard_map/ppermute | solution.py:195
  54.0 0.0 collective-permute-start.8
  54.0 0.5 collective-permute-start.9
  54.6 0.1 collective-permute-start.16
  54.6 0.0 collective-permute-done.18.refs_17_
  54.6 0.4 collective-permute-start.14
  55.1 0.8 %shard_map.87.refs_0_ = bf16[128,256]{1,0:T(8,128)(2,1)S(1)} custom-call(s32[16]{0:T(128)S(1)} %copy-done.9, s32[16]{0:T(128)S(1)} %copy-done.8, s32[16,16]{1,0:T(8,128)S(1)} %copy-done.6, s32[16,16]{1,0:T(8,128)S(1)} %copy-done.7, bf16[16,16,64]{2,1,0:T(8,128)(2,1)S(1)} %copy-done.4), custom_call_target="tpu_custom_call" | custom-call | tf_op jit(solution)/shard_map/pallas_call | solution.py:231
  55.9 0.1 collective-permute-done.14.refs_13_
  56.0 0.0 collective-permute-done.7.refs_7_
  56.0 0.0 collective-permute-done.8.refs_8_
  56.0 0.0 collective-permute-done.9.refs_9_
  56.0 0.9 %copy-done.3 = bf16[2,1,128,512]{3,2,1,0:T(8,128)(2,1)S(1)} copy-done((bf16[2,1,128,512]{3,2,1,0:T(8,128)(2,1)S(1)}, bf16[2,1,128,512]{3,2,1,0:T(8,128)(2,1)}, u32[]{:S(2)}) %copy-start.3) | copy-done | bytes 262168
  57.0 2.4 %shard_map.90 = (bf16[2,128,4096]{2,1,0:T(8,128)(2,1)}, bf16[1,2,4096]{2,1,0:T(2,128)(2,1)}) custom-call(bf16[128,256]{1,0:T(8,128)(2,1)S(1)} %shard_map.87.refs_0_, bf16[8,144,512]{2,1,0:T(8,128)(2,1)S(1)} %copy-done.1, bf16[2,1,128,512]{3,2,1,0:T(8,128)(2,1)S(1)} %copy-done.3, bf16[2,1,128,512]{3,2,1,0:T(8,128)(2,1)S(1)} %collective-permute-done.3.refs_3_, ...), custom_call_target="tpu_custom_call" | custom-call | tf_op jit(solution)/shard_map/pallas_call | solution.py:264
  (31 shorter events, 0.1 us)
Async XLA Ops:
  0.6 9.2 %copy-start.4 = (bf16[16,16,64]{2,1,0:T(8,128)(2,1)S(1)}, bf16[16,16,64]{2,1,0:T(8,128)(2,1)}, u32[]{:S(2)}) copy-start(bf16[16,16,64]{2,1,0:T(8,128)(2,1)} %refs_3_.3) | copy-start | bytes 98308
  0.6 9.2 %copy-start.6 = (s32[16,16]{1,0:T(8,128)S(1)}, s32[16,16]{1,0:T(8,128)}, u32[]{:S(2)}) copy-start(s32[16,16]{1,0:T(8,128)} %refs_1_.3) | copy-start | bytes 3076
  0.7 9.2 %copy-start.7 = (s32[16,16]{1,0:T(8,128)S(1)}, s32[16,16]{1,0:T(8,128)}, u32[]{:S(2)}) copy-start(s32[16,16]{1,0:T(8,128)} %refs_2_.5) | copy-start | bytes 3076
  0.7 9.2 %copy-start.8 = (s32[16]{0:T(128)S(1)}, s32[16]{0:T(128)}, u32[]{:S(2)}) copy-start(s32[16]{0:T(128)} %refs_0_.3) | copy-start | bytes 196
  4.5 5.4 %copy-start.2 = (bf16[16,2,64,512]{3,2,1,0:T(8,128)(2,1)S(1)}, bf16[16,2,64,512]{3,2,1,0:T(8,128)(2,1)}, u32[]{:S(2)}) copy-start(bf16[16,2,64,512]{3,2,1,0:T(8,128)(2,1)} %refs_4_.3) | copy-start | bytes 6291460
  4.5 5.4 %copy-start.9 = (s32[16]{0:T(128)S(1)}, s32[16]{0:T(128)}, u32[]{:S(2)}) copy-start(s32[16]{0:T(128)} %get-tuple-element.19.refs_0_.refs_5_) | copy-start | bytes 196
  4.5 22.1 %all-to-all-start = ((bf16[8,144,512]{2,1,0:T(8,128)(2,1)}), bf16[8,144,512]{2,1,0:T(8,128)(2,1)S(1)}, u32[]{:S(2)}, u32[]{:S(2)}) async-start(bf16[8,144,512]{2,1,0:T(8,128)(2,1)} %get-tuple-element.20), calls=%async_computation | async-start | bytes 2359296 | tf_op jit(solution)/shard_map/all_to_all | solution.py:219
  11.1 0.6 %copy-start.5 = (f32[16,512]{1,0:T(8,128)}, f32[16,512]{1,0:T(8,128)S(1)}, u32[]{:S(2)}) copy-start(f32[16,512]{1,0:T(8,128)S(1)} %get-tuple-element.21.refs_0_) | copy-start | bytes 98308
  11.7 4.4 %collective-permute-start = (f32[16,512]{1,0:T(8,128)S(1)}, f32[16,512]{1,0:T(8,128)S(1)}, u32[]{:S(2)}, u32[]{:S(2)}) collective-permute-start(f32[16,512]{1,0:T(8,128)S(1)} %get-tuple-element.22), channel_id=1, source_target_pairs={{0,8},{8,0},{16,24},{24,16},{1,9},{9,1},{17,25},{25,17},{2,10},{10... | collective-permute-start | bytes 98312 | tf_op jit(solution)/shard_map/ppermute | solution.py:192
  13.3 5.4 %collective-permute-start.1 = (f32[16,512]{1,0:T(8,128)S(1)}, f32[16,512]{1,0:T(8,128)S(1)}, u32[]{:S(2)}, u32[]{:S(2)}) collective-permute-start(f32[16,512]{1,0:T(8,128)S(1)} %get-tuple-element.23), channel_id=1, source_target_pairs={{0,16},{8,24},{16,0},{24,8},{1,17},{9,25},{17,1},{25,9},{2,18},{10... | collective-permute-start | bytes 98312 | tf_op jit(solution)/shard_map/ppermute | solution.py:192
  15.9 5.7 %collective-permute-start.2 = (f32[16,512]{1,0:T(8,128)S(1)}, f32[16,512]{1,0:T(8,128)S(1)}, u32[]{:S(2)}, u32[]{:S(2)}) collective-permute-start(f32[16,512]{1,0:T(8,128)S(1)} %get-tuple-element.24), channel_id=1, source_target_pairs={{0,24},{8,16},{16,8},{24,0},{1,25},{9,17},{17,9},{25,1},{2,26},{10... | collective-permute-start | bytes 98312 | tf_op jit(solution)/shard_map/ppermute | solution.py:192
  16.1 10.5 %copy-start.10 = (f32[16,512]{1,0:T(8,128)}, f32[16,512]{1,0:T(8,128)S(1)}, u32[]{:S(2)}) copy-start(f32[16,512]{1,0:T(8,128)S(1)} %collective-permute-done.refs_1_) | copy-start | bytes 98308
  18.7 7.9 %copy-start.11 = (f32[16,512]{1,0:T(8,128)}, f32[16,512]{1,0:T(8,128)S(1)}, u32[]{:S(2)}) copy-start(f32[16,512]{1,0:T(8,128)S(1)} %collective-permute-done.1.refs_2_) | copy-start | bytes 98308
  21.6 5.0 %copy-start.12 = (f32[16,512]{1,0:T(8,128)}, f32[16,512]{1,0:T(8,128)S(1)}, u32[]{:S(2)}) copy-start(f32[16,512]{1,0:T(8,128)S(1)} %collective-permute-done.2.refs_3_) | copy-start | bytes 98308
  26.6 1.0 %copy-start = (bf16[8,144,512]{2,1,0:T(8,128)(2,1)}, bf16[8,144,512]{2,1,0:T(8,128)(2,1)S(1)}, u32[]{:S(2)}) copy-start(bf16[8,144,512]{2,1,0:T(8,128)(2,1)S(1)} %all-to-all-done.refs_4_.refs_1_) | copy-start | bytes 3538948
  30.1 25.9 %copy-start.1 = (bf16[8,144,512]{2,1,0:T(8,128)(2,1)S(1)}, bf16[8,144,512]{2,1,0:T(8,128)(2,1)}, u32[]{:S(2)}) copy-start(bf16[8,144,512]{2,1,0:T(8,128)(2,1)} %copy-done) | copy-start | bytes 3538948
  30.1 6.8 %collective-permute-start.10 = (bf16[16,512]{1,0:T(8,128)(2,1)}, bf16[16,512]{1,0:T(8,128)(2,1)S(1)}, u32[]{:S(2)}, u32[]{:S(2)}) collective-permute-start(bf16[16,512]{1,0:T(8,128)(2,1)} %get-tuple-element.33), channel_id=1, source_target_pairs={{0,8},{8,0},{16,24},{24,16},{1,9},{9,1},{17,25},{25,17},{2,10},{10... | collective-permute-start | bytes 49160 | tf_op jit(solution)/shard_map/ppermute | solution.py:192
  33.4 21.2 %collective-permute-start.6 = (bf16[1,128,512]{2,1,0:T(8,128)(2,1)S(1)}, bf16[1,128,512]{2,1,0:T(8,128)(2,1)S(1)}, u32[]{:S(2)}, u32[]{:S(2)}) collective-permute-start(bf16[1,128,512]{2,1,0:T(8,128)(2,1)S(1)} %slice_bitcast_fusion.3), channel_id=1, source_target_pairs={{0,1},{1,0},{2,3},{3,2},{4,5},{5,4},{6,7},{7,6},{8,9},{9,8},{10,11... | collective-permute-start | bytes 393224 | tf_op jit(solution)/shard_map/ppermute | solution.py:195
  33.4 9.9 %collective-permute-start.3 = (bf16[2,1,128,512]{3,2,1,0:T(8,128)(2,1)}, bf16[2,1,128,512]{3,2,1,0:T(8,128)(2,1)S(1)}, u32[]{:S(2)}, u32[]{:S(2)}) collective-permute-start(bf16[2,1,128,512]{3,2,1,0:T(8,128)(2,1)} %get-tuple-element.30), channel_id=1, source_target_pairs={{0,2},{1,3},{2,0},{3,1},{4,6},{5,7},{6,4},{7,5},{8,10},{9,11},{10,... | collective-permute-start | bytes 786440 | tf_op jit(solution)/shard_map/ppermute | solution.py:195
  33.9 15.6 %collective-permute-start.4 = (bf16[2,1,128,512]{3,2,1,0:T(8,128)(2,1)}, bf16[2,1,128,512]{3,2,1,0:T(8,128)(2,1)S(1)}, u32[]{:S(2)}, u32[]{:S(2)}) collective-permute-start(bf16[2,1,128,512]{3,2,1,0:T(8,128)(2,1)} %get-tuple-element.31), channel_id=1, source_target_pairs={{0,4},{1,5},{2,6},{3,7},{4,0},{5,1},{6,2},{7,3},{8,12},{9,13},{10,... | collective-permute-start | bytes 786440 | tf_op jit(solution)/shard_map/ppermute | solution.py:195
  34.6 17.3 %collective-permute-start.5 = (bf16[2,1,128,512]{3,2,1,0:T(8,128)(2,1)}, bf16[2,1,128,512]{3,2,1,0:T(8,128)(2,1)S(1)}, u32[]{:S(2)}, u32[]{:S(2)}) collective-permute-start(bf16[2,1,128,512]{3,2,1,0:T(8,128)(2,1)} %get-tuple-element.32), channel_id=1, source_target_pairs={{0,6},{1,7},{2,4},{3,5},{4,2},{5,3},{6,0},{7,1},{8,14},{9,15},{10,... | collective-permute-start | bytes 786440 | tf_op jit(solution)/shard_map/ppermute | solution.py:195
  37.6 5.1 %collective-permute-start.11 = (bf16[32,512]{1,0:T(8,128)(2,1)S(1)}, bf16[32,512]{1,0:T(8,128)(2,1)S(1)}, u32[]{:S(2)}, u32[]{:S(2)}) collective-permute-start(bf16[32,512]{1,0:T(8,128)(2,1)S(1)} %pad_maximum_fusion), channel_id=1, source_target_pairs={{0,16},{8,24},{16,0},{24,8},{1,17},{9,25},{17,1},{25,9},{2,18},{10... | collective-permute-start | bytes 98312 | tf_op jit(solution)/shard_map/ppermute | solution.py:192
  42.7 9.1 %collective-permute-start.17 = (bf16[64,512]{1,0:T(8,128)(2,1)S(1)}, bf16[64,512]{1,0:T(8,128)(2,1)S(1)}, u32[]{:S(2)}, u32[]{:S(2)}) collective-permute-start(bf16[64,512]{1,0:T(8,128)(2,1)S(1)} %constant_dynamic-update-slice_fusion.refs_10_), channel_id=1, source_target_pairs={{0,6},{1,7},{2,4},{3,5},{4,2},{5,3},{6,0},{7,1},{8,14},{9,15},{10,... | collective-permute-start | bytes 196616 | tf_op jit(solution)/shard_map/ppermute | solution.py:195
  43.3 9.1 %collective-permute-start.15 = (bf16[64,512]{1,0:T(8,128)(2,1)S(1)}, bf16[64,512]{1,0:T(8,128)(2,1)S(1)}, u32[]{:S(2)}, u32[]{:S(2)}) collective-permute-start(bf16[64,512]{1,0:T(8,128)(2,1)S(1)} %constant_dynamic-update-slice_fusion.refs_10_), channel_id=1, source_target_pairs={{0,4},{1,5},{2,6},{3,7},{4,0},{5,1},{6,2},{7,3},{8,12},{9,13},{10,... | collective-permute-start | bytes 196616 | tf_op jit(solution)/shard_map/ppermute | solution.py:195
  49.5 4.5 %collective-permute-start.13 = (bf16[64,512]{1,0:T(8,128)(2,1)S(1)}, bf16[64,512]{1,0:T(8,128)(2,1)S(1)}, u32[]{:S(2)}, u32[]{:S(2)}) collective-permute-start(bf16[64,512]{1,0:T(8,128)(2,1)S(1)} %constant_dynamic-update-slice_fusion.refs_10_), channel_id=1, source_target_pairs={{0,2},{1,3},{2,0},{3,1},{4,6},{5,7},{6,4},{7,5},{8,10},{9,11},{10,... | collective-permute-start | bytes 196616 | tf_op jit(solution)/shard_map/ppermute | solution.py:195
  51.8 2.2 %collective-permute-start.12 = (bf16[64,512]{1,0:T(8,128)(2,1)S(1)}, bf16[64,512]{1,0:T(8,128)(2,1)S(1)}, u32[]{:S(2)}, u32[]{:S(2)}) collective-permute-start(bf16[64,512]{1,0:T(8,128)(2,1)S(1)} %constant_dynamic-update-slice_fusion.refs_10_), channel_id=1, source_target_pairs={{0,1},{1,0},{2,3},{3,2},{4,5},{5,4},{6,7},{7,6},{8,9},{9,8},{10,11... | collective-permute-start | bytes 196616 | tf_op jit(solution)/shard_map/ppermute | solution.py:195
  51.9 2.7 %collective-permute-start.18 = (bf16[64,512]{1,0:T(8,128)(2,1)S(1)}, bf16[64,512]{1,0:T(8,128)(2,1)S(1)}, u32[]{:S(2)}, u32[]{:S(2)}) collective-permute-start(bf16[64,512]{1,0:T(8,128)(2,1)S(1)} %collective-permute-done.17.refs_16_), channel_id=1, source_target_pairs={{0,1},{1,0},{2,3},{3,2},{4,5},{5,4},{6,7},{7,6},{8,9},{9,8},{10,11... | collective-permute-start | bytes 196616 | tf_op jit(solution)/shard_map/ppermute | solution.py:195
  52.4 3.6 %collective-permute-start.7 = (bf16[1,128,512]{2,1,0:T(8,128)(2,1)S(1)}, bf16[1,128,512]{2,1,0:T(8,128)(2,1)S(1)}, u32[]{:S(2)}, u32[]{:S(2)}) collective-permute-start(bf16[1,128,512]{2,1,0:T(8,128)(2,1)S(1)} %slice_bitcast_fusion.2), channel_id=1, source_target_pairs={{0,1},{1,0},{2,3},{3,2},{4,5},{5,4},{6,7},{7,6},{8,9},{9,8},{10,11... | collective-permute-start | bytes 393224 | tf_op jit(solution)/shard_map/ppermute | solution.py:195
  54.0 1.9 %collective-permute-start.8 = (bf16[1,128,512]{2,1,0:T(8,128)(2,1)S(1)}, bf16[1,128,512]{2,1,0:T(8,128)(2,1)S(1)}, u32[]{:S(2)}, u32[]{:S(2)}) collective-permute-start(bf16[1,128,512]{2,1,0:T(8,128)(2,1)S(1)} %slice_bitcast_fusion.1), channel_id=1, source_target_pairs={{0,1},{1,0},{2,3},{3,2},{4,5},{5,4},{6,7},{7,6},{8,9},{9,8},{10,11... | collective-permute-start | bytes 393224 | tf_op jit(solution)/shard_map/ppermute | solution.py:195
  54.0 1.9 %collective-permute-start.9 = (bf16[1,128,512]{2,1,0:T(8,128)(2,1)S(1)}, bf16[1,128,512]{2,1,0:T(8,128)(2,1)S(1)}, u32[]{:S(2)}, u32[]{:S(2)}) collective-permute-start(bf16[1,128,512]{2,1,0:T(8,128)(2,1)S(1)} %slice_bitcast_fusion), channel_id=1, source_target_pairs={{0,1},{1,0},{2,3},{3,2},{4,5},{5,4},{6,7},{7,6},{8,9},{9,8},{10,11... | collective-permute-start | bytes 393224 | tf_op jit(solution)/shard_map/ppermute | solution.py:195
  54.6 1.3 %collective-permute-start.16 = (bf16[64,512]{1,0:T(8,128)(2,1)S(1)}, bf16[64,512]{1,0:T(8,128)(2,1)S(1)}, u32[]{:S(2)}, u32[]{:S(2)}) collective-permute-start(bf16[64,512]{1,0:T(8,128)(2,1)S(1)} %collective-permute-done.15.refs_14_), channel_id=1, source_target_pairs={{0,1},{1,0},{2,3},{3,2},{4,5},{5,4},{6,7},{7,6},{8,9},{9,8},{10,11... | collective-permute-start | bytes 196616 | tf_op jit(solution)/shard_map/ppermute | solution.py:195
  54.6 1.3 %collective-permute-start.14 = (bf16[64,512]{1,0:T(8,128)(2,1)S(1)}, bf16[64,512]{1,0:T(8,128)(2,1)S(1)}, u32[]{:S(2)}, u32[]{:S(2)}) collective-permute-start(bf16[64,512]{1,0:T(8,128)(2,1)S(1)} %collective-permute-done.13.refs_12_), channel_id=1, source_target_pairs={{0,1},{1,0},{2,3},{3,2},{4,5},{5,4},{6,7},{7,6},{8,9},{9,8},{10,11... | collective-permute-start | bytes 196616 | tf_op jit(solution)/shard_map/ppermute | solution.py:195
  56.0 1.0 %copy-start.3 = (bf16[2,1,128,512]{3,2,1,0:T(8,128)(2,1)S(1)}, bf16[2,1,128,512]{3,2,1,0:T(8,128)(2,1)}, u32[]{:S(2)}) copy-start(bf16[2,1,128,512]{3,2,1,0:T(8,128)(2,1)} %get-tuple-element.29.refs_2_) | copy-start | bytes 786436

commit v6 on v4

--- a/solution.py
+++ b/solution.py
@@ -18,27 +18,32 @@
     return hi, (value - hi.astype(F32)).astype(BF16)
 
 
-def order_blocks(per_owner, owner_ref, spectrum_ref, out_ref, inverse_ref, held, owner, count,
-                 owner_sem, in_sems, out_sems):
+def order_blocks(n_pen, per_owner, owner_ref, spectrum_ref, *rest):
+    chips = n_pen // 2
+    outs, (inverse_ref, held, owner, count, owner_sem, in_sems, out_sems) = rest[:chips], rest[chips:]
     blocks = spectrum_ref.shape[0]
+    pen = lax.axis_index("pen")
     get_owner = pltpu.make_async_copy(owner_ref, owner, owner_sem)
     get_owner.start()
     gets, puts = [], []
     for b in range(blocks):
         gets.append(pltpu.make_async_copy(spectrum_ref.at[b], held.at[b], in_sems.at[b]))
         gets[b].start()
-    for o in range(blocks // per_owner):
+    for o in range(n_pen):
         count[o] = 0
     get_owner.wait()
     for b in range(blocks):
         o = owner[b]
         r = count[o]
         count[o] = r + 1
-        at = o * per_owner + r
-        inverse_ref[at] = b
-        gets[b].wait()
-        puts.append(pltpu.make_async_copy(held.at[b], out_ref.at[at], out_sems.at[b]))
-        puts[b].start()
+        inverse_ref[o * per_owner + r] = b
+    for get in gets:
+        get.wait()
+    for q in range(n_pen):
+        for r in range(per_owner):
+            from_ref = held.at[inverse_ref[(pen ^ q) * per_owner + r]]
+            puts.append(pltpu.make_async_copy(from_ref, outs[q // 2].at[q % 2, r], out_sems.at[q, r]))
+            puts[-1].start()
     for put in puts:
         put.wait()
 
@@ -51,9 +56,8 @@
 
 
 def forward(n_kz, chunk, tiles_per_tilt, tilt_pos_ref, tilt_ref, within_ref, weights_ref,
-            spectrum_ref, after_ref, *rest):
+            spectrum_ref, after_ref, kept_ref, sent_ref, table):
     del after_ref
-    outs, table = rest[:n_kz], rest[n_kz]
     blocks, pairs, depth = weights_ref.shape
     columns = spectrum_ref.shape[3]
     tiles = n_kz * chunk
@@ -73,7 +77,8 @@
         )
         total = both[:tiles] + both[tiles:]
         for k in range(n_kz):
-            outs[k][c * chunk : (c + 1) * chunk, :] = total[k * chunk : (k + 1) * chunk]
+            out_ref = sent_ref if k % 2 else kept_ref
+            out_ref[k // 2, c * chunk : (c + 1) * chunk, :] = total[k * chunk : (k + 1) * chunk]
 
 
 def adjoint_table(n_kz, chunk, per_owner, tiles_per_tilt, inverse_ref, tilt_pos_ref, tilt_ref,
@@ -97,10 +102,23 @@
             out_ref[rows_all:, first : first + depth] = lo
 
 
-def adjoint(n_pen, chunk, per_owner, table_ref, blocks_ref, *rest):
-    tile_refs, rest = rest[:n_pen], rest[n_pen:]
+def other_core(*refs):
+    count = len(refs) // 2
+    in_refs, out_refs = refs[: count - 1], refs[count:-1]
+    sems = refs[-1]
+    copies = []
+    for i, (in_ref, out_ref) in enumerate(zip(in_refs, out_refs)):
+        copies.append(pltpu.make_async_copy(in_ref.at[1], out_ref, sems.at[i]))
+        copies[i].start()
+    for copy in copies:
+        copy.wait()
+
+
+def adjoint(n_pen, chunk, per_owner, table_ref, *rest):
+    chips = n_pen // 2
+    kept, swapped, tile_refs, rest = rest[:chips], rest[chips:n_pen], rest[n_pen : 2 * n_pen], rest[2 * n_pen :]
     out_ref, residual_ref, made, out_sems = rest
-    depth, columns = blocks_ref.shape[3:]
+    depth, columns = swapped[0].shape[2:]
     rows = tile_refs[0].shape[0]
     pen = lax.axis_index("pen")
     puts = []
@@ -108,9 +126,10 @@
     pick_at = lax.broadcasted_iota(I32, (16, rows), 1)
     pick = jnp.where(pick_at == pick_row * chunk + pen, 1.0, 0.0)
     pick = jnp.where(pick_row < 2, pick, 0.0).astype(BF16)
-    for j in range(n_pen):
-        first_column = pl.multiple_of((pen ^ j) * columns, columns)
-        here = tile_refs[j][...]
+    for q in range(n_pen):
+        first_column = pl.multiple_of((pen ^ q) * columns, columns)
+        blocks = swapped[q // 2] if q % 2 else kept[q // 2].at[0]
+        here = tile_refs[q][...]
         own = jnp.dot(pick, here, preferred_element_type=F32)
         residual_ref[0, :, pl.ds(first_column, columns)] = own[:2].astype(BF16)
         step = lax.dot_general(
@@ -122,11 +141,11 @@
         for r in range(per_owner):
             for c in range(2):
                 first = (c * per_owner + r) * depth
-                held = blocks_ref[pen ^ j, r, c].astype(F32)
-                made[j, r, c] = (held + step[first : first + depth]).astype(BF16)
+                held = blocks[r, c].astype(F32)
+                made[q, r, c] = (held + step[first : first + depth]).astype(BF16)
         to = out_ref.at[:, :, :, pl.ds(first_column, columns)]
-        puts.append(pltpu.make_async_copy(made.at[j], to, out_sems.at[j]))
-        puts[j].start()
+        puts.append(pltpu.make_async_copy(made.at[q], to, out_sems.at[q]))
+        puts[-1].start()
     for put in puts:
         put.wait()
 
@@ -142,45 +161,53 @@
     tiles = chunk * n_kz
     tiles_per_tilt = tiles // tilt_pos.shape[0]
 
+    chips = n_pen // 2
+
     def call(kernel, *static):
         def bound(*refs):
             return kernel(*static, *refs)
         return bound
 
-    ordered, inverse = pl.pallas_call(
-        call(order_blocks, per_owner),
-        out_shape=[
-            jax.ShapeDtypeStruct(spectrum.shape, BF16),
-            jax.ShapeDtypeStruct((blocks,), I32),
-        ],
+    def across(value, k):
+        return lax.ppermute(value, "kz", [(i, i ^ k) for i in range(n_kz)])
+
+    def between(value, k):
+        return lax.ppermute(value, "pen", [(i, i ^ k) for i in range(n_pen)])
+
+    *outs, inverse = pl.pallas_call(
+        call(order_blocks, n_pen, per_owner),
+        out_shape=[jax.ShapeDtypeStruct((2, per_owner, 2, depth, columns), BF16)] * chips
+        + [jax.ShapeDtypeStruct((blocks,), I32)],
         in_specs=[ANY, ANY],
-        out_specs=[ANY, SMEM],
+        out_specs=[ANY] * chips + [SMEM],
         scratch_shapes=[
             pltpu.VMEM(spectrum.shape, BF16),
             pltpu.SMEM((blocks,), I32),
             pltpu.SMEM((n_pen,), I32),
             pltpu.SemaphoreType.DMA,
             pltpu.SemaphoreType.DMA((blocks,)),
-            pltpu.SemaphoreType.DMA((blocks,)),
+            pltpu.SemaphoreType.DMA((n_pen, per_owner)),
         ],
         compiler_params=pltpu.CompilerParams(vmem_limit_bytes=62 << 20),
     )(owner, spectrum)
-    outgoing = ordered.reshape(n_pen, per_owner, 2, depth, columns)
-    incoming = lax.all_to_all(outgoing, "pen", split_axis=0, concat_axis=0, tiled=True)
-
-    parts = pl.pallas_call(
+    far_first = [between(outs[i], 2 * i) for i in range(chips - 1, 0, -1)]
+    kept = [outs[0]] + far_first[::-1]
+
+    sums, sent = pl.pallas_call(
         call(forward, n_kz, chunk, tiles_per_tilt),
-        out_shape=[jax.ShapeDtypeStruct((2 * chunk, columns), F32)] * n_kz,
+        out_shape=[jax.ShapeDtypeStruct((n_kz // 2, 2 * chunk, columns), F32)] * 2,
         in_specs=[SMEM, VMEM, VMEM, VMEM, VMEM, ANY],
-        out_specs=[VMEM] * n_kz,
+        out_specs=[VMEM, VMEM],
         scratch_shapes=[pltpu.VMEM((2 * tiles, blocks * depth), BF16)],
         compiler_params=pltpu.CompilerParams(vmem_limit_bytes=16 << 20),
     )(tilt_pos, pair_tilt, pair_tile_within, depth_weights, spectrum, inverse)
-
-    def across(value, k):
-        return lax.ppermute(value, "kz", [(i, i ^ k) for i in range(n_kz)])
-
-    summed = [parts[0]] + [across(parts[k], k) for k in range(1, n_kz)]
+    sums = sums + across(sent, 1)
+    step = 2
+    while step < n_kz:
+        sums = sums.reshape(-1, 2, 2 * chunk, columns)
+        sums = sums[:, 0] + across(sums[:, 1], step)
+        step *= 2
+
     table = pl.pallas_call(
         call(adjoint_table, n_kz, chunk, per_owner, tiles_per_tilt),
         out_shape=jax.ShapeDtypeStruct((4 * tiles, 2 * per_owner * depth), BF16),
@@ -193,17 +220,24 @@
     sent = measured.reshape(2, n_pen, columns).transpose(1, 0, 2)
     got = lax.all_to_all(sent, "pen", split_axis=0, concat_axis=0, tiled=True)
     measured_rows = got.transpose(1, 0, 2).reshape(2 * chunk, columns)
-    total = summed[0]
-    for part in summed[1:]:
-        total = total + part
-    own = (total - measured_rows.astype(F32)).astype(BF16)
-
-    def between(value, k):
-        return lax.ppermute(value, "pen", [(i, i ^ k) for i in range(n_pen)])
-
-    held = jnp.concatenate([own] + [across(own, k) for k in range(1, n_kz)], axis=0)
+    own = (sums.reshape(2 * chunk, columns) - measured_rows.astype(F32)).astype(BF16)
+
+    held = own
+    step = 1
+    while step < n_kz:
+        held = jnp.concatenate([held, across(held, step)], axis=0)
+        step *= 2
+    other = pl.pallas_call(
+        other_core,
+        out_shape=[jax.ShapeDtypeStruct(outs[0].shape[1:], BF16)] * (chips - 1),
+        in_specs=[ANY] * chips,
+        out_specs=[ANY] * (chips - 1),
+        scratch_shapes=[pltpu.SemaphoreType.DMA((chips - 1,))],
+        compiler_params=pltpu.CompilerParams(vmem_limit_bytes=8 << 20),
+    )(*kept[1:], held)
+    swapped = [between(one, 1) for one in [outs[0][1], *other]]
     every = [held] + [between(held, k) for k in range(2, n_pen, 2)]
-    every = [tile for kept in every for tile in (kept, between(kept, 1))]
+    every = [tile for one in every for tile in (one, between(one, 1))]
 
     updated, residual = pl.pallas_call(
         call(adjoint, n_pen, chunk, per_owner),
@@ -211,14 +245,14 @@
             jax.ShapeDtypeStruct((per_owner, 2, depth, cells), BF16),
             jax.ShapeDtypeStruct((tile_dev, 2, cells), BF16),
         ],
-        in_specs=[VMEM] * (n_pen + 2),
+        in_specs=[VMEM] * (2 * n_pen + 1),
         out_specs=[ANY, VMEM],
         scratch_shapes=[
             pltpu.VMEM((n_pen, per_owner, 2, depth, columns), BF16),
             pltpu.SemaphoreType.DMA((n_pen,)),
         ],
         compiler_params=pltpu.CompilerParams(vmem_limit_bytes=16 << 20),
-    )(table, incoming, *every)
+    )(table, *kept, *swapped, *every)
     return (updated, residual)
 
 

time: 49.6 us -> 58.6 us (1.18)
  waiting for transfers between devices: 16.9 us -> 28 us
  starting transfers between devices: 22.6 us -> 19 us
  local copies, waits for them, and re-layouts: 0.03 us -> 2.3 us
  Pallas kernels: 9.05 us -> 8.17 us
    ppermute x7 -> x14, waiting for transfers between devices: 8.02 us -> 21.2 us  [between(): return lax.ppermute(value, 'pen', [(i, i ^ k) for i in range(n_pen)])]
    all_to_all x1 -> x0, starting transfers between devices: 4.51 us -> none  [body(): lax.all_to_all(outgoing, 'pen', split_axis=0, concat_axis=0, tiled=True)]
    ppermute x7 -> x14, starting transfers between devices: 4 us -> 6.94 us  [between(): return lax.ppermute(value, 'pen', [(i, i ^ k) for i in range(n_pen)])]
    unnamed x12 -> x22, local copies, waits for them, and re-layouts: 0.03 us -> 2.28 us
    all_to_all x1, waiting for transfers between devices: 1.65 us -> 0.07 us  [body(): got = lax.all_to_all(sent, 'pen', split_axis=0, concat_axis=0, tiled=True)]
    pallas_call x1, Pallas kernels: 3.94 us -> 2.36 us  [body(): pl.pallas_call(call(adjoint, n_pen, chunk, per_owner), out_shape=[jax.Sha...]
    all_to_all x1, starting transfers between devices: 5.18 us -> 3.73 us  [body(): got = lax.all_to_all(sent, 'pen', split_axis=0, concat_axis=0, tiled=True)]
    pallas_call x1 -> x2, Pallas kernels: 3.09 us -> 3.8 us  [the longest x1 3.71 us: body(): pl.pallas_call(call(order_blocks, n_pen, per_owner), out_shape=[jax.Shape...]
  transfers between devices with their start and end apart: 15 -> 19, of which waited for: 8 -> 9; matrix products, arithmetic and copies ran while one was open for 0% -> 0% of each run, Pallas kernels for 10% -> 2%
where the time goes in v6:
time: 58.6 us; the launch traced here: 58.3 us
  waiting for transfers between devices  28 us (48%)
  starting transfers between devices  19 us (32%)
  Pallas kernels  8.17 us (14%)
  local copies, waits for them, and re-layouts  2.3 us (4%)
  between operations  0.82 us (1%)
    ppermute x14, waiting for transfers between devices, between(): return lax.ppermute(value, 'pen', [(i, i ^ k) for i in range(n_pen)])  21.2 us
    ppermute x4, starting transfers between devices, across(): return lax.ppermute(value, 'kz', [(i, i ^ k) for i in range(n_kz)])  8.35 us
    ppermute x14, starting transfers between devices, between(): return lax.ppermute(value, 'pen', [(i, i ^ k) for i in range(n_pen)])  6.94 us
    ppermute x4, waiting for transfers between devices, across(): return lax.ppermute(value, 'kz', [(i, i ^ k) for i in range(n_kz)])  6.73 us
    all_to_all x1, starting transfers between devices, body(): got = lax.all_to_all(sent, 'pen', split_axis=0, concat_axis=0, tiled=True)  3.73 us
    pallas_call x1, Pallas kernels, body(): pl.pallas_call(call(order_blocks, n_pen, per_owner), out_shape=[jax.Shape...  3.71 us
    pallas_call x1, Pallas kernels, body(): pl.pallas_call(call(adjoint, n_pen, chunk, per_owner), out_shape=[jax.Sha...  2.36 us
    unnamed x22, local copies, waits for them, and re-layouts  2.28 us
  transfers between devices with their start and end apart: 19, of which 9 were waited for; matrix products, arithmetic and copies ran while one was open for 0% of the time, Pallas kernels for 2%

profile of v6, /device:TPU:0, one launch (start us, length us, event | category | flops | bytes accessed | tf_op | source)
XLA Modules:
  0.0 58.3 jit_solution(5272823039303396126)
XLA Ops:
  0.6 0.0 copy-start.5
  0.6 0.0 copy-start.4
  0.7 3.7 %shard_map.86 = (bf16[2,2,2,64,512]{4,3,2,1,0:T(8,128)(2,1)}, bf16[2,2,2,64,512]{4,3,2,1,0:T(8,128)(2,1)}, bf16[2,2,2,64,512]{4,3,2,1,0:T(8,128)(2,1)}, bf16[2,2,2,64,512]{4,3,2,1,0:T(8,128)(2,1)}, s32[16]{0:T(128)}) custom-call(s32[16]{0:T(128)} %refs_0_.2, bf16[16,2,64,512]{3,2,1,0:T(8,128)(2,1)} %refs_4_.3), custom_call_target="tpu_custom_call" | custom-call | tf_op jit(solution)/shard_map/pallas_call | solution.py:177
  4.4 0.0 copy-start
  4.4 1.6 %copy-done = bf16[16,2,64,512]{3,2,1,0:T(8,128)(2,1)S(1)} copy-done((bf16[16,2,64,512]{3,2,1,0:T(8,128)(2,1)S(1)}, bf16[16,2,64,512]{3,2,1,0:T(8,128)(2,1)}, u32[]{:S(2)}) %copy-start) | copy-done | bytes 2097176
  6.0 0.7 %copy-done.6 = s32[16]{0:T(128)S(1)} copy-done((s32[16]{0:T(128)S(1)}, s32[16]{0:T(128)}, u32[]{:S(2)}) %copy-start.6) | copy-done | bytes 88
  6.7 1.2 %shard_map.88 = (f32[2,16,512]{2,1,0:T(8,128)S(1)}, f32[2,16,512]{2,1,0:T(8,128)S(1)}) custom-call(s32[16]{0:T(128)S(1)} %copy-done.5, s32[16,16]{1,0:T(8,128)S(1)} %copy-done.3, s32[16,16]{1,0:T(8,128)S(1)} %copy-done.4, bf16[16,16,64]{2,1,0:T(8,128)(2,1)S(1)} %copy-done.2, bf16[16,2,64,512]{3,2,1,0:T(8,128)(2,1)S(1)} %copy-done, s32[16]{0:T(128)S(1)} %copy-done.6), custom_call_target="tpu_custom_call" | custom-call | tf_op jit(solution)/shard_map/pallas_call | solution.py:196
  7.9 3.0 %collective-permute-start.4 = (f32[2,16,512]{2,1,0:T(8,128)S(1)}, f32[2,16,512]{2,1,0:T(8,128)S(1)}, u32[]{:S(2)}, u32[]{:S(2)}) collective-permute-start(f32[2,16,512]{2,1,0:T(8,128)S(1)} %get-tuple-element.18), channel_id=1, source_target_pairs={{0,8},{8,0},{16,24},{24,16},{1,9},{9,1},{17,25},{25,17},{2,10},{10... | collective-permute-start | bytes 196616 | tf_op jit(solution)/shard_map/ppermute | solution.py:172
  11.0 3.7 %all-to-all-start = ((bf16[8,2,512]{2,1,0:T(2,128)(2,1)}), bf16[8,2,512]{2,1,0:T(2,128)(2,1)S(1)}, u32[]{:S(2)}, u32[]{:S(2)}) async-start(bf16[8,2,512]{2,1,0:T(2,128)(2,1)} %bitcast.6), calls=%async_computation | async-start | bytes 32768 | tf_op jit(solution)/shard_map/all_to_all | solution.py:221
  14.7 2.0 %collective-permute-start = (bf16[2,2,2,64,512]{4,3,2,1,0:T(8,128)(2,1)S(1)}, bf16[2,2,2,64,512]{4,3,2,1,0:T(8,128)(2,1)S(1)}, u32[]{:S(2)}, u32[]{:S(2)}) collective-permute-start(bf16[2,2,2,64,512]{4,3,2,1,0:T(8,128)(2,1)S(1)} %copy-done.10), channel_id=1, source_target_pairs={{0,2},{1,3},{2,0},{3,1},{4,6},{5,7},{6,4},{7,5},{8,10},{9,11},{10,... | collective-permute-start | bytes 1572872 | tf_op jit(solution)/shard_map/ppermute | solution.py:175
  16.7 0.0 collective-permute-done.4
  16.7 2.7 %collective-permute-start.5 = (f32[1,16,512]{2,1,0:T(8,128)S(1)}, f32[1,16,512]{2,1,0:T(8,128)S(1)}, u32[]{:S(2)}, u32[]{:S(2)}) collective-permute-start(f32[1,16,512]{2,1,0:T(8,128)S(1)} %slice_bitcast_fusion.1), channel_id=1, source_target_pairs={{0,16},{8,24},{16,0},{24,8},{1,17},{9,25},{17,1},{25,9},{2,18},{10... | collective-permute-start | bytes 98312 | tf_op jit(solution)/shard_map/ppermute | solution.py:172
  19.4 0.1 all-to-all-done
  19.5 2.4 %collective-permute-done.5 = f32[1,16,512]{2,1,0:T(8,128)S(1)} collective-permute-done((f32[1,16,512]{2,1,0:T(8,128)S(1)}, f32[1,16,512]{2,1,0:T(8,128)S(1)}, u32[]{:S(2)}, u32[]{:S(2)}) %collective-permute-start.5) | collective-permute-done | bytes 32800 | tf_op jit(solution)/shard_map/ppermute | solution.py:172
  21.9 0.3 collective-permute-start.6
  22.2 1.5 %collective-permute-start.1 = (bf16[2,2,2,64,512]{4,3,2,1,0:T(8,128)(2,1)S(1)}, bf16[2,2,2,64,512]{4,3,2,1,0:T(8,128)(2,1)S(1)}, u32[]{:S(2)}, u32[]{:S(2)}) collective-permute-start(bf16[2,2,2,64,512]{4,3,2,1,0:T(8,128)(2,1)S(1)} %copy-done.9), channel_id=1, source_target_pairs={{0,4},{1,5},{2,6},{3,7},{4,0},{5,1},{6,2},{7,3},{8,12},{9,13},{10,... | collective-permute-start | bytes 1572872 | tf_op jit(solution)/shard_map/ppermute | solution.py:175
  23.6 0.1 collective-permute-start.2
  23.7 2.0 %collective-permute-done.6 = bf16[16,512]{1,0:T(8,128)(2,1)S(1)} collective-permute-done((bf16[16,512]{1,0:T(8,128)(2,1)S(1)}, bf16[16,512]{1,0:T(8,128)(2,1)S(1)}, u32[]{:S(2)}, u32[]{:S(2)}) %collective-permute-start.6) | collective-permute-done | bytes 16416 | tf_op jit(solution)/shard_map/ppermute | solution.py:172
  25.7 2.4 %collective-permute-start.7 = (bf16[32,512]{1,0:T(8,128)(2,1)S(1)}, bf16[32,512]{1,0:T(8,128)(2,1)S(1)}, u32[]{:S(2)}, u32[]{:S(2)}) collective-permute-start(bf16[32,512]{1,0:T(8,128)(2,1)S(1)} %pad_maximum_fusion.1), channel_id=1, source_target_pairs={{0,16},{8,24},{16,0},{24,8},{1,17},{9,25},{17,1},{25,9},{2,18},{10... | collective-permute-start | bytes 98312 | tf_op jit(solution)/shard_map/ppermute | solution.py:172
  28.1 0.1 collective-permute-start.3
  28.1 2.4 %collective-permute-done.7 = bf16[32,512]{1,0:T(8,128)(2,1)S(1)} collective-permute-done((bf16[32,512]{1,0:T(8,128)(2,1)S(1)}, bf16[32,512]{1,0:T(8,128)(2,1)S(1)}, u32[]{:S(2)}, u32[]{:S(2)}) %collective-permute-start.7) | collective-permute-done | bytes 32800 | tf_op jit(solution)/shard_map/ppermute | solution.py:172
  30.5 1.4 %collective-permute-start.16 = (bf16[64,512]{1,0:T(8,128)(2,1)S(1)}, bf16[64,512]{1,0:T(8,128)(2,1)S(1)}, u32[]{:S(2)}, u32[]{:S(2)}) collective-permute-start(bf16[64,512]{1,0:T(8,128)(2,1)S(1)} %pad_maximum_fusion.refs_3_.refs_9_), channel_id=1, source_target_pairs={{0,6},{1,7},{2,4},{3,5},{4,2},{5,3},{6,0},{7,1},{8,14},{9,15},{10,... | collective-permute-start | bytes 196616 | tf_op jit(solution)/shard_map/ppermute | solution.py:175
  32.0 0.0 collective-permute-done.refs_0_.refs_2_
  32.0 0.2 collective-permute-start.14
  32.2 15.8 %collective-permute-done.1.refs_1_.refs_3_ = bf16[2,2,2,64,512]{4,3,2,1,0:T(8,128)(2,1)S(1)} collective-permute-done((bf16[2,2,2,64,512]{4,3,2,1,0:T(8,128)(2,1)S(1)}, bf16[2,2,2,64,512]{4,3,2,1,0:T(8,128)(2,1)S(1)}, u32[]{:S(2)}, u32[]{:S(2)}) %collective-permute-start.1) | collective-permute-done | bytes 524320 | tf_op jit(solution)/shard_map/ppermute | solution.py:175
  47.9 0.4 collective-permute-start.12
  48.3 0.0 collective-permute-done.2.refs_2_.refs_4_
  48.3 0.1 shard_map.89
  48.4 0.1 collective-permute-start.8
  48.5 0.0 collective-permute-done.16.refs_15_
  48.5 0.5 collective-permute-start.9
  49.0 0.0 collective-permute-done.14.refs_13_
  49.0 0.1 collective-permute-start.10
  49.1 3.1 %collective-permute-done.12.refs_11_ = bf16[64,512]{1,0:T(8,128)(2,1)S(1)} collective-permute-done((bf16[64,512]{1,0:T(8,128)(2,1)S(1)}, bf16[64,512]{1,0:T(8,128)(2,1)S(1)}, u32[]{:S(2)}, u32[]{:S(2)}) %collective-permute-start.12) | collective-permute-done | bytes 65568 | tf_op jit(solution)/shard_map/ppermute | solution.py:175
  52.2 0.0 collective-permute-start.11
  52.2 1.3 %collective-permute-done.11.refs_10_ = bf16[64,512]{1,0:T(8,128)(2,1)S(1)} collective-permute-done((bf16[64,512]{1,0:T(8,128)(2,1)S(1)}, bf16[64,512]{1,0:T(8,128)(2,1)S(1)}, u32[]{:S(2)}, u32[]{:S(2)}) %collective-permute-start.11) | collective-permute-done | bytes 65568 | tf_op jit(solution)/shard_map/ppermute | solution.py:175
  53.4 0.2 collective-permute-start.17
  53.6 0.0 collective-permute-done.3.refs_5_
  53.6 0.4 collective-permute-start.15
  54.0 0.7 %collective-permute-done.17.refs_16_ = bf16[64,512]{1,0:T(8,128)(2,1)S(1)} collective-permute-done((bf16[64,512]{1,0:T(8,128)(2,1)S(1)}, bf16[64,512]{1,0:T(8,128)(2,1)S(1)}, u32[]{:S(2)}, u32[]{:S(2)}) %collective-permute-start.17) | collective-permute-done | bytes 65568 | tf_op jit(solution)/shard_map/ppermute | solution.py:175
  54.7 0.2 collective-permute-start.13
  54.9 0.8 %shard_map.87.refs_0_ = bf16[128,256]{1,0:T(8,128)(2,1)S(1)} custom-call(s32[16]{0:T(128)S(1)} %copy-done.7, s32[16]{0:T(128)S(1)} %copy-done.5, s32[16,16]{1,0:T(8,128)S(1)} %copy-done.3, s32[16,16]{1,0:T(8,128)S(1)} %copy-done.4, bf16[16,16,64]{2,1,0:T(8,128)(2,1)S(1)} %copy-done.2), custom_call_target="tpu_custom_call" | custom-call | tf_op jit(solution)/shard_map/pallas_call | solution.py:211
  55.7 0.0 collective-permute-done.15.refs_14_
  55.7 0.3 collective-permute-done.13.refs_12_
  56.0 0.0 collective-permute-done.8.refs_6_
  56.0 0.0 collective-permute-done.9.refs_7_
  56.0 0.0 collective-permute-done.10.refs_8_
  56.0 2.4 %shard_map.90 = (bf16[2,2,64,4096]{3,2,1,0:T(8,128)(2,1)}, bf16[1,2,4096]{2,1,0:T(2,128)(2,1)}) custom-call(bf16[128,256]{1,0:T(8,128)(2,1)S(1)} %shard_map.87.refs_0_, bf16[2,2,2,64,512]{4,3,2,1,0:T(8,128)(2,1)S(1)} %copy-done.1, bf16[2,2,2,64,512]{4,3,2,1,0:T(8,128)(2,1)S(1)} %collective-permute-done.refs_0_.refs_2_, ...), custom_call_target="tpu_custom_call" | custom-call | tf_op jit(solution)/shard_map/pallas_call | solution.py:242
  (24 shorter events, 0.1 us)
Async XLA Ops:
  0.6 3.8 %copy-start.5 = (s32[16]{0:T(128)S(1)}, s32[16]{0:T(128)}, u32[]{:S(2)}) copy-start(s32[16]{0:T(128)} %refs_0_.3) | copy-start | bytes 196
  0.6 3.8 %copy-start.4 = (s32[16,16]{1,0:T(8,128)S(1)}, s32[16,16]{1,0:T(8,128)}, u32[]{:S(2)}) copy-start(s32[16,16]{1,0:T(8,128)} %refs_2_.3) | copy-start | bytes 3076
  0.7 3.8 %copy-start.3 = (s32[16,16]{1,0:T(8,128)S(1)}, s32[16,16]{1,0:T(8,128)}, u32[]{:S(2)}) copy-start(s32[16,16]{1,0:T(8,128)} %refs_1_.5) | copy-start | bytes 3076
  0.7 3.8 %copy-start.2 = (bf16[16,16,64]{2,1,0:T(8,128)(2,1)S(1)}, bf16[16,16,64]{2,1,0:T(8,128)(2,1)}, u32[]{:S(2)}) copy-start(bf16[16,16,64]{2,1,0:T(8,128)(2,1)} %refs_3_.3) | copy-start | bytes 98308
  4.4 1.6 %copy-start = (bf16[16,2,64,512]{3,2,1,0:T(8,128)(2,1)S(1)}, bf16[16,2,64,512]{3,2,1,0:T(8,128)(2,1)}, u32[]{:S(2)}) copy-start(bf16[16,2,64,512]{3,2,1,0:T(8,128)(2,1)} %refs_4_.3) | copy-start | bytes 6291460
  6.0 0.7 %copy-start.6 = (s32[16]{0:T(128)S(1)}, s32[16]{0:T(128)}, u32[]{:S(2)}) copy-start(s32[16]{0:T(128)} %get-tuple-element.12.refs_0_.refs_5_) | copy-start | bytes 196
  6.7 8.0 %copy-start.10 = (bf16[2,2,2,64,512]{4,3,2,1,0:T(8,128)(2,1)S(1)}, bf16[2,2,2,64,512]{4,3,2,1,0:T(8,128)(2,1)}, u32[]{:S(2)}) copy-start(bf16[2,2,2,64,512]{4,3,2,1,0:T(8,128)(2,1)} %get-tuple-element.14) | copy-start | bytes 1572868
  6.7 15.5 %copy-start.9 = (bf16[2,2,2,64,512]{4,3,2,1,0:T(8,128)(2,1)S(1)}, bf16[2,2,2,64,512]{4,3,2,1,0:T(8,128)(2,1)}, u32[]{:S(2)}) copy-start(bf16[2,2,2,64,512]{4,3,2,1,0:T(8,128)(2,1)} %get-tuple-element.15) | copy-start | bytes 1572868
  6.7 17.0 %copy-start.8 = (bf16[2,2,2,64,512]{4,3,2,1,0:T(8,128)(2,1)S(1)}, bf16[2,2,2,64,512]{4,3,2,1,0:T(8,128)(2,1)}, u32[]{:S(2)}) copy-start(bf16[2,2,2,64,512]{4,3,2,1,0:T(8,128)(2,1)} %get-tuple-element.16) | copy-start | bytes 1572868
  6.7 21.4 %copy-start.1 = (bf16[2,2,2,64,512]{4,3,2,1,0:T(8,128)(2,1)S(1)}, bf16[2,2,2,64,512]{4,3,2,1,0:T(8,128)(2,1)}, u32[]{:S(2)}) copy-start(bf16[2,2,2,64,512]{4,3,2,1,0:T(8,128)(2,1)} %get-tuple-element.13.refs_1_) | copy-start | bytes 1572868
  6.7 48.2 %copy-start.7 = (s32[16]{0:T(128)S(1)}, s32[16]{0:T(128)}, u32[]{:S(2)}) copy-start(s32[16]{0:T(128)} %get-tuple-element.12.refs_0_.refs_5_) | copy-start | bytes 196
  7.9 8.8 %collective-permute-start.4 = (f32[2,16,512]{2,1,0:T(8,128)S(1)}, f32[2,16,512]{2,1,0:T(8,128)S(1)}, u32[]{:S(2)}, u32[]{:S(2)}) collective-permute-start(f32[2,16,512]{2,1,0:T(8,128)S(1)} %get-tuple-element.18), channel_id=1, source_target_pairs={{0,8},{8,0},{16,24},{24,16},{1,9},{9,1},{17,25},{25,17},{2,10},{10... | collective-permute-start | bytes 196616 | tf_op jit(solution)/shard_map/ppermute | solution.py:172
  11.0 8.5 %all-to-all-start = ((bf16[8,2,512]{2,1,0:T(2,128)(2,1)}), bf16[8,2,512]{2,1,0:T(2,128)(2,1)S(1)}, u32[]{:S(2)}, u32[]{:S(2)}) async-start(bf16[8,2,512]{2,1,0:T(2,128)(2,1)} %bitcast.6), calls=%async_computation | async-start | bytes 32768 | tf_op jit(solution)/shard_map/all_to_all | solution.py:221
  14.7 17.3 %collective-permute-start = (bf16[2,2,2,64,512]{4,3,2,1,0:T(8,128)(2,1)S(1)}, bf16[2,2,2,64,512]{4,3,2,1,0:T(8,128)(2,1)S(1)}, u32[]{:S(2)}, u32[]{:S(2)}) collective-permute-start(bf16[2,2,2,64,512]{4,3,2,1,0:T(8,128)(2,1)S(1)} %copy-done.10), channel_id=1, source_target_pairs={{0,2},{1,3},{2,0},{3,1},{4,6},{5,7},{6,4},{7,5},{8,10},{9,11},{10,... | collective-permute-start | bytes 1572872 | tf_op jit(solution)/shard_map/ppermute | solution.py:175
  16.7 5.1 %collective-permute-start.5 = (f32[1,16,512]{2,1,0:T(8,128)S(1)}, f32[1,16,512]{2,1,0:T(8,128)S(1)}, u32[]{:S(2)}, u32[]{:S(2)}) collective-permute-start(f32[1,16,512]{2,1,0:T(8,128)S(1)} %slice_bitcast_fusion.1), channel_id=1, source_target_pairs={{0,16},{8,24},{16,0},{24,8},{1,17},{9,25},{17,1},{25,9},{2,18},{10... | collective-permute-start | bytes 98312 | tf_op jit(solution)/shard_map/ppermute | solution.py:172
  21.9 3.8 %collective-permute-start.6 = (bf16[16,512]{1,0:T(8,128)(2,1)S(1)}, bf16[16,512]{1,0:T(8,128)(2,1)S(1)}, u32[]{:S(2)}, u32[]{:S(2)}) collective-permute-start(bf16[16,512]{1,0:T(8,128)(2,1)S(1)} %fusion.3), channel_id=1, source_target_pairs={{0,8},{8,0},{16,24},{24,16},{1,9},{9,1},{17,25},{25,17},{2,10},{10... | collective-permute-start | bytes 49160 | tf_op jit(solution)/shard_map/ppermute | solution.py:172
  22.2 25.7 %collective-permute-start.1 = (bf16[2,2,2,64,512]{4,3,2,1,0:T(8,128)(2,1)S(1)}, bf16[2,2,2,64,512]{4,3,2,1,0:T(8,128)(2,1)S(1)}, u32[]{:S(2)}, u32[]{:S(2)}) collective-permute-start(bf16[2,2,2,64,512]{4,3,2,1,0:T(8,128)(2,1)S(1)} %copy-done.9), channel_id=1, source_target_pairs={{0,4},{1,5},{2,6},{3,7},{4,0},{5,1},{6,2},{7,3},{8,12},{9,13},{10,... | collective-permute-start | bytes 1572872 | tf_op jit(solution)/shard_map/ppermute | solution.py:175
  23.6 24.6 %collective-permute-start.2 = (bf16[2,2,2,64,512]{4,3,2,1,0:T(8,128)(2,1)S(1)}, bf16[2,2,2,64,512]{4,3,2,1,0:T(8,128)(2,1)S(1)}, u32[]{:S(2)}, u32[]{:S(2)}) collective-permute-start(bf16[2,2,2,64,512]{4,3,2,1,0:T(8,128)(2,1)S(1)} %copy-done.8), channel_id=1, source_target_pairs={{0,6},{1,7},{2,4},{3,5},{4,2},{5,3},{6,0},{7,1},{8,14},{9,15},{10,... | collective-permute-start | bytes 1572872 | tf_op jit(solution)/shard_map/ppermute | solution.py:175
  25.7 4.8 %collective-permute-start.7 = (bf16[32,512]{1,0:T(8,128)(2,1)S(1)}, bf16[32,512]{1,0:T(8,128)(2,1)S(1)}, u32[]{:S(2)}, u32[]{:S(2)}) collective-permute-start(bf16[32,512]{1,0:T(8,128)(2,1)S(1)} %pad_maximum_fusion.1), channel_id=1, source_target_pairs={{0,16},{8,24},{16,0},{24,8},{1,17},{9,25},{17,1},{25,9},{2,18},{10... | collective-permute-start | bytes 98312 | tf_op jit(solution)/shard_map/ppermute | solution.py:172
  28.1 25.5 %collective-permute-start.3 = (bf16[2,2,64,512]{3,2,1,0:T(8,128)(2,1)S(1)}, bf16[2,2,64,512]{3,2,1,0:T(8,128)(2,1)S(1)}, u32[]{:S(2)}, u32[]{:S(2)}) collective-permute-start(bf16[2,2,64,512]{3,2,1,0:T(8,128)(2,1)S(1)} %slice_bitcast_fusion), channel_id=1, source_target_pairs={{0,1},{1,0},{2,3},{3,2},{4,5},{5,4},{6,7},{7,6},{8,9},{9,8},{10,11... | collective-permute-start | bytes 786440 | tf_op jit(solution)/shard_map/ppermute | solution.py:175
  30.5 17.9 %collective-permute-start.16 = (bf16[64,512]{1,0:T(8,128)(2,1)S(1)}, bf16[64,512]{1,0:T(8,128)(2,1)S(1)}, u32[]{:S(2)}, u32[]{:S(2)}) collective-permute-start(bf16[64,512]{1,0:T(8,128)(2,1)S(1)} %pad_maximum_fusion.refs_3_.refs_9_), channel_id=1, source_target_pairs={{0,6},{1,7},{2,4},{3,5},{4,2},{5,3},{6,0},{7,1},{8,14},{9,15},{10,... | collective-permute-start | bytes 196616 | tf_op jit(solution)/shard_map/ppermute | solution.py:175
  32.0 17.0 %collective-permute-start.14 = (bf16[64,512]{1,0:T(8,128)(2,1)S(1)}, bf16[64,512]{1,0:T(8,128)(2,1)S(1)}, u32[]{:S(2)}, u32[]{:S(2)}) collective-permute-start(bf16[64,512]{1,0:T(8,128)(2,1)S(1)} %pad_maximum_fusion.refs_3_.refs_9_), channel_id=1, source_target_pairs={{0,4},{1,5},{2,6},{3,7},{4,0},{5,1},{6,2},{7,3},{8,12},{9,13},{10,... | collective-permute-start | bytes 196616 | tf_op jit(solution)/shard_map/ppermute | solution.py:175
  47.9 4.3 %collective-permute-start.12 = (bf16[64,512]{1,0:T(8,128)(2,1)S(1)}, bf16[64,512]{1,0:T(8,128)(2,1)S(1)}, u32[]{:S(2)}, u32[]{:S(2)}) collective-permute-start(bf16[64,512]{1,0:T(8,128)(2,1)S(1)} %pad_maximum_fusion.refs_3_.refs_9_), channel_id=1, source_target_pairs={{0,2},{1,3},{2,0},{3,1},{4,6},{5,7},{6,4},{7,5},{8,10},{9,11},{10,... | collective-permute-start | bytes 196616 | tf_op jit(solution)/shard_map/ppermute | solution.py:175
  48.4 7.6 %collective-permute-start.8 = (bf16[2,2,64,512]{3,2,1,0:T(8,128)(2,1)S(1)}, bf16[2,2,64,512]{3,2,1,0:T(8,128)(2,1)S(1)}, u32[]{:S(2)}, u32[]{:S(2)}) collective-permute-start(bf16[2,2,64,512]{3,2,1,0:T(8,128)(2,1)S(1)} %get-tuple-element.19), channel_id=1, source_target_pairs={{0,1},{1,0},{2,3},{3,2},{4,5},{5,4},{6,7},{7,6},{8,9},{9,8},{10,11... | collective-permute-start | bytes 786440 | tf_op jit(solution)/shard_map/ppermute | solution.py:175
  48.5 7.5 %collective-permute-start.9 = (bf16[2,2,64,512]{3,2,1,0:T(8,128)(2,1)S(1)}, bf16[2,2,64,512]{3,2,1,0:T(8,128)(2,1)S(1)}, u32[]{:S(2)}, u32[]{:S(2)}) collective-permute-start(bf16[2,2,64,512]{3,2,1,0:T(8,128)(2,1)S(1)} %get-tuple-element.20), channel_id=1, source_target_pairs={{0,1},{1,0},{2,3},{3,2},{4,5},{5,4},{6,7},{7,6},{8,9},{9,8},{10,11... | collective-permute-start | bytes 786440 | tf_op jit(solution)/shard_map/ppermute | solution.py:175
  49.0 7.0 %collective-permute-start.10 = (bf16[2,2,64,512]{3,2,1,0:T(8,128)(2,1)S(1)}, bf16[2,2,64,512]{3,2,1,0:T(8,128)(2,1)S(1)}, u32[]{:S(2)}, u32[]{:S(2)}) collective-permute-start(bf16[2,2,64,512]{3,2,1,0:T(8,128)(2,1)S(1)} %get-tuple-element.21), channel_id=1, source_target_pairs={{0,1},{1,0},{2,3},{3,2},{4,5},{5,4},{6,7},{7,6},{8,9},{9,8},{10,11... | collective-permute-start | bytes 786440 | tf_op jit(solution)/shard_map/ppermute | solution.py:175
  52.2 1.3 %collective-permute-start.11 = (bf16[64,512]{1,0:T(8,128)(2,1)S(1)}, bf16[64,512]{1,0:T(8,128)(2,1)S(1)}, u32[]{:S(2)}, u32[]{:S(2)}) collective-permute-start(bf16[64,512]{1,0:T(8,128)(2,1)S(1)} %pad_maximum_fusion.refs_3_.refs_9_), channel_id=1, source_target_pairs={{0,1},{1,0},{2,3},{3,2},{4,5},{5,4},{6,7},{7,6},{8,9},{9,8},{10,11... | collective-permute-start | bytes 196616 | tf_op jit(solution)/shard_map/ppermute | solution.py:175
  53.4 1.3 %collective-permute-start.17 = (bf16[64,512]{1,0:T(8,128)(2,1)S(1)}, bf16[64,512]{1,0:T(8,128)(2,1)S(1)}, u32[]{:S(2)}, u32[]{:S(2)}) collective-permute-start(bf16[64,512]{1,0:T(8,128)(2,1)S(1)} %collective-permute-done.16.refs_15_), channel_id=1, source_target_pairs={{0,1},{1,0},{2,3},{3,2},{4,5},{5,4},{6,7},{7,6},{8,9},{9,8},{10,11... | collective-permute-start | bytes 196616 | tf_op jit(solution)/shard_map/ppermute | solution.py:175
  53.6 2.1 %collective-permute-start.15 = (bf16[64,512]{1,0:T(8,128)(2,1)S(1)}, bf16[64,512]{1,0:T(8,128)(2,1)S(1)}, u32[]{:S(2)}, u32[]{:S(2)}) collective-permute-start(bf16[64,512]{1,0:T(8,128)(2,1)S(1)} %collective-permute-done.14.refs_13_), channel_id=1, source_target_pairs={{0,1},{1,0},{2,3},{3,2},{4,5},{5,4},{6,7},{7,6},{8,9},{9,8},{10,11... | collective-permute-start | bytes 196616 | tf_op jit(solution)/shard_map/ppermute | solution.py:175
  54.7 1.3 %collective-permute-start.13 = (bf16[64,512]{1,0:T(8,128)(2,1)S(1)}, bf16[64,512]{1,0:T(8,128)(2,1)S(1)}, u32[]{:S(2)}, u32[]{:S(2)}) collective-permute-start(bf16[64,512]{1,0:T(8,128)(2,1)S(1)} %collective-permute-done.12.refs_11_), channel_id=1, source_target_pairs={{0,1},{1,0},{2,3},{3,2},{4,5},{5,4},{6,7},{7,6},{8,9},{9,8},{10,11... | collective-permute-start | bytes 196616 | tf_op jit(solution)/shard_map/ppermute | solution.py:175

commit v7 on v6

--- a/solution.py
+++ b/solution.py
@@ -18,73 +18,82 @@
     return hi, (value - hi.astype(F32)).astype(BF16)
 
 
-def order_blocks(n_pen, per_owner, owner_ref, spectrum_ref, *rest):
+def distance(n_pen, q):
+    return (n_pen - q // 2 * 2) % n_pen + q % 2
+
+
+def slots(tilt_pos_ref, tilt, within, tiles_per_tilt, flip):
+    place = jnp.zeros_like(tilt)
+    for t in range(tilt_pos_ref.shape[0]):
+        place = jnp.where(tilt == t, tilt_pos_ref[t], place)
+    return (place * tiles_per_tilt + within) ^ flip
+
+
+def order_and_forward(n_pen, n_kz, chunk, per_owner, tiles_per_tilt, owner_ref, tilt_pos_ref, tilt_ref,
+                      within_ref, weights_ref, spectrum_ref, *rest):
     chips = n_pen // 2
-    outs, (inverse_ref, held, owner, count, owner_sem, in_sems, out_sems) = rest[:chips], rest[chips:]
-    blocks = spectrum_ref.shape[0]
+    outs, rest = rest[:chips], rest[chips:]
+    inverse_ref, kept_ref, sent_ref, held, owner, tilt_pos, tilt, within, weights, rest = *rest[:9], rest[9:]
+    count, table, kept, sent, small_sems, in_sems, out_sems, sum_sems = rest
+    blocks, pairs, depth = weights_ref.shape
+    columns = spectrum_ref.shape[3]
+    tiles = n_kz * chunk
     pen = lax.axis_index("pen")
-    get_owner = pltpu.make_async_copy(owner_ref, owner, owner_sem)
-    get_owner.start()
+    small = []
+    for i, (from_ref, to) in enumerate(
+        ((owner_ref, owner), (tilt_pos_ref, tilt_pos), (tilt_ref, tilt), (within_ref, within), (weights_ref, weights))
+    ):
+        small.append(pltpu.make_async_copy(from_ref, to, small_sems.at[i]))
+        small[i].start()
     gets, puts = [], []
     for b in range(blocks):
         gets.append(pltpu.make_async_copy(spectrum_ref.at[b], held.at[b], in_sems.at[b]))
         gets[b].start()
     for o in range(n_pen):
         count[o] = 0
-    get_owner.wait()
+    for copy in small:
+        copy.wait()
     for b in range(blocks):
         o = owner[b]
         r = count[o]
         count[o] = r + 1
         inverse_ref[o * per_owner + r] = b
+    slot = slots(tilt_pos, tilt[...], within[...], tiles_per_tilt, lax.axis_index("kz") * chunk)
+    rows = lax.broadcasted_iota(I32, (tiles, pairs), 0)
+    for b in range(blocks):
+        hot = jnp.where(slot[b : b + 1, :] == rows, 1.0, 0.0).astype(BF16)
+        hi, lo = split_hi_lo(jnp.dot(hot, weights[b], preferred_element_type=F32))
+        table[:tiles, b * depth : (b + 1) * depth] = hi
+        table[tiles:, b * depth : (b + 1) * depth] = lo
     for get in gets:
         get.wait()
     for q in range(n_pen):
         for r in range(per_owner):
-            from_ref = held.at[inverse_ref[(pen ^ q) * per_owner + r]]
+            from_ref = held.at[inverse_ref[(pen ^ distance(n_pen, q)) * per_owner + r]]
             puts.append(pltpu.make_async_copy(from_ref, outs[q // 2].at[q % 2, r], out_sems.at[q, r]))
             puts[-1].start()
-    for put in puts:
-        put.wait()
-
-
-def slots(tilt_pos_ref, tilt, within, tiles_per_tilt, flip):
-    place = jnp.zeros_like(tilt)
-    for t in range(tilt_pos_ref.shape[0]):
-        place = jnp.where(tilt == t, tilt_pos_ref[t], place)
-    return (place * tiles_per_tilt + within) ^ flip
-
-
-def forward(n_kz, chunk, tiles_per_tilt, tilt_pos_ref, tilt_ref, within_ref, weights_ref,
-            spectrum_ref, after_ref, kept_ref, sent_ref, table):
-    del after_ref
-    blocks, pairs, depth = weights_ref.shape
-    columns = spectrum_ref.shape[3]
-    tiles = n_kz * chunk
-    flip = lax.axis_index("kz") * chunk
-    slot = slots(tilt_pos_ref, tilt_ref[...], within_ref[...], tiles_per_tilt, flip)
-    rows = lax.broadcasted_iota(I32, (tiles, pairs), 0)
-    for b in range(blocks):
-        hot = jnp.where(slot[b : b + 1, :] == rows, 1.0, 0.0).astype(BF16)
-        hi, lo = split_hi_lo(jnp.dot(hot, weights_ref[b], preferred_element_type=F32))
-        table[:tiles, b * depth : (b + 1) * depth] = hi
-        table[tiles:, b * depth : (b + 1) * depth] = lo
     for c in range(2):
         both = jnp.dot(
             table[...],
-            spectrum_ref[:, c].reshape(blocks * depth, columns),
+            held[:, c].reshape(blocks * depth, columns),
             preferred_element_type=F32,
         )
         total = both[:tiles] + both[tiles:]
         for k in range(n_kz):
-            out_ref = sent_ref if k % 2 else kept_ref
-            out_ref[k // 2, c * chunk : (c + 1) * chunk, :] = total[k * chunk : (k + 1) * chunk]
-
-
-def adjoint_table(n_kz, chunk, per_owner, tiles_per_tilt, inverse_ref, tilt_pos_ref, tilt_ref,
-                  within_ref, weights_ref, out_ref, slot_ref):
-    depth = weights_ref.shape[2]
-    pairs = weights_ref.shape[1]
+            to = sent if k % 2 else kept
+            to[k // 2, c * chunk : (c + 1) * chunk, :] = total[k * chunk : (k + 1) * chunk]
+    puts.append(pltpu.make_async_copy(kept, kept_ref, sum_sems.at[0]))
+    puts[-1].start()
+    puts.append(pltpu.make_async_copy(sent, sent_ref, sum_sems.at[1]))
+    puts[-1].start()
+    for put in puts:
+        put.wait()
+
+
+def residual_and_table(n_kz, chunk, per_owner, tiles_per_tilt, inverse_ref, tilt_pos_ref, tilt_ref, within_ref,
+                       weights_ref, sums_ref, arrived_ref, measured_ref, own_ref, out_ref, slot_ref):
+    own_ref[...] = (sums_ref[...] + arrived_ref[...] - measured_ref[...].astype(F32)).astype(BF16)
+    pairs, depth = weights_ref.shape[1:]
     rows_all = n_kz * 2 * chunk
     flip = lax.axis_index("kz") * chunk
     slot_ref[...] = slots(tilt_pos_ref, tilt_ref[...], within_ref[...], tiles_per_tilt, flip)
@@ -127,7 +136,7 @@
     pick = jnp.where(pick_at == pick_row * chunk + pen, 1.0, 0.0)
     pick = jnp.where(pick_row < 2, pick, 0.0).astype(BF16)
     for q in range(n_pen):
-        first_column = pl.multiple_of((pen ^ q) * columns, columns)
+        first_column = pl.multiple_of((pen ^ distance(n_pen, q)) * columns, columns)
         blocks = swapped[q // 2] if q % 2 else kept[q // 2].at[0]
         here = tile_refs[q][...]
         own = jnp.dot(pick, here, preferred_element_type=F32)
@@ -174,53 +183,63 @@
     def between(value, k):
         return lax.ppermute(value, "pen", [(i, i ^ k) for i in range(n_pen)])
 
-    *outs, inverse = pl.pallas_call(
-        call(order_blocks, n_pen, per_owner),
+    group = jax.ShapeDtypeStruct((n_kz // 2, 2 * chunk, columns), F32)
+    *outs, inverse, sums, sent_sums = pl.pallas_call(
+        call(order_and_forward, n_pen, n_kz, chunk, per_owner, tiles_per_tilt),
         out_shape=[jax.ShapeDtypeStruct((2, per_owner, 2, depth, columns), BF16)] * chips
-        + [jax.ShapeDtypeStruct((blocks,), I32)],
-        in_specs=[ANY, ANY],
-        out_specs=[ANY] * chips + [SMEM],
+        + [jax.ShapeDtypeStruct((blocks,), I32), group, group],
+        in_specs=[ANY] * 6,
+        out_specs=[ANY] * chips + [SMEM, ANY, ANY],
         scratch_shapes=[
             pltpu.VMEM(spectrum.shape, BF16),
             pltpu.SMEM((blocks,), I32),
+            pltpu.SMEM(tilt_pos.shape, I32),
+            pltpu.VMEM(pair_tilt.shape, I32),
+            pltpu.VMEM(pair_tile_within.shape, I32),
+            pltpu.VMEM(depth_weights.shape, BF16),
             pltpu.SMEM((n_pen,), I32),
-            pltpu.SemaphoreType.DMA,
+            pltpu.VMEM((2 * tiles, blocks * depth), BF16),
+            pltpu.VMEM(group.shape, F32),
+            pltpu.VMEM(group.shape, F32),
+            pltpu.SemaphoreType.DMA((5,)),
             pltpu.SemaphoreType.DMA((blocks,)),
             pltpu.SemaphoreType.DMA((n_pen, per_owner)),
+            pltpu.SemaphoreType.DMA((2,)),
         ],
         compiler_params=pltpu.CompilerParams(vmem_limit_bytes=62 << 20),
-    )(owner, spectrum)
-    far_first = [between(outs[i], 2 * i) for i in range(chips - 1, 0, -1)]
-    kept = [outs[0]] + far_first[::-1]
-
-    sums, sent = pl.pallas_call(
-        call(forward, n_kz, chunk, tiles_per_tilt),
-        out_shape=[jax.ShapeDtypeStruct((n_kz // 2, 2 * chunk, columns), F32)] * 2,
-        in_specs=[SMEM, VMEM, VMEM, VMEM, VMEM, ANY],
-        out_specs=[VMEM, VMEM],
-        scratch_shapes=[pltpu.VMEM((2 * tiles, blocks * depth), BF16)],
-        compiler_params=pltpu.CompilerParams(vmem_limit_bytes=16 << 20),
-    )(tilt_pos, pair_tilt, pair_tile_within, depth_weights, spectrum, inverse)
-    sums = sums + across(sent, 1)
+    )(owner, tilt_pos, pair_tilt, pair_tile_within, depth_weights, spectrum)
+    kept = [outs[0]] + [between(outs[i], distance(n_pen, 2 * i)) for i in range(1, chips)]
+
+    arrived = across(sent_sums, 1)
     step = 2
     while step < n_kz:
-        sums = sums.reshape(-1, 2, 2 * chunk, columns)
-        sums = sums[:, 0] + across(sums[:, 1], step)
+        sums = (sums + arrived).reshape(-1, 2, 2 * chunk, columns)
+        sums, arrived = sums[:, 0], across(sums[:, 1], step)
         step *= 2
-
-    table = pl.pallas_call(
-        call(adjoint_table, n_kz, chunk, per_owner, tiles_per_tilt),
-        out_shape=jax.ShapeDtypeStruct((4 * tiles, 2 * per_owner * depth), BF16),
-        in_specs=[SMEM, SMEM, VMEM, VMEM, VMEM],
-        out_specs=VMEM,
-        scratch_shapes=[pltpu.VMEM((blocks, pairs), I32)],
-        compiler_params=pltpu.CompilerParams(vmem_limit_bytes=8 << 20),
-    )(inverse, tilt_pos, pair_tilt, pair_tile_within, depth_weights)
 
     sent = measured.reshape(2, n_pen, columns).transpose(1, 0, 2)
     got = lax.all_to_all(sent, "pen", split_axis=0, concat_axis=0, tiled=True)
     measured_rows = got.transpose(1, 0, 2).reshape(2 * chunk, columns)
-    own = (sums.reshape(2 * chunk, columns) - measured_rows.astype(F32)).astype(BF16)
+    own, table = pl.pallas_call(
+        call(residual_and_table, n_kz, chunk, per_owner, tiles_per_tilt),
+        out_shape=[
+            jax.ShapeDtypeStruct((2 * chunk, columns), BF16),
+            jax.ShapeDtypeStruct((4 * tiles, 2 * per_owner * depth), BF16),
+        ],
+        in_specs=[SMEM, SMEM] + [VMEM] * 6,
+        out_specs=[VMEM, VMEM],
+        scratch_shapes=[pltpu.VMEM((blocks, pairs), I32)],
+        compiler_params=pltpu.CompilerParams(vmem_limit_bytes=8 << 20),
+    )(
+        inverse,
+        tilt_pos,
+        pair_tilt,
+        pair_tile_within,
+        depth_weights,
+        sums.reshape(2 * chunk, columns),
+        arrived.reshape(2 * chunk, columns),
+        measured_rows,
+    )
 
     held = own
     step = 1
@@ -236,7 +255,7 @@
         compiler_params=pltpu.CompilerParams(vmem_limit_bytes=8 << 20),
     )(*kept[1:], held)
     swapped = [between(one, 1) for one in [outs[0][1], *other]]
-    every = [held] + [between(held, k) for k in range(2, n_pen, 2)]
+    every = [held] + [between(held, distance(n_pen, 2 * i)) for i in range(1, chips)]
     every = [tile for one in every for tile in (one, between(one, 1))]
 
     updated, residual = pl.pallas_call(

time: 58.6 us -> 50.1 us (0.85)
  waiting for transfers between devices: 28 us -> 16.2 us
  starting transfers between devices: 19 us -> 22.9 us
  Pallas kernels: 8.17 us -> 7.33 us
  other arithmetic: 0.04 us -> 0.85 us
  local copies, waits for them, and re-layouts: 2.3 us -> 1.66 us
    ppermute x14, waiting for transfers between devices: 21.2 us -> 9.01 us  [between(): return lax.ppermute(value, 'pen', [(i, i ^ k) for i in range(n_pen)])]
    ppermute x14, starting transfers between devices: 6.94 us -> 10.6 us  [between(): return lax.ppermute(value, 'pen', [(i, i ^ k) for i in range(n_pen)])]
    unnamed x22 -> x14, local copies, waits for them, and re-layouts: 2.28 us -> 0.68 us
    squeeze x1, local copies, waits for them, and re-layouts: 0.02 us -> 0.97 us  [body(): swapped = [between(one, 1) for one in [outs[0][1], *other]]]
    reshape x1, other arithmetic: 0.01 us -> 0.85 us  [body(): sums = (sums + arrived).reshape(-1, 2, 2 * chunk, columns)]
    pallas_call x3 -> x2, Pallas kernels: 5.73 us -> 4.89 us  [the longest x1 4.08 us: body(): pl.pallas_call(call(order_and_forward, n_pen, n_kz, chunk, per_owner, til...]
  transfers between devices with their start and end apart: 19 -> 19, of which waited for: 9 -> 8; matrix products, arithmetic and copies ran while one was open for 0% -> 4% of each run, Pallas kernels for 2% -> 2%
where the time goes in v7:
time: 50.1 us; the launch traced here: 49.8 us
  starting transfers between devices  22.9 us (46%)
  waiting for transfers between devices  16.2 us (32%)
  Pallas kernels  7.33 us (15%)
  local copies, waits for them, and re-layouts  1.66 us (3%)
  other arithmetic  0.85 us (2%)
  between operations  0.8 us (2%)
    ppermute x14, starting transfers between devices, between(): return lax.ppermute(value, 'pen', [(i, i ^ k) for i in range(n_pen)])  10.6 us
    ppermute x14, waiting for transfers between devices, between(): return lax.ppermute(value, 'pen', [(i, i ^ k) for i in range(n_pen)])  9.01 us
    ppermute x4, starting transfers between devices, across(): return lax.ppermute(value, 'kz', [(i, i ^ k) for i in range(n_kz)])  8.53 us
    ppermute x4, waiting for transfers between devices, across(): return lax.ppermute(value, 'kz', [(i, i ^ k) for i in range(n_kz)])  7.23 us
    pallas_call x1, Pallas kernels, body(): pl.pallas_call(call(order_and_forward, n_pen, n_kz, chunk, per_owner, til...  4.08 us
    all_to_all x1, starting transfers between devices, body(): got = lax.all_to_all(sent, 'pen', split_axis=0, concat_axis=0, tiled=True)  3.72 us
    pallas_call x1, Pallas kernels, body(): pl.pallas_call(call(adjoint, n_pen, chunk, per_owner), out_shape=[jax.Sha...  2.36 us
  transfers between devices with their start and end apart: 19, of which 8 were waited for; matrix products, arithmetic and copies ran while one was open for 4% of the time, Pallas kernels for 2%

profile of v7, /device:TPU:0, one launch (start us, length us, event | category | flops | bytes accessed | tf_op | source)
XLA Modules:
  0.0 49.8 jit_solution(13227914686927696547)
XLA Ops:
  0.6 0.0 copy-start.4
  0.7 4.1 %shard_map.86 = (bf16[2,2,2,64,512]{4,3,2,1,0:T(8,128)(2,1)}, bf16[2,2,2,64,512]{4,3,2,1,0:T(8,128)(2,1)}, bf16[2,2,2,64,512]{4,3,2,1,0:T(8,128)(2,1)}, bf16[2,2...) custom-call(s32[16]{0:T(128)} %refs_0_.1, s32[16]{0:T(128)} %refs_1_.3, ...), custom_call_target="tpu_custom_call" | custom-call | tf_op jit(solution)/shard_map/pallas_call | solution.py:187
  4.8 0.0 copy-start
  4.8 3.1 %collective-permute-start = (f32[2,16,512]{2,1,0:T(8,128)}, f32[2,16,512]{2,1,0:T(8,128)S(1)}, u32[]{:S(2)}, u32[]{:S(2)}) collective-permute-start(f32[2,16,512]{2,1,0:T(8,128)} %get-tuple-element.16), channel_id=1, source_target_pairs={{0,8},{8,0},{16,24},{24,16},{1,9},{9,1},{17,25},{25,17},{2,10},{10... | collective-permute-start | bytes 196616 | tf_op jit(solution)/shard_map/ppermute | solution.py:181
  7.9 3.7 %all-to-all-start = ((bf16[8,2,512]{2,1,0:T(2,128)(2,1)}), bf16[8,2,512]{2,1,0:T(2,128)(2,1)S(1)}, u32[]{:S(2)}, u32[]{:S(2)}) async-start(bf16[8,2,512]{2,1,0:T(2,128)(2,1)} %bitcast.5), calls=%async_computation | async-start | bytes 32768 | tf_op jit(solution)/shard_map/all_to_all | solution.py:221
  11.6 2.9 %collective-permute-start.2 = (bf16[2,2,2,64,512]{4,3,2,1,0:T(8,128)(2,1)}, bf16[2,2,2,64,512]{4,3,2,1,0:T(8,128)(2,1)S(1)}, u32[]{:S(2)}, u32[]{:S(2)}) collective-permute-start(bf16[2,2,2,64,512]{4,3,2,1,0:T(8,128)(2,1)} %get-tuple-element.19), channel_id=1, source_target_pairs={{0,6},{1,7},{2,4},{3,5},{4,2},{5,3},{6,0},{7,1},{8,14},{9,15},{10,... | collective-permute-start | bytes 1572872 | tf_op jit(solution)/shard_map/ppermute | solution.py:184
  14.5 0.6 %collective-permute-start.3 = (bf16[2,2,2,64,512]{4,3,2,1,0:T(8,128)(2,1)}, bf16[2,2,2,64,512]{4,3,2,1,0:T(8,128)(2,1)S(1)}, u32[]{:S(2)}, u32[]{:S(2)}) collective-permute-start(bf16[2,2,2,64,512]{4,3,2,1,0:T(8,128)(2,1)} %get-tuple-element.20), channel_id=1, source_target_pairs={{0,4},{1,5},{2,6},{3,7},{4,0},{5,1},{6,2},{7,3},{8,12},{9,13},{10,... | collective-permute-start | bytes 1572872 | tf_op jit(solution)/shard_map/ppermute | solution.py:184
  15.1 0.1 collective-permute-start.4
  15.1 0.0 collective-permute-done
  15.1 0.8 %add_bitcast_fusion = f32[1,2,16,512]{3,2,1,0:T(8,128)S(1)} fusion(f32[2,16,512]{2,1,0:T(8,128)} %get-tuple-element.15, f32[2,16,512]{2,1,0:T(8,128)S(1)} %collective-permute-done), kind=kLoop, calls=%fused_computation.1 | loop fusion | flops 16384 | bytes 196608 | tf_op jit(solution)/shard_map/reshape | solution.py:216
  16.0 2.7 %collective-permute-start.1 = (f32[1,16,512]{2,1,0:T(8,128)S(1)}, f32[1,16,512]{2,1,0:T(8,128)S(1)}, u32[]{:S(2)}, u32[]{:S(2)}) collective-permute-start(f32[1,16,512]{2,1,0:T(8,128)S(1)} %get-tuple-element.26), channel_id=1, source_target_pairs={{0,16},{8,24},{16,0},{24,8},{1,17},{9,25},{17,1},{25,9},{2,18},{10... | collective-permute-start | bytes 98312 | tf_op jit(solution)/shard_map/ppermute | solution.py:181
  18.6 1.0 %slice_bitcast_fusion = bf16[2,2,64,512]{3,2,1,0:T(8,128)(2,1)S(1)} fusion(bf16[2,2,2,64,512]{4,3,2,1,0:T(8,128)(2,1)} %get-tuple-element.18.refs_1_), kind=kLoop, calls=%fused_computation | loop fusion | bytes 524288 | tf_op jit(solution)/shard_map/squeeze | solution.py:257
  19.6 0.1 collective-permute-start.5
  19.7 0.0 all-to-all-done
  19.7 1.4 %collective-permute-done.1 = f32[1,16,512]{2,1,0:T(8,128)S(1)} collective-permute-done((f32[1,16,512]{2,1,0:T(8,128)S(1)}, f32[1,16,512]{2,1,0:T(8,128)S(1)}, u32[]{:S(2)}, u32[]{:S(2)}) %collective-permute-start.1) | collective-permute-done | bytes 32800 | tf_op jit(solution)/shard_map/ppermute | solution.py:181
  21.1 0.0 copy-start.5
  21.1 0.6 %copy-done.5 = s32[16]{0:T(128)S(1)} copy-done((s32[16]{0:T(128)S(1)}, s32[16]{0:T(128)}, u32[]{:S(2)}) %copy-start.5) | copy-done | bytes 88
  21.8 0.8 %shard_map.87 = (bf16[16,512]{1,0:T(8,128)(2,1)S(1)}, bf16[128,256]{1,0:T(8,128)(2,1)S(1)}) custom-call(s32[16]{0:T(128)S(1)} %copy-done.5, s32[16]{0:T(128)S(1)} %copy-done.4, s32[16,16]{1,0:T(8,128)S(1)} %copy-done.2, s32[16,16]{1,0:T(8,128)S(1)} %copy-done.3, bf16[16,16,64]{2,1,0:T(8,128)(2,1)S(1)} %copy-done.1, f32[16,512]{1,0:T(8,128)S(1)} %get-tuple-element.27.refs_5_, ...), custom_call_target="tpu_custom_call" | custom-call | tf_op jit(solution)/shard_map/pallas_call | solution.py:223
  22.6 0.3 collective-permute-start.6
  22.9 3.5 %collective-permute-done.6 = bf16[16,512]{1,0:T(8,128)(2,1)S(1)} collective-permute-done((bf16[16,512]{1,0:T(8,128)(2,1)S(1)}, bf16[16,512]{1,0:T(8,128)(2,1)S(1)}, u32[]{:S(2)}, u32[]{:S(2)}) %collective-permute-start.6) | collective-permute-done | bytes 16416 | tf_op jit(solution)/shard_map/ppermute | solution.py:181
  26.4 2.5 %collective-permute-start.7 = (bf16[32,512]{1,0:T(8,128)(2,1)S(1)}, bf16[32,512]{1,0:T(8,128)(2,1)S(1)}, u32[]{:S(2)}, u32[]{:S(2)}) collective-permute-start(bf16[32,512]{1,0:T(8,128)(2,1)S(1)} %pad_maximum_fusion), channel_id=1, source_target_pairs={{0,16},{8,24},{16,0},{24,8},{1,17},{9,25},{17,1},{25,9},{2,18},{10... | collective-permute-start | bytes 98312 | tf_op jit(solution)/shard_map/ppermute | solution.py:181
  28.9 2.3 %collective-permute-done.7 = bf16[32,512]{1,0:T(8,128)(2,1)S(1)} collective-permute-done((bf16[32,512]{1,0:T(8,128)(2,1)S(1)}, bf16[32,512]{1,0:T(8,128)(2,1)S(1)}, u32[]{:S(2)}, u32[]{:S(2)}) %collective-permute-start.7) | collective-permute-done | bytes 32800 | tf_op jit(solution)/shard_map/ppermute | solution.py:181
  31.2 2.0 %collective-permute-start.16 = (bf16[64,512]{1,0:T(8,128)(2,1)S(1)}, bf16[64,512]{1,0:T(8,128)(2,1)S(1)}, u32[]{:S(2)}, u32[]{:S(2)}) collective-permute-start(bf16[64,512]{1,0:T(8,128)(2,1)S(1)} %constant_dynamic-update-slice_fusion.refs_3_.refs_9_), channel_id=1, source_target_pairs={{0,2},{1,3},{2,0},{3,1},{4,6},{5,7},{6,4},{7,5},{8,10},{9,11},{10,... | collective-permute-start | bytes 196616 | tf_op jit(solution)/shard_map/ppermute | solution.py:184
  33.2 0.0 collective-permute-done.2.refs_0_.refs_2_
  33.2 1.5 %collective-permute-start.14 = (bf16[64,512]{1,0:T(8,128)(2,1)S(1)}, bf16[64,512]{1,0:T(8,128)(2,1)S(1)}, u32[]{:S(2)}, u32[]{:S(2)}) collective-permute-start(bf16[64,512]{1,0:T(8,128)(2,1)S(1)} %constant_dynamic-update-slice_fusion.refs_3_.refs_9_), channel_id=1, source_target_pairs={{0,4},{1,5},{2,6},{3,7},{4,0},{5,1},{6,2},{7,3},{8,12},{9,13},{10,... | collective-permute-start | bytes 196616 | tf_op jit(solution)/shard_map/ppermute | solution.py:184
  34.7 3.8 %collective-permute-done.3.refs_1_.refs_3_ = bf16[2,2,2,64,512]{4,3,2,1,0:T(8,128)(2,1)S(1)} collective-permute-done((bf16[2,2,2,64,512]{4,3,2,1,0:T(8,128)(2,1)}, bf16[2,2,2,64,512]{4,3,2,1,0:T(8,128)(2,1)S(1)}, u32[]{:S(2)}, u32[]{:S(2)}) %collective-permute-start.3) | collective-permute-done | bytes 524320 | tf_op jit(solution)/shard_map/ppermute | solution.py:184
  38.5 2.3 %collective-permute-start.12 = (bf16[64,512]{1,0:T(8,128)(2,1)S(1)}, bf16[64,512]{1,0:T(8,128)(2,1)S(1)}, u32[]{:S(2)}, u32[]{:S(2)}) collective-permute-start(bf16[64,512]{1,0:T(8,128)(2,1)S(1)} %constant_dynamic-update-slice_fusion.refs_3_.refs_9_), channel_id=1, source_target_pairs={{0,6},{1,7},{2,4},{3,5},{4,2},{5,3},{6,0},{7,1},{8,14},{9,15},{10,... | collective-permute-start | bytes 196616 | tf_op jit(solution)/shard_map/ppermute | solution.py:184
  40.7 0.0 collective-permute-done.4.refs_2_.refs_4_
  40.7 0.1 shard_map.88
  40.8 0.1 collective-permute-start.8
  40.9 0.0 collective-permute-done.16.refs_15_
  40.9 0.5 collective-permute-start.9
  41.4 0.0 collective-permute-done.14.refs_13_
  41.4 0.1 collective-permute-start.10
  41.5 2.1 %collective-permute-done.12.refs_11_ = bf16[64,512]{1,0:T(8,128)(2,1)S(1)} collective-permute-done((bf16[64,512]{1,0:T(8,128)(2,1)S(1)}, bf16[64,512]{1,0:T(8,128)(2,1)S(1)}, u32[]{:S(2)}, u32[]{:S(2)}) %collective-permute-start.12) | collective-permute-done | bytes 65568 | tf_op jit(solution)/shard_map/ppermute | solution.py:184
  43.6 0.0 collective-permute-start.11
  43.6 1.3 %collective-permute-done.11.refs_10_ = bf16[64,512]{1,0:T(8,128)(2,1)S(1)} collective-permute-done((bf16[64,512]{1,0:T(8,128)(2,1)S(1)}, bf16[64,512]{1,0:T(8,128)(2,1)S(1)}, u32[]{:S(2)}, u32[]{:S(2)}) %collective-permute-start.11) | collective-permute-done | bytes 65568 | tf_op jit(solution)/shard_map/ppermute | solution.py:184
  44.9 0.2 collective-permute-start.17
  45.0 0.0 collective-permute-done.5.refs_5_
  45.0 0.4 collective-permute-start.15
  45.4 0.7 %collective-permute-done.17.refs_16_ = bf16[64,512]{1,0:T(8,128)(2,1)S(1)} collective-permute-done((bf16[64,512]{1,0:T(8,128)(2,1)S(1)}, bf16[64,512]{1,0:T(8,128)(2,1)S(1)}, u32[]{:S(2)}, u32[]{:S(2)}) %collective-permute-start.17) | collective-permute-done | bytes 65568 | tf_op jit(solution)/shard_map/ppermute | solution.py:184
  46.1 0.2 collective-permute-start.13
  46.3 0.0 collective-permute-done.15.refs_14_
  46.3 1.1 %collective-permute-done.13.refs_12_ = bf16[64,512]{1,0:T(8,128)(2,1)S(1)} collective-permute-done((bf16[64,512]{1,0:T(8,128)(2,1)S(1)}, bf16[64,512]{1,0:T(8,128)(2,1)S(1)}, u32[]{:S(2)}, u32[]{:S(2)}) %collective-permute-start.13) | collective-permute-done | bytes 65568 | tf_op jit(solution)/shard_map/ppermute | solution.py:184
  47.4 0.0 collective-permute-done.8.refs_6_
  47.4 0.0 collective-permute-done.9.refs_7_
  47.4 0.0 collective-permute-done.10.refs_8_
  47.4 2.4 %shard_map.89 = (bf16[2,2,64,4096]{3,2,1,0:T(8,128)(2,1)}, bf16[1,2,4096]{2,1,0:T(2,128)(2,1)}) custom-call(bf16[128,256]{1,0:T(8,128)(2,1)S(1)} %get-tuple-element.17.refs_0_, bf16[2,2,2,64,512]{4,3,2,1,0:T(8,128)(2,1)S(1)} %copy-done, bf16[2,2,2,64,512]{4,3,2,1,0:T(8,128)(2,1)S(1)} %collective-permute-done.2.refs_0_.refs_2_, ...), custom_call_target="tpu_custom_call" | custom-call | tf_op jit(solution)/shard_map/pallas_call | solution.py:261
  (14 shorter events, 0.0 us)
Async XLA Ops:
  0.6 20.5 %copy-start.4 = (s32[16]{0:T(128)S(1)}, s32[16]{0:T(128)}, u32[]{:S(2)}) copy-start(s32[16]{0:T(128)} %refs_1_.3) | copy-start | bytes 196
  0.6 20.5 %copy-start.3 = (s32[16,16]{1,0:T(8,128)S(1)}, s32[16,16]{1,0:T(8,128)}, u32[]{:S(2)}) copy-start(s32[16,16]{1,0:T(8,128)} %refs_3_.3) | copy-start | bytes 3076
  0.7 20.5 %copy-start.2 = (s32[16,16]{1,0:T(8,128)S(1)}, s32[16,16]{1,0:T(8,128)}, u32[]{:S(2)}) copy-start(s32[16,16]{1,0:T(8,128)} %refs_2_.3) | copy-start | bytes 3076
  0.7 20.5 %copy-start.1 = (bf16[16,16,64]{2,1,0:T(8,128)(2,1)S(1)}, bf16[16,16,64]{2,1,0:T(8,128)(2,1)}, u32[]{:S(2)}) copy-start(bf16[16,16,64]{2,1,0:T(8,128)(2,1)} %refs_4_.3) | copy-start | bytes 98308
  4.8 42.6 %copy-start = (bf16[2,2,2,64,512]{4,3,2,1,0:T(8,128)(2,1)S(1)}, bf16[2,2,2,64,512]{4,3,2,1,0:T(8,128)(2,1)}, u32[]{:S(2)}) copy-start(bf16[2,2,2,64,512]{4,3,2,1,0:T(8,128)(2,1)} %get-tuple-element.18.refs_1_) | copy-start | bytes 1572868
  4.8 10.4 %collective-permute-start = (f32[2,16,512]{2,1,0:T(8,128)}, f32[2,16,512]{2,1,0:T(8,128)S(1)}, u32[]{:S(2)}, u32[]{:S(2)}) collective-permute-start(f32[2,16,512]{2,1,0:T(8,128)} %get-tuple-element.16), channel_id=1, source_target_pairs={{0,8},{8,0},{16,24},{24,16},{1,9},{9,1},{17,25},{25,17},{2,10},{10... | collective-permute-start | bytes 196616 | tf_op jit(solution)/shard_map/ppermute | solution.py:181
  7.9 11.8 %all-to-all-start = ((bf16[8,2,512]{2,1,0:T(2,128)(2,1)}), bf16[8,2,512]{2,1,0:T(2,128)(2,1)S(1)}, u32[]{:S(2)}, u32[]{:S(2)}) async-start(bf16[8,2,512]{2,1,0:T(2,128)(2,1)} %bitcast.5), calls=%async_computation | async-start | bytes 32768 | tf_op jit(solution)/shard_map/all_to_all | solution.py:221
  11.6 21.6 %collective-permute-start.2 = (bf16[2,2,2,64,512]{4,3,2,1,0:T(8,128)(2,1)}, bf16[2,2,2,64,512]{4,3,2,1,0:T(8,128)(2,1)S(1)}, u32[]{:S(2)}, u32[]{:S(2)}) collective-permute-start(bf16[2,2,2,64,512]{4,3,2,1,0:T(8,128)(2,1)} %get-tuple-element.19), channel_id=1, source_target_pairs={{0,6},{1,7},{2,4},{3,5},{4,2},{5,3},{6,0},{7,1},{8,14},{9,15},{10,... | collective-permute-start | bytes 1572872 | tf_op jit(solution)/shard_map/ppermute | solution.py:184
  14.5 23.9 %collective-permute-start.3 = (bf16[2,2,2,64,512]{4,3,2,1,0:T(8,128)(2,1)}, bf16[2,2,2,64,512]{4,3,2,1,0:T(8,128)(2,1)S(1)}, u32[]{:S(2)}, u32[]{:S(2)}) collective-permute-start(bf16[2,2,2,64,512]{4,3,2,1,0:T(8,128)(2,1)} %get-tuple-element.20), channel_id=1, source_target_pairs={{0,4},{1,5},{2,6},{3,7},{4,0},{5,1},{6,2},{7,3},{8,12},{9,13},{10,... | collective-permute-start | bytes 1572872 | tf_op jit(solution)/shard_map/ppermute | solution.py:184
  15.1 25.6 %collective-permute-start.4 = (bf16[2,2,2,64,512]{4,3,2,1,0:T(8,128)(2,1)}, bf16[2,2,2,64,512]{4,3,2,1,0:T(8,128)(2,1)S(1)}, u32[]{:S(2)}, u32[]{:S(2)}) collective-permute-start(bf16[2,2,2,64,512]{4,3,2,1,0:T(8,128)(2,1)} %get-tuple-element.21), channel_id=1, source_target_pairs={{0,2},{1,3},{2,0},{3,1},{4,6},{5,7},{6,4},{7,5},{8,10},{9,11},{10,... | collective-permute-start | bytes 1572872 | tf_op jit(solution)/shard_map/ppermute | solution.py:184
  16.0 5.1 %collective-permute-start.1 = (f32[1,16,512]{2,1,0:T(8,128)S(1)}, f32[1,16,512]{2,1,0:T(8,128)S(1)}, u32[]{:S(2)}, u32[]{:S(2)}) collective-permute-start(f32[1,16,512]{2,1,0:T(8,128)S(1)} %get-tuple-element.26), channel_id=1, source_target_pairs={{0,16},{8,24},{16,0},{24,8},{1,17},{9,25},{17,1},{25,9},{2,18},{10... | collective-permute-start | bytes 98312 | tf_op jit(solution)/shard_map/ppermute | solution.py:181
  19.6 25.4 %collective-permute-start.5 = (bf16[2,2,64,512]{3,2,1,0:T(8,128)(2,1)S(1)}, bf16[2,2,64,512]{3,2,1,0:T(8,128)(2,1)S(1)}, u32[]{:S(2)}, u32[]{:S(2)}) collective-permute-start(bf16[2,2,64,512]{3,2,1,0:T(8,128)(2,1)S(1)} %slice_bitcast_fusion), channel_id=1, source_target_pairs={{0,1},{1,0},{2,3},{3,2},{4,5},{5,4},{6,7},{7,6},{8,9},{9,8},{10,11... | collective-permute-start | bytes 786440 | tf_op jit(solution)/shard_map/ppermute | solution.py:184
  21.1 0.7 %copy-start.5 = (s32[16]{0:T(128)S(1)}, s32[16]{0:T(128)}, u32[]{:S(2)}) copy-start(s32[16]{0:T(128)} %get-tuple-element.14.refs_0_) | copy-start | bytes 196
  22.6 3.8 %collective-permute-start.6 = (bf16[16,512]{1,0:T(8,128)(2,1)S(1)}, bf16[16,512]{1,0:T(8,128)(2,1)S(1)}, u32[]{:S(2)}, u32[]{:S(2)}) collective-permute-start(bf16[16,512]{1,0:T(8,128)(2,1)S(1)} %get-tuple-element.22), channel_id=1, source_target_pairs={{0,8},{8,0},{16,24},{24,16},{1,9},{9,1},{17,25},{25,17},{2,10},{10... | collective-permute-start | bytes 49160 | tf_op jit(solution)/shard_map/ppermute | solution.py:181
  26.4 4.8 %collective-permute-start.7 = (bf16[32,512]{1,0:T(8,128)(2,1)S(1)}, bf16[32,512]{1,0:T(8,128)(2,1)S(1)}, u32[]{:S(2)}, u32[]{:S(2)}) collective-permute-start(bf16[32,512]{1,0:T(8,128)(2,1)S(1)} %pad_maximum_fusion), channel_id=1, source_target_pairs={{0,16},{8,24},{16,0},{24,8},{1,17},{9,25},{17,1},{25,9},{2,18},{10... | collective-permute-start | bytes 98312 | tf_op jit(solution)/shard_map/ppermute | solution.py:181
  31.2 9.6 %collective-permute-start.16 = (bf16[64,512]{1,0:T(8,128)(2,1)S(1)}, bf16[64,512]{1,0:T(8,128)(2,1)S(1)}, u32[]{:S(2)}, u32[]{:S(2)}) collective-permute-start(bf16[64,512]{1,0:T(8,128)(2,1)S(1)} %constant_dynamic-update-slice_fusion.refs_3_.refs_9_), channel_id=1, source_target_pairs={{0,2},{1,3},{2,0},{3,1},{4,6},{5,7},{6,4},{7,5},{8,10},{9,11},{10,... | collective-permute-start | bytes 196616 | tf_op jit(solution)/shard_map/ppermute | solution.py:184
  33.2 8.2 %collective-permute-start.14 = (bf16[64,512]{1,0:T(8,128)(2,1)S(1)}, bf16[64,512]{1,0:T(8,128)(2,1)S(1)}, u32[]{:S(2)}, u32[]{:S(2)}) collective-permute-start(bf16[64,512]{1,0:T(8,128)(2,1)S(1)} %constant_dynamic-update-slice_fusion.refs_3_.refs_9_), channel_id=1, source_target_pairs={{0,4},{1,5},{2,6},{3,7},{4,0},{5,1},{6,2},{7,3},{8,12},{9,13},{10,... | collective-permute-start | bytes 196616 | tf_op jit(solution)/shard_map/ppermute | solution.py:184
  38.5 5.2 %collective-permute-start.12 = (bf16[64,512]{1,0:T(8,128)(2,1)S(1)}, bf16[64,512]{1,0:T(8,128)(2,1)S(1)}, u32[]{:S(2)}, u32[]{:S(2)}) collective-permute-start(bf16[64,512]{1,0:T(8,128)(2,1)S(1)} %constant_dynamic-update-slice_fusion.refs_3_.refs_9_), channel_id=1, source_target_pairs={{0,6},{1,7},{2,4},{3,5},{4,2},{5,3},{6,0},{7,1},{8,14},{9,15},{10,... | collective-permute-start | bytes 196616 | tf_op jit(solution)/shard_map/ppermute | solution.py:184
  40.8 6.6 %collective-permute-start.8 = (bf16[2,2,64,512]{3,2,1,0:T(8,128)(2,1)S(1)}, bf16[2,2,64,512]{3,2,1,0:T(8,128)(2,1)S(1)}, u32[]{:S(2)}, u32[]{:S(2)}) collective-permute-start(bf16[2,2,64,512]{3,2,1,0:T(8,128)(2,1)S(1)} %get-tuple-element.23), channel_id=1, source_target_pairs={{0,1},{1,0},{2,3},{3,2},{4,5},{5,4},{6,7},{7,6},{8,9},{9,8},{10,11... | collective-permute-start | bytes 786440 | tf_op jit(solution)/shard_map/ppermute | solution.py:184
  40.9 6.5 %collective-permute-start.9 = (bf16[2,2,64,512]{3,2,1,0:T(8,128)(2,1)S(1)}, bf16[2,2,64,512]{3,2,1,0:T(8,128)(2,1)S(1)}, u32[]{:S(2)}, u32[]{:S(2)}) collective-permute-start(bf16[2,2,64,512]{3,2,1,0:T(8,128)(2,1)S(1)} %get-tuple-element.24), channel_id=1, source_target_pairs={{0,1},{1,0},{2,3},{3,2},{4,5},{5,4},{6,7},{7,6},{8,9},{9,8},{10,11... | collective-permute-start | bytes 786440 | tf_op jit(solution)/shard_map/ppermute | solution.py:184
  41.4 6.0 %collective-permute-start.10 = (bf16[2,2,64,512]{3,2,1,0:T(8,128)(2,1)S(1)}, bf16[2,2,64,512]{3,2,1,0:T(8,128)(2,1)S(1)}, u32[]{:S(2)}, u32[]{:S(2)}) collective-permute-start(bf16[2,2,64,512]{3,2,1,0:T(8,128)(2,1)S(1)} %get-tuple-element.25), channel_id=1, source_target_pairs={{0,1},{1,0},{2,3},{3,2},{4,5},{5,4},{6,7},{7,6},{8,9},{9,8},{10,11... | collective-permute-start | bytes 786440 | tf_op jit(solution)/shard_map/ppermute | solution.py:184
  43.6 1.3 %collective-permute-start.11 = (bf16[64,512]{1,0:T(8,128)(2,1)S(1)}, bf16[64,512]{1,0:T(8,128)(2,1)S(1)}, u32[]{:S(2)}, u32[]{:S(2)}) collective-permute-start(bf16[64,512]{1,0:T(8,128)(2,1)S(1)} %constant_dynamic-update-slice_fusion.refs_3_.refs_9_), channel_id=1, source_target_pairs={{0,1},{1,0},{2,3},{3,2},{4,5},{5,4},{6,7},{7,6},{8,9},{9,8},{10,11... | collective-permute-start | bytes 196616 | tf_op jit(solution)/shard_map/ppermute | solution.py:184
  44.9 1.3 %collective-permute-start.17 = (bf16[64,512]{1,0:T(8,128)(2,1)S(1)}, bf16[64,512]{1,0:T(8,128)(2,1)S(1)}, u32[]{:S(2)}, u32[]{:S(2)}) collective-permute-start(bf16[64,512]{1,0:T(8,128)(2,1)S(1)} %collective-permute-done.16.refs_15_), channel_id=1, source_target_pairs={{0,1},{1,0},{2,3},{3,2},{4,5},{5,4},{6,7},{7,6},{8,9},{9,8},{10,11... | collective-permute-start | bytes 196616 | tf_op jit(solution)/shard_map/ppermute | solution.py:184
  45.0 1.3 %collective-permute-start.15 = (bf16[64,512]{1,0:T(8,128)(2,1)S(1)}, bf16[64,512]{1,0:T(8,128)(2,1)S(1)}, u32[]{:S(2)}, u32[]{:S(2)}) collective-permute-start(bf16[64,512]{1,0:T(8,128)(2,1)S(1)} %collective-permute-done.14.refs_13_), channel_id=1, source_target_pairs={{0,1},{1,0},{2,3},{3,2},{4,5},{5,4},{6,7},{7,6},{8,9},{9,8},{10,11... | collective-permute-start | bytes 196616 | tf_op jit(solution)/shard_map/ppermute | solution.py:184
  46.1 1.3 %collective-permute-start.13 = (bf16[64,512]{1,0:T(8,128)(2,1)S(1)}, bf16[64,512]{1,0:T(8,128)(2,1)S(1)}, u32[]{:S(2)}, u32[]{:S(2)}) collective-permute-start(bf16[64,512]{1,0:T(8,128)(2,1)S(1)} %collective-permute-done.12.refs_11_), channel_id=1, source_target_pairs={{0,1},{1,0},{2,3},{3,2},{4,5},{5,4},{6,7},{7,6},{8,9},{9,8},{10,11... | collective-permute-start | bytes 196616 | tf_op jit(solution)/shard_map/ppermute | solution.py:184

commit v8 on v7

--- a/solution.py
+++ b/solution.py
@@ -111,10 +111,15 @@
             out_ref[rows_all:, first : first + depth] = lo
 
 
-def other_core(*refs):
-    count = len(refs) // 2
-    in_refs, out_refs = refs[: count - 1], refs[count:-1]
-    sems = refs[-1]
+def join_tiles(first_ref, second_ref, *rest):
+    out_ref = rest[-1]
+    rows = first_ref.shape[0]
+    out_ref[:rows] = first_ref[...]
+    out_ref[rows:] = second_ref[...]
+
+
+def other_core(count, *refs):
+    in_refs, out_refs, sems = refs[:count], refs[-1 - count : -1], refs[-1]
     copies = []
     for i, (in_ref, out_ref) in enumerate(zip(in_refs, out_refs)):
         copies.append(pltpu.make_async_copy(in_ref.at[1], out_ref, sems.at[i]))
@@ -123,24 +128,13 @@
         copy.wait()
 
 
-def adjoint(n_pen, chunk, per_owner, table_ref, *rest):
-    chips = n_pen // 2
-    kept, swapped, tile_refs, rest = rest[:chips], rest[chips:n_pen], rest[n_pen : 2 * n_pen], rest[2 * n_pen :]
-    out_ref, residual_ref, made, out_sems = rest
-    depth, columns = swapped[0].shape[2:]
-    rows = tile_refs[0].shape[0]
+def adjoint(n_pen, per_owner, core, table_ref, blocks, tile_refs, out_ref, made, out_sems):
     pen = lax.axis_index("pen")
+    depth, columns = made.shape[3:]
     puts = []
-    pick_row = lax.broadcasted_iota(I32, (16, rows), 0)
-    pick_at = lax.broadcasted_iota(I32, (16, rows), 1)
-    pick = jnp.where(pick_at == pick_row * chunk + pen, 1.0, 0.0)
-    pick = jnp.where(pick_row < 2, pick, 0.0).astype(BF16)
-    for q in range(n_pen):
-        first_column = pl.multiple_of((pen ^ distance(n_pen, q)) * columns, columns)
-        blocks = swapped[q // 2] if q % 2 else kept[q // 2].at[0]
-        here = tile_refs[q][...]
-        own = jnp.dot(pick, here, preferred_element_type=F32)
-        residual_ref[0, :, pl.ds(first_column, columns)] = own[:2].astype(BF16)
+    for i in range(n_pen // 2):
+        first_column = pl.multiple_of((pen ^ distance(n_pen, 2 * i + core)) * columns, columns)
+        here = tile_refs[i][...]
         step = lax.dot_general(
             table_ref[...],
             jnp.concatenate([here, here], axis=0),
@@ -150,11 +144,38 @@
         for r in range(per_owner):
             for c in range(2):
                 first = (c * per_owner + r) * depth
-                held = blocks[r, c].astype(F32)
-                made[q, r, c] = (held + step[first : first + depth]).astype(BF16)
+                held = blocks[i][r, c].astype(F32)
+                made[i, r, c] = (held + step[first : first + depth]).astype(BF16)
         to = out_ref.at[:, :, :, pl.ds(first_column, columns)]
-        puts.append(pltpu.make_async_copy(made.at[q], to, out_sems.at[q]))
+        puts.append(pltpu.make_async_copy(made.at[i], to, out_sems.at[i]))
         puts[-1].start()
+    return puts
+
+
+def adjoint_like(n_pen, per_owner, table_ref, *rest):
+    chips = n_pen // 2
+    kept, tile_refs, (out_ref, made, out_sems) = rest[:chips], rest[chips:n_pen], rest[n_pen:]
+    blocks = [one.at[0] for one in kept]
+    for put in adjoint(n_pen, per_owner, 0, table_ref, blocks, tile_refs, out_ref, made, out_sems):
+        put.wait()
+
+
+def adjoint_other(n_pen, chunk, per_owner, table_ref, begun_ref, *rest):
+    del begun_ref
+    chips = n_pen // 2
+    swapped, tile_refs, rest = rest[:chips], rest[chips : chips + n_pen], rest[chips + n_pen :]
+    out_ref, residual_ref, made, out_sems = rest
+    rows, columns = tile_refs[0].shape
+    pen = lax.axis_index("pen")
+    puts = adjoint(n_pen, per_owner, 1, table_ref, swapped, tile_refs[1::2], out_ref, made, out_sems)
+    pick_row = lax.broadcasted_iota(I32, (16, rows), 0)
+    pick_at = lax.broadcasted_iota(I32, (16, rows), 1)
+    pick = jnp.where(pick_at == pick_row * chunk + pen, 1.0, 0.0)
+    pick = jnp.where(pick_row < 2, pick, 0.0).astype(BF16)
+    for q in range(n_pen):
+        first_column = pl.multiple_of((pen ^ distance(n_pen, q)) * columns, columns)
+        own = jnp.dot(pick, tile_refs[q][...], preferred_element_type=F32)
+        residual_ref[0, :, pl.ds(first_column, columns)] = own[:2].astype(BF16)
     for put in puts:
         put.wait()
 
@@ -183,6 +204,7 @@
     def between(value, k):
         return lax.ppermute(value, "pen", [(i, i ^ k) for i in range(n_pen)])
 
+    pair = (per_owner, 2, depth, columns)
     group = jax.ShapeDtypeStruct((n_kz // 2, 2 * chunk, columns), F32)
     *outs, inverse, sums, sent_sums = pl.pallas_call(
         call(order_and_forward, n_pen, n_kz, chunk, per_owner, tiles_per_tilt),
@@ -243,35 +265,52 @@
 
     held = own
     step = 1
-    while step < n_kz:
+    while 2 * step < n_kz:
         held = jnp.concatenate([held, across(held, step)], axis=0)
         step *= 2
-    other = pl.pallas_call(
-        other_core,
-        out_shape=[jax.ShapeDtypeStruct(outs[0].shape[1:], BF16)] * (chips - 1),
-        in_specs=[ANY] * chips,
-        out_specs=[ANY] * (chips - 1),
-        scratch_shapes=[pltpu.SemaphoreType.DMA((chips - 1,))],
+    def take_other(arrived, after):
+        return pl.pallas_call(
+            call(other_core, len(arrived)),
+            out_shape=[jax.ShapeDtypeStruct(pair, BF16)] * len(arrived),
+            in_specs=[ANY] * (len(arrived) + len(after)),
+            out_specs=[ANY] * len(arrived),
+            scratch_shapes=[pltpu.SemaphoreType.DMA((len(arrived),))],
+            compiler_params=pltpu.CompilerParams(vmem_limit_bytes=8 << 20),
+        )(*arrived, *after)
+
+    swapped = [between(one, 1) for one in [outs[0][1], *take_other(kept[1:2], [held])]]
+    held = pl.pallas_call(
+        join_tiles,
+        out_shape=jax.ShapeDtypeStruct((2 * tiles, columns), BF16),
+        in_specs=[VMEM, VMEM, ANY, ANY],
+        out_specs=VMEM,
         compiler_params=pltpu.CompilerParams(vmem_limit_bytes=8 << 20),
-    )(*kept[1:], held)
-    swapped = [between(one, 1) for one in [outs[0][1], *other]]
-    every = [held] + [between(held, distance(n_pen, 2 * i)) for i in range(1, chips)]
-    every = [tile for one in every for tile in (one, between(one, 1))]
-
+    )(held, across(held, step), *swapped)
+    like = [held] + [between(held, distance(n_pen, 2 * i)) for i in range(1, chips)]
+    swapped = swapped + [between(one, 1) for one in take_other(kept[2:], like[1:])]
+    every = [tile for one in like for tile in (one, between(one, 1))]
+
+    scratch = [pltpu.VMEM((chips, *pair), BF16), pltpu.SemaphoreType.DMA((chips,))]
+    begun = pl.pallas_call(
+        call(adjoint_like, n_pen, per_owner),
+        out_shape=jax.ShapeDtypeStruct((per_owner, 2, depth, cells), BF16),
+        in_specs=[VMEM] * (n_pen + 1),
+        out_specs=ANY,
+        scratch_shapes=scratch,
+        compiler_params=pltpu.CompilerParams(vmem_limit_bytes=16 << 20),
+    )(table, *kept, *like)
     updated, residual = pl.pallas_call(
-        call(adjoint, n_pen, chunk, per_owner),
+        call(adjoint_other, n_pen, chunk, per_owner),
         out_shape=[
-            jax.ShapeDtypeStruct((per_owner, 2, depth, cells), BF16),
+            jax.ShapeDtypeStruct(begun.shape, BF16),
             jax.ShapeDtypeStruct((tile_dev, 2, cells), BF16),
         ],
-        in_specs=[VMEM] * (2 * n_pen + 1),
+        in_specs=[VMEM, ANY] + [VMEM] * (chips + n_pen),
         out_specs=[ANY, VMEM],
-        scratch_shapes=[
-            pltpu.VMEM((n_pen, per_owner, 2, depth, columns), BF16),
-            pltpu.SemaphoreType.DMA((n_pen,)),
-        ],
+        scratch_shapes=scratch,
+        input_output_aliases={1: 0},
         compiler_params=pltpu.CompilerParams(vmem_limit_bytes=16 << 20),
-    )(table, *kept, *swapped, *every)
+    )(table, begun, *swapped, *every)
     return (updated, residual)
 
 

time: 50.1 us -> 47.4 us (0.946)
  starting transfers between devices: 22.9 us -> 21 us
  waiting for transfers between devices: 16.2 us -> 14.6 us
  Pallas kernels: 7.33 us -> 8.08 us
    ppermute x14, starting transfers between devices: 10.6 us -> 8.63 us  [between(): return lax.ppermute(value, 'pen', [(i, i ^ k) for i in range(n_pen)])]
    ppermute x14, waiting for transfers between devices: 9.01 us -> 7.8 us  [between(): return lax.ppermute(value, 'pen', [(i, i ^ k) for i in range(n_pen)])]
    pallas_call x2 -> x5, Pallas kernels: 2.44 us -> 3.2 us  [the longest x1 1.86 us: body(): pl.pallas_call(call(adjoint_other, n_pen, chunk, per_owner), out_shape=[j...]
  transfers between devices with their start and end apart: 19 -> 19, of which waited for: 8 -> 9; matrix products, arithmetic and copies ran while one was open for 4% -> 4% of each run, Pallas kernels for 2% -> 4%
where the time goes in v8:
time: 47.4 us; the launch traced here: 47.1 us
  starting transfers between devices  21 us (44%)
  waiting for transfers between devices  14.6 us (31%)
  Pallas kernels  8.08 us (17%)
  local copies, waits for them, and re-layouts  1.66 us (4%)
  other arithmetic  0.85 us (2%)
  between operations  0.83 us (2%)
    ppermute x4, starting transfers between devices, across(): return lax.ppermute(value, 'kz', [(i, i ^ k) for i in range(n_kz)])  8.69 us
    ppermute x14, starting transfers between devices, between(): return lax.ppermute(value, 'pen', [(i, i ^ k) for i in range(n_pen)])  8.63 us
    ppermute x14, waiting for transfers between devices, between(): return lax.ppermute(value, 'pen', [(i, i ^ k) for i in range(n_pen)])  7.8 us
    ppermute x4, waiting for transfers between devices, across(): return lax.ppermute(value, 'kz', [(i, i ^ k) for i in range(n_kz)])  6.83 us
    pallas_call x1, Pallas kernels, body(): pl.pallas_call(call(order_and_forward, n_pen, n_kz, chunk, per_owner, til...  4.08 us
    all_to_all x1, starting transfers between devices, body(): got = lax.all_to_all(sent, 'pen', split_axis=0, concat_axis=0, tiled=True)  3.72 us
    pallas_call x1, Pallas kernels, body(): pl.pallas_call(call(adjoint_other, n_pen, chunk, per_owner), out_shape=[j...  1.86 us
    pallas_call x1, Pallas kernels, body(): pl.pallas_call(call(adjoint_like, n_pen, per_owner), out_shape=jax.ShapeD...  1.25 us
  transfers between devices with their start and end apart: 19, of which 9 were waited for; matrix products, arithmetic and copies ran while one was open for 4% of the time, Pallas kernels for 4%

profile of v8, /device:TPU:0, one launch (start us, length us, event | category | flops | bytes accessed | tf_op | source)
XLA Modules:
  0.0 47.1 jit_solution(2005234942435407573)
XLA Ops:
  0.7 4.1 %shard_map.86 = (bf16[2,2,2,64,512]{4,3,2,1,0:T(8,128)(2,1)}, bf16[2,2,2,64,512]{4,3,2,1,0:T(8,128)(2,1)}, bf16[2,2,2,64,512]{4,3,2,1,0:T(8,128)(2,1)}, bf16[2,2...) custom-call(s32[16]{0:T(128)} %refs_0_.1, s32[16]{0:T(128)} %refs_1_.3, ...), custom_call_target="tpu_custom_call" | custom-call | tf_op jit(solution)/shard_map/pallas_call | solution.py:209
  4.8 0.0 copy-start
  4.8 3.1 %collective-permute-start = (f32[2,16,512]{2,1,0:T(8,128)}, f32[2,16,512]{2,1,0:T(8,128)S(1)}, u32[]{:S(2)}, u32[]{:S(2)}) collective-permute-start(f32[2,16,512]{2,1,0:T(8,128)} %get-tuple-element.15), channel_id=1, source_target_pairs={{0,8},{8,0},{16,24},{24,16},{1,9},{9,1},{17,25},{25,17},{2,10},{10... | collective-permute-start | bytes 196616 | tf_op jit(solution)/shard_map/ppermute | solution.py:202
  7.9 3.7 %all-to-all-start = ((bf16[8,2,512]{2,1,0:T(2,128)(2,1)}), bf16[8,2,512]{2,1,0:T(2,128)(2,1)S(1)}, u32[]{:S(2)}, u32[]{:S(2)}) async-start(bf16[8,2,512]{2,1,0:T(2,128)(2,1)} %bitcast.5), calls=%async_computation | async-start | bytes 32768 | tf_op jit(solution)/shard_map/all_to_all | solution.py:243
  11.6 2.9 %collective-permute-start.2 = (bf16[2,2,2,64,512]{4,3,2,1,0:T(8,128)(2,1)}, bf16[2,2,2,64,512]{4,3,2,1,0:T(8,128)(2,1)S(1)}, u32[]{:S(2)}, u32[]{:S(2)}) collective-permute-start(bf16[2,2,2,64,512]{4,3,2,1,0:T(8,128)(2,1)} %get-tuple-element.18), channel_id=1, source_target_pairs={{0,6},{1,7},{2,4},{3,5},{4,2},{5,3},{6,0},{7,1},{8,14},{9,15},{10,... | collective-permute-start | bytes 1572872 | tf_op jit(solution)/shard_map/ppermute | solution.py:205
  14.5 0.0 collective-permute-done
  14.5 0.8 %add_bitcast_fusion = f32[1,2,16,512]{3,2,1,0:T(8,128)S(1)} fusion(f32[2,16,512]{2,1,0:T(8,128)} %get-tuple-element.14, f32[2,16,512]{2,1,0:T(8,128)S(1)} %collective-permute-done), kind=kLoop, calls=%fused_computation.1 | loop fusion | flops 16384 | bytes 196608 | tf_op jit(solution)/shard_map/reshape | solution.py:238
  15.4 2.7 %collective-permute-start.1 = (f32[1,16,512]{2,1,0:T(8,128)S(1)}, f32[1,16,512]{2,1,0:T(8,128)S(1)}, u32[]{:S(2)}, u32[]{:S(2)}) collective-permute-start(f32[1,16,512]{2,1,0:T(8,128)S(1)} %get-tuple-element.24), channel_id=1, source_target_pairs={{0,16},{8,24},{16,0},{24,8},{1,17},{9,25},{17,1},{25,9},{2,18},{10... | collective-permute-start | bytes 98312 | tf_op jit(solution)/shard_map/ppermute | solution.py:202
  18.0 1.0 %slice_bitcast_fusion = bf16[2,2,64,512]{3,2,1,0:T(8,128)(2,1)S(1)} fusion(bf16[2,2,2,64,512]{4,3,2,1,0:T(8,128)(2,1)} %get-tuple-element.17.refs_1_), kind=kLoop, calls=%fused_computation | loop fusion | bytes 524288 | tf_op jit(solution)/shard_map/squeeze | solution.py:281
  19.0 0.1 collective-permute-start.7
  19.1 0.6 %collective-permute-start.3 = (bf16[2,2,2,64,512]{4,3,2,1,0:T(8,128)(2,1)}, bf16[2,2,2,64,512]{4,3,2,1,0:T(8,128)(2,1)S(1)}, u32[]{:S(2)}, u32[]{:S(2)}) collective-permute-start(bf16[2,2,2,64,512]{4,3,2,1,0:T(8,128)(2,1)} %get-tuple-element.19), channel_id=1, source_target_pairs={{0,4},{1,5},{2,6},{3,7},{4,0},{5,1},{6,2},{7,3},{8,12},{9,13},{10,... | collective-permute-start | bytes 1572872 | tf_op jit(solution)/shard_map/ppermute | solution.py:205
  19.7 0.1 collective-permute-start.4
  19.8 0.0 all-to-all-done
  19.8 0.7 %collective-permute-done.1 = f32[1,16,512]{2,1,0:T(8,128)S(1)} collective-permute-done((f32[1,16,512]{2,1,0:T(8,128)S(1)}, f32[1,16,512]{2,1,0:T(8,128)S(1)}, u32[]{:S(2)}, u32[]{:S(2)}) %collective-permute-start.1) | collective-permute-done | bytes 32800 | tf_op jit(solution)/shard_map/ppermute | solution.py:202
  20.5 0.0 copy-start.5
  20.5 0.6 %copy-done.5 = s32[16]{0:T(128)S(1)} copy-done((s32[16]{0:T(128)S(1)}, s32[16]{0:T(128)}, u32[]{:S(2)}) %copy-start.5) | copy-done | bytes 88
  21.2 0.8 %shard_map.87 = (bf16[16,512]{1,0:T(8,128)(2,1)S(1)}, bf16[128,256]{1,0:T(8,128)(2,1)S(1)}) custom-call(s32[16]{0:T(128)S(1)} %copy-done.5, s32[16]{0:T(128)S(1)} %copy-done.4, s32[16,16]{1,0:T(8,128)S(1)} %copy-done.2, s32[16,16]{1,0:T(8,128)S(1)} %copy-done.3, bf16[16,16,64]{2,1,0:T(8,128)(2,1)S(1)} %copy-done.1, f32[16,512]{1,0:T(8,128)S(1)} %get-tuple-element.25.refs_5_, ...), custom_call_target="tpu_custom_call" | custom-call | tf_op jit(solution)/shard_map/pallas_call | solution.py:245
  22.0 0.3 collective-permute-start.5
  22.3 3.5 %collective-permute-done.5 = bf16[16,512]{1,0:T(8,128)(2,1)S(1)} collective-permute-done((bf16[16,512]{1,0:T(8,128)(2,1)S(1)}, bf16[16,512]{1,0:T(8,128)(2,1)S(1)}, u32[]{:S(2)}, u32[]{:S(2)}) %collective-permute-start.5) | collective-permute-done | bytes 16416 | tf_op jit(solution)/shard_map/ppermute | solution.py:202
  25.8 1.8 %collective-permute-done.2.refs_0_.refs_2_ = bf16[2,2,2,64,512]{4,3,2,1,0:T(8,128)(2,1)S(1)} collective-permute-done((bf16[2,2,2,64,512]{4,3,2,1,0:T(8,128)(2,1)}, bf16[2,2,2,64,512]{4,3,2,1,0:T(8,128)(2,1)S(1)}, u32[]{:S(2)}, u32[]{:S(2)}) %collective-permute-start.2) | collective-permute-done | bytes 524320 | tf_op jit(solution)/shard_map/ppermute | solution.py:205
  27.7 0.1 collective-permute-start.8
  27.8 2.7 %collective-permute-start.6 = (bf16[32,512]{1,0:T(8,128)(2,1)S(1)}, bf16[32,512]{1,0:T(8,128)(2,1)S(1)}, u32[]{:S(2)}, u32[]{:S(2)}) collective-permute-start(bf16[32,512]{1,0:T(8,128)(2,1)S(1)} %constant_dynamic-update-slice_fusion.refs_1_.first_ref), channel_id=1, source_target_pairs={{0,16},{8,24},{16,0},{24,8},{1,17},{9,25},{17,1},{25,9},{2,18},{10... | collective-permute-start | bytes 98312 | tf_op jit(solution)/shard_map/ppermute | solution.py:202
  30.4 2.6 %collective-permute-done.6.second_ref = bf16[32,512]{1,0:T(8,128)(2,1)S(1)} collective-permute-done((bf16[32,512]{1,0:T(8,128)(2,1)S(1)}, bf16[32,512]{1,0:T(8,128)(2,1)S(1)}, u32[]{:S(2)}, u32[]{:S(2)}) %collective-permute-start.6) | collective-permute-done | bytes 32800 | tf_op jit(solution)/shard_map/ppermute | solution.py:202
  33.1 0.0 collective-permute-done.7.rest_0_.refs_2_
  33.1 0.0 collective-permute-done.8.rest_1_.refs_3_
  33.1 2.0 %collective-permute-start.11 = (bf16[64,512]{1,0:T(8,128)(2,1)S(1)}, bf16[64,512]{1,0:T(8,128)(2,1)S(1)}, u32[]{:S(2)}, u32[]{:S(2)}) collective-permute-start(bf16[64,512]{1,0:T(8,128)(2,1)S(1)} %shard_map.89.refs_5_.refs_6_), channel_id=1, source_target_pairs={{0,2},{1,3},{2,0},{3,1},{4,6},{5,7},{6,4},{7,5},{8,10},{9,11},{10,... | collective-permute-start | bytes 196616 | tf_op jit(solution)/shard_map/ppermute | solution.py:205
  35.0 1.5 %collective-permute-start.10 = (bf16[64,512]{1,0:T(8,128)(2,1)S(1)}, bf16[64,512]{1,0:T(8,128)(2,1)S(1)}, u32[]{:S(2)}, u32[]{:S(2)}) collective-permute-start(bf16[64,512]{1,0:T(8,128)(2,1)S(1)} %shard_map.89.refs_5_.refs_6_), channel_id=1, source_target_pairs={{0,4},{1,5},{2,6},{3,7},{4,0},{5,1},{6,2},{7,3},{8,12},{9,13},{10,... | collective-permute-start | bytes 196616 | tf_op jit(solution)/shard_map/ppermute | solution.py:205
  36.5 0.1 collective-permute-start.9
  36.6 1.8 %collective-permute-done.3.refs_3_.refs_0_ = bf16[2,2,2,64,512]{4,3,2,1,0:T(8,128)(2,1)S(1)} collective-permute-done((bf16[2,2,2,64,512]{4,3,2,1,0:T(8,128)(2,1)}, bf16[2,2,2,64,512]{4,3,2,1,0:T(8,128)(2,1)S(1)}, u32[]{:S(2)}, u32[]{:S(2)}) %collective-permute-start.3) | collective-permute-done | bytes 524320 | tf_op jit(solution)/shard_map/ppermute | solution.py:205
  38.4 0.9 %collective-permute-done.4.refs_4_.refs_1_ = bf16[2,2,2,64,512]{4,3,2,1,0:T(8,128)(2,1)S(1)} collective-permute-done((bf16[2,2,2,64,512]{4,3,2,1,0:T(8,128)(2,1)}, bf16[2,2,2,64,512]{4,3,2,1,0:T(8,128)(2,1)S(1)}, u32[]{:S(2)}, u32[]{:S(2)}) %collective-permute-start.4) | collective-permute-done | bytes 524320 | tf_op jit(solution)/shard_map/ppermute | solution.py:205
  39.3 1.3 %collective-permute-done.11.refs_8_.refs_4_.refs_12_ = bf16[64,512]{1,0:T(8,128)(2,1)S(1)} collective-permute-done((bf16[64,512]{1,0:T(8,128)(2,1)S(1)}, bf16[64,512]{1,0:T(8,128)(2,1)S(1)}, u32[]{:S(2)}, u32[]{:S(2)}) %collective-permute-start.11) | collective-permute-done | bytes 65568 | tf_op jit(solution)/shard_map/ppermute | solution.py:205
  40.6 0.0 collective-permute-done.10.refs_7_.refs_3_.refs_10_
  40.6 1.0 %collective-permute-done.9.refs_6_.refs_2_.refs_8_ = bf16[64,512]{1,0:T(8,128)(2,1)S(1)} collective-permute-done((bf16[64,512]{1,0:T(8,128)(2,1)S(1)}, bf16[64,512]{1,0:T(8,128)(2,1)S(1)}, u32[]{:S(2)}, u32[]{:S(2)}) %collective-permute-start.9) | collective-permute-done | bytes 65568 | tf_op jit(solution)/shard_map/ppermute | solution.py:205
  41.7 0.1 shard_map.91
  41.7 0.1 collective-permute-start.12
  41.8 0.5 %collective-permute-start.13 = (bf16[2,2,64,512]{3,2,1,0:T(8,128)(2,1)S(1)}, bf16[2,2,64,512]{3,2,1,0:T(8,128)(2,1)S(1)}, u32[]{:S(2)}, u32[]{:S(2)}) collective-permute-start(bf16[2,2,64,512]{3,2,1,0:T(8,128)(2,1)S(1)} %get-tuple-element.23), channel_id=1, source_target_pairs={{0,1},{1,0},{2,3},{3,2},{4,5},{5,4},{6,7},{7,6},{8,9},{9,8},{10,11... | collective-permute-start | bytes 786440 | tf_op jit(solution)/shard_map/ppermute | solution.py:205
  42.3 0.1 collective-permute-start.14
  42.4 0.4 collective-permute-start.17
  42.8 0.1 collective-permute-start.16
  42.9 0.9 %collective-permute-done.14.refs_7_ = bf16[64,512]{1,0:T(8,128)(2,1)S(1)} collective-permute-done((bf16[64,512]{1,0:T(8,128)(2,1)S(1)}, bf16[64,512]{1,0:T(8,128)(2,1)S(1)}, u32[]{:S(2)}, u32[]{:S(2)}) %collective-permute-start.14) | collective-permute-done | bytes 65568 | tf_op jit(solution)/shard_map/ppermute | solution.py:205
  43.8 0.1 collective-permute-start.15
  43.9 1.2 %shard_map.90.refs_1_ = bf16[2,2,64,4096]{3,2,1,0:T(8,128)(2,1)} custom-call(bf16[128,256]{1,0:T(8,128)(2,1)S(1)} %get-tuple-element.16.refs_0_, bf16[2,2,2,64,512]{4,3,2,1,0:T(8,128)(2,1)S(1)} %copy-done, bf16[2,2,2,64,512]{4,3,2,1,0:T(8,128)(2,1)S(1)} %collective-permute-done.2.refs_0_.refs_2_, ...), custom_call_target="tpu_custom_call" | custom-call | tf_op jit(solution)/shard_map/pallas_call | solution.py:294
  45.2 0.0 collective-permute-done.17.refs_13_
  45.2 0.0 collective-permute-done.16.refs_11_
  45.2 0.0 collective-permute-done.15.refs_9_
  45.2 0.0 collective-permute-done.12.refs_4_
  45.2 0.0 collective-permute-done.13.refs_5_
  45.2 1.9 %shard_map.92 = (bf16[2,2,64,4096]{3,2,1,0:T(8,128)(2,1)}, bf16[1,2,4096]{2,1,0:T(2,128)(2,1)}) custom-call(bf16[128,256]{1,0:T(8,128)(2,1)S(1)} %get-tuple-element.16.refs_0_, bf16[2,2,64,4096]{3,2,1,0:T(8,128)(2,1)} %shard_map.90.refs_1_, bf16[2,2,64,512]{3,2,1,0:T(8,128)(2,1)S(1)} %collective-permute-done.7.rest_0_.refs_2_, ...), custom_call_target="tpu_custom_call", output_to_operand_aliasing={{0}: (1, {})} | custom-call | tf_op jit(solution)/shard_map/pallas_call | solution.py:302
  (15 shorter events, 0.1 us)
Async XLA Ops:
  0.6 19.9 %copy-start.4 = (s32[16]{0:T(128)S(1)}, s32[16]{0:T(128)}, u32[]{:S(2)}) copy-start(s32[16]{0:T(128)} %refs_1_.3) | copy-start | bytes 196
  0.6 19.9 %copy-start.3 = (s32[16,16]{1,0:T(8,128)S(1)}, s32[16,16]{1,0:T(8,128)}, u32[]{:S(2)}) copy-start(s32[16,16]{1,0:T(8,128)} %refs_3_.3) | copy-start | bytes 3076
  0.7 19.9 %copy-start.2 = (s32[16,16]{1,0:T(8,128)S(1)}, s32[16,16]{1,0:T(8,128)}, u32[]{:S(2)}) copy-start(s32[16,16]{1,0:T(8,128)} %refs_2_.3) | copy-start | bytes 3076
  0.7 19.9 %copy-start.1 = (bf16[16,16,64]{2,1,0:T(8,128)(2,1)S(1)}, bf16[16,16,64]{2,1,0:T(8,128)(2,1)}, u32[]{:S(2)}) copy-start(bf16[16,16,64]{2,1,0:T(8,128)(2,1)} %refs_4_.3) | copy-start | bytes 98308
  4.8 39.2 %copy-start = (bf16[2,2,2,64,512]{4,3,2,1,0:T(8,128)(2,1)S(1)}, bf16[2,2,2,64,512]{4,3,2,1,0:T(8,128)(2,1)}, u32[]{:S(2)}) copy-start(bf16[2,2,2,64,512]{4,3,2,1,0:T(8,128)(2,1)} %get-tuple-element.17.refs_1_) | copy-start | bytes 1572868
  4.8 9.7 %collective-permute-start = (f32[2,16,512]{2,1,0:T(8,128)}, f32[2,16,512]{2,1,0:T(8,128)S(1)}, u32[]{:S(2)}, u32[]{:S(2)}) collective-permute-start(f32[2,16,512]{2,1,0:T(8,128)} %get-tuple-element.15), channel_id=1, source_target_pairs={{0,8},{8,0},{16,24},{24,16},{1,9},{9,1},{17,25},{25,17},{2,10},{10... | collective-permute-start | bytes 196616 | tf_op jit(solution)/shard_map/ppermute | solution.py:202
  7.9 11.9 %all-to-all-start = ((bf16[8,2,512]{2,1,0:T(2,128)(2,1)}), bf16[8,2,512]{2,1,0:T(2,128)(2,1)S(1)}, u32[]{:S(2)}, u32[]{:S(2)}) async-start(bf16[8,2,512]{2,1,0:T(2,128)(2,1)} %bitcast.5), calls=%async_computation | async-start | bytes 32768 | tf_op jit(solution)/shard_map/all_to_all | solution.py:243
  11.6 16.1 %collective-permute-start.2 = (bf16[2,2,2,64,512]{4,3,2,1,0:T(8,128)(2,1)}, bf16[2,2,2,64,512]{4,3,2,1,0:T(8,128)(2,1)S(1)}, u32[]{:S(2)}, u32[]{:S(2)}) collective-permute-start(bf16[2,2,2,64,512]{4,3,2,1,0:T(8,128)(2,1)} %get-tuple-element.18), channel_id=1, source_target_pairs={{0,6},{1,7},{2,4},{3,5},{4,2},{5,3},{6,0},{7,1},{8,14},{9,15},{10,... | collective-permute-start | bytes 1572872 | tf_op jit(solution)/shard_map/ppermute | solution.py:205
  15.4 5.1 %collective-permute-start.1 = (f32[1,16,512]{2,1,0:T(8,128)S(1)}, f32[1,16,512]{2,1,0:T(8,128)S(1)}, u32[]{:S(2)}, u32[]{:S(2)}) collective-permute-start(f32[1,16,512]{2,1,0:T(8,128)S(1)} %get-tuple-element.24), channel_id=1, source_target_pairs={{0,16},{8,24},{16,0},{24,8},{1,17},{9,25},{17,1},{25,9},{2,18},{10... | collective-permute-start | bytes 98312 | tf_op jit(solution)/shard_map/ppermute | solution.py:202
  19.0 14.0 %collective-permute-start.7 = (bf16[2,2,64,512]{3,2,1,0:T(8,128)(2,1)S(1)}, bf16[2,2,64,512]{3,2,1,0:T(8,128)(2,1)S(1)}, u32[]{:S(2)}, u32[]{:S(2)}) collective-permute-start(bf16[2,2,64,512]{3,2,1,0:T(8,128)(2,1)S(1)} %slice_bitcast_fusion), channel_id=1, source_target_pairs={{0,1},{1,0},{2,3},{3,2},{4,5},{5,4},{6,7},{7,6},{8,9},{9,8},{10,11... | collective-permute-start | bytes 786440 | tf_op jit(solution)/shard_map/ppermute | solution.py:205
  19.1 19.3 %collective-permute-start.3 = (bf16[2,2,2,64,512]{4,3,2,1,0:T(8,128)(2,1)}, bf16[2,2,2,64,512]{4,3,2,1,0:T(8,128)(2,1)S(1)}, u32[]{:S(2)}, u32[]{:S(2)}) collective-permute-start(bf16[2,2,2,64,512]{4,3,2,1,0:T(8,128)(2,1)} %get-tuple-element.19), channel_id=1, source_target_pairs={{0,4},{1,5},{2,6},{3,7},{4,0},{5,1},{6,2},{7,3},{8,12},{9,13},{10,... | collective-permute-start | bytes 1572872 | tf_op jit(solution)/shard_map/ppermute | solution.py:205
  19.7 19.6 %collective-permute-start.4 = (bf16[2,2,2,64,512]{4,3,2,1,0:T(8,128)(2,1)}, bf16[2,2,2,64,512]{4,3,2,1,0:T(8,128)(2,1)S(1)}, u32[]{:S(2)}, u32[]{:S(2)}) collective-permute-start(bf16[2,2,2,64,512]{4,3,2,1,0:T(8,128)(2,1)} %get-tuple-element.20), channel_id=1, source_target_pairs={{0,2},{1,3},{2,0},{3,1},{4,6},{5,7},{6,4},{7,5},{8,10},{9,11},{10,... | collective-permute-start | bytes 1572872 | tf_op jit(solution)/shard_map/ppermute | solution.py:205
  20.5 0.7 %copy-start.5 = (s32[16]{0:T(128)S(1)}, s32[16]{0:T(128)}, u32[]{:S(2)}) copy-start(s32[16]{0:T(128)} %get-tuple-element.13.refs_0_) | copy-start | bytes 196
  22.0 3.8 %collective-permute-start.5 = (bf16[16,512]{1,0:T(8,128)(2,1)S(1)}, bf16[16,512]{1,0:T(8,128)(2,1)S(1)}, u32[]{:S(2)}, u32[]{:S(2)}) collective-permute-start(bf16[16,512]{1,0:T(8,128)(2,1)S(1)} %get-tuple-element.21), channel_id=1, source_target_pairs={{0,8},{8,0},{16,24},{24,16},{1,9},{9,1},{17,25},{25,17},{2,10},{10... | collective-permute-start | bytes 49160 | tf_op jit(solution)/shard_map/ppermute | solution.py:202
  27.7 5.4 %collective-permute-start.8 = (bf16[2,2,64,512]{3,2,1,0:T(8,128)(2,1)S(1)}, bf16[2,2,64,512]{3,2,1,0:T(8,128)(2,1)S(1)}, u32[]{:S(2)}, u32[]{:S(2)}) collective-permute-start(bf16[2,2,64,512]{3,2,1,0:T(8,128)(2,1)S(1)} %shard_map.88), channel_id=1, source_target_pairs={{0,1},{1,0},{2,3},{3,2},{4,5},{5,4},{6,7},{7,6},{8,9},{9,8},{10,11... | collective-permute-start | bytes 786440 | tf_op jit(solution)/shard_map/ppermute | solution.py:205
  27.8 5.3 %collective-permute-start.6 = (bf16[32,512]{1,0:T(8,128)(2,1)S(1)}, bf16[32,512]{1,0:T(8,128)(2,1)S(1)}, u32[]{:S(2)}, u32[]{:S(2)}) collective-permute-start(bf16[32,512]{1,0:T(8,128)(2,1)S(1)} %constant_dynamic-update-slice_fusion.refs_1_.first_ref), channel_id=1, source_target_pairs={{0,16},{8,24},{16,0},{24,8},{1,17},{9,25},{17,1},{25,9},{2,18},{10... | collective-permute-start | bytes 98312 | tf_op jit(solution)/shard_map/ppermute | solution.py:202
  33.1 7.6 %collective-permute-start.11 = (bf16[64,512]{1,0:T(8,128)(2,1)S(1)}, bf16[64,512]{1,0:T(8,128)(2,1)S(1)}, u32[]{:S(2)}, u32[]{:S(2)}) collective-permute-start(bf16[64,512]{1,0:T(8,128)(2,1)S(1)} %shard_map.89.refs_5_.refs_6_), channel_id=1, source_target_pairs={{0,2},{1,3},{2,0},{3,1},{4,6},{5,7},{6,4},{7,5},{8,10},{9,11},{10,... | collective-permute-start | bytes 196616 | tf_op jit(solution)/shard_map/ppermute | solution.py:205
  35.0 5.6 %collective-permute-start.10 = (bf16[64,512]{1,0:T(8,128)(2,1)S(1)}, bf16[64,512]{1,0:T(8,128)(2,1)S(1)}, u32[]{:S(2)}, u32[]{:S(2)}) collective-permute-start(bf16[64,512]{1,0:T(8,128)(2,1)S(1)} %shard_map.89.refs_5_.refs_6_), channel_id=1, source_target_pairs={{0,4},{1,5},{2,6},{3,7},{4,0},{5,1},{6,2},{7,3},{8,12},{9,13},{10,... | collective-permute-start | bytes 196616 | tf_op jit(solution)/shard_map/ppermute | solution.py:205
  36.5 5.2 %collective-permute-start.9 = (bf16[64,512]{1,0:T(8,128)(2,1)S(1)}, bf16[64,512]{1,0:T(8,128)(2,1)S(1)}, u32[]{:S(2)}, u32[]{:S(2)}) collective-permute-start(bf16[64,512]{1,0:T(8,128)(2,1)S(1)} %shard_map.89.refs_5_.refs_6_), channel_id=1, source_target_pairs={{0,6},{1,7},{2,4},{3,5},{4,2},{5,3},{6,0},{7,1},{8,14},{9,15},{10,... | collective-permute-start | bytes 196616 | tf_op jit(solution)/shard_map/ppermute | solution.py:205
  41.7 3.5 %collective-permute-start.12 = (bf16[2,2,64,512]{3,2,1,0:T(8,128)(2,1)S(1)}, bf16[2,2,64,512]{3,2,1,0:T(8,128)(2,1)S(1)}, u32[]{:S(2)}, u32[]{:S(2)}) collective-permute-start(bf16[2,2,64,512]{3,2,1,0:T(8,128)(2,1)S(1)} %get-tuple-element.22), channel_id=1, source_target_pairs={{0,1},{1,0},{2,3},{3,2},{4,5},{5,4},{6,7},{7,6},{8,9},{9,8},{10,11... | collective-permute-start | bytes 786440 | tf_op jit(solution)/shard_map/ppermute | solution.py:205
  41.8 3.4 %collective-permute-start.13 = (bf16[2,2,64,512]{3,2,1,0:T(8,128)(2,1)S(1)}, bf16[2,2,64,512]{3,2,1,0:T(8,128)(2,1)S(1)}, u32[]{:S(2)}, u32[]{:S(2)}) collective-permute-start(bf16[2,2,64,512]{3,2,1,0:T(8,128)(2,1)S(1)} %get-tuple-element.23), channel_id=1, source_target_pairs={{0,1},{1,0},{2,3},{3,2},{4,5},{5,4},{6,7},{7,6},{8,9},{9,8},{10,11... | collective-permute-start | bytes 786440 | tf_op jit(solution)/shard_map/ppermute | solution.py:205
  42.3 1.5 %collective-permute-start.14 = (bf16[64,512]{1,0:T(8,128)(2,1)S(1)}, bf16[64,512]{1,0:T(8,128)(2,1)S(1)}, u32[]{:S(2)}, u32[]{:S(2)}) collective-permute-start(bf16[64,512]{1,0:T(8,128)(2,1)S(1)} %shard_map.89.refs_5_.refs_6_), channel_id=1, source_target_pairs={{0,1},{1,0},{2,3},{3,2},{4,5},{5,4},{6,7},{7,6},{8,9},{9,8},{10,11... | collective-permute-start | bytes 196616 | tf_op jit(solution)/shard_map/ppermute | solution.py:205
  42.4 2.8 %collective-permute-start.17 = (bf16[64,512]{1,0:T(8,128)(2,1)S(1)}, bf16[64,512]{1,0:T(8,128)(2,1)S(1)}, u32[]{:S(2)}, u32[]{:S(2)}) collective-permute-start(bf16[64,512]{1,0:T(8,128)(2,1)S(1)} %collective-permute-done.11.refs_8_.refs_4_.refs_12_), channel_id=1, source_target_pairs={{0,1},{1,0},{2,3},{3,2},{4,5},{5,4},{6,7},{7,6},{8,9},{9,8},{10,11... | collective-permute-start | bytes 196616 | tf_op jit(solution)/shard_map/ppermute | solution.py:205
  42.8 2.4 %collective-permute-start.16 = (bf16[64,512]{1,0:T(8,128)(2,1)S(1)}, bf16[64,512]{1,0:T(8,128)(2,1)S(1)}, u32[]{:S(2)}, u32[]{:S(2)}) collective-permute-start(bf16[64,512]{1,0:T(8,128)(2,1)S(1)} %collective-permute-done.10.refs_7_.refs_3_.refs_10_), channel_id=1, source_target_pairs={{0,1},{1,0},{2,3},{3,2},{4,5},{5,4},{6,7},{7,6},{8,9},{9,8},{10,11... | collective-permute-start | bytes 196616 | tf_op jit(solution)/shard_map/ppermute | solution.py:205
  43.8 1.4 %collective-permute-start.15 = (bf16[64,512]{1,0:T(8,128)(2,1)S(1)}, bf16[64,512]{1,0:T(8,128)(2,1)S(1)}, u32[]{:S(2)}, u32[]{:S(2)}) collective-permute-start(bf16[64,512]{1,0:T(8,128)(2,1)S(1)} %collective-permute-done.9.refs_6_.refs_2_.refs_8_), channel_id=1, source_target_pairs={{0,1},{1,0},{2,3},{3,2},{4,5},{5,4},{6,7},{7,6},{8,9},{9,8},{10,11... | collective-permute-start | bytes 196616 | tf_op jit(solution)/shard_map/ppermute | solution.py:205

commit v9 on v8

--- a/solution.py
+++ b/solution.py
@@ -119,22 +119,33 @@
 
 
 def other_core(count, *refs):
-    in_refs, out_refs, sems = refs[:count], refs[-1 - count : -1], refs[-1]
+    in_refs, (out_ref, sems) = refs[:count], refs[-2:]
     copies = []
-    for i, (in_ref, out_ref) in enumerate(zip(in_refs, out_refs)):
-        copies.append(pltpu.make_async_copy(in_ref.at[1], out_ref, sems.at[i]))
+    for i, in_ref in enumerate(in_refs):
+        copies.append(pltpu.make_async_copy(in_ref.at[1], out_ref.at[i], sems.at[i]))
         copies[i].start()
     for copy in copies:
         copy.wait()
 
 
-def adjoint(n_pen, per_owner, core, table_ref, blocks, tile_refs, out_ref, made, out_sems):
+def stack_tiles(*refs):
+    in_refs, out_ref = refs[:-1], refs[-1]
+    for i, in_ref in enumerate(in_refs):
+        out_ref[i] = in_ref[...]
+
+
+def adjoint(n_pen, chunk, per_owner, core, table_ref, blocks, tiles, out_ref, residual_ref, made, out_sems):
     pen = lax.axis_index("pen")
     depth, columns = made.shape[3:]
+    rows = tiles[0].shape[0]
+    pick_row = lax.broadcasted_iota(I32, (16, rows), 0)
+    pick_at = lax.broadcasted_iota(I32, (16, rows), 1)
+    pick = jnp.where(pick_at == pick_row * chunk + pen, 1.0, 0.0)
+    pick = jnp.where(pick_row < 2, pick, 0.0).astype(BF16)
     puts = []
     for i in range(n_pen // 2):
         first_column = pl.multiple_of((pen ^ distance(n_pen, 2 * i + core)) * columns, columns)
-        here = tile_refs[i][...]
+        here = tiles[i][...]
         step = lax.dot_general(
             table_ref[...],
             jnp.concatenate([here, here], axis=0),
@@ -149,35 +160,28 @@
         to = out_ref.at[:, :, :, pl.ds(first_column, columns)]
         puts.append(pltpu.make_async_copy(made.at[i], to, out_sems.at[i]))
         puts[-1].start()
-    return puts
-
-
-def adjoint_like(n_pen, per_owner, table_ref, *rest):
-    chips = n_pen // 2
-    kept, tile_refs, (out_ref, made, out_sems) = rest[:chips], rest[chips:n_pen], rest[n_pen:]
-    blocks = [one.at[0] for one in kept]
-    for put in adjoint(n_pen, per_owner, 0, table_ref, blocks, tile_refs, out_ref, made, out_sems):
-        put.wait()
-
-
-def adjoint_other(n_pen, chunk, per_owner, table_ref, begun_ref, *rest):
-    del begun_ref
-    chips = n_pen // 2
-    swapped, tile_refs, rest = rest[:chips], rest[chips : chips + n_pen], rest[chips + n_pen :]
-    out_ref, residual_ref, made, out_sems = rest
-    rows, columns = tile_refs[0].shape
-    pen = lax.axis_index("pen")
-    puts = adjoint(n_pen, per_owner, 1, table_ref, swapped, tile_refs[1::2], out_ref, made, out_sems)
-    pick_row = lax.broadcasted_iota(I32, (16, rows), 0)
-    pick_at = lax.broadcasted_iota(I32, (16, rows), 1)
-    pick = jnp.where(pick_at == pick_row * chunk + pen, 1.0, 0.0)
-    pick = jnp.where(pick_row < 2, pick, 0.0).astype(BF16)
-    for q in range(n_pen):
-        first_column = pl.multiple_of((pen ^ distance(n_pen, q)) * columns, columns)
-        own = jnp.dot(pick, tile_refs[q][...], preferred_element_type=F32)
+        own = jnp.dot(pick, here, preferred_element_type=F32)
         residual_ref[0, :, pl.ds(first_column, columns)] = own[:2].astype(BF16)
     for put in puts:
         put.wait()
+
+
+def adjoint_like(n_pen, chunk, per_owner, table_ref, *rest):
+    chips = n_pen // 2
+    kept, tiles, (out_ref, residual_ref, made, out_sems) = rest[:chips], rest[chips:n_pen], rest[n_pen:]
+    residual_ref[...] = jnp.zeros_like(residual_ref)
+    blocks = [one.at[0] for one in kept]
+    adjoint(n_pen, chunk, per_owner, 0, table_ref, blocks, tiles, out_ref, residual_ref, made, out_sems)
+
+
+def adjoint_other(n_pen, chunk, per_owner, table_ref, begun_ref, part_ref, own_ref, far_ref, near_ref, tiles_ref,
+                  out_ref, residual_ref, made, out_sems):
+    del begun_ref
+    chips = n_pen // 2
+    residual_ref[...] = part_ref[...]
+    blocks = [own_ref, far_ref] + [near_ref.at[i] for i in range(chips - 2)]
+    tiles = [tiles_ref.at[i] for i in range(chips)]
+    adjoint(n_pen, chunk, per_owner, 1, table_ref, blocks, tiles, out_ref, residual_ref, made, out_sems)
 
 
 def body(spectrum, depth_weights, pair_tilt, pair_tile_within, tilt_pos, owner, measured):
@@ -271,46 +275,55 @@
     def take_other(arrived, after):
         return pl.pallas_call(
             call(other_core, len(arrived)),
-            out_shape=[jax.ShapeDtypeStruct(pair, BF16)] * len(arrived),
+            out_shape=jax.ShapeDtypeStruct((len(arrived), *pair), BF16),
             in_specs=[ANY] * (len(arrived) + len(after)),
-            out_specs=[ANY] * len(arrived),
+            out_specs=ANY,
             scratch_shapes=[pltpu.SemaphoreType.DMA((len(arrived),))],
             compiler_params=pltpu.CompilerParams(vmem_limit_bytes=8 << 20),
         )(*arrived, *after)
 
-    swapped = [between(one, 1) for one in [outs[0][1], *take_other(kept[1:2], [held])]]
+    own_swapped = between(outs[0][1], 1)
+    far_swapped = between(take_other(kept[1:2], [held]), 1).reshape(pair)
     held = pl.pallas_call(
         join_tiles,
         out_shape=jax.ShapeDtypeStruct((2 * tiles, columns), BF16),
         in_specs=[VMEM, VMEM, ANY, ANY],
         out_specs=VMEM,
         compiler_params=pltpu.CompilerParams(vmem_limit_bytes=8 << 20),
-    )(held, across(held, step), *swapped)
+    )(held, across(held, step), own_swapped, far_swapped)
     like = [held] + [between(held, distance(n_pen, 2 * i)) for i in range(1, chips)]
-    swapped = swapped + [between(one, 1) for one in take_other(kept[2:], like[1:])]
-    every = [tile for one in like for tile in (one, between(one, 1))]
+    near_swapped = between(take_other(kept[2:], like[1:]), 1)
+    stacked = pl.pallas_call(
+        stack_tiles,
+        out_shape=jax.ShapeDtypeStruct((chips, 2 * tiles, columns), BF16),
+        in_specs=[VMEM] * chips,
+        out_specs=VMEM,
+        compiler_params=pltpu.CompilerParams(vmem_limit_bytes=8 << 20),
+    )(*like)
+    other = between(stacked, 1)
 
     scratch = [pltpu.VMEM((chips, *pair), BF16), pltpu.SemaphoreType.DMA((chips,))]
-    begun = pl.pallas_call(
-        call(adjoint_like, n_pen, per_owner),
-        out_shape=jax.ShapeDtypeStruct((per_owner, 2, depth, cells), BF16),
+    shapes = [
+        jax.ShapeDtypeStruct((per_owner, 2, depth, cells), BF16),
+        jax.ShapeDtypeStruct((tile_dev, 2, cells), BF16),
+    ]
+    begun, part = pl.pallas_call(
+        call(adjoint_like, n_pen, chunk, per_owner),
+        out_shape=shapes,
         in_specs=[VMEM] * (n_pen + 1),
-        out_specs=ANY,
+        out_specs=[ANY, VMEM],
         scratch_shapes=scratch,
         compiler_params=pltpu.CompilerParams(vmem_limit_bytes=16 << 20),
     )(table, *kept, *like)
     updated, residual = pl.pallas_call(
         call(adjoint_other, n_pen, chunk, per_owner),
-        out_shape=[
-            jax.ShapeDtypeStruct(begun.shape, BF16),
-            jax.ShapeDtypeStruct((tile_dev, 2, cells), BF16),
-        ],
-        in_specs=[VMEM, ANY] + [VMEM] * (chips + n_pen),
+        out_shape=shapes,
+        in_specs=[VMEM, ANY] + [VMEM] * 5,
         out_specs=[ANY, VMEM],
         scratch_shapes=scratch,
         input_output_aliases={1: 0},
         compiler_params=pltpu.CompilerParams(vmem_limit_bytes=16 << 20),
-    )(table, begun, *swapped, *every)
+    )(table, begun, part, own_swapped, far_swapped, near_swapped, other)
     return (updated, residual)
 
 

time: 47.4 us -> 45.9 us (0.968)
  starting transfers between devices: 21 us -> 20.3 us
  waiting for transfers between devices: 14.6 us -> 13.9 us
    ppermute x14 -> x10, waiting for transfers between devices: 7.8 us -> 6.34 us  [between(): return lax.ppermute(value, 'pen', [(i, i ^ k) for i in range(n_pen)])]
    ppermute x14 -> x10, starting transfers between devices: 8.63 us -> 7.86 us  [between(): return lax.ppermute(value, 'pen', [(i, i ^ k) for i in range(n_pen)])]
    ppermute x4, waiting for transfers between devices: 6.83 us -> 7.52 us  [across(): return lax.ppermute(value, 'kz', [(i, i ^ k) for i in range(n_kz)])]
    pallas_call x4 -> x5, Pallas kernels: 3.19 us -> 3.27 us  [the longest x1 1.89 us: body(): pl.pallas_call(call(adjoint_other, n_pen, chunk, per_owner), out_shape=sh...]
  transfers between devices with their start and end apart: 19 -> 15, of which waited for: 9 -> 10; matrix products, arithmetic and copies ran while one was open for 4% -> 4% of each run, Pallas kernels for 4% -> 5%
where the time goes in v9:
time: 45.9 us; the launch traced here: 45.6 us
  starting transfers between devices  20.3 us (44%)
  waiting for transfers between devices  13.9 us (30%)
  Pallas kernels  8.15 us (18%)
  local copies, waits for them, and re-layouts  1.66 us (4%)
  other arithmetic  0.85 us (2%)
  between operations  0.81 us (2%)
    ppermute x4, starting transfers between devices, across(): return lax.ppermute(value, 'kz', [(i, i ^ k) for i in range(n_kz)])  8.7 us
    ppermute x10, starting transfers between devices, between(): return lax.ppermute(value, 'pen', [(i, i ^ k) for i in range(n_pen)])  7.86 us
    ppermute x4, waiting for transfers between devices, across(): return lax.ppermute(value, 'kz', [(i, i ^ k) for i in range(n_kz)])  7.52 us
    ppermute x10, waiting for transfers between devices, between(): return lax.ppermute(value, 'pen', [(i, i ^ k) for i in range(n_pen)])  6.34 us
    pallas_call x1, Pallas kernels, body(): pl.pallas_call(call(order_and_forward, n_pen, n_kz, chunk, per_owner, til...  4.07 us
    all_to_all x1, starting transfers between devices, body(): got = lax.all_to_all(sent, 'pen', split_axis=0, concat_axis=0, tiled=True)  3.72 us
    pallas_call x1, Pallas kernels, body(): pl.pallas_call(call(adjoint_other, n_pen, chunk, per_owner), out_shape=sh...  1.89 us
    pallas_call x1, Pallas kernels, body(): pl.pallas_call(call(adjoint_like, n_pen, chunk, per_owner), out_shape=sha...  1.27 us
  transfers between devices with their start and end apart: 15, of which 10 were waited for; matrix products, arithmetic and copies ran while one was open for 4% of the time, Pallas kernels for 5%

profile of v9, /device:TPU:0, one launch (start us, length us, event | category | flops | bytes accessed | tf_op | source)
XLA Modules:
  0.0 45.6 jit_solution(9774794399807406499)
XLA Ops:
  0.6 0.0 copy-start.4
  0.6 0.0 copy-start.2
  0.7 0.0 copy-start.3
  0.7 0.0 copy-start.1
  0.7 4.1 %shard_map.86 = (bf16[2,2,2,64,512]{4,3,2,1,0:T(8,128)(2,1)}, bf16[2,2,2,64,512]{4,3,2,1,0:T(8,128)(2,1)}, bf16[2,2,2,64,512]{4,3,2,1,0:T(8,128)(2,1)}, bf16[2,2...) custom-call(s32[16]{0:T(128)} %refs_0_.1, s32[16]{0:T(128)} %refs_1_.3, ...), custom_call_target="tpu_custom_call" | custom-call | tf_op jit(solution)/shard_map/pallas_call | solution.py:213
  4.8 3.1 %collective-permute-start = (f32[2,16,512]{2,1,0:T(8,128)}, f32[2,16,512]{2,1,0:T(8,128)S(1)}, u32[]{:S(2)}, u32[]{:S(2)}) collective-permute-start(f32[2,16,512]{2,1,0:T(8,128)} %get-tuple-element.15), channel_id=1, source_target_pairs={{0,8},{8,0},{16,24},{24,16},{1,9},{9,1},{17,25},{25,17},{2,10},{10... | collective-permute-start | bytes 196616 | tf_op jit(solution)/shard_map/ppermute | solution.py:206
  7.8 3.7 %all-to-all-start = ((bf16[8,2,512]{2,1,0:T(2,128)(2,1)}), bf16[8,2,512]{2,1,0:T(2,128)(2,1)S(1)}, u32[]{:S(2)}, u32[]{:S(2)}) async-start(bf16[8,2,512]{2,1,0:T(2,128)(2,1)} %bitcast.5), calls=%async_computation | async-start | bytes 32768 | tf_op jit(solution)/shard_map/all_to_all | solution.py:247
  11.6 2.9 %collective-permute-start.2 = (bf16[2,2,2,64,512]{4,3,2,1,0:T(8,128)(2,1)}, bf16[2,2,2,64,512]{4,3,2,1,0:T(8,128)(2,1)S(1)}, u32[]{:S(2)}, u32[]{:S(2)}) collective-permute-start(bf16[2,2,2,64,512]{4,3,2,1,0:T(8,128)(2,1)} %get-tuple-element.18), channel_id=1, source_target_pairs={{0,6},{1,7},{2,4},{3,5},{4,2},{5,3},{6,0},{7,1},{8,14},{9,15},{10,... | collective-permute-start | bytes 1572872 | tf_op jit(solution)/shard_map/ppermute | solution.py:209
  14.5 0.6 %collective-permute-start.3 = (bf16[2,2,2,64,512]{4,3,2,1,0:T(8,128)(2,1)}, bf16[2,2,2,64,512]{4,3,2,1,0:T(8,128)(2,1)S(1)}, u32[]{:S(2)}, u32[]{:S(2)}) collective-permute-start(bf16[2,2,2,64,512]{4,3,2,1,0:T(8,128)(2,1)} %get-tuple-element.19), channel_id=1, source_target_pairs={{0,4},{1,5},{2,6},{3,7},{4,0},{5,1},{6,2},{7,3},{8,12},{9,13},{10,... | collective-permute-start | bytes 1572872 | tf_op jit(solution)/shard_map/ppermute | solution.py:209
  15.1 0.1 collective-permute-start.4
  15.1 0.0 collective-permute-done
  15.1 0.8 %add_bitcast_fusion = f32[1,2,16,512]{3,2,1,0:T(8,128)S(1)} fusion(f32[2,16,512]{2,1,0:T(8,128)} %get-tuple-element.14, f32[2,16,512]{2,1,0:T(8,128)S(1)} %collective-permute-done), kind=kLoop, calls=%fused_computation.1 | loop fusion | flops 16384 | bytes 196608 | tf_op jit(solution)/shard_map/reshape | solution.py:242
  16.0 2.7 %collective-permute-start.1 = (f32[1,16,512]{2,1,0:T(8,128)S(1)}, f32[1,16,512]{2,1,0:T(8,128)S(1)}, u32[]{:S(2)}, u32[]{:S(2)}) collective-permute-start(f32[1,16,512]{2,1,0:T(8,128)S(1)} %get-tuple-element.24), channel_id=1, source_target_pairs={{0,16},{8,24},{16,0},{24,8},{1,17},{9,25},{17,1},{25,9},{2,18},{10... | collective-permute-start | bytes 98312 | tf_op jit(solution)/shard_map/ppermute | solution.py:206
  18.6 1.0 %slice_bitcast_fusion = bf16[2,2,64,512]{3,2,1,0:T(8,128)(2,1)S(1)} fusion(bf16[2,2,2,64,512]{4,3,2,1,0:T(8,128)(2,1)} %get-tuple-element.17.refs_1_), kind=kLoop, calls=%fused_computation | loop fusion | bytes 524288 | tf_op jit(solution)/shard_map/squeeze | solution.py:285
  19.6 0.0 copy-start
  19.6 0.1 collective-permute-start.7
  19.7 0.0 all-to-all-done
  19.7 1.4 %collective-permute-done.1 = f32[1,16,512]{2,1,0:T(8,128)S(1)} collective-permute-done((f32[1,16,512]{2,1,0:T(8,128)S(1)}, f32[1,16,512]{2,1,0:T(8,128)S(1)}, u32[]{:S(2)}, u32[]{:S(2)}) %collective-permute-start.1) | collective-permute-done | bytes 32800 | tf_op jit(solution)/shard_map/ppermute | solution.py:206
  21.1 0.0 copy-done.4
  21.1 0.0 copy-done.2
  21.1 0.0 copy-done.3
  21.1 0.0 copy-done.1
  21.1 0.0 copy-start.5
  21.1 0.6 %copy-done.5 = s32[16]{0:T(128)S(1)} copy-done((s32[16]{0:T(128)S(1)}, s32[16]{0:T(128)}, u32[]{:S(2)}) %copy-start.5) | copy-done | bytes 88
  21.8 0.8 %shard_map.87 = (bf16[16,512]{1,0:T(8,128)(2,1)S(1)}, bf16[128,256]{1,0:T(8,128)(2,1)S(1)}) custom-call(s32[16]{0:T(128)S(1)} %copy-done.5, s32[16]{0:T(128)S(1)} %copy-done.4, s32[16,16]{1,0:T(8,128)S(1)} %copy-done.2, s32[16,16]{1,0:T(8,128)S(1)} %copy-done.3, bf16[16,16,64]{2,1,0:T(8,128)(2,1)S(1)} %copy-done.1, f32[16,512]{1,0:T(8,128)S(1)} %get-tuple-element.25.refs_5_, ...), custom_call_target="tpu_custom_call" | custom-call | tf_op jit(solution)/shard_map/pallas_call | solution.py:249
  22.6 0.3 collective-permute-start.5
  22.9 3.5 %collective-permute-done.5 = bf16[16,512]{1,0:T(8,128)(2,1)S(1)} collective-permute-done((bf16[16,512]{1,0:T(8,128)(2,1)S(1)}, bf16[16,512]{1,0:T(8,128)(2,1)S(1)}, u32[]{:S(2)}, u32[]{:S(2)}) %collective-permute-start.5) | collective-permute-done | bytes 16416 | tf_op jit(solution)/shard_map/ppermute | solution.py:206
  26.4 1.2 %collective-permute-done.2.refs_0_.refs_2_ = bf16[2,2,2,64,512]{4,3,2,1,0:T(8,128)(2,1)S(1)} collective-permute-done((bf16[2,2,2,64,512]{4,3,2,1,0:T(8,128)(2,1)}, bf16[2,2,2,64,512]{4,3,2,1,0:T(8,128)(2,1)S(1)}, u32[]{:S(2)}, u32[]{:S(2)}) %collective-permute-start.2) | collective-permute-done | bytes 524320 | tf_op jit(solution)/shard_map/ppermute | solution.py:209
  27.7 0.1 collective-permute-start.8
  27.7 2.7 %collective-permute-start.6 = (bf16[32,512]{1,0:T(8,128)(2,1)S(1)}, bf16[32,512]{1,0:T(8,128)(2,1)S(1)}, u32[]{:S(2)}, u32[]{:S(2)}) collective-permute-start(bf16[32,512]{1,0:T(8,128)(2,1)S(1)} %constant_dynamic-update-slice_fusion.refs_1_.first_ref), channel_id=1, source_target_pairs={{0,16},{8,24},{16,0},{24,8},{1,17},{9,25},{17,1},{25,9},{2,18},{10... | collective-permute-start | bytes 98312 | tf_op jit(solution)/shard_map/ppermute | solution.py:206
  30.4 2.6 %collective-permute-done.6.second_ref = bf16[32,512]{1,0:T(8,128)(2,1)S(1)} collective-permute-done((bf16[32,512]{1,0:T(8,128)(2,1)S(1)}, bf16[32,512]{1,0:T(8,128)(2,1)S(1)}, u32[]{:S(2)}, u32[]{:S(2)}) %collective-permute-start.6) | collective-permute-done | bytes 32800 | tf_op jit(solution)/shard_map/ppermute | solution.py:206
  33.0 0.0 collective-permute-done.7.rest_0_.refs_3_
  33.0 0.0 collective-permute-done.8
  33.0 2.9 %collective-permute-start.9 = (bf16[64,512]{1,0:T(8,128)(2,1)S(1)}, bf16[64,512]{1,0:T(8,128)(2,1)S(1)}, u32[]{:S(2)}, u32[]{:S(2)}) collective-permute-start(bf16[64,512]{1,0:T(8,128)(2,1)S(1)} %shard_map.89.refs_5_.refs_0_), channel_id=1, source_target_pairs={{0,6},{1,7},{2,4},{3,5},{4,2},{5,3},{6,0},{7,1},{8,14},{9,15},{10,... | collective-permute-start | bytes 196616 | tf_op jit(solution)/shard_map/ppermute | solution.py:209
  35.9 0.6 %collective-permute-start.10 = (bf16[64,512]{1,0:T(8,128)(2,1)S(1)}, bf16[64,512]{1,0:T(8,128)(2,1)S(1)}, u32[]{:S(2)}, u32[]{:S(2)}) collective-permute-start(bf16[64,512]{1,0:T(8,128)(2,1)S(1)} %shard_map.89.refs_5_.refs_0_), channel_id=1, source_target_pairs={{0,4},{1,5},{2,6},{3,7},{4,0},{5,1},{6,2},{7,3},{8,12},{9,13},{10,... | collective-permute-start | bytes 196616 | tf_op jit(solution)/shard_map/ppermute | solution.py:209
  36.5 0.1 collective-permute-start.11
  36.6 2.3 %collective-permute-done.3.refs_3_.refs_0_ = bf16[2,2,2,64,512]{4,3,2,1,0:T(8,128)(2,1)S(1)} collective-permute-done((bf16[2,2,2,64,512]{4,3,2,1,0:T(8,128)(2,1)}, bf16[2,2,2,64,512]{4,3,2,1,0:T(8,128)(2,1)S(1)}, u32[]{:S(2)}, u32[]{:S(2)}) %collective-permute-start.3) | collective-permute-done | bytes 524320 | tf_op jit(solution)/shard_map/ppermute | solution.py:209
  38.9 0.4 collective-permute-done.4.refs_4_.refs_1_
  39.3 0.9 %collective-permute-done.9.refs_6_.refs_2_.refs_1_ = bf16[64,512]{1,0:T(8,128)(2,1)S(1)} collective-permute-done((bf16[64,512]{1,0:T(8,128)(2,1)S(1)}, bf16[64,512]{1,0:T(8,128)(2,1)S(1)}, u32[]{:S(2)}, u32[]{:S(2)}) %collective-permute-start.9) | collective-permute-done | bytes 65568 | tf_op jit(solution)/shard_map/ppermute | solution.py:209
  40.2 1.0 %collective-permute-done.10.refs_7_.refs_3_.refs_2_ = bf16[64,512]{1,0:T(8,128)(2,1)S(1)} collective-permute-done((bf16[64,512]{1,0:T(8,128)(2,1)S(1)}, bf16[64,512]{1,0:T(8,128)(2,1)S(1)}, u32[]{:S(2)}, u32[]{:S(2)}) %collective-permute-start.10) | collective-permute-done | bytes 65568 | tf_op jit(solution)/shard_map/ppermute | solution.py:209
  41.1 0.2 collective-permute-done.11.refs_8_.refs_4_.refs_3_
  41.3 0.1 shard_map.91
  41.4 0.1 collective-permute-start.12
  41.5 0.6 %collective-permute-start.13 = (bf16[4,64,512]{2,1,0:T(8,128)(2,1)S(1)}, bf16[4,64,512]{2,1,0:T(8,128)(2,1)S(1)}, u32[]{:S(2)}, u32[]{:S(2)}) collective-permute-start(bf16[4,64,512]{2,1,0:T(8,128)(2,1)S(1)} %shard_map.92), channel_id=1, source_target_pairs={{0,1},{1,0},{2,3},{3,2},{4,5},{5,4},{6,7},{7,6},{8,9},{9,8},{10,11... | collective-permute-start | bytes 786440 | tf_op jit(solution)/shard_map/ppermute | solution.py:209
  42.0 1.3 %shard_map.90 = (bf16[2,2,64,4096]{3,2,1,0:T(8,128)(2,1)}, bf16[1,2,4096]{2,1,0:T(2,128)(2,1)S(1)}) custom-call(bf16[128,256]{1,0:T(8,128)(2,1)S(1)} %get-tuple-element.16.refs_0_, bf16[2,2,2,64,512]{4,3,2,1,0:T(8,128)(2,1)S(1)} %copy-done, bf16[2,2,2,64,512]{4,3,2,1,0:T(8,128)(2,1)S(1)} %collective-permute-done.2.refs_0_.refs_2_, ...), custom_call_target="tpu_custom_call" | custom-call | tf_op jit(solution)/shard_map/pallas_call | solution.py:310
  43.3 0.4 collective-permute-done.13.refs_6_
  43.7 0.0 collective-permute-done.12.refs_5_
  43.7 1.9 %shard_map.93 = (bf16[2,2,64,4096]{3,2,1,0:T(8,128)(2,1)}, bf16[1,2,4096]{2,1,0:T(2,128)(2,1)}) custom-call(bf16[128,256]{1,0:T(8,128)(2,1)S(1)} %get-tuple-element.16.refs_0_, bf16[2,2,64,4096]{3,2,1,0:T(8,128)(2,1)} %get-tuple-element.22.refs_1_, bf16[1,2,4096]{2,1,0:T(2,128)(2,1)S(1)} %get-tuple-element.23.refs_2_, ...), custom_call_target="tpu_custom_call", output_to_operand_aliasing={{0}: (1, {})} | custom-call | tf_op jit(solution)/shard_map/pallas_call | solution.py:318
  (8 shorter events, 0.1 us)
Async XLA Ops:
  0.6 20.5 %copy-start.4 = (s32[16]{0:T(128)S(1)}, s32[16]{0:T(128)}, u32[]{:S(2)}) copy-start(s32[16]{0:T(128)} %refs_1_.3) | copy-start | bytes 196
  0.6 20.5 %copy-start.2 = (s32[16,16]{1,0:T(8,128)S(1)}, s32[16,16]{1,0:T(8,128)}, u32[]{:S(2)}) copy-start(s32[16,16]{1,0:T(8,128)} %refs_2_.3) | copy-start | bytes 3076
  0.7 20.4 %copy-start.3 = (s32[16,16]{1,0:T(8,128)S(1)}, s32[16,16]{1,0:T(8,128)}, u32[]{:S(2)}) copy-start(s32[16,16]{1,0:T(8,128)} %refs_3_.3) | copy-start | bytes 3076
  0.7 20.4 %copy-start.1 = (bf16[16,16,64]{2,1,0:T(8,128)(2,1)S(1)}, bf16[16,16,64]{2,1,0:T(8,128)(2,1)}, u32[]{:S(2)}) copy-start(bf16[16,16,64]{2,1,0:T(8,128)(2,1)} %refs_4_.3) | copy-start | bytes 98308
  4.8 10.4 %collective-permute-start = (f32[2,16,512]{2,1,0:T(8,128)}, f32[2,16,512]{2,1,0:T(8,128)S(1)}, u32[]{:S(2)}, u32[]{:S(2)}) collective-permute-start(f32[2,16,512]{2,1,0:T(8,128)} %get-tuple-element.15), channel_id=1, source_target_pairs={{0,8},{8,0},{16,24},{24,16},{1,9},{9,1},{17,25},{25,17},{2,10},{10... | collective-permute-start | bytes 196616 | tf_op jit(solution)/shard_map/ppermute | solution.py:206
  7.8 11.8 %all-to-all-start = ((bf16[8,2,512]{2,1,0:T(2,128)(2,1)}), bf16[8,2,512]{2,1,0:T(2,128)(2,1)S(1)}, u32[]{:S(2)}, u32[]{:S(2)}) async-start(bf16[8,2,512]{2,1,0:T(2,128)(2,1)} %bitcast.5), calls=%async_computation | async-start | bytes 32768 | tf_op jit(solution)/shard_map/all_to_all | solution.py:247
  11.6 16.1 %collective-permute-start.2 = (bf16[2,2,2,64,512]{4,3,2,1,0:T(8,128)(2,1)}, bf16[2,2,2,64,512]{4,3,2,1,0:T(8,128)(2,1)S(1)}, u32[]{:S(2)}, u32[]{:S(2)}) collective-permute-start(bf16[2,2,2,64,512]{4,3,2,1,0:T(8,128)(2,1)} %get-tuple-element.18), channel_id=1, source_target_pairs={{0,6},{1,7},{2,4},{3,5},{4,2},{5,3},{6,0},{7,1},{8,14},{9,15},{10,... | collective-permute-start | bytes 1572872 | tf_op jit(solution)/shard_map/ppermute | solution.py:209
  14.5 24.4 %collective-permute-start.3 = (bf16[2,2,2,64,512]{4,3,2,1,0:T(8,128)(2,1)}, bf16[2,2,2,64,512]{4,3,2,1,0:T(8,128)(2,1)S(1)}, u32[]{:S(2)}, u32[]{:S(2)}) collective-permute-start(bf16[2,2,2,64,512]{4,3,2,1,0:T(8,128)(2,1)} %get-tuple-element.19), channel_id=1, source_target_pairs={{0,4},{1,5},{2,6},{3,7},{4,0},{5,1},{6,2},{7,3},{8,12},{9,13},{10,... | collective-permute-start | bytes 1572872 | tf_op jit(solution)/shard_map/ppermute | solution.py:209
  15.1 24.2 %collective-permute-start.4 = (bf16[2,2,2,64,512]{4,3,2,1,0:T(8,128)(2,1)}, bf16[2,2,2,64,512]{4,3,2,1,0:T(8,128)(2,1)S(1)}, u32[]{:S(2)}, u32[]{:S(2)}) collective-permute-start(bf16[2,2,2,64,512]{4,3,2,1,0:T(8,128)(2,1)} %get-tuple-element.20), channel_id=1, source_target_pairs={{0,2},{1,3},{2,0},{3,1},{4,6},{5,7},{6,4},{7,5},{8,10},{9,11},{10,... | collective-permute-start | bytes 1572872 | tf_op jit(solution)/shard_map/ppermute | solution.py:209
  16.0 5.1 %collective-permute-start.1 = (f32[1,16,512]{2,1,0:T(8,128)S(1)}, f32[1,16,512]{2,1,0:T(8,128)S(1)}, u32[]{:S(2)}, u32[]{:S(2)}) collective-permute-start(f32[1,16,512]{2,1,0:T(8,128)S(1)} %get-tuple-element.24), channel_id=1, source_target_pairs={{0,16},{8,24},{16,0},{24,8},{1,17},{9,25},{17,1},{25,9},{2,18},{10... | collective-permute-start | bytes 98312 | tf_op jit(solution)/shard_map/ppermute | solution.py:206
  19.6 22.4 %copy-start = (bf16[2,2,2,64,512]{4,3,2,1,0:T(8,128)(2,1)S(1)}, bf16[2,2,2,64,512]{4,3,2,1,0:T(8,128)(2,1)}, u32[]{:S(2)}) copy-start(bf16[2,2,2,64,512]{4,3,2,1,0:T(8,128)(2,1)} %get-tuple-element.17.refs_1_) | copy-start | bytes 1572868
  19.6 13.4 %collective-permute-start.7 = (bf16[2,2,64,512]{3,2,1,0:T(8,128)(2,1)S(1)}, bf16[2,2,64,512]{3,2,1,0:T(8,128)(2,1)S(1)}, u32[]{:S(2)}, u32[]{:S(2)}) collective-permute-start(bf16[2,2,64,512]{3,2,1,0:T(8,128)(2,1)S(1)} %slice_bitcast_fusion), channel_id=1, source_target_pairs={{0,1},{1,0},{2,3},{3,2},{4,5},{5,4},{6,7},{7,6},{8,9},{9,8},{10,11... | collective-permute-start | bytes 786440 | tf_op jit(solution)/shard_map/ppermute | solution.py:209
  21.1 0.7 %copy-start.5 = (s32[16]{0:T(128)S(1)}, s32[16]{0:T(128)}, u32[]{:S(2)}) copy-start(s32[16]{0:T(128)} %get-tuple-element.13.refs_0_) | copy-start | bytes 196
  22.6 3.8 %collective-permute-start.5 = (bf16[16,512]{1,0:T(8,128)(2,1)S(1)}, bf16[16,512]{1,0:T(8,128)(2,1)S(1)}, u32[]{:S(2)}, u32[]{:S(2)}) collective-permute-start(bf16[16,512]{1,0:T(8,128)(2,1)S(1)} %get-tuple-element.21), channel_id=1, source_target_pairs={{0,8},{8,0},{16,24},{24,16},{1,9},{9,1},{17,25},{25,17},{2,10},{10... | collective-permute-start | bytes 49160 | tf_op jit(solution)/shard_map/ppermute | solution.py:206
  27.7 5.4 %collective-permute-start.8 = (bf16[1,2,2,64,512]{4,3,2,1,0:T(8,128)(2,1)S(1)}, bf16[1,2,2,64,512]{4,3,2,1,0:T(8,128)(2,1)S(1)}, u32[]{:S(2)}, u32[]{:S(2)}) collective-permute-start(bf16[1,2,2,64,512]{4,3,2,1,0:T(8,128)(2,1)S(1)} %shard_map.88), channel_id=1, source_target_pairs={{0,1},{1,0},{2,3},{3,2},{4,5},{5,4},{6,7},{7,6},{8,9},{9,8},{10,11... | collective-permute-start | bytes 786440 | tf_op jit(solution)/shard_map/ppermute | solution.py:209
  27.7 5.3 %collective-permute-start.6 = (bf16[32,512]{1,0:T(8,128)(2,1)S(1)}, bf16[32,512]{1,0:T(8,128)(2,1)S(1)}, u32[]{:S(2)}, u32[]{:S(2)}) collective-permute-start(bf16[32,512]{1,0:T(8,128)(2,1)S(1)} %constant_dynamic-update-slice_fusion.refs_1_.first_ref), channel_id=1, source_target_pairs={{0,16},{8,24},{16,0},{24,8},{1,17},{9,25},{17,1},{25,9},{2,18},{10... | collective-permute-start | bytes 98312 | tf_op jit(solution)/shard_map/ppermute | solution.py:206
  33.0 7.1 %collective-permute-start.9 = (bf16[64,512]{1,0:T(8,128)(2,1)S(1)}, bf16[64,512]{1,0:T(8,128)(2,1)S(1)}, u32[]{:S(2)}, u32[]{:S(2)}) collective-permute-start(bf16[64,512]{1,0:T(8,128)(2,1)S(1)} %shard_map.89.refs_5_.refs_0_), channel_id=1, source_target_pairs={{0,6},{1,7},{2,4},{3,5},{4,2},{5,3},{6,0},{7,1},{8,14},{9,15},{10,... | collective-permute-start | bytes 196616 | tf_op jit(solution)/shard_map/ppermute | solution.py:209
  35.9 5.2 %collective-permute-start.10 = (bf16[64,512]{1,0:T(8,128)(2,1)S(1)}, bf16[64,512]{1,0:T(8,128)(2,1)S(1)}, u32[]{:S(2)}, u32[]{:S(2)}) collective-permute-start(bf16[64,512]{1,0:T(8,128)(2,1)S(1)} %shard_map.89.refs_5_.refs_0_), channel_id=1, source_target_pairs={{0,4},{1,5},{2,6},{3,7},{4,0},{5,1},{6,2},{7,3},{8,12},{9,13},{10,... | collective-permute-start | bytes 196616 | tf_op jit(solution)/shard_map/ppermute | solution.py:209
  36.5 4.8 %collective-permute-start.11 = (bf16[64,512]{1,0:T(8,128)(2,1)S(1)}, bf16[64,512]{1,0:T(8,128)(2,1)S(1)}, u32[]{:S(2)}, u32[]{:S(2)}) collective-permute-start(bf16[64,512]{1,0:T(8,128)(2,1)S(1)} %shard_map.89.refs_5_.refs_0_), channel_id=1, source_target_pairs={{0,2},{1,3},{2,0},{3,1},{4,6},{5,7},{6,4},{7,5},{8,10},{9,11},{10,... | collective-permute-start | bytes 196616 | tf_op jit(solution)/shard_map/ppermute | solution.py:209
  41.4 2.4 %collective-permute-start.12 = (bf16[2,2,2,64,512]{4,3,2,1,0:T(8,128)(2,1)S(1)}, bf16[2,2,2,64,512]{4,3,2,1,0:T(8,128)(2,1)S(1)}, u32[]{:S(2)}, u32[]{:S(2)}) collective-permute-start(bf16[2,2,2,64,512]{4,3,2,1,0:T(8,128)(2,1)S(1)} %shard_map.91), channel_id=1, source_target_pairs={{0,1},{1,0},{2,3},{3,2},{4,5},{5,4},{6,7},{7,6},{8,9},{9,8},{10,11... | collective-permute-start | bytes 1572872 | tf_op jit(solution)/shard_map/ppermute | solution.py:209
  41.5 2.2 %collective-permute-start.13 = (bf16[4,64,512]{2,1,0:T(8,128)(2,1)S(1)}, bf16[4,64,512]{2,1,0:T(8,128)(2,1)S(1)}, u32[]{:S(2)}, u32[]{:S(2)}) collective-permute-start(bf16[4,64,512]{2,1,0:T(8,128)(2,1)S(1)} %shard_map.92), channel_id=1, source_target_pairs={{0,1},{1,0},{2,3},{3,2},{4,5},{5,4},{6,7},{7,6},{8,9},{9,8},{10,11... | collective-permute-start | bytes 786440 | tf_op jit(solution)/shard_map/ppermute | solution.py:209

commit v10 on v9

--- a/solution.py
+++ b/solution.py
@@ -16,10 +16,6 @@
 def split_hi_lo(value):
     hi = value.astype(BF16)
     return hi, (value - hi.astype(F32)).astype(BF16)
-
-
-def distance(n_pen, q):
-    return (n_pen - q // 2 * 2) % n_pen + q % 2
 
 
 def slots(tilt_pos_ref, tilt, within, tiles_per_tilt, flip):
@@ -69,7 +65,7 @@
         get.wait()
     for q in range(n_pen):
         for r in range(per_owner):
-            from_ref = held.at[inverse_ref[(pen ^ distance(n_pen, q)) * per_owner + r]]
+            from_ref = held.at[inverse_ref[(pen ^ q) * per_owner + r]]
             puts.append(pltpu.make_async_copy(from_ref, outs[q // 2].at[q % 2, r], out_sems.at[q, r]))
             puts[-1].start()
     for c in range(2):
@@ -144,7 +140,7 @@
     pick = jnp.where(pick_row < 2, pick, 0.0).astype(BF16)
     puts = []
     for i in range(n_pen // 2):
-        first_column = pl.multiple_of((pen ^ distance(n_pen, 2 * i + core)) * columns, columns)
+        first_column = pl.multiple_of((pen ^ (2 * i + core)) * columns, columns)
         here = tiles[i][...]
         step = lax.dot_general(
             table_ref[...],
@@ -162,8 +158,7 @@
         puts[-1].start()
         own = jnp.dot(pick, here, preferred_element_type=F32)
         residual_ref[0, :, pl.ds(first_column, columns)] = own[:2].astype(BF16)
-    for put in puts:
-        put.wait()
+    return puts
 
 
 def adjoint_like(n_pen, chunk, per_owner, table_ref, *rest):
@@ -171,17 +166,22 @@
     kept, tiles, (out_ref, residual_ref, made, out_sems) = rest[:chips], rest[chips:n_pen], rest[n_pen:]
     residual_ref[...] = jnp.zeros_like(residual_ref)
     blocks = [one.at[0] for one in kept]
-    adjoint(n_pen, chunk, per_owner, 0, table_ref, blocks, tiles, out_ref, residual_ref, made, out_sems)
-
-
-def adjoint_other(n_pen, chunk, per_owner, table_ref, begun_ref, part_ref, own_ref, far_ref, near_ref, tiles_ref,
-                  out_ref, residual_ref, made, out_sems):
+    for put in adjoint(n_pen, chunk, per_owner, 0, table_ref, blocks, tiles, out_ref, residual_ref, made, out_sems):
+        put.wait()
+
+
+def adjoint_other(n_pen, chunk, per_owner, table_ref, begun_ref, part_ref, own_ref, near_ref, far_ref, tiles_ref,
+                  out_ref, residual_ref, made, out_sems, whole, whole_sem):
     del begun_ref
     chips = n_pen // 2
-    residual_ref[...] = part_ref[...]
-    blocks = [own_ref, far_ref] + [near_ref.at[i] for i in range(chips - 2)]
+    whole[...] = part_ref[...]
+    blocks = [own_ref, near_ref.at[0]] + [far_ref.at[i] for i in range(chips - 2)]
     tiles = [tiles_ref.at[i] for i in range(chips)]
-    adjoint(n_pen, chunk, per_owner, 1, table_ref, blocks, tiles, out_ref, residual_ref, made, out_sems)
+    puts = adjoint(n_pen, chunk, per_owner, 1, table_ref, blocks, tiles, out_ref, whole, made, out_sems)
+    puts.append(pltpu.make_async_copy(whole, residual_ref, whole_sem))
+    puts[-1].start()
+    for put in puts:
+        put.wait()
 
 
 def body(spectrum, depth_weights, pair_tilt, pair_tile_within, tilt_pos, owner, measured):
@@ -234,7 +234,7 @@
         ],
         compiler_params=pltpu.CompilerParams(vmem_limit_bytes=62 << 20),
     )(owner, tilt_pos, pair_tilt, pair_tile_within, depth_weights, spectrum)
-    kept = [outs[0]] + [between(outs[i], distance(n_pen, 2 * i)) for i in range(1, chips)]
+    kept = [outs[0]] + [between(outs[i], 2 * i) for i in range(1, chips)]
 
     arrived = across(sent_sums, 1)
     step = 2
@@ -283,16 +283,16 @@
         )(*arrived, *after)
 
     own_swapped = between(outs[0][1], 1)
-    far_swapped = between(take_other(kept[1:2], [held]), 1).reshape(pair)
+    near_swapped = between(take_other(kept[1:2], [held]), 1)
     held = pl.pallas_call(
         join_tiles,
         out_shape=jax.ShapeDtypeStruct((2 * tiles, columns), BF16),
         in_specs=[VMEM, VMEM, ANY, ANY],
         out_specs=VMEM,
         compiler_params=pltpu.CompilerParams(vmem_limit_bytes=8 << 20),
-    )(held, across(held, step), own_swapped, far_swapped)
-    like = [held] + [between(held, distance(n_pen, 2 * i)) for i in range(1, chips)]
-    near_swapped = between(take_other(kept[2:], like[1:]), 1)
+    )(held, across(held, step), own_swapped, near_swapped)
+    like = [held] + [between(held, 2 * i) for i in range(1, chips)]
+    far_swapped = between(take_other(kept[2:], like[1:]), 1)
     stacked = pl.pallas_call(
         stack_tiles,
         out_shape=jax.ShapeDtypeStruct((chips, 2 * tiles, columns), BF16),
@@ -319,11 +319,11 @@
         call(adjoint_other, n_pen, chunk, per_owner),
         out_shape=shapes,
         in_specs=[VMEM, ANY] + [VMEM] * 5,
-        out_specs=[ANY, VMEM],
-        scratch_shapes=scratch,
+        out_specs=[ANY, ANY],
+        scratch_shapes=[*scratch, pltpu.VMEM(measured.shape, BF16), pltpu.SemaphoreType.DMA],
         input_output_aliases={1: 0},
         compiler_params=pltpu.CompilerParams(vmem_limit_bytes=16 << 20),
-    )(table, begun, part, own_swapped, far_swapped, near_swapped, other)
+    )(table, begun, part, own_swapped, near_swapped, far_swapped, other)
     return (updated, residual)
 
 

time: 45.9 us -> 45.6 us (level)
  Pallas kernels: 8.15 us -> 7.57 us
    pallas_call x1, Pallas kernels: 1.89 us -> 1.29 us  [body(): pl.pallas_call(call(adjoint_other, n_pen, chunk, per_owner), out_shape=sh...]
  transfers between devices with their start and end apart: 15 -> 15, of which waited for: 10 -> 7; matrix products, arithmetic and copies ran while one was open for 4% -> 4% of each run, Pallas kernels for 5% -> 5%
where the time goes in v10:
time: 45.6 us; the launch traced here: 45.3 us
  starting transfers between devices  20.3 us (45%)
  waiting for transfers between devices  14.1 us (31%)
  Pallas kernels  7.57 us (17%)
  local copies, waits for them, and re-layouts  1.66 us (4%)
  other arithmetic  0.85 us (2%)
  between operations  0.8 us (2%)
    ppermute x4, starting transfers between devices, across(): return lax.ppermute(value, 'kz', [(i, i ^ k) for i in range(n_kz)])  8.69 us
    ppermute x10, starting transfers between devices, between(): return lax.ppermute(value, 'pen', [(i, i ^ k) for i in range(n_pen)])  7.87 us
    ppermute x4, waiting for transfers between devices, across(): return lax.ppermute(value, 'kz', [(i, i ^ k) for i in range(n_kz)])  7.52 us
    ppermute x10, waiting for transfers between devices, between(): return lax.ppermute(value, 'pen', [(i, i ^ k) for i in range(n_pen)])  6.61 us
    pallas_call x1, Pallas kernels, body(): pl.pallas_call(call(order_and_forward, n_pen, n_kz, chunk, per_owner, til...  4.07 us
    all_to_all x1, starting transfers between devices, body(): got = lax.all_to_all(sent, 'pen', split_axis=0, concat_axis=0, tiled=True)  3.72 us
    pallas_call x1, Pallas kernels, body(): pl.pallas_call(call(adjoint_other, n_pen, chunk, per_owner), out_shape=sh...  1.29 us
    pallas_call x1, Pallas kernels, body(): pl.pallas_call(call(adjoint_like, n_pen, chunk, per_owner), out_shape=sha...  1.29 us
  transfers between devices with their start and end apart: 15, of which 7 were waited for; matrix products, arithmetic and copies ran while one was open for 4% of the time, Pallas kernels for 5%

profile of v10, /device:TPU:0, one launch (start us, length us, event | category | flops | bytes accessed | tf_op | source)
XLA Modules:
  0.0 45.3 jit_solution(5108376882014743280)
XLA Ops:
  0.6 0.0 copy-start.4
  0.6 0.0 copy-start.2
  0.7 0.0 copy-start.3
  0.7 0.0 copy-start.1
  0.7 4.1 %shard_map.86 = (bf16[2,2,2,64,512]{4,3,2,1,0:T(8,128)(2,1)}, bf16[2,2,2,64,512]{4,3,2,1,0:T(8,128)(2,1)}, bf16[2,2,2,64,512]{4,3,2,1,0:T(8,128)(2,1)}, bf16[2,2...) custom-call(s32[16]{0:T(128)} %refs_0_.1, s32[16]{0:T(128)} %refs_1_.3, ...), custom_call_target="tpu_custom_call" | custom-call | tf_op jit(solution)/shard_map/pallas_call | solution.py:213
  4.8 3.1 %collective-permute-start = (f32[2,16,512]{2,1,0:T(8,128)}, f32[2,16,512]{2,1,0:T(8,128)S(1)}, u32[]{:S(2)}, u32[]{:S(2)}) collective-permute-start(f32[2,16,512]{2,1,0:T(8,128)} %get-tuple-element.15), channel_id=1, source_target_pairs={{0,8},{8,0},{16,24},{24,16},{1,9},{9,1},{17,25},{25,17},{2,10},{10... | collective-permute-start | bytes 196616 | tf_op jit(solution)/shard_map/ppermute | solution.py:206
  7.8 3.7 %all-to-all-start = ((bf16[8,2,512]{2,1,0:T(2,128)(2,1)}), bf16[8,2,512]{2,1,0:T(2,128)(2,1)S(1)}, u32[]{:S(2)}, u32[]{:S(2)}) async-start(bf16[8,2,512]{2,1,0:T(2,128)(2,1)} %bitcast.5), calls=%async_computation | async-start | bytes 32768 | tf_op jit(solution)/shard_map/all_to_all | solution.py:247
  11.6 2.0 %collective-permute-start.2 = (bf16[2,2,2,64,512]{4,3,2,1,0:T(8,128)(2,1)}, bf16[2,2,2,64,512]{4,3,2,1,0:T(8,128)(2,1)S(1)}, u32[]{:S(2)}, u32[]{:S(2)}) collective-permute-start(bf16[2,2,2,64,512]{4,3,2,1,0:T(8,128)(2,1)} %get-tuple-element.18), channel_id=1, source_target_pairs={{0,2},{1,3},{2,0},{3,1},{4,6},{5,7},{6,4},{7,5},{8,10},{9,11},{10,... | collective-permute-start | bytes 1572872 | tf_op jit(solution)/shard_map/ppermute | solution.py:209
  13.6 1.5 %collective-permute-start.3 = (bf16[2,2,2,64,512]{4,3,2,1,0:T(8,128)(2,1)}, bf16[2,2,2,64,512]{4,3,2,1,0:T(8,128)(2,1)S(1)}, u32[]{:S(2)}, u32[]{:S(2)}) collective-permute-start(bf16[2,2,2,64,512]{4,3,2,1,0:T(8,128)(2,1)} %get-tuple-element.19), channel_id=1, source_target_pairs={{0,4},{1,5},{2,6},{3,7},{4,0},{5,1},{6,2},{7,3},{8,12},{9,13},{10,... | collective-permute-start | bytes 1572872 | tf_op jit(solution)/shard_map/ppermute | solution.py:209
  15.1 0.0 collective-permute-start.4
  15.1 0.0 collective-permute-done
  15.1 0.8 %add_bitcast_fusion = f32[1,2,16,512]{3,2,1,0:T(8,128)S(1)} fusion(f32[2,16,512]{2,1,0:T(8,128)} %get-tuple-element.14, f32[2,16,512]{2,1,0:T(8,128)S(1)} %collective-permute-done), kind=kLoop, calls=%fused_computation.1 | loop fusion | flops 16384 | bytes 196608 | tf_op jit(solution)/shard_map/reshape | solution.py:242
  16.0 2.7 %collective-permute-start.1 = (f32[1,16,512]{2,1,0:T(8,128)S(1)}, f32[1,16,512]{2,1,0:T(8,128)S(1)}, u32[]{:S(2)}, u32[]{:S(2)}) collective-permute-start(f32[1,16,512]{2,1,0:T(8,128)S(1)} %get-tuple-element.24), channel_id=1, source_target_pairs={{0,16},{8,24},{16,0},{24,8},{1,17},{9,25},{17,1},{25,9},{2,18},{10... | collective-permute-start | bytes 98312 | tf_op jit(solution)/shard_map/ppermute | solution.py:206
  18.6 1.0 %slice_bitcast_fusion = bf16[2,2,64,512]{3,2,1,0:T(8,128)(2,1)S(1)} fusion(bf16[2,2,2,64,512]{4,3,2,1,0:T(8,128)(2,1)} %get-tuple-element.17.refs_1_), kind=kLoop, calls=%fused_computation | loop fusion | bytes 524288 | tf_op jit(solution)/shard_map/squeeze | solution.py:285
  19.6 0.0 copy-start
  19.6 0.1 collective-permute-start.7
  19.7 0.0 all-to-all-done
  19.7 1.4 %collective-permute-done.1 = f32[1,16,512]{2,1,0:T(8,128)S(1)} collective-permute-done((f32[1,16,512]{2,1,0:T(8,128)S(1)}, f32[1,16,512]{2,1,0:T(8,128)S(1)}, u32[]{:S(2)}, u32[]{:S(2)}) %collective-permute-start.1) | collective-permute-done | bytes 32800 | tf_op jit(solution)/shard_map/ppermute | solution.py:206
  21.1 0.0 copy-done.4
  21.1 0.0 copy-done.2
  21.1 0.0 copy-done.3
  21.1 0.0 copy-done.1
  21.1 0.0 copy-start.5
  21.1 0.6 %copy-done.5 = s32[16]{0:T(128)S(1)} copy-done((s32[16]{0:T(128)S(1)}, s32[16]{0:T(128)}, u32[]{:S(2)}) %copy-start.5) | copy-done | bytes 88
  21.8 0.8 %shard_map.87 = (bf16[16,512]{1,0:T(8,128)(2,1)S(1)}, bf16[128,256]{1,0:T(8,128)(2,1)S(1)}) custom-call(s32[16]{0:T(128)S(1)} %copy-done.5, s32[16]{0:T(128)S(1)} %copy-done.4, s32[16,16]{1,0:T(8,128)S(1)} %copy-done.2, s32[16,16]{1,0:T(8,128)S(1)} %copy-done.3, bf16[16,16,64]{2,1,0:T(8,128)(2,1)S(1)} %copy-done.1, f32[16,512]{1,0:T(8,128)S(1)} %get-tuple-element.25.refs_5_, ...), custom_call_target="tpu_custom_call" | custom-call | tf_op jit(solution)/shard_map/pallas_call | solution.py:249
  22.6 0.3 collective-permute-start.5
  22.9 3.5 %collective-permute-done.5 = bf16[16,512]{1,0:T(8,128)(2,1)S(1)} collective-permute-done((bf16[16,512]{1,0:T(8,128)(2,1)S(1)}, bf16[16,512]{1,0:T(8,128)(2,1)S(1)}, u32[]{:S(2)}, u32[]{:S(2)}) %collective-permute-start.5) | collective-permute-done | bytes 16416 | tf_op jit(solution)/shard_map/ppermute | solution.py:206
  26.4 0.3 collective-permute-done.2.refs_0_.refs_2_
  26.7 0.1 collective-permute-start.8
  26.8 2.7 %collective-permute-start.6 = (bf16[32,512]{1,0:T(8,128)(2,1)S(1)}, bf16[32,512]{1,0:T(8,128)(2,1)S(1)}, u32[]{:S(2)}, u32[]{:S(2)}) collective-permute-start(bf16[32,512]{1,0:T(8,128)(2,1)S(1)} %constant_dynamic-update-slice_fusion.refs_1_.first_ref), channel_id=1, source_target_pairs={{0,16},{8,24},{16,0},{24,8},{1,17},{9,25},{17,1},{25,9},{2,18},{10... | collective-permute-start | bytes 98312 | tf_op jit(solution)/shard_map/ppermute | solution.py:206
  29.4 2.6 %collective-permute-done.6.second_ref = bf16[32,512]{1,0:T(8,128)(2,1)S(1)} collective-permute-done((bf16[32,512]{1,0:T(8,128)(2,1)S(1)}, bf16[32,512]{1,0:T(8,128)(2,1)S(1)}, u32[]{:S(2)}, u32[]{:S(2)}) %collective-permute-start.6) | collective-permute-done | bytes 32800 | tf_op jit(solution)/shard_map/ppermute | solution.py:206
  32.1 0.0 collective-permute-done.7.rest_0_.refs_3_
  32.1 0.0 collective-permute-done.8.rest_1_.refs_4_
  32.1 2.0 %collective-permute-start.9 = (bf16[64,512]{1,0:T(8,128)(2,1)S(1)}, bf16[64,512]{1,0:T(8,128)(2,1)S(1)}, u32[]{:S(2)}, u32[]{:S(2)}) collective-permute-start(bf16[64,512]{1,0:T(8,128)(2,1)S(1)} %shard_map.89.refs_5_.refs_0_), channel_id=1, source_target_pairs={{0,2},{1,3},{2,0},{3,1},{4,6},{5,7},{6,4},{7,5},{8,10},{9,11},{10,... | collective-permute-start | bytes 196616 | tf_op jit(solution)/shard_map/ppermute | solution.py:209
  34.1 1.5 %collective-permute-start.10 = (bf16[64,512]{1,0:T(8,128)(2,1)S(1)}, bf16[64,512]{1,0:T(8,128)(2,1)S(1)}, u32[]{:S(2)}, u32[]{:S(2)}) collective-permute-start(bf16[64,512]{1,0:T(8,128)(2,1)S(1)} %shard_map.89.refs_5_.refs_0_), channel_id=1, source_target_pairs={{0,4},{1,5},{2,6},{3,7},{4,0},{5,1},{6,2},{7,3},{8,12},{9,13},{10,... | collective-permute-start | bytes 196616 | tf_op jit(solution)/shard_map/ppermute | solution.py:209
  35.5 0.1 collective-permute-start.11
  35.7 4.3 %collective-permute-done.3.refs_3_.refs_0_ = bf16[2,2,2,64,512]{4,3,2,1,0:T(8,128)(2,1)S(1)} collective-permute-done((bf16[2,2,2,64,512]{4,3,2,1,0:T(8,128)(2,1)}, bf16[2,2,2,64,512]{4,3,2,1,0:T(8,128)(2,1)S(1)}, u32[]{:S(2)}, u32[]{:S(2)}) %collective-permute-start.3) | collective-permute-done | bytes 524320 | tf_op jit(solution)/shard_map/ppermute | solution.py:209
  40.0 0.0 collective-permute-done.4.refs_4_.refs_1_
  40.0 0.0 collective-permute-done.9.refs_6_.refs_2_.refs_1_
  40.0 1.6 %collective-permute-done.10.refs_7_.refs_3_.refs_2_ = bf16[64,512]{1,0:T(8,128)(2,1)S(1)} collective-permute-done((bf16[64,512]{1,0:T(8,128)(2,1)S(1)}, bf16[64,512]{1,0:T(8,128)(2,1)S(1)}, u32[]{:S(2)}, u32[]{:S(2)}) %collective-permute-start.10) | collective-permute-done | bytes 65568 | tf_op jit(solution)/shard_map/ppermute | solution.py:209
  41.6 0.0 collective-permute-done.11.refs_8_.refs_4_.refs_3_
  41.6 0.1 shard_map.91
  41.7 0.1 collective-permute-start.12
  41.8 0.5 %collective-permute-start.13 = (bf16[4,64,512]{2,1,0:T(8,128)(2,1)S(1)}, bf16[4,64,512]{2,1,0:T(8,128)(2,1)S(1)}, u32[]{:S(2)}, u32[]{:S(2)}) collective-permute-start(bf16[4,64,512]{2,1,0:T(8,128)(2,1)S(1)} %shard_map.92), channel_id=1, source_target_pairs={{0,1},{1,0},{2,3},{3,2},{4,5},{5,4},{6,7},{7,6},{8,9},{9,8},{10,11... | collective-permute-start | bytes 786440 | tf_op jit(solution)/shard_map/ppermute | solution.py:209
  42.3 1.3 %shard_map.90 = (bf16[2,2,64,4096]{3,2,1,0:T(8,128)(2,1)}, bf16[1,2,4096]{2,1,0:T(2,128)(2,1)S(1)}) custom-call(bf16[128,256]{1,0:T(8,128)(2,1)S(1)} %get-tuple-element.16.refs_0_, bf16[2,2,2,64,512]{4,3,2,1,0:T(8,128)(2,1)S(1)} %copy-done, bf16[2,2,2,64,512]{4,3,2,1,0:T(8,128)(2,1)S(1)} %collective-permute-done.2.refs_0_.refs_2_, ...), custom_call_target="tpu_custom_call" | custom-call | tf_op jit(solution)/shard_map/pallas_call | solution.py:310
  43.6 0.4 collective-permute-done.13.refs_6_
  44.0 0.0 collective-permute-done.12.refs_5_
  44.0 1.3 %shard_map.93 = (bf16[2,2,64,4096]{3,2,1,0:T(8,128)(2,1)}, bf16[1,2,4096]{2,1,0:T(2,128)(2,1)}) custom-call(bf16[128,256]{1,0:T(8,128)(2,1)S(1)} %get-tuple-element.16.refs_0_, bf16[2,2,64,4096]{3,2,1,0:T(8,128)(2,1)} %get-tuple-element.22.refs_1_, bf16[1,2,4096]{2,1,0:T(2,128)(2,1)S(1)} %get-tuple-element.23.refs_2_, ...), custom_call_target="tpu_custom_call", output_to_operand_aliasing={{0}: (1, {})} | custom-call | tf_op jit(solution)/shard_map/pallas_call | solution.py:318
  (8 shorter events, 0.1 us)
Async XLA Ops:
  0.6 20.5 %copy-start.4 = (s32[16]{0:T(128)S(1)}, s32[16]{0:T(128)}, u32[]{:S(2)}) copy-start(s32[16]{0:T(128)} %refs_1_.3) | copy-start | bytes 196
  0.6 20.5 %copy-start.2 = (s32[16,16]{1,0:T(8,128)S(1)}, s32[16,16]{1,0:T(8,128)}, u32[]{:S(2)}) copy-start(s32[16,16]{1,0:T(8,128)} %refs_2_.3) | copy-start | bytes 3076
  0.7 20.4 %copy-start.3 = (s32[16,16]{1,0:T(8,128)S(1)}, s32[16,16]{1,0:T(8,128)}, u32[]{:S(2)}) copy-start(s32[16,16]{1,0:T(8,128)} %refs_3_.3) | copy-start | bytes 3076
  0.7 20.4 %copy-start.1 = (bf16[16,16,64]{2,1,0:T(8,128)(2,1)S(1)}, bf16[16,16,64]{2,1,0:T(8,128)(2,1)}, u32[]{:S(2)}) copy-start(bf16[16,16,64]{2,1,0:T(8,128)(2,1)} %refs_4_.3) | copy-start | bytes 98308
  4.8 10.4 %collective-permute-start = (f32[2,16,512]{2,1,0:T(8,128)}, f32[2,16,512]{2,1,0:T(8,128)S(1)}, u32[]{:S(2)}, u32[]{:S(2)}) collective-permute-start(f32[2,16,512]{2,1,0:T(8,128)} %get-tuple-element.15), channel_id=1, source_target_pairs={{0,8},{8,0},{16,24},{24,16},{1,9},{9,1},{17,25},{25,17},{2,10},{10... | collective-permute-start | bytes 196616 | tf_op jit(solution)/shard_map/ppermute | solution.py:206
  7.8 11.8 %all-to-all-start = ((bf16[8,2,512]{2,1,0:T(2,128)(2,1)}), bf16[8,2,512]{2,1,0:T(2,128)(2,1)S(1)}, u32[]{:S(2)}, u32[]{:S(2)}) async-start(bf16[8,2,512]{2,1,0:T(2,128)(2,1)} %bitcast.5), calls=%async_computation | async-start | bytes 32768 | tf_op jit(solution)/shard_map/all_to_all | solution.py:247
  11.6 15.1 %collective-permute-start.2 = (bf16[2,2,2,64,512]{4,3,2,1,0:T(8,128)(2,1)}, bf16[2,2,2,64,512]{4,3,2,1,0:T(8,128)(2,1)S(1)}, u32[]{:S(2)}, u32[]{:S(2)}) collective-permute-start(bf16[2,2,2,64,512]{4,3,2,1,0:T(8,128)(2,1)} %get-tuple-element.18), channel_id=1, source_target_pairs={{0,2},{1,3},{2,0},{3,1},{4,6},{5,7},{6,4},{7,5},{8,10},{9,11},{10,... | collective-permute-start | bytes 1572872 | tf_op jit(solution)/shard_map/ppermute | solution.py:209
  13.6 26.4 %collective-permute-start.3 = (bf16[2,2,2,64,512]{4,3,2,1,0:T(8,128)(2,1)}, bf16[2,2,2,64,512]{4,3,2,1,0:T(8,128)(2,1)S(1)}, u32[]{:S(2)}, u32[]{:S(2)}) collective-permute-start(bf16[2,2,2,64,512]{4,3,2,1,0:T(8,128)(2,1)} %get-tuple-element.19), channel_id=1, source_target_pairs={{0,4},{1,5},{2,6},{3,7},{4,0},{5,1},{6,2},{7,3},{8,12},{9,13},{10,... | collective-permute-start | bytes 1572872 | tf_op jit(solution)/shard_map/ppermute | solution.py:209
  15.1 24.9 %collective-permute-start.4 = (bf16[2,2,2,64,512]{4,3,2,1,0:T(8,128)(2,1)}, bf16[2,2,2,64,512]{4,3,2,1,0:T(8,128)(2,1)S(1)}, u32[]{:S(2)}, u32[]{:S(2)}) collective-permute-start(bf16[2,2,2,64,512]{4,3,2,1,0:T(8,128)(2,1)} %get-tuple-element.20), channel_id=1, source_target_pairs={{0,6},{1,7},{2,4},{3,5},{4,2},{5,3},{6,0},{7,1},{8,14},{9,15},{10,... | collective-permute-start | bytes 1572872 | tf_op jit(solution)/shard_map/ppermute | solution.py:209
  16.0 5.1 %collective-permute-start.1 = (f32[1,16,512]{2,1,0:T(8,128)S(1)}, f32[1,16,512]{2,1,0:T(8,128)S(1)}, u32[]{:S(2)}, u32[]{:S(2)}) collective-permute-start(f32[1,16,512]{2,1,0:T(8,128)S(1)} %get-tuple-element.24), channel_id=1, source_target_pairs={{0,16},{8,24},{16,0},{24,8},{1,17},{9,25},{17,1},{25,9},{2,18},{10... | collective-permute-start | bytes 98312 | tf_op jit(solution)/shard_map/ppermute | solution.py:206
  19.6 22.7 %copy-start = (bf16[2,2,2,64,512]{4,3,2,1,0:T(8,128)(2,1)S(1)}, bf16[2,2,2,64,512]{4,3,2,1,0:T(8,128)(2,1)}, u32[]{:S(2)}) copy-start(bf16[2,2,2,64,512]{4,3,2,1,0:T(8,128)(2,1)} %get-tuple-element.17.refs_1_) | copy-start | bytes 1572868
  19.6 12.5 %collective-permute-start.7 = (bf16[2,2,64,512]{3,2,1,0:T(8,128)(2,1)S(1)}, bf16[2,2,64,512]{3,2,1,0:T(8,128)(2,1)S(1)}, u32[]{:S(2)}, u32[]{:S(2)}) collective-permute-start(bf16[2,2,64,512]{3,2,1,0:T(8,128)(2,1)S(1)} %slice_bitcast_fusion), channel_id=1, source_target_pairs={{0,1},{1,0},{2,3},{3,2},{4,5},{5,4},{6,7},{7,6},{8,9},{9,8},{10,11... | collective-permute-start | bytes 786440 | tf_op jit(solution)/shard_map/ppermute | solution.py:209
  21.1 0.7 %copy-start.5 = (s32[16]{0:T(128)S(1)}, s32[16]{0:T(128)}, u32[]{:S(2)}) copy-start(s32[16]{0:T(128)} %get-tuple-element.13.refs_0_) | copy-start | bytes 196
  22.6 3.8 %collective-permute-start.5 = (bf16[16,512]{1,0:T(8,128)(2,1)S(1)}, bf16[16,512]{1,0:T(8,128)(2,1)S(1)}, u32[]{:S(2)}, u32[]{:S(2)}) collective-permute-start(bf16[16,512]{1,0:T(8,128)(2,1)S(1)} %get-tuple-element.21), channel_id=1, source_target_pairs={{0,8},{8,0},{16,24},{24,16},{1,9},{9,1},{17,25},{25,17},{2,10},{10... | collective-permute-start | bytes 49160 | tf_op jit(solution)/shard_map/ppermute | solution.py:206
  26.7 5.4 %collective-permute-start.8 = (bf16[1,2,2,64,512]{4,3,2,1,0:T(8,128)(2,1)S(1)}, bf16[1,2,2,64,512]{4,3,2,1,0:T(8,128)(2,1)S(1)}, u32[]{:S(2)}, u32[]{:S(2)}) collective-permute-start(bf16[1,2,2,64,512]{4,3,2,1,0:T(8,128)(2,1)S(1)} %shard_map.88), channel_id=1, source_target_pairs={{0,1},{1,0},{2,3},{3,2},{4,5},{5,4},{6,7},{7,6},{8,9},{9,8},{10,11... | collective-permute-start | bytes 786440 | tf_op jit(solution)/shard_map/ppermute | solution.py:209
  26.8 5.3 %collective-permute-start.6 = (bf16[32,512]{1,0:T(8,128)(2,1)S(1)}, bf16[32,512]{1,0:T(8,128)(2,1)S(1)}, u32[]{:S(2)}, u32[]{:S(2)}) collective-permute-start(bf16[32,512]{1,0:T(8,128)(2,1)S(1)} %constant_dynamic-update-slice_fusion.refs_1_.first_ref), channel_id=1, source_target_pairs={{0,16},{8,24},{16,0},{24,8},{1,17},{9,25},{17,1},{25,9},{2,18},{10... | collective-permute-start | bytes 98312 | tf_op jit(solution)/shard_map/ppermute | solution.py:206
  32.1 7.9 %collective-permute-start.9 = (bf16[64,512]{1,0:T(8,128)(2,1)S(1)}, bf16[64,512]{1,0:T(8,128)(2,1)S(1)}, u32[]{:S(2)}, u32[]{:S(2)}) collective-permute-start(bf16[64,512]{1,0:T(8,128)(2,1)S(1)} %shard_map.89.refs_5_.refs_0_), channel_id=1, source_target_pairs={{0,2},{1,3},{2,0},{3,1},{4,6},{5,7},{6,4},{7,5},{8,10},{9,11},{10,... | collective-permute-start | bytes 196616 | tf_op jit(solution)/shard_map/ppermute | solution.py:209
  34.1 7.5 %collective-permute-start.10 = (bf16[64,512]{1,0:T(8,128)(2,1)S(1)}, bf16[64,512]{1,0:T(8,128)(2,1)S(1)}, u32[]{:S(2)}, u32[]{:S(2)}) collective-permute-start(bf16[64,512]{1,0:T(8,128)(2,1)S(1)} %shard_map.89.refs_5_.refs_0_), channel_id=1, source_target_pairs={{0,4},{1,5},{2,6},{3,7},{4,0},{5,1},{6,2},{7,3},{8,12},{9,13},{10,... | collective-permute-start | bytes 196616 | tf_op jit(solution)/shard_map/ppermute | solution.py:209
  35.5 6.1 %collective-permute-start.11 = (bf16[64,512]{1,0:T(8,128)(2,1)S(1)}, bf16[64,512]{1,0:T(8,128)(2,1)S(1)}, u32[]{:S(2)}, u32[]{:S(2)}) collective-permute-start(bf16[64,512]{1,0:T(8,128)(2,1)S(1)} %shard_map.89.refs_5_.refs_0_), channel_id=1, source_target_pairs={{0,6},{1,7},{2,4},{3,5},{4,2},{5,3},{6,0},{7,1},{8,14},{9,15},{10,... | collective-permute-start | bytes 196616 | tf_op jit(solution)/shard_map/ppermute | solution.py:209
  41.7 2.4 %collective-permute-start.12 = (bf16[2,2,2,64,512]{4,3,2,1,0:T(8,128)(2,1)S(1)}, bf16[2,2,2,64,512]{4,3,2,1,0:T(8,128)(2,1)S(1)}, u32[]{:S(2)}, u32[]{:S(2)}) collective-permute-start(bf16[2,2,2,64,512]{4,3,2,1,0:T(8,128)(2,1)S(1)} %shard_map.91), channel_id=1, source_target_pairs={{0,1},{1,0},{2,3},{3,2},{4,5},{5,4},{6,7},{7,6},{8,9},{9,8},{10,11... | collective-permute-start | bytes 1572872 | tf_op jit(solution)/shard_map/ppermute | solution.py:209
  41.8 2.2 %collective-permute-start.13 = (bf16[4,64,512]{2,1,0:T(8,128)(2,1)S(1)}, bf16[4,64,512]{2,1,0:T(8,128)(2,1)S(1)}, u32[]{:S(2)}, u32[]{:S(2)}) collective-permute-start(bf16[4,64,512]{2,1,0:T(8,128)(2,1)S(1)} %shard_map.92), channel_id=1, source_target_pairs={{0,1},{1,0},{2,3},{3,2},{4,5},{5,4},{6,7},{7,6},{8,9},{9,8},{10,11... | collective-permute-start | bytes 786440 | tf_op jit(solution)/shard_map/ppermute | solution.py:209

commit v11 on v10

--- a/solution.py
+++ b/solution.py
@@ -61,11 +61,11 @@
         hi, lo = split_hi_lo(jnp.dot(hot, weights[b], preferred_element_type=F32))
         table[:tiles, b * depth : (b + 1) * depth] = hi
         table[tiles:, b * depth : (b + 1) * depth] = lo
-    for get in gets:
-        get.wait()
     for q in range(n_pen):
         for r in range(per_owner):
-            from_ref = held.at[inverse_ref[(pen ^ q) * per_owner + r]]
+            b = inverse_ref[(pen ^ q) * per_owner + r]
+            from_ref = held.at[b]
+            pltpu.make_async_copy(spectrum_ref.at[b], from_ref, in_sems.at[b]).wait()
             puts.append(pltpu.make_async_copy(from_ref, outs[q // 2].at[q % 2, r], out_sems.at[q, r]))
             puts[-1].start()
     for c in range(2):
@@ -87,8 +87,16 @@
 
 
 def residual_and_table(n_kz, chunk, per_owner, tiles_per_tilt, inverse_ref, tilt_pos_ref, tilt_ref, within_ref,
-                       weights_ref, sums_ref, arrived_ref, measured_ref, own_ref, out_ref, slot_ref):
-    own_ref[...] = (sums_ref[...] + arrived_ref[...] - measured_ref[...].astype(F32)).astype(BF16)
+                       weights_ref, sums_ref, arrived_ref, got_ref, swapped_ref, own_ref, out_ref, slot_ref, measured):
+    core = lax.axis_index("pen") & 1
+    for i in range(got_ref.shape[0]):
+        mine, theirs = got_ref[i, core].astype(F32), swapped_ref[i, core].astype(F32)
+        first, second = jnp.where(core == 0, mine, theirs), jnp.where(core == 0, theirs, mine)
+        for c in range(2):
+            row = c * chunk + 2 * i
+            measured[row : row + 1, :] = first[c : c + 1]
+            measured[row + 1 : row + 2, :] = second[c : c + 1]
+    own_ref[...] = (sums_ref[...] + arrived_ref[...] - measured[...]).astype(BF16)
     pairs, depth = weights_ref.shape[1:]
     rows_all = n_kz * 2 * chunk
     flip = lax.axis_index("kz") * chunk
@@ -244,17 +252,19 @@
         step *= 2
 
     sent = measured.reshape(2, n_pen, columns).transpose(1, 0, 2)
-    got = lax.all_to_all(sent, "pen", split_axis=0, concat_axis=0, tiled=True)
-    measured_rows = got.transpose(1, 0, 2).reshape(2 * chunk, columns)
+    cores = [[2 * i + core for i in range(chips)] for core in range(2)]
+    got = lax.all_to_all(sent, "pen", split_axis=0, concat_axis=0, tiled=True, axis_index_groups=cores)
+    got = got.reshape(chips, 2, 2, columns)
+    got_swapped = between(got, 1)
     own, table = pl.pallas_call(
         call(residual_and_table, n_kz, chunk, per_owner, tiles_per_tilt),
         out_shape=[
             jax.ShapeDtypeStruct((2 * chunk, columns), BF16),
             jax.ShapeDtypeStruct((4 * tiles, 2 * per_owner * depth), BF16),
         ],
-        in_specs=[SMEM, SMEM] + [VMEM] * 6,
+        in_specs=[SMEM, SMEM] + [VMEM] * 7,
         out_specs=[VMEM, VMEM],
-        scratch_shapes=[pltpu.VMEM((blocks, pairs), I32)],
+        scratch_shapes=[pltpu.VMEM((blocks, pairs), I32), pltpu.VMEM((2 * chunk, columns), F32)],
         compiler_params=pltpu.CompilerParams(vmem_limit_bytes=8 << 20),
     )(
         inverse,
@@ -264,7 +274,8 @@
         depth_weights,
         sums.reshape(2 * chunk, columns),
         arrived.reshape(2 * chunk, columns),
-        measured_rows,
+        got,
+        got_swapped,
     )
 
     held = own

time: 45.6 us -> 44.8 us (0.982)
  starting transfers between devices: 20.3 us -> 19.8 us
    ppermute x10 -> x11, waiting for transfers between devices: 6.61 us -> 4.56 us  [between(): return lax.ppermute(value, 'pen', [(i, i ^ k) for i in range(n_pen)])]
    all_to_all x1, waiting for transfers between devices: 0.01 us -> 1.3 us  [body(): lax.all_to_all(sent, 'pen', split_axis=0, concat_axis=0, tiled=True, axis...]
    ppermute x4, starting transfers between devices: 8.69 us -> 7.99 us  [across(): return lax.ppermute(value, 'kz', [(i, i ^ k) for i in range(n_kz)])]
    ppermute x10 -> x11, starting transfers between devices: 7.87 us -> 8.06 us  [between(): return lax.ppermute(value, 'pen', [(i, i ^ k) for i in range(n_pen)])]
  transfers between devices with their start and end apart: 15 -> 16, of which waited for: 7 -> 8; matrix products, arithmetic and copies ran while one was open for 4% -> 4% of each run, Pallas kernels for 5% -> 5%
where the time goes in v11:
time: 44.8 us; the launch traced here: 44.5 us
  starting transfers between devices  19.8 us (44%)
  waiting for transfers between devices  13.8 us (31%)
  Pallas kernels  7.54 us (17%)
  local copies, waits for them, and re-layouts  1.65 us (4%)
  other arithmetic  0.85 us (2%)
  between operations  0.81 us (2%)
    ppermute x11, starting transfers between devices, between(): return lax.ppermute(value, 'pen', [(i, i ^ k) for i in range(n_pen)])  8.06 us
    ppermute x4, starting transfers between devices, across(): return lax.ppermute(value, 'kz', [(i, i ^ k) for i in range(n_kz)])  7.99 us
    ppermute x4, waiting for transfers between devices, across(): return lax.ppermute(value, 'kz', [(i, i ^ k) for i in range(n_kz)])  7.98 us
    ppermute x11, waiting for transfers between devices, between(): return lax.ppermute(value, 'pen', [(i, i ^ k) for i in range(n_pen)])  4.56 us
    pallas_call x1, Pallas kernels, body(): pl.pallas_call(call(order_and_forward, n_pen, n_kz, chunk, per_owner, til...  4.04 us
    all_to_all x1, starting transfers between devices, body(): lax.all_to_all(sent, 'pen', split_axis=0, concat_axis=0, tiled=True, axis...  3.72 us
    all_to_all x1, waiting for transfers between devices, body(): lax.all_to_all(sent, 'pen', split_axis=0, concat_axis=0, tiled=True, axis...  1.3 us
    pallas_call x1, Pallas kernels, body(): pl.pallas_call(call(adjoint_other, n_pen, chunk, per_owner), out_shape=sh...  1.29 us
  transfers between devices with their start and end apart: 16, of which 8 were waited for; matrix products, arithmetic and copies ran while one was open for 4% of the time, Pallas kernels for 5%

profile of v11, /device:TPU:0, one launch (start us, length us, event | category | flops | bytes accessed | tf_op | source)
XLA Modules:
  0.0 44.5 jit_solution(11564038787926093161)
XLA Ops:
  0.6 0.0 copy-start.4
  0.6 0.0 copy-start.2
  0.7 0.0 copy-start.3
  0.7 0.0 copy-start.1
  0.7 4.0 %shard_map.86 = (bf16[2,2,2,64,512]{4,3,2,1,0:T(8,128)(2,1)}, bf16[2,2,2,64,512]{4,3,2,1,0:T(8,128)(2,1)}, bf16[2,2,2,64,512]{4,3,2,1,0:T(8,128)(2,1)}, bf16[2,2...) custom-call(s32[16]{0:T(128)} %refs_0_.1, s32[16]{0:T(128)} %refs_1_.3, ...), custom_call_target="tpu_custom_call" | custom-call | tf_op jit(solution)/shard_map/pallas_call | solution.py:221
  4.7 3.1 %collective-permute-start = (f32[2,16,512]{2,1,0:T(8,128)}, f32[2,16,512]{2,1,0:T(8,128)S(1)}, u32[]{:S(2)}, u32[]{:S(2)}) collective-permute-start(f32[2,16,512]{2,1,0:T(8,128)} %get-tuple-element.15), channel_id=1, source_target_pairs={{0,8},{8,0},{16,24},{24,16},{1,9},{9,1},{17,25},{25,17},{2,10},{10... | collective-permute-start | bytes 196616 | tf_op jit(solution)/shard_map/ppermute | solution.py:214
  7.8 3.7 %all-to-all-start = ((bf16[8,2,512]{2,1,0:T(2,128)(2,1)}), bf16[8,2,512]{2,1,0:T(2,128)(2,1)S(1)}, u32[]{:S(2)}, u32[]{:S(2)}) async-start(bf16[8,2,512]{2,1,0:T(2,128)(2,1)} %bitcast.5), calls=%async_computation | async-start | bytes 32768 | tf_op jit(solution)/shard_map/all_to_all | solution.py:256
  11.5 2.0 %collective-permute-start.3 = (bf16[2,2,2,64,512]{4,3,2,1,0:T(8,128)(2,1)}, bf16[2,2,2,64,512]{4,3,2,1,0:T(8,128)(2,1)S(1)}, u32[]{:S(2)}, u32[]{:S(2)}) collective-permute-start(bf16[2,2,2,64,512]{4,3,2,1,0:T(8,128)(2,1)} %get-tuple-element.18), channel_id=1, source_target_pairs={{0,2},{1,3},{2,0},{3,1},{4,6},{5,7},{6,4},{7,5},{8,10},{9,11},{10,... | collective-permute-start | bytes 1572872 | tf_op jit(solution)/shard_map/ppermute | solution.py:217
  13.5 1.5 %collective-permute-start.4 = (bf16[2,2,2,64,512]{4,3,2,1,0:T(8,128)(2,1)}, bf16[2,2,2,64,512]{4,3,2,1,0:T(8,128)(2,1)S(1)}, u32[]{:S(2)}, u32[]{:S(2)}) collective-permute-start(bf16[2,2,2,64,512]{4,3,2,1,0:T(8,128)(2,1)} %get-tuple-element.19), channel_id=1, source_target_pairs={{0,4},{1,5},{2,6},{3,7},{4,0},{5,1},{6,2},{7,3},{8,12},{9,13},{10,... | collective-permute-start | bytes 1572872 | tf_op jit(solution)/shard_map/ppermute | solution.py:217
  15.0 0.0 collective-permute-start.5
  15.0 1.3 %all-to-all-done = bf16[8,2,512]{2,1,0:T(2,128)(2,1)S(1)} async-done(((bf16[8,2,512]{2,1,0:T(2,128)(2,1)}), bf16[8,2,512]{2,1,0:T(2,128)(2,1)S(1)}, u32[]{:S(2)}, u32[]{:S(2)}) %all-to-all-start) | async-done | bytes 16416 | tf_op jit(solution)/shard_map/all_to_all | solution.py:256
  16.3 0.0 collective-permute-start.2
  16.3 0.0 collective-permute-done
  16.3 0.9 %add_bitcast_fusion = f32[1,2,16,512]{3,2,1,0:T(8,128)S(1)} fusion(f32[2,16,512]{2,1,0:T(8,128)} %get-tuple-element.14, f32[2,16,512]{2,1,0:T(8,128)S(1)} %collective-permute-done), kind=kLoop, calls=%fused_computation.1 | loop fusion | flops 16384 | bytes 196608 | tf_op jit(solution)/shard_map/reshape | solution.py:250
  17.2 2.7 %collective-permute-start.1 = (f32[1,16,512]{2,1,0:T(8,128)S(1)}, f32[1,16,512]{2,1,0:T(8,128)S(1)}, u32[]{:S(2)}, u32[]{:S(2)}) collective-permute-start(f32[1,16,512]{2,1,0:T(8,128)S(1)} %get-tuple-element.24), channel_id=1, source_target_pairs={{0,16},{8,24},{16,0},{24,8},{1,17},{9,25},{17,1},{25,9},{2,18},{10... | collective-permute-start | bytes 98312 | tf_op jit(solution)/shard_map/ppermute | solution.py:214
  19.9 1.0 %slice_bitcast_fusion = bf16[2,2,64,512]{3,2,1,0:T(8,128)(2,1)S(1)} fusion(bf16[2,2,2,64,512]{4,3,2,1,0:T(8,128)(2,1)} %get-tuple-element.17.refs_1_), kind=kLoop, calls=%fused_computation | loop fusion | bytes 524288 | tf_op jit(solution)/shard_map/squeeze | solution.py:296
  20.8 0.0 copy-start
  20.9 0.0 collective-permute-done.2.refs_8_
  20.9 0.3 collective-permute-start.8
  21.2 1.4 %collective-permute-done.1 = f32[1,16,512]{2,1,0:T(8,128)S(1)} collective-permute-done((f32[1,16,512]{2,1,0:T(8,128)S(1)}, f32[1,16,512]{2,1,0:T(8,128)S(1)}, u32[]{:S(2)}, u32[]{:S(2)}) %collective-permute-start.1) | collective-permute-done | bytes 32800 | tf_op jit(solution)/shard_map/ppermute | solution.py:214
  22.6 0.0 copy-done.4
  22.6 0.0 copy-done.3
  22.6 0.0 copy-start.5
  22.6 0.6 %copy-done.5 = s32[16]{0:T(128)S(1)} copy-done((s32[16]{0:T(128)S(1)}, s32[16]{0:T(128)}, u32[]{:S(2)}) %copy-start.5) | copy-done | bytes 88
  23.2 0.8 %shard_map.87 = (bf16[16,512]{1,0:T(8,128)(2,1)S(1)}, bf16[128,256]{1,0:T(8,128)(2,1)S(1)}) custom-call(s32[16]{0:T(128)S(1)} %copy-done.5, s32[16]{0:T(128)S(1)} %copy-done.4, s32[16,16]{1,0:T(8,128)S(1)} %copy-done.2, s32[16,16]{1,0:T(8,128)S(1)} %copy-done.3, bf16[16,16,64]{2,1,0:T(8,128)(2,1)S(1)} %copy-done.1, f32[16,512]{1,0:T(8,128)S(1)} %get-tuple-element.25.refs_5_, ...), custom_call_target="tpu_custom_call" | custom-call | tf_op jit(solution)/shard_map/pallas_call | solution.py:259
  24.1 0.1 collective-permute-start.6
  24.2 3.7 %collective-permute-done.6 = bf16[16,512]{1,0:T(8,128)(2,1)S(1)} collective-permute-done((bf16[16,512]{1,0:T(8,128)(2,1)S(1)}, bf16[16,512]{1,0:T(8,128)(2,1)S(1)}, u32[]{:S(2)}, u32[]{:S(2)}) %collective-permute-start.6) | collective-permute-done | bytes 16416 | tf_op jit(solution)/shard_map/ppermute | solution.py:214
  27.9 0.0 collective-permute-done.3.refs_0_.refs_2_
  27.9 0.1 collective-permute-start.9
  28.0 2.2 %collective-permute-start.7 = (bf16[32,512]{1,0:T(8,128)(2,1)S(1)}, bf16[32,512]{1,0:T(8,128)(2,1)S(1)}, u32[]{:S(2)}, u32[]{:S(2)}) collective-permute-start(bf16[32,512]{1,0:T(8,128)(2,1)S(1)} %constant_dynamic-update-slice_fusion.refs_1_.first_ref), channel_id=1, source_target_pairs={{0,16},{8,24},{16,0},{24,8},{1,17},{9,25},{17,1},{25,9},{2,18},{10... | collective-permute-start | bytes 98312 | tf_op jit(solution)/shard_map/ppermute | solution.py:214
  30.2 2.8 %collective-permute-done.7.second_ref = bf16[32,512]{1,0:T(8,128)(2,1)S(1)} collective-permute-done((bf16[32,512]{1,0:T(8,128)(2,1)S(1)}, bf16[32,512]{1,0:T(8,128)(2,1)S(1)}, u32[]{:S(2)}, u32[]{:S(2)}) %collective-permute-start.7) | collective-permute-done | bytes 32800 | tf_op jit(solution)/shard_map/ppermute | solution.py:214
  33.0 0.0 collective-permute-done.8.rest_0_.refs_3_
  33.0 0.0 collective-permute-done.9.rest_1_.refs_4_
  33.0 1.1 %collective-permute-start.10 = (bf16[64,512]{1,0:T(8,128)(2,1)S(1)}, bf16[64,512]{1,0:T(8,128)(2,1)S(1)}, u32[]{:S(2)}, u32[]{:S(2)}) collective-permute-start(bf16[64,512]{1,0:T(8,128)(2,1)S(1)} %shard_map.89.refs_5_.refs_0_), channel_id=1, source_target_pairs={{0,2},{1,3},{2,0},{3,1},{4,6},{5,7},{6,4},{7,5},{8,10},{9,11},{10,... | collective-permute-start | bytes 196616 | tf_op jit(solution)/shard_map/ppermute | solution.py:217
  34.1 1.5 %collective-permute-start.11 = (bf16[64,512]{1,0:T(8,128)(2,1)S(1)}, bf16[64,512]{1,0:T(8,128)(2,1)S(1)}, u32[]{:S(2)}, u32[]{:S(2)}) collective-permute-start(bf16[64,512]{1,0:T(8,128)(2,1)S(1)} %shard_map.89.refs_5_.refs_0_), channel_id=1, source_target_pairs={{0,4},{1,5},{2,6},{3,7},{4,0},{5,1},{6,2},{7,3},{8,12},{9,13},{10,... | collective-permute-start | bytes 196616 | tf_op jit(solution)/shard_map/ppermute | solution.py:217
  35.6 1.0 %collective-permute-start.12 = (bf16[64,512]{1,0:T(8,128)(2,1)S(1)}, bf16[64,512]{1,0:T(8,128)(2,1)S(1)}, u32[]{:S(2)}, u32[]{:S(2)}) collective-permute-start(bf16[64,512]{1,0:T(8,128)(2,1)S(1)} %shard_map.89.refs_5_.refs_0_), channel_id=1, source_target_pairs={{0,6},{1,7},{2,4},{3,5},{4,2},{5,3},{6,0},{7,1},{8,14},{9,15},{10,... | collective-permute-start | bytes 196616 | tf_op jit(solution)/shard_map/ppermute | solution.py:217
  36.6 1.5 %collective-permute-done.4.refs_3_.refs_0_ = bf16[2,2,2,64,512]{4,3,2,1,0:T(8,128)(2,1)S(1)} collective-permute-done((bf16[2,2,2,64,512]{4,3,2,1,0:T(8,128)(2,1)}, bf16[2,2,2,64,512]{4,3,2,1,0:T(8,128)(2,1)S(1)}, u32[]{:S(2)}, u32[]{:S(2)}) %collective-permute-start.4) | collective-permute-done | bytes 524320 | tf_op jit(solution)/shard_map/ppermute | solution.py:217
  38.1 0.0 collective-permute-done.5.refs_4_.refs_1_
  38.1 0.0 collective-permute-done.10.refs_6_.refs_2_.refs_1_
  38.2 1.6 %collective-permute-done.11.refs_7_.refs_3_.refs_2_ = bf16[64,512]{1,0:T(8,128)(2,1)S(1)} collective-permute-done((bf16[64,512]{1,0:T(8,128)(2,1)S(1)}, bf16[64,512]{1,0:T(8,128)(2,1)S(1)}, u32[]{:S(2)}, u32[]{:S(2)}) %collective-permute-start.11) | collective-permute-done | bytes 65568 | tf_op jit(solution)/shard_map/ppermute | solution.py:217
  39.7 1.0 %collective-permute-done.12.refs_8_.refs_4_.refs_3_ = bf16[64,512]{1,0:T(8,128)(2,1)S(1)} collective-permute-done((bf16[64,512]{1,0:T(8,128)(2,1)S(1)}, bf16[64,512]{1,0:T(8,128)(2,1)S(1)}, u32[]{:S(2)}, u32[]{:S(2)}) %collective-permute-start.12) | collective-permute-done | bytes 65568 | tf_op jit(solution)/shard_map/ppermute | solution.py:217
  40.7 0.1 shard_map.91
  40.8 0.1 collective-permute-start.13
  40.9 0.6 %collective-permute-start.14 = (bf16[4,64,512]{2,1,0:T(8,128)(2,1)S(1)}, bf16[4,64,512]{2,1,0:T(8,128)(2,1)S(1)}, u32[]{:S(2)}, u32[]{:S(2)}) collective-permute-start(bf16[4,64,512]{2,1,0:T(8,128)(2,1)S(1)} %shard_map.92), channel_id=1, source_target_pairs={{0,1},{1,0},{2,3},{3,2},{4,5},{5,4},{6,7},{7,6},{8,9},{9,8},{10,11... | collective-permute-start | bytes 786440 | tf_op jit(solution)/shard_map/ppermute | solution.py:217
  41.5 1.3 %shard_map.90 = (bf16[2,2,64,4096]{3,2,1,0:T(8,128)(2,1)}, bf16[1,2,4096]{2,1,0:T(2,128)(2,1)S(1)}) custom-call(bf16[128,256]{1,0:T(8,128)(2,1)S(1)} %get-tuple-element.16.refs_0_, bf16[2,2,2,64,512]{4,3,2,1,0:T(8,128)(2,1)S(1)} %copy-done, bf16[2,2,2,64,512]{4,3,2,1,0:T(8,128)(2,1)S(1)} %collective-permute-done.3.refs_0_.refs_2_, ...), custom_call_target="tpu_custom_call" | custom-call | tf_op jit(solution)/shard_map/pallas_call | solution.py:321
  42.8 0.4 collective-permute-done.14.refs_6_
  43.2 0.0 collective-permute-done.13.refs_5_
  43.2 1.3 %shard_map.93 = (bf16[2,2,64,4096]{3,2,1,0:T(8,128)(2,1)}, bf16[1,2,4096]{2,1,0:T(2,128)(2,1)}) custom-call(bf16[128,256]{1,0:T(8,128)(2,1)S(1)} %get-tuple-element.16.refs_0_, bf16[2,2,64,4096]{3,2,1,0:T(8,128)(2,1)} %get-tuple-element.22.refs_1_, bf16[1,2,4096]{2,1,0:T(2,128)(2,1)S(1)} %get-tuple-element.23.refs_2_, ...), custom_call_target="tpu_custom_call", output_to_operand_aliasing={{0}: (1, {})} | custom-call | tf_op jit(solution)/shard_map/pallas_call | solution.py:329
  (9 shorter events, 0.1 us)
Async XLA Ops:
  0.6 21.9 %copy-start.4 = (s32[16]{0:T(128)S(1)}, s32[16]{0:T(128)}, u32[]{:S(2)}) copy-start(s32[16]{0:T(128)} %refs_1_.3) | copy-start | bytes 196
  0.6 21.9 %copy-start.2 = (s32[16,16]{1,0:T(8,128)S(1)}, s32[16,16]{1,0:T(8,128)}, u32[]{:S(2)}) copy-start(s32[16,16]{1,0:T(8,128)} %refs_2_.3) | copy-start | bytes 3076
  0.7 21.9 %copy-start.3 = (s32[16,16]{1,0:T(8,128)S(1)}, s32[16,16]{1,0:T(8,128)}, u32[]{:S(2)}) copy-start(s32[16,16]{1,0:T(8,128)} %refs_3_.3) | copy-start | bytes 3076
  0.7 21.9 %copy-start.1 = (bf16[16,16,64]{2,1,0:T(8,128)(2,1)S(1)}, bf16[16,16,64]{2,1,0:T(8,128)(2,1)}, u32[]{:S(2)}) copy-start(bf16[16,16,64]{2,1,0:T(8,128)(2,1)} %refs_4_.3) | copy-start | bytes 98308
  4.7 11.6 %collective-permute-start = (f32[2,16,512]{2,1,0:T(8,128)}, f32[2,16,512]{2,1,0:T(8,128)S(1)}, u32[]{:S(2)}, u32[]{:S(2)}) collective-permute-start(f32[2,16,512]{2,1,0:T(8,128)} %get-tuple-element.15), channel_id=1, source_target_pairs={{0,8},{8,0},{16,24},{24,16},{1,9},{9,1},{17,25},{25,17},{2,10},{10... | collective-permute-start | bytes 196616 | tf_op jit(solution)/shard_map/ppermute | solution.py:214
  7.8 8.5 %all-to-all-start = ((bf16[8,2,512]{2,1,0:T(2,128)(2,1)}), bf16[8,2,512]{2,1,0:T(2,128)(2,1)S(1)}, u32[]{:S(2)}, u32[]{:S(2)}) async-start(bf16[8,2,512]{2,1,0:T(2,128)(2,1)} %bitcast.5), calls=%async_computation | async-start | bytes 32768 | tf_op jit(solution)/shard_map/all_to_all | solution.py:256
  11.5 16.4 %collective-permute-start.3 = (bf16[2,2,2,64,512]{4,3,2,1,0:T(8,128)(2,1)}, bf16[2,2,2,64,512]{4,3,2,1,0:T(8,128)(2,1)S(1)}, u32[]{:S(2)}, u32[]{:S(2)}) collective-permute-start(bf16[2,2,2,64,512]{4,3,2,1,0:T(8,128)(2,1)} %get-tuple-element.18), channel_id=1, source_target_pairs={{0,2},{1,3},{2,0},{3,1},{4,6},{5,7},{6,4},{7,5},{8,10},{9,11},{10,... | collective-permute-start | bytes 1572872 | tf_op jit(solution)/shard_map/ppermute | solution.py:217
  13.5 24.6 %collective-permute-start.4 = (bf16[2,2,2,64,512]{4,3,2,1,0:T(8,128)(2,1)}, bf16[2,2,2,64,512]{4,3,2,1,0:T(8,128)(2,1)S(1)}, u32[]{:S(2)}, u32[]{:S(2)}) collective-permute-start(bf16[2,2,2,64,512]{4,3,2,1,0:T(8,128)(2,1)} %get-tuple-element.19), channel_id=1, source_target_pairs={{0,4},{1,5},{2,6},{3,7},{4,0},{5,1},{6,2},{7,3},{8,12},{9,13},{10,... | collective-permute-start | bytes 1572872 | tf_op jit(solution)/shard_map/ppermute | solution.py:217
  15.0 23.1 %collective-permute-start.5 = (bf16[2,2,2,64,512]{4,3,2,1,0:T(8,128)(2,1)}, bf16[2,2,2,64,512]{4,3,2,1,0:T(8,128)(2,1)S(1)}, u32[]{:S(2)}, u32[]{:S(2)}) collective-permute-start(bf16[2,2,2,64,512]{4,3,2,1,0:T(8,128)(2,1)} %get-tuple-element.20), channel_id=1, source_target_pairs={{0,6},{1,7},{2,4},{3,5},{4,2},{5,3},{6,0},{7,1},{8,14},{9,15},{10,... | collective-permute-start | bytes 1572872 | tf_op jit(solution)/shard_map/ppermute | solution.py:217
  16.3 4.5 %collective-permute-start.2 = (bf16[4,2,2,512]{3,2,1,0:T(2,128)(2,1)S(1)}, bf16[4,2,2,512]{3,2,1,0:T(2,128)(2,1)S(1)}, u32[]{:S(2)}, u32[]{:S(2)}) collective-permute-start(bf16[4,2,2,512]{3,2,1,0:T(2,128)(2,1)S(1)} %bitcast.13), channel_id=1, source_target_pairs={{0,1},{1,0},{2,3},{3,2},{4,5},{5,4},{6,7},{7,6},{8,9},{9,8},{10,11... | collective-permute-start | bytes 49160 | tf_op jit(solution)/shard_map/ppermute | solution.py:217
  17.2 5.4 %collective-permute-start.1 = (f32[1,16,512]{2,1,0:T(8,128)S(1)}, f32[1,16,512]{2,1,0:T(8,128)S(1)}, u32[]{:S(2)}, u32[]{:S(2)}) collective-permute-start(f32[1,16,512]{2,1,0:T(8,128)S(1)} %get-tuple-element.24), channel_id=1, source_target_pairs={{0,16},{8,24},{16,0},{24,8},{1,17},{9,25},{17,1},{25,9},{2,18},{10... | collective-permute-start | bytes 98312 | tf_op jit(solution)/shard_map/ppermute | solution.py:214
  20.8 20.6 %copy-start = (bf16[2,2,2,64,512]{4,3,2,1,0:T(8,128)(2,1)S(1)}, bf16[2,2,2,64,512]{4,3,2,1,0:T(8,128)(2,1)}, u32[]{:S(2)}) copy-start(bf16[2,2,2,64,512]{4,3,2,1,0:T(8,128)(2,1)} %get-tuple-element.17.refs_1_) | copy-start | bytes 1572868
  20.9 12.2 %collective-permute-start.8 = (bf16[2,2,64,512]{3,2,1,0:T(8,128)(2,1)S(1)}, bf16[2,2,64,512]{3,2,1,0:T(8,128)(2,1)S(1)}, u32[]{:S(2)}, u32[]{:S(2)}) collective-permute-start(bf16[2,2,64,512]{3,2,1,0:T(8,128)(2,1)S(1)} %slice_bitcast_fusion), channel_id=1, source_target_pairs={{0,1},{1,0},{2,3},{3,2},{4,5},{5,4},{6,7},{7,6},{8,9},{9,8},{10,11... | collective-permute-start | bytes 786440 | tf_op jit(solution)/shard_map/ppermute | solution.py:217
  22.6 0.7 %copy-start.5 = (s32[16]{0:T(128)S(1)}, s32[16]{0:T(128)}, u32[]{:S(2)}) copy-start(s32[16]{0:T(128)} %get-tuple-element.13.refs_0_) | copy-start | bytes 196
  24.1 3.8 %collective-permute-start.6 = (bf16[16,512]{1,0:T(8,128)(2,1)S(1)}, bf16[16,512]{1,0:T(8,128)(2,1)S(1)}, u32[]{:S(2)}, u32[]{:S(2)}) collective-permute-start(bf16[16,512]{1,0:T(8,128)(2,1)S(1)} %get-tuple-element.21), channel_id=1, source_target_pairs={{0,8},{8,0},{16,24},{24,16},{1,9},{9,1},{17,25},{25,17},{2,10},{10... | collective-permute-start | bytes 49160 | tf_op jit(solution)/shard_map/ppermute | solution.py:214
  27.9 5.1 %collective-permute-start.9 = (bf16[1,2,2,64,512]{4,3,2,1,0:T(8,128)(2,1)S(1)}, bf16[1,2,2,64,512]{4,3,2,1,0:T(8,128)(2,1)S(1)}, u32[]{:S(2)}, u32[]{:S(2)}) collective-permute-start(bf16[1,2,2,64,512]{4,3,2,1,0:T(8,128)(2,1)S(1)} %shard_map.88), channel_id=1, source_target_pairs={{0,1},{1,0},{2,3},{3,2},{4,5},{5,4},{6,7},{7,6},{8,9},{9,8},{10,11... | collective-permute-start | bytes 786440 | tf_op jit(solution)/shard_map/ppermute | solution.py:217
  28.0 5.0 %collective-permute-start.7 = (bf16[32,512]{1,0:T(8,128)(2,1)S(1)}, bf16[32,512]{1,0:T(8,128)(2,1)S(1)}, u32[]{:S(2)}, u32[]{:S(2)}) collective-permute-start(bf16[32,512]{1,0:T(8,128)(2,1)S(1)} %constant_dynamic-update-slice_fusion.refs_1_.first_ref), channel_id=1, source_target_pairs={{0,16},{8,24},{16,0},{24,8},{1,17},{9,25},{17,1},{25,9},{2,18},{10... | collective-permute-start | bytes 98312 | tf_op jit(solution)/shard_map/ppermute | solution.py:214
  33.0 5.1 %collective-permute-start.10 = (bf16[64,512]{1,0:T(8,128)(2,1)S(1)}, bf16[64,512]{1,0:T(8,128)(2,1)S(1)}, u32[]{:S(2)}, u32[]{:S(2)}) collective-permute-start(bf16[64,512]{1,0:T(8,128)(2,1)S(1)} %shard_map.89.refs_5_.refs_0_), channel_id=1, source_target_pairs={{0,2},{1,3},{2,0},{3,1},{4,6},{5,7},{6,4},{7,5},{8,10},{9,11},{10,... | collective-permute-start | bytes 196616 | tf_op jit(solution)/shard_map/ppermute | solution.py:217
  34.1 5.6 %collective-permute-start.11 = (bf16[64,512]{1,0:T(8,128)(2,1)S(1)}, bf16[64,512]{1,0:T(8,128)(2,1)S(1)}, u32[]{:S(2)}, u32[]{:S(2)}) collective-permute-start(bf16[64,512]{1,0:T(8,128)(2,1)S(1)} %shard_map.89.refs_5_.refs_0_), channel_id=1, source_target_pairs={{0,4},{1,5},{2,6},{3,7},{4,0},{5,1},{6,2},{7,3},{8,12},{9,13},{10,... | collective-permute-start | bytes 196616 | tf_op jit(solution)/shard_map/ppermute | solution.py:217
  35.6 5.2 %collective-permute-start.12 = (bf16[64,512]{1,0:T(8,128)(2,1)S(1)}, bf16[64,512]{1,0:T(8,128)(2,1)S(1)}, u32[]{:S(2)}, u32[]{:S(2)}) collective-permute-start(bf16[64,512]{1,0:T(8,128)(2,1)S(1)} %shard_map.89.refs_5_.refs_0_), channel_id=1, source_target_pairs={{0,6},{1,7},{2,4},{3,5},{4,2},{5,3},{6,0},{7,1},{8,14},{9,15},{10,... | collective-permute-start | bytes 196616 | tf_op jit(solution)/shard_map/ppermute | solution.py:217
  40.8 2.4 %collective-permute-start.13 = (bf16[2,2,2,64,512]{4,3,2,1,0:T(8,128)(2,1)S(1)}, bf16[2,2,2,64,512]{4,3,2,1,0:T(8,128)(2,1)S(1)}, u32[]{:S(2)}, u32[]{:S(2)}) collective-permute-start(bf16[2,2,2,64,512]{4,3,2,1,0:T(8,128)(2,1)S(1)} %shard_map.91), channel_id=1, source_target_pairs={{0,1},{1,0},{2,3},{3,2},{4,5},{5,4},{6,7},{7,6},{8,9},{9,8},{10,11... | collective-permute-start | bytes 1572872 | tf_op jit(solution)/shard_map/ppermute | solution.py:217
  40.9 2.2 %collective-permute-start.14 = (bf16[4,64,512]{2,1,0:T(8,128)(2,1)S(1)}, bf16[4,64,512]{2,1,0:T(8,128)(2,1)S(1)}, u32[]{:S(2)}, u32[]{:S(2)}) collective-permute-start(bf16[4,64,512]{2,1,0:T(8,128)(2,1)S(1)} %shard_map.92), channel_id=1, source_target_pairs={{0,1},{1,0},{2,3},{3,2},{4,5},{5,4},{6,7},{7,6},{8,9},{9,8},{10,11... | collective-permute-start | bytes 786440 | tf_op jit(solution)/shard_map/ppermute | solution.py:217

commit v12 on v11

--- a/solution.py
+++ b/solution.py
@@ -29,7 +29,7 @@
                       within_ref, weights_ref, spectrum_ref, *rest):
     chips = n_pen // 2
     outs, rest = rest[:chips], rest[chips:]
-    inverse_ref, kept_ref, sent_ref, held, owner, tilt_pos, tilt, within, weights, rest = *rest[:9], rest[9:]
+    kept_ref, sent_ref, held, owner, tilt_pos, tilt, within, weights, rest = *rest[:8], rest[8:]
     count, table, kept, sent, small_sems, in_sems, out_sems, sum_sems = rest
     blocks, pairs, depth = weights_ref.shape
     columns = spectrum_ref.shape[3]
@@ -49,11 +49,6 @@
         count[o] = 0
     for copy in small:
         copy.wait()
-    for b in range(blocks):
-        o = owner[b]
-        r = count[o]
-        count[o] = r + 1
-        inverse_ref[o * per_owner + r] = b
     slot = slots(tilt_pos, tilt[...], within[...], tiles_per_tilt, lax.axis_index("kz") * chunk)
     rows = lax.broadcasted_iota(I32, (tiles, pairs), 0)
     for b in range(blocks):
@@ -61,13 +56,21 @@
         hi, lo = split_hi_lo(jnp.dot(hot, weights[b], preferred_element_type=F32))
         table[:tiles, b * depth : (b + 1) * depth] = hi
         table[tiles:, b * depth : (b + 1) * depth] = lo
+    for b in range(blocks):
+        o = owner[b]
+        r = count[o]
+        count[o] = r + 1
+        q = o ^ pen
+        gets[b].wait()
+        for i in range(chips):
+
+            @pl.when(q >> 1 == i)
+            def _(b=b, r=r, q=q, i=i):
+                pltpu.make_async_copy(held.at[b], outs[i].at[q & 1, r], out_sems.at[q, r]).start()
+
     for q in range(n_pen):
         for r in range(per_owner):
-            b = inverse_ref[(pen ^ q) * per_owner + r]
-            from_ref = held.at[b]
-            pltpu.make_async_copy(spectrum_ref.at[b], from_ref, in_sems.at[b]).wait()
-            puts.append(pltpu.make_async_copy(from_ref, outs[q // 2].at[q % 2, r], out_sems.at[q, r]))
-            puts[-1].start()
+            puts.append(pltpu.make_async_copy(held.at[0], outs[q // 2].at[q % 2, r], out_sems.at[q, r]))
     for c in range(2):
         both = jnp.dot(
             table[...],
@@ -86,8 +89,8 @@
         put.wait()
 
 
-def residual_and_table(n_kz, chunk, per_owner, tiles_per_tilt, inverse_ref, tilt_pos_ref, tilt_ref, within_ref,
-                       weights_ref, sums_ref, arrived_ref, got_ref, swapped_ref, own_ref, out_ref, slot_ref, measured):
+def residual_and_table(n_kz, chunk, per_owner, tiles_per_tilt, owner_ref, tilt_pos_ref, tilt_ref, within_ref,
+                       weights_ref, sums_ref, arrived_ref, got_ref, swapped_ref, own_ref, out_ref, slot_ref, measured, owned):
     core = lax.axis_index("pen") & 1
     for i in range(got_ref.shape[0]):
         mine, theirs = got_ref[i, core].astype(F32), swapped_ref[i, core].astype(F32)
@@ -102,8 +105,18 @@
     flip = lax.axis_index("kz") * chunk
     slot_ref[...] = slots(tilt_pos_ref, tilt_ref[...], within_ref[...], tiles_per_tilt, flip)
     rows = lax.broadcasted_iota(I32, (rows_all, pairs), 0)
+    pen = lax.axis_index("pen")
+    seen = jnp.int32(0)
+    for b in range(owner_ref.shape[0]):
+        hit = owner_ref[b] == pen
+
+        @pl.when(hit)
+        def _(b=b, seen=seen):
+            owned[seen] = b
+
+        seen = seen + hit.astype(I32)
     for r in range(per_owner):
-        b = inverse_ref[lax.axis_index("pen") * per_owner + r]
+        b = owned[r]
         at = slot_ref[pl.ds(b, 1), :]
         low = at & (chunk - 1)
         for c in range(2):
@@ -218,12 +231,12 @@
 
     pair = (per_owner, 2, depth, columns)
     group = jax.ShapeDtypeStruct((n_kz // 2, 2 * chunk, columns), F32)
-    *outs, inverse, sums, sent_sums = pl.pallas_call(
+    *outs, sums, sent_sums = pl.pallas_call(
         call(order_and_forward, n_pen, n_kz, chunk, per_owner, tiles_per_tilt),
         out_shape=[jax.ShapeDtypeStruct((2, per_owner, 2, depth, columns), BF16)] * chips
-        + [jax.ShapeDtypeStruct((blocks,), I32), group, group],
+        + [group, group],
         in_specs=[ANY] * 6,
-        out_specs=[ANY] * chips + [SMEM, ANY, ANY],
+        out_specs=[ANY] * (chips + 2),
         scratch_shapes=[
             pltpu.VMEM(spectrum.shape, BF16),
             pltpu.SMEM((blocks,), I32),
@@ -264,10 +277,14 @@
         ],
         in_specs=[SMEM, SMEM] + [VMEM] * 7,
         out_specs=[VMEM, VMEM],
-        scratch_shapes=[pltpu.VMEM((blocks, pairs), I32), pltpu.VMEM((2 * chunk, columns), F32)],
+        scratch_shapes=[
+            pltpu.VMEM((blocks, pairs), I32),
+            pltpu.VMEM((2 * chunk, columns), F32),
+            pltpu.SMEM((per_owner,), I32),
+        ],
         compiler_params=pltpu.CompilerParams(vmem_limit_bytes=8 << 20),
     )(
-        inverse,
+        owner,
         tilt_pos,
         pair_tilt,
         pair_tile_within,

time: 44.8 us -> 44.3 us (0.989)
  local copies, waits for them, and re-layouts: 1.65 us -> 1.01 us
  waiting for transfers between devices: 13.8 us -> 14.4 us
  Pallas kernels: 7.54 us -> 7.07 us
    unnamed x13, local copies, waits for them, and re-layouts: 0.68 us -> 0.03 us
    ppermute x11, waiting for transfers between devices: 4.56 us -> 5.17 us  [between(): return lax.ppermute(value, 'pen', [(i, i ^ k) for i in range(n_pen)])]
    pallas_call x1, Pallas kernels: 4.04 us -> 3.53 us  [body(): pl.pallas_call(call(order_and_forward, n_pen, n_kz, chunk, per_owner, til...]
  transfers between devices with their start and end apart: 16 -> 16, of which waited for: 8 -> 9; matrix products, arithmetic and copies ran while one was open for 4% -> 4% of each run, Pallas kernels for 5% -> 5%
where the time goes in v12:
time: 44.3 us; the launch traced here: 44 us
  starting transfers between devices  19.8 us (45%)
  waiting for transfers between devices  14.4 us (33%)
  Pallas kernels  7.07 us (16%)
  local copies, waits for them, and re-layouts  1.01 us (2%)
  other arithmetic  0.85 us (2%)
  between operations  0.82 us (2%)
    ppermute x11, starting transfers between devices, between(): return lax.ppermute(value, 'pen', [(i, i ^ k) for i in range(n_pen)])  8.06 us
    ppermute x4, starting transfers between devices, across(): return lax.ppermute(value, 'kz', [(i, i ^ k) for i in range(n_kz)])  7.99 us
    ppermute x4, waiting for transfers between devices, across(): return lax.ppermute(value, 'kz', [(i, i ^ k) for i in range(n_kz)])  7.98 us
    ppermute x11, waiting for transfers between devices, between(): return lax.ppermute(value, 'pen', [(i, i ^ k) for i in range(n_pen)])  5.17 us
    all_to_all x1, starting transfers between devices, body(): lax.all_to_all(sent, 'pen', split_axis=0, concat_axis=0, tiled=True, axis...  3.72 us
    pallas_call x1, Pallas kernels, body(): pl.pallas_call(call(order_and_forward, n_pen, n_kz, chunk, per_owner, til...  3.53 us
    pallas_call x1, Pallas kernels, body(): pl.pallas_call(call(adjoint_other, n_pen, chunk, per_owner), out_shape=sh...  1.3 us
    all_to_all x1, waiting for transfers between devices, body(): lax.all_to_all(sent, 'pen', split_axis=0, concat_axis=0, tiled=True, axis...  1.3 us
  transfers between devices with their start and end apart: 16, of which 9 were waited for; matrix products, arithmetic and copies ran while one was open for 4% of the time, Pallas kernels for 5%

profile of v12, /device:TPU:0, one launch (start us, length us, event | category | flops | bytes accessed | tf_op | source)
XLA Modules:
  0.0 44.0 jit_solution(7421453112464540405)
XLA Ops:
  0.6 0.0 copy-start.4
  0.6 0.0 copy-start.5
  0.7 0.0 copy-start.2
  0.7 0.0 copy-start.3
  0.7 0.0 copy-start.1
  0.7 3.5 %shard_map.86 = (bf16[2,2,2,64,512]{4,3,2,1,0:T(8,128)(2,1)}, bf16[2,2,2,64,512]{4,3,2,1,0:T(8,128)(2,1)}, bf16[2,2,2,64,512]{4,3,2,1,0:T(8,128)(2,1)}, bf16[2,2...) custom-call(s32[16]{0:T(128)} %refs_0_.3, s32[16]{0:T(128)} %refs_1_.3, ...), custom_call_target="tpu_custom_call" | custom-call | tf_op jit(solution)/shard_map/pallas_call | solution.py:234
  4.2 3.1 %collective-permute-start = (f32[2,16,512]{2,1,0:T(8,128)}, f32[2,16,512]{2,1,0:T(8,128)S(1)}, u32[]{:S(2)}, u32[]{:S(2)}) collective-permute-start(f32[2,16,512]{2,1,0:T(8,128)} %get-tuple-element.13), channel_id=1, source_target_pairs={{0,8},{8,0},{16,24},{24,16},{1,9},{9,1},{17,25},{25,17},{2,10},{10... | collective-permute-start | bytes 196616 | tf_op jit(solution)/shard_map/ppermute | solution.py:227
  7.3 3.7 %all-to-all-start = ((bf16[8,2,512]{2,1,0:T(2,128)(2,1)}), bf16[8,2,512]{2,1,0:T(2,128)(2,1)S(1)}, u32[]{:S(2)}, u32[]{:S(2)}) async-start(bf16[8,2,512]{2,1,0:T(2,128)(2,1)} %bitcast.5), calls=%async_computation | async-start | bytes 32768 | tf_op jit(solution)/shard_map/all_to_all | solution.py:269
  11.0 2.0 %collective-permute-start.3 = (bf16[2,2,2,64,512]{4,3,2,1,0:T(8,128)(2,1)}, bf16[2,2,2,64,512]{4,3,2,1,0:T(8,128)(2,1)S(1)}, u32[]{:S(2)}, u32[]{:S(2)}) collective-permute-start(bf16[2,2,2,64,512]{4,3,2,1,0:T(8,128)(2,1)} %get-tuple-element.16), channel_id=1, source_target_pairs={{0,2},{1,3},{2,0},{3,1},{4,6},{5,7},{6,4},{7,5},{8,10},{9,11},{10,... | collective-permute-start | bytes 1572872 | tf_op jit(solution)/shard_map/ppermute | solution.py:230
  13.0 1.5 %collective-permute-start.4 = (bf16[2,2,2,64,512]{4,3,2,1,0:T(8,128)(2,1)}, bf16[2,2,2,64,512]{4,3,2,1,0:T(8,128)(2,1)S(1)}, u32[]{:S(2)}, u32[]{:S(2)}) collective-permute-start(bf16[2,2,2,64,512]{4,3,2,1,0:T(8,128)(2,1)} %get-tuple-element.17), channel_id=1, source_target_pairs={{0,4},{1,5},{2,6},{3,7},{4,0},{5,1},{6,2},{7,3},{8,12},{9,13},{10,... | collective-permute-start | bytes 1572872 | tf_op jit(solution)/shard_map/ppermute | solution.py:230
  14.5 0.0 collective-permute-start.5
  14.5 1.3 %all-to-all-done = bf16[8,2,512]{2,1,0:T(2,128)(2,1)S(1)} async-done(((bf16[8,2,512]{2,1,0:T(2,128)(2,1)}), bf16[8,2,512]{2,1,0:T(2,128)(2,1)S(1)}, u32[]{:S(2)}, u32[]{:S(2)}) %all-to-all-start) | async-done | bytes 16416 | tf_op jit(solution)/shard_map/all_to_all | solution.py:269
  15.8 0.0 collective-permute-start.2
  15.8 0.0 collective-permute-done
  15.8 0.9 %add_bitcast_fusion = f32[1,2,16,512]{3,2,1,0:T(8,128)S(1)} fusion(f32[2,16,512]{2,1,0:T(8,128)} %get-tuple-element.12, f32[2,16,512]{2,1,0:T(8,128)S(1)} %collective-permute-done), kind=kLoop, calls=%fused_computation.1 | loop fusion | flops 16384 | bytes 196608 | tf_op jit(solution)/shard_map/reshape | solution.py:263
  16.7 2.7 %collective-permute-start.1 = (f32[1,16,512]{2,1,0:T(8,128)S(1)}, f32[1,16,512]{2,1,0:T(8,128)S(1)}, u32[]{:S(2)}, u32[]{:S(2)}) collective-permute-start(f32[1,16,512]{2,1,0:T(8,128)S(1)} %get-tuple-element.22), channel_id=1, source_target_pairs={{0,16},{8,24},{16,0},{24,8},{1,17},{9,25},{17,1},{25,9},{2,18},{10... | collective-permute-start | bytes 98312 | tf_op jit(solution)/shard_map/ppermute | solution.py:227
  19.4 1.0 %slice_bitcast_fusion = bf16[2,2,64,512]{3,2,1,0:T(8,128)(2,1)S(1)} fusion(bf16[2,2,2,64,512]{4,3,2,1,0:T(8,128)(2,1)} %get-tuple-element.15.refs_1_), kind=kLoop, calls=%fused_computation | loop fusion | bytes 524288 | tf_op jit(solution)/shard_map/squeeze | solution.py:313
  20.3 0.0 copy-start
  20.3 0.0 collective-permute-done.2.refs_8_
  20.4 0.3 collective-permute-start.8
  20.6 1.4 %collective-permute-done.1 = f32[1,16,512]{2,1,0:T(8,128)S(1)} collective-permute-done((f32[1,16,512]{2,1,0:T(8,128)S(1)}, f32[1,16,512]{2,1,0:T(8,128)S(1)}, u32[]{:S(2)}, u32[]{:S(2)}) %collective-permute-start.1) | collective-permute-done | bytes 32800 | tf_op jit(solution)/shard_map/ppermute | solution.py:227
  22.1 0.0 copy-done.3
  22.1 0.0 copy-done.1
  22.1 0.8 %shard_map.87 = (bf16[16,512]{1,0:T(8,128)(2,1)S(1)}, bf16[128,256]{1,0:T(8,128)(2,1)S(1)}) custom-call(s32[16]{0:T(128)S(1)} %copy-done.4, s32[16]{0:T(128)S(1)} %copy-done.5, s32[16,16]{1,0:T(8,128)S(1)} %copy-done.2, s32[16,16]{1,0:T(8,128)S(1)} %copy-done.3, bf16[16,16,64]{2,1,0:T(8,128)(2,1)S(1)} %copy-done.1, f32[16,512]{1,0:T(8,128)S(1)} %get-tuple-element.23.refs_5_, ...), custom_call_target="tpu_custom_call" | custom-call | tf_op jit(solution)/shard_map/pallas_call | solution.py:272
  22.9 0.1 collective-permute-start.6
  23.0 3.7 %collective-permute-done.6 = bf16[16,512]{1,0:T(8,128)(2,1)S(1)} collective-permute-done((bf16[16,512]{1,0:T(8,128)(2,1)S(1)}, bf16[16,512]{1,0:T(8,128)(2,1)S(1)}, u32[]{:S(2)}, u32[]{:S(2)}) %collective-permute-start.6) | collective-permute-done | bytes 16416 | tf_op jit(solution)/shard_map/ppermute | solution.py:227
  26.7 0.0 collective-permute-done.3.refs_0_.refs_2_
  26.8 0.1 collective-permute-start.9
  26.9 2.2 %collective-permute-start.7 = (bf16[32,512]{1,0:T(8,128)(2,1)S(1)}, bf16[32,512]{1,0:T(8,128)(2,1)S(1)}, u32[]{:S(2)}, u32[]{:S(2)}) collective-permute-start(bf16[32,512]{1,0:T(8,128)(2,1)S(1)} %constant_dynamic-update-slice_fusion.refs_1_.first_ref), channel_id=1, source_target_pairs={{0,16},{8,24},{16,0},{24,8},{1,17},{9,25},{17,1},{25,9},{2,18},{10... | collective-permute-start | bytes 98312 | tf_op jit(solution)/shard_map/ppermute | solution.py:227
  29.0 2.8 %collective-permute-done.7.second_ref = bf16[32,512]{1,0:T(8,128)(2,1)S(1)} collective-permute-done((bf16[32,512]{1,0:T(8,128)(2,1)S(1)}, bf16[32,512]{1,0:T(8,128)(2,1)S(1)}, u32[]{:S(2)}, u32[]{:S(2)}) %collective-permute-start.7) | collective-permute-done | bytes 32800 | tf_op jit(solution)/shard_map/ppermute | solution.py:227
  31.9 0.0 collective-permute-done.8.rest_0_.refs_3_
  31.9 0.0 collective-permute-done.9.rest_1_.refs_4_
  31.9 1.7 %collective-permute-start.10 = (bf16[64,512]{1,0:T(8,128)(2,1)S(1)}, bf16[64,512]{1,0:T(8,128)(2,1)S(1)}, u32[]{:S(2)}, u32[]{:S(2)}) collective-permute-start(bf16[64,512]{1,0:T(8,128)(2,1)S(1)} %shard_map.89.refs_5_.refs_0_), channel_id=1, source_target_pairs={{0,2},{1,3},{2,0},{3,1},{4,6},{5,7},{6,4},{7,5},{8,10},{9,11},{10,... | collective-permute-start | bytes 196616 | tf_op jit(solution)/shard_map/ppermute | solution.py:230
  33.6 1.5 %collective-permute-start.11 = (bf16[64,512]{1,0:T(8,128)(2,1)S(1)}, bf16[64,512]{1,0:T(8,128)(2,1)S(1)}, u32[]{:S(2)}, u32[]{:S(2)}) collective-permute-start(bf16[64,512]{1,0:T(8,128)(2,1)S(1)} %shard_map.89.refs_5_.refs_0_), channel_id=1, source_target_pairs={{0,4},{1,5},{2,6},{3,7},{4,0},{5,1},{6,2},{7,3},{8,12},{9,13},{10,... | collective-permute-start | bytes 196616 | tf_op jit(solution)/shard_map/ppermute | solution.py:230
  35.1 0.4 collective-permute-start.12
  35.5 1.2 %collective-permute-done.4.refs_3_.refs_0_ = bf16[2,2,2,64,512]{4,3,2,1,0:T(8,128)(2,1)S(1)} collective-permute-done((bf16[2,2,2,64,512]{4,3,2,1,0:T(8,128)(2,1)}, bf16[2,2,2,64,512]{4,3,2,1,0:T(8,128)(2,1)S(1)}, u32[]{:S(2)}, u32[]{:S(2)}) %collective-permute-start.4) | collective-permute-done | bytes 524320 | tf_op jit(solution)/shard_map/ppermute | solution.py:230
  36.7 1.0 %collective-permute-done.5.refs_4_.refs_1_ = bf16[2,2,2,64,512]{4,3,2,1,0:T(8,128)(2,1)S(1)} collective-permute-done((bf16[2,2,2,64,512]{4,3,2,1,0:T(8,128)(2,1)}, bf16[2,2,2,64,512]{4,3,2,1,0:T(8,128)(2,1)S(1)}, u32[]{:S(2)}, u32[]{:S(2)}) %collective-permute-start.5) | collective-permute-done | bytes 524320 | tf_op jit(solution)/shard_map/ppermute | solution.py:230
  37.6 0.0 collective-permute-done.10.refs_6_.refs_2_.refs_1_
  37.6 1.6 %collective-permute-done.11.refs_7_.refs_3_.refs_2_ = bf16[64,512]{1,0:T(8,128)(2,1)S(1)} collective-permute-done((bf16[64,512]{1,0:T(8,128)(2,1)S(1)}, bf16[64,512]{1,0:T(8,128)(2,1)S(1)}, u32[]{:S(2)}, u32[]{:S(2)}) %collective-permute-start.11) | collective-permute-done | bytes 65568 | tf_op jit(solution)/shard_map/ppermute | solution.py:230
  39.2 1.0 %collective-permute-done.12.refs_8_.refs_4_.refs_3_ = bf16[64,512]{1,0:T(8,128)(2,1)S(1)} collective-permute-done((bf16[64,512]{1,0:T(8,128)(2,1)S(1)}, bf16[64,512]{1,0:T(8,128)(2,1)S(1)}, u32[]{:S(2)}, u32[]{:S(2)}) %collective-permute-start.12) | collective-permute-done | bytes 65568 | tf_op jit(solution)/shard_map/ppermute | solution.py:230
  40.2 0.1 shard_map.91
  40.3 0.1 collective-permute-start.13
  40.4 0.6 %collective-permute-start.14 = (bf16[4,64,512]{2,1,0:T(8,128)(2,1)S(1)}, bf16[4,64,512]{2,1,0:T(8,128)(2,1)S(1)}, u32[]{:S(2)}, u32[]{:S(2)}) collective-permute-start(bf16[4,64,512]{2,1,0:T(8,128)(2,1)S(1)} %shard_map.92), channel_id=1, source_target_pairs={{0,1},{1,0},{2,3},{3,2},{4,5},{5,4},{6,7},{7,6},{8,9},{9,8},{10,11... | collective-permute-start | bytes 786440 | tf_op jit(solution)/shard_map/ppermute | solution.py:230
  41.0 0.0 copy-done
  41.0 1.3 %shard_map.90 = (bf16[2,2,64,4096]{3,2,1,0:T(8,128)(2,1)}, bf16[1,2,4096]{2,1,0:T(2,128)(2,1)S(1)}) custom-call(bf16[128,256]{1,0:T(8,128)(2,1)S(1)} %get-tuple-element.14.refs_0_, bf16[2,2,2,64,512]{4,3,2,1,0:T(8,128)(2,1)S(1)} %copy-done, bf16[2,2,2,64,512]{4,3,2,1,0:T(8,128)(2,1)S(1)} %collective-permute-done.3.refs_0_.refs_2_, ...), custom_call_target="tpu_custom_call" | custom-call | tf_op jit(solution)/shard_map/pallas_call | solution.py:338
  42.3 0.4 collective-permute-done.14.refs_6_
  42.7 0.0 collective-permute-done.13.refs_5_
  42.7 1.3 %shard_map.93 = (bf16[2,2,64,4096]{3,2,1,0:T(8,128)(2,1)}, bf16[1,2,4096]{2,1,0:T(2,128)(2,1)}) custom-call(bf16[128,256]{1,0:T(8,128)(2,1)S(1)} %get-tuple-element.14.refs_0_, bf16[2,2,64,4096]{3,2,1,0:T(8,128)(2,1)} %get-tuple-element.20.refs_1_, bf16[1,2,4096]{2,1,0:T(2,128)(2,1)S(1)} %get-tuple-element.21.refs_2_, ...), custom_call_target="tpu_custom_call", output_to_operand_aliasing={{0}: (1, {})} | custom-call | tf_op jit(solution)/shard_map/pallas_call | solution.py:346
  (9 shorter events, 0.1 us)
Async XLA Ops:
  0.6 21.4 %copy-start.4 = (s32[16]{0:T(128)S(1)}, s32[16]{0:T(128)}, u32[]{:S(2)}) copy-start(s32[16]{0:T(128)} %refs_0_.3) | copy-start | bytes 196
  0.6 21.4 %copy-start.5 = (s32[16]{0:T(128)S(1)}, s32[16]{0:T(128)}, u32[]{:S(2)}) copy-start(s32[16]{0:T(128)} %refs_1_.3) | copy-start | bytes 196
  0.7 21.4 %copy-start.2 = (s32[16,16]{1,0:T(8,128)S(1)}, s32[16,16]{1,0:T(8,128)}, u32[]{:S(2)}) copy-start(s32[16,16]{1,0:T(8,128)} %refs_2_.3) | copy-start | bytes 3076
  0.7 21.4 %copy-start.3 = (s32[16,16]{1,0:T(8,128)S(1)}, s32[16,16]{1,0:T(8,128)}, u32[]{:S(2)}) copy-start(s32[16,16]{1,0:T(8,128)} %refs_3_.3) | copy-start | bytes 3076
  0.7 21.4 %copy-start.1 = (bf16[16,16,64]{2,1,0:T(8,128)(2,1)S(1)}, bf16[16,16,64]{2,1,0:T(8,128)(2,1)}, u32[]{:S(2)}) copy-start(bf16[16,16,64]{2,1,0:T(8,128)(2,1)} %refs_4_.3) | copy-start | bytes 98308
  4.2 11.6 %collective-permute-start = (f32[2,16,512]{2,1,0:T(8,128)}, f32[2,16,512]{2,1,0:T(8,128)S(1)}, u32[]{:S(2)}, u32[]{:S(2)}) collective-permute-start(f32[2,16,512]{2,1,0:T(8,128)} %get-tuple-element.13), channel_id=1, source_target_pairs={{0,8},{8,0},{16,24},{24,16},{1,9},{9,1},{17,25},{25,17},{2,10},{10... | collective-permute-start | bytes 196616 | tf_op jit(solution)/shard_map/ppermute | solution.py:227
  7.3 8.5 %all-to-all-start = ((bf16[8,2,512]{2,1,0:T(2,128)(2,1)}), bf16[8,2,512]{2,1,0:T(2,128)(2,1)S(1)}, u32[]{:S(2)}, u32[]{:S(2)}) async-start(bf16[8,2,512]{2,1,0:T(2,128)(2,1)} %bitcast.5), calls=%async_computation | async-start | bytes 32768 | tf_op jit(solution)/shard_map/all_to_all | solution.py:269
  11.0 15.7 %collective-permute-start.3 = (bf16[2,2,2,64,512]{4,3,2,1,0:T(8,128)(2,1)}, bf16[2,2,2,64,512]{4,3,2,1,0:T(8,128)(2,1)S(1)}, u32[]{:S(2)}, u32[]{:S(2)}) collective-permute-start(bf16[2,2,2,64,512]{4,3,2,1,0:T(8,128)(2,1)} %get-tuple-element.16), channel_id=1, source_target_pairs={{0,2},{1,3},{2,0},{3,1},{4,6},{5,7},{6,4},{7,5},{8,10},{9,11},{10,... | collective-permute-start | bytes 1572872 | tf_op jit(solution)/shard_map/ppermute | solution.py:230
  13.0 23.6 %collective-permute-start.4 = (bf16[2,2,2,64,512]{4,3,2,1,0:T(8,128)(2,1)}, bf16[2,2,2,64,512]{4,3,2,1,0:T(8,128)(2,1)S(1)}, u32[]{:S(2)}, u32[]{:S(2)}) collective-permute-start(bf16[2,2,2,64,512]{4,3,2,1,0:T(8,128)(2,1)} %get-tuple-element.17), channel_id=1, source_target_pairs={{0,4},{1,5},{2,6},{3,7},{4,0},{5,1},{6,2},{7,3},{8,12},{9,13},{10,... | collective-permute-start | bytes 1572872 | tf_op jit(solution)/shard_map/ppermute | solution.py:230
  14.5 23.1 %collective-permute-start.5 = (bf16[2,2,2,64,512]{4,3,2,1,0:T(8,128)(2,1)}, bf16[2,2,2,64,512]{4,3,2,1,0:T(8,128)(2,1)S(1)}, u32[]{:S(2)}, u32[]{:S(2)}) collective-permute-start(bf16[2,2,2,64,512]{4,3,2,1,0:T(8,128)(2,1)} %get-tuple-element.18), channel_id=1, source_target_pairs={{0,6},{1,7},{2,4},{3,5},{4,2},{5,3},{6,0},{7,1},{8,14},{9,15},{10,... | collective-permute-start | bytes 1572872 | tf_op jit(solution)/shard_map/ppermute | solution.py:230
  15.8 4.5 %collective-permute-start.2 = (bf16[4,2,2,512]{3,2,1,0:T(2,128)(2,1)S(1)}, bf16[4,2,2,512]{3,2,1,0:T(2,128)(2,1)S(1)}, u32[]{:S(2)}, u32[]{:S(2)}) collective-permute-start(bf16[4,2,2,512]{3,2,1,0:T(2,128)(2,1)S(1)} %bitcast.13), channel_id=1, source_target_pairs={{0,1},{1,0},{2,3},{3,2},{4,5},{5,4},{6,7},{7,6},{8,9},{9,8},{10,11... | collective-permute-start | bytes 49160 | tf_op jit(solution)/shard_map/ppermute | solution.py:230
  16.7 5.4 %collective-permute-start.1 = (f32[1,16,512]{2,1,0:T(8,128)S(1)}, f32[1,16,512]{2,1,0:T(8,128)S(1)}, u32[]{:S(2)}, u32[]{:S(2)}) collective-permute-start(f32[1,16,512]{2,1,0:T(8,128)S(1)} %get-tuple-element.22), channel_id=1, source_target_pairs={{0,16},{8,24},{16,0},{24,8},{1,17},{9,25},{17,1},{25,9},{2,18},{10... | collective-permute-start | bytes 98312 | tf_op jit(solution)/shard_map/ppermute | solution.py:227
  20.3 20.6 %copy-start = (bf16[2,2,2,64,512]{4,3,2,1,0:T(8,128)(2,1)S(1)}, bf16[2,2,2,64,512]{4,3,2,1,0:T(8,128)(2,1)}, u32[]{:S(2)}) copy-start(bf16[2,2,2,64,512]{4,3,2,1,0:T(8,128)(2,1)} %get-tuple-element.15.refs_1_) | copy-start | bytes 1572868
  20.4 11.5 %collective-permute-start.8 = (bf16[2,2,64,512]{3,2,1,0:T(8,128)(2,1)S(1)}, bf16[2,2,64,512]{3,2,1,0:T(8,128)(2,1)S(1)}, u32[]{:S(2)}, u32[]{:S(2)}) collective-permute-start(bf16[2,2,64,512]{3,2,1,0:T(8,128)(2,1)S(1)} %slice_bitcast_fusion), channel_id=1, source_target_pairs={{0,1},{1,0},{2,3},{3,2},{4,5},{5,4},{6,7},{7,6},{8,9},{9,8},{10,11... | collective-permute-start | bytes 786440 | tf_op jit(solution)/shard_map/ppermute | solution.py:230
  22.9 3.8 %collective-permute-start.6 = (bf16[16,512]{1,0:T(8,128)(2,1)S(1)}, bf16[16,512]{1,0:T(8,128)(2,1)S(1)}, u32[]{:S(2)}, u32[]{:S(2)}) collective-permute-start(bf16[16,512]{1,0:T(8,128)(2,1)S(1)} %get-tuple-element.19), channel_id=1, source_target_pairs={{0,8},{8,0},{16,24},{24,16},{1,9},{9,1},{17,25},{25,17},{2,10},{10... | collective-permute-start | bytes 49160 | tf_op jit(solution)/shard_map/ppermute | solution.py:227
  26.8 5.1 %collective-permute-start.9 = (bf16[1,2,2,64,512]{4,3,2,1,0:T(8,128)(2,1)S(1)}, bf16[1,2,2,64,512]{4,3,2,1,0:T(8,128)(2,1)S(1)}, u32[]{:S(2)}, u32[]{:S(2)}) collective-permute-start(bf16[1,2,2,64,512]{4,3,2,1,0:T(8,128)(2,1)S(1)} %shard_map.88), channel_id=1, source_target_pairs={{0,1},{1,0},{2,3},{3,2},{4,5},{5,4},{6,7},{7,6},{8,9},{9,8},{10,11... | collective-permute-start | bytes 786440 | tf_op jit(solution)/shard_map/ppermute | solution.py:230
  26.9 5.0 %collective-permute-start.7 = (bf16[32,512]{1,0:T(8,128)(2,1)S(1)}, bf16[32,512]{1,0:T(8,128)(2,1)S(1)}, u32[]{:S(2)}, u32[]{:S(2)}) collective-permute-start(bf16[32,512]{1,0:T(8,128)(2,1)S(1)} %constant_dynamic-update-slice_fusion.refs_1_.first_ref), channel_id=1, source_target_pairs={{0,16},{8,24},{16,0},{24,8},{1,17},{9,25},{17,1},{25,9},{2,18},{10... | collective-permute-start | bytes 98312 | tf_op jit(solution)/shard_map/ppermute | solution.py:227
  31.9 5.7 %collective-permute-start.10 = (bf16[64,512]{1,0:T(8,128)(2,1)S(1)}, bf16[64,512]{1,0:T(8,128)(2,1)S(1)}, u32[]{:S(2)}, u32[]{:S(2)}) collective-permute-start(bf16[64,512]{1,0:T(8,128)(2,1)S(1)} %shard_map.89.refs_5_.refs_0_), channel_id=1, source_target_pairs={{0,2},{1,3},{2,0},{3,1},{4,6},{5,7},{6,4},{7,5},{8,10},{9,11},{10,... | collective-permute-start | bytes 196616 | tf_op jit(solution)/shard_map/ppermute | solution.py:230
  33.6 5.6 %collective-permute-start.11 = (bf16[64,512]{1,0:T(8,128)(2,1)S(1)}, bf16[64,512]{1,0:T(8,128)(2,1)S(1)}, u32[]{:S(2)}, u32[]{:S(2)}) collective-permute-start(bf16[64,512]{1,0:T(8,128)(2,1)S(1)} %shard_map.89.refs_5_.refs_0_), channel_id=1, source_target_pairs={{0,4},{1,5},{2,6},{3,7},{4,0},{5,1},{6,2},{7,3},{8,12},{9,13},{10,... | collective-permute-start | bytes 196616 | tf_op jit(solution)/shard_map/ppermute | solution.py:230
  35.1 5.2 %collective-permute-start.12 = (bf16[64,512]{1,0:T(8,128)(2,1)S(1)}, bf16[64,512]{1,0:T(8,128)(2,1)S(1)}, u32[]{:S(2)}, u32[]{:S(2)}) collective-permute-start(bf16[64,512]{1,0:T(8,128)(2,1)S(1)} %shard_map.89.refs_5_.refs_0_), channel_id=1, source_target_pairs={{0,6},{1,7},{2,4},{3,5},{4,2},{5,3},{6,0},{7,1},{8,14},{9,15},{10,... | collective-permute-start | bytes 196616 | tf_op jit(solution)/shard_map/ppermute | solution.py:230
  40.3 2.4 %collective-permute-start.13 = (bf16[2,2,2,64,512]{4,3,2,1,0:T(8,128)(2,1)S(1)}, bf16[2,2,2,64,512]{4,3,2,1,0:T(8,128)(2,1)S(1)}, u32[]{:S(2)}, u32[]{:S(2)}) collective-permute-start(bf16[2,2,2,64,512]{4,3,2,1,0:T(8,128)(2,1)S(1)} %shard_map.91), channel_id=1, source_target_pairs={{0,1},{1,0},{2,3},{3,2},{4,5},{5,4},{6,7},{7,6},{8,9},{9,8},{10,11... | collective-permute-start | bytes 1572872 | tf_op jit(solution)/shard_map/ppermute | solution.py:230
  40.4 2.2 %collective-permute-start.14 = (bf16[4,64,512]{2,1,0:T(8,128)(2,1)S(1)}, bf16[4,64,512]{2,1,0:T(8,128)(2,1)S(1)}, u32[]{:S(2)}, u32[]{:S(2)}) collective-permute-start(bf16[4,64,512]{2,1,0:T(8,128)(2,1)S(1)} %shard_map.92), channel_id=1, source_target_pairs={{0,1},{1,0},{2,3},{3,2},{4,5},{5,4},{6,7},{7,6},{8,9},{9,8},{10,11... | collective-permute-start | bytes 786440 | tf_op jit(solution)/shard_map/ppermute | solution.py:230

commit v13 on v12

--- a/solution.py
+++ b/solution.py
@@ -56,31 +56,32 @@
         hi, lo = split_hi_lo(jnp.dot(hot, weights[b], preferred_element_type=F32))
         table[:tiles, b * depth : (b + 1) * depth] = hi
         table[tiles:, b * depth : (b + 1) * depth] = lo
-    for b in range(blocks):
-        o = owner[b]
-        r = count[o]
-        count[o] = r + 1
-        q = o ^ pen
-        gets[b].wait()
-        for i in range(chips):
-
-            @pl.when(q >> 1 == i)
-            def _(b=b, r=r, q=q, i=i):
-                pltpu.make_async_copy(held.at[b], outs[i].at[q & 1, r], out_sems.at[q, r]).start()
-
+    both = [jnp.zeros((2 * tiles, columns), F32)] * 2
+    for first in range(0, blocks, 4):
+        for b in range(first, first + 4):
+            o = owner[b]
+            r = count[o]
+            count[o] = r + 1
+            q = o ^ pen
+            gets[b].wait()
+            for i in range(chips):
+
+                @pl.when(q >> 1 == i)
+                def _(b=b, r=r, q=q, i=i):
+                    pltpu.make_async_copy(held.at[b], outs[i].at[q & 1, r], out_sems.at[q, r]).start()
+
+        weight = table[:, first * depth : (first + 4) * depth]
+        for c in range(2):
+            here = held[first : first + 4, c].reshape(4 * depth, columns)
+            both[c] = both[c] + jnp.dot(weight, here, preferred_element_type=F32)
+    for c in range(2):
+        total = both[c][:tiles] + both[c][tiles:]
+        for k in range(n_kz):
+            to = sent if k % 2 else kept
+            to[k // 2, c * chunk : (c + 1) * chunk, :] = total[k * chunk : (k + 1) * chunk]
     for q in range(n_pen):
         for r in range(per_owner):
             puts.append(pltpu.make_async_copy(held.at[0], outs[q // 2].at[q % 2, r], out_sems.at[q, r]))
-    for c in range(2):
-        both = jnp.dot(
-            table[...],
-            held[:, c].reshape(blocks * depth, columns),
-            preferred_element_type=F32,
-        )
-        total = both[:tiles] + both[tiles:]
-        for k in range(n_kz):
-            to = sent if k % 2 else kept
-            to[k // 2, c * chunk : (c + 1) * chunk, :] = total[k * chunk : (k + 1) * chunk]
     puts.append(pltpu.make_async_copy(kept, kept_ref, sum_sems.at[0]))
     puts[-1].start()
     puts.append(pltpu.make_async_copy(sent, sent_ref, sum_sems.at[1]))

time: 44.3 us -> 44.3 us (level)
  no operation moved by 1% of the time
where the time goes in v13:
time: 44.3 us; the launch traced here: 44 us
  starting transfers between devices  19.8 us (45%)
  waiting for transfers between devices  14.4 us (33%)
  Pallas kernels  7.07 us (16%)
  local copies, waits for them, and re-layouts  1.01 us (2%)
  other arithmetic  0.85 us (2%)
  between operations  0.82 us (2%)
    ppermute x11, starting transfers between devices, between(): return lax.ppermute(value, 'pen', [(i, i ^ k) for i in range(n_pen)])  8.06 us
    ppermute x4, starting transfers between devices, across(): return lax.ppermute(value, 'kz', [(i, i ^ k) for i in range(n_kz)])  7.99 us
    ppermute x4, waiting for transfers between devices, across(): return lax.ppermute(value, 'kz', [(i, i ^ k) for i in range(n_kz)])  7.98 us
    ppermute x11, waiting for transfers between devices, between(): return lax.ppermute(value, 'pen', [(i, i ^ k) for i in range(n_pen)])  5.17 us
    all_to_all x1, starting transfers between devices, body(): lax.all_to_all(sent, 'pen', split_axis=0, concat_axis=0, tiled=True, axis...  3.72 us
    pallas_call x1, Pallas kernels, body(): pl.pallas_call(call(order_and_forward, n_pen, n_kz, chunk, per_owner, til...  3.53 us
    pallas_call x1, Pallas kernels, body(): pl.pallas_call(call(adjoint_other, n_pen, chunk, per_owner), out_shape=sh...  1.3 us
    all_to_all x1, waiting for transfers between devices, body(): lax.all_to_all(sent, 'pen', split_axis=0, concat_axis=0, tiled=True, axis...  1.3 us
  transfers between devices with their start and end apart: 16, of which 9 were waited for; matrix products, arithmetic and copies ran while one was open for 4% of the time, Pallas kernels for 5%

profile of v13, /device:TPU:0, one launch (start us, length us, event | category | flops | bytes accessed | tf_op | source)
XLA Modules:
  0.0 44.0 jit_solution(13735648930737984858)
XLA Ops:
  0.6 0.0 copy-start.4
  0.6 0.0 copy-start.5
  0.7 0.0 copy-start.2
  0.7 0.0 copy-start.3
  0.7 0.0 copy-start.1
  0.7 3.5 %shard_map.86 = (bf16[2,2,2,64,512]{4,3,2,1,0:T(8,128)(2,1)}, bf16[2,2,2,64,512]{4,3,2,1,0:T(8,128)(2,1)}, bf16[2,2,2,64,512]{4,3,2,1,0:T(8,128)(2,1)}, bf16[2,2...) custom-call(s32[16]{0:T(128)} %refs_0_.3, s32[16]{0:T(128)} %refs_1_.3, ...), custom_call_target="tpu_custom_call" | custom-call | tf_op jit(solution)/shard_map/pallas_call | solution.py:235
  4.2 3.1 %collective-permute-start = (f32[2,16,512]{2,1,0:T(8,128)}, f32[2,16,512]{2,1,0:T(8,128)S(1)}, u32[]{:S(2)}, u32[]{:S(2)}) collective-permute-start(f32[2,16,512]{2,1,0:T(8,128)} %get-tuple-element.13), channel_id=1, source_target_pairs={{0,8},{8,0},{16,24},{24,16},{1,9},{9,1},{17,25},{25,17},{2,10},{10... | collective-permute-start | bytes 196616 | tf_op jit(solution)/shard_map/ppermute | solution.py:228
  7.3 3.7 %all-to-all-start = ((bf16[8,2,512]{2,1,0:T(2,128)(2,1)}), bf16[8,2,512]{2,1,0:T(2,128)(2,1)S(1)}, u32[]{:S(2)}, u32[]{:S(2)}) async-start(bf16[8,2,512]{2,1,0:T(2,128)(2,1)} %bitcast.5), calls=%async_computation | async-start | bytes 32768 | tf_op jit(solution)/shard_map/all_to_all | solution.py:270
  11.0 2.0 %collective-permute-start.3 = (bf16[2,2,2,64,512]{4,3,2,1,0:T(8,128)(2,1)}, bf16[2,2,2,64,512]{4,3,2,1,0:T(8,128)(2,1)S(1)}, u32[]{:S(2)}, u32[]{:S(2)}) collective-permute-start(bf16[2,2,2,64,512]{4,3,2,1,0:T(8,128)(2,1)} %get-tuple-element.16), channel_id=1, source_target_pairs={{0,2},{1,3},{2,0},{3,1},{4,6},{5,7},{6,4},{7,5},{8,10},{9,11},{10,... | collective-permute-start | bytes 1572872 | tf_op jit(solution)/shard_map/ppermute | solution.py:231
  13.0 1.5 %collective-permute-start.4 = (bf16[2,2,2,64,512]{4,3,2,1,0:T(8,128)(2,1)}, bf16[2,2,2,64,512]{4,3,2,1,0:T(8,128)(2,1)S(1)}, u32[]{:S(2)}, u32[]{:S(2)}) collective-permute-start(bf16[2,2,2,64,512]{4,3,2,1,0:T(8,128)(2,1)} %get-tuple-element.17), channel_id=1, source_target_pairs={{0,4},{1,5},{2,6},{3,7},{4,0},{5,1},{6,2},{7,3},{8,12},{9,13},{10,... | collective-permute-start | bytes 1572872 | tf_op jit(solution)/shard_map/ppermute | solution.py:231
  14.5 0.0 collective-permute-start.5
  14.5 1.3 %all-to-all-done = bf16[8,2,512]{2,1,0:T(2,128)(2,1)S(1)} async-done(((bf16[8,2,512]{2,1,0:T(2,128)(2,1)}), bf16[8,2,512]{2,1,0:T(2,128)(2,1)S(1)}, u32[]{:S(2)}, u32[]{:S(2)}) %all-to-all-start) | async-done | bytes 16416 | tf_op jit(solution)/shard_map/all_to_all | solution.py:270
  15.8 0.0 collective-permute-start.2
  15.8 0.0 collective-permute-done
  15.8 0.9 %add_bitcast_fusion = f32[1,2,16,512]{3,2,1,0:T(8,128)S(1)} fusion(f32[2,16,512]{2,1,0:T(8,128)} %get-tuple-element.12, f32[2,16,512]{2,1,0:T(8,128)S(1)} %collective-permute-done), kind=kLoop, calls=%fused_computation.1 | loop fusion | flops 16384 | bytes 196608 | tf_op jit(solution)/shard_map/reshape | solution.py:264
  16.7 2.7 %collective-permute-start.1 = (f32[1,16,512]{2,1,0:T(8,128)S(1)}, f32[1,16,512]{2,1,0:T(8,128)S(1)}, u32[]{:S(2)}, u32[]{:S(2)}) collective-permute-start(f32[1,16,512]{2,1,0:T(8,128)S(1)} %get-tuple-element.22), channel_id=1, source_target_pairs={{0,16},{8,24},{16,0},{24,8},{1,17},{9,25},{17,1},{25,9},{2,18},{10... | collective-permute-start | bytes 98312 | tf_op jit(solution)/shard_map/ppermute | solution.py:228
  19.4 1.0 %slice_bitcast_fusion = bf16[2,2,64,512]{3,2,1,0:T(8,128)(2,1)S(1)} fusion(bf16[2,2,2,64,512]{4,3,2,1,0:T(8,128)(2,1)} %get-tuple-element.15.refs_1_), kind=kLoop, calls=%fused_computation | loop fusion | bytes 524288 | tf_op jit(solution)/shard_map/squeeze | solution.py:314
  20.3 0.0 copy-start
  20.3 0.0 collective-permute-done.2.refs_8_
  20.4 0.3 collective-permute-start.8
  20.6 1.4 %collective-permute-done.1 = f32[1,16,512]{2,1,0:T(8,128)S(1)} collective-permute-done((f32[1,16,512]{2,1,0:T(8,128)S(1)}, f32[1,16,512]{2,1,0:T(8,128)S(1)}, u32[]{:S(2)}, u32[]{:S(2)}) %collective-permute-start.1) | collective-permute-done | bytes 32800 | tf_op jit(solution)/shard_map/ppermute | solution.py:228
  22.1 0.0 copy-done.3
  22.1 0.0 copy-done.1
  22.1 0.8 %shard_map.87 = (bf16[16,512]{1,0:T(8,128)(2,1)S(1)}, bf16[128,256]{1,0:T(8,128)(2,1)S(1)}) custom-call(s32[16]{0:T(128)S(1)} %copy-done.4, s32[16]{0:T(128)S(1)} %copy-done.5, s32[16,16]{1,0:T(8,128)S(1)} %copy-done.2, s32[16,16]{1,0:T(8,128)S(1)} %copy-done.3, bf16[16,16,64]{2,1,0:T(8,128)(2,1)S(1)} %copy-done.1, f32[16,512]{1,0:T(8,128)S(1)} %get-tuple-element.23.refs_5_, ...), custom_call_target="tpu_custom_call" | custom-call | tf_op jit(solution)/shard_map/pallas_call | solution.py:273
  22.9 0.1 collective-permute-start.6
  23.0 3.7 %collective-permute-done.6 = bf16[16,512]{1,0:T(8,128)(2,1)S(1)} collective-permute-done((bf16[16,512]{1,0:T(8,128)(2,1)S(1)}, bf16[16,512]{1,0:T(8,128)(2,1)S(1)}, u32[]{:S(2)}, u32[]{:S(2)}) %collective-permute-start.6) | collective-permute-done | bytes 16416 | tf_op jit(solution)/shard_map/ppermute | solution.py:228
  26.7 0.0 collective-permute-done.3.refs_0_.refs_2_
  26.8 0.1 collective-permute-start.9
  26.9 2.2 %collective-permute-start.7 = (bf16[32,512]{1,0:T(8,128)(2,1)S(1)}, bf16[32,512]{1,0:T(8,128)(2,1)S(1)}, u32[]{:S(2)}, u32[]{:S(2)}) collective-permute-start(bf16[32,512]{1,0:T(8,128)(2,1)S(1)} %constant_dynamic-update-slice_fusion.refs_1_.first_ref), channel_id=1, source_target_pairs={{0,16},{8,24},{16,0},{24,8},{1,17},{9,25},{17,1},{25,9},{2,18},{10... | collective-permute-start | bytes 98312 | tf_op jit(solution)/shard_map/ppermute | solution.py:228
  29.0 2.8 %collective-permute-done.7.second_ref = bf16[32,512]{1,0:T(8,128)(2,1)S(1)} collective-permute-done((bf16[32,512]{1,0:T(8,128)(2,1)S(1)}, bf16[32,512]{1,0:T(8,128)(2,1)S(1)}, u32[]{:S(2)}, u32[]{:S(2)}) %collective-permute-start.7) | collective-permute-done | bytes 32800 | tf_op jit(solution)/shard_map/ppermute | solution.py:228
  31.9 0.0 collective-permute-done.8.rest_0_.refs_3_
  31.9 0.0 collective-permute-done.9.rest_1_.refs_4_
  31.9 1.7 %collective-permute-start.10 = (bf16[64,512]{1,0:T(8,128)(2,1)S(1)}, bf16[64,512]{1,0:T(8,128)(2,1)S(1)}, u32[]{:S(2)}, u32[]{:S(2)}) collective-permute-start(bf16[64,512]{1,0:T(8,128)(2,1)S(1)} %shard_map.89.refs_5_.refs_0_), channel_id=1, source_target_pairs={{0,2},{1,3},{2,0},{3,1},{4,6},{5,7},{6,4},{7,5},{8,10},{9,11},{10,... | collective-permute-start | bytes 196616 | tf_op jit(solution)/shard_map/ppermute | solution.py:231
  33.6 1.5 %collective-permute-start.11 = (bf16[64,512]{1,0:T(8,128)(2,1)S(1)}, bf16[64,512]{1,0:T(8,128)(2,1)S(1)}, u32[]{:S(2)}, u32[]{:S(2)}) collective-permute-start(bf16[64,512]{1,0:T(8,128)(2,1)S(1)} %shard_map.89.refs_5_.refs_0_), channel_id=1, source_target_pairs={{0,4},{1,5},{2,6},{3,7},{4,0},{5,1},{6,2},{7,3},{8,12},{9,13},{10,... | collective-permute-start | bytes 196616 | tf_op jit(solution)/shard_map/ppermute | solution.py:231
  35.1 0.4 collective-permute-start.12
  35.5 1.2 %collective-permute-done.4.refs_3_.refs_0_ = bf16[2,2,2,64,512]{4,3,2,1,0:T(8,128)(2,1)S(1)} collective-permute-done((bf16[2,2,2,64,512]{4,3,2,1,0:T(8,128)(2,1)}, bf16[2,2,2,64,512]{4,3,2,1,0:T(8,128)(2,1)S(1)}, u32[]{:S(2)}, u32[]{:S(2)}) %collective-permute-start.4) | collective-permute-done | bytes 524320 | tf_op jit(solution)/shard_map/ppermute | solution.py:231
  36.7 1.0 %collective-permute-done.5.refs_4_.refs_1_ = bf16[2,2,2,64,512]{4,3,2,1,0:T(8,128)(2,1)S(1)} collective-permute-done((bf16[2,2,2,64,512]{4,3,2,1,0:T(8,128)(2,1)}, bf16[2,2,2,64,512]{4,3,2,1,0:T(8,128)(2,1)S(1)}, u32[]{:S(2)}, u32[]{:S(2)}) %collective-permute-start.5) | collective-permute-done | bytes 524320 | tf_op jit(solution)/shard_map/ppermute | solution.py:231
  37.6 0.0 collective-permute-done.10.refs_6_.refs_2_.refs_1_
  37.6 1.6 %collective-permute-done.11.refs_7_.refs_3_.refs_2_ = bf16[64,512]{1,0:T(8,128)(2,1)S(1)} collective-permute-done((bf16[64,512]{1,0:T(8,128)(2,1)S(1)}, bf16[64,512]{1,0:T(8,128)(2,1)S(1)}, u32[]{:S(2)}, u32[]{:S(2)}) %collective-permute-start.11) | collective-permute-done | bytes 65568 | tf_op jit(solution)/shard_map/ppermute | solution.py:231
  39.2 1.0 %collective-permute-done.12.refs_8_.refs_4_.refs_3_ = bf16[64,512]{1,0:T(8,128)(2,1)S(1)} collective-permute-done((bf16[64,512]{1,0:T(8,128)(2,1)S(1)}, bf16[64,512]{1,0:T(8,128)(2,1)S(1)}, u32[]{:S(2)}, u32[]{:S(2)}) %collective-permute-start.12) | collective-permute-done | bytes 65568 | tf_op jit(solution)/shard_map/ppermute | solution.py:231
  40.2 0.1 shard_map.91
  40.3 0.1 collective-permute-start.13
  40.4 0.6 %collective-permute-start.14 = (bf16[4,64,512]{2,1,0:T(8,128)(2,1)S(1)}, bf16[4,64,512]{2,1,0:T(8,128)(2,1)S(1)}, u32[]{:S(2)}, u32[]{:S(2)}) collective-permute-start(bf16[4,64,512]{2,1,0:T(8,128)(2,1)S(1)} %shard_map.92), channel_id=1, source_target_pairs={{0,1},{1,0},{2,3},{3,2},{4,5},{5,4},{6,7},{7,6},{8,9},{9,8},{10,11... | collective-permute-start | bytes 786440 | tf_op jit(solution)/shard_map/ppermute | solution.py:231
  41.0 0.0 copy-done
  41.0 1.3 %shard_map.90 = (bf16[2,2,64,4096]{3,2,1,0:T(8,128)(2,1)}, bf16[1,2,4096]{2,1,0:T(2,128)(2,1)S(1)}) custom-call(bf16[128,256]{1,0:T(8,128)(2,1)S(1)} %get-tuple-element.14.refs_0_, bf16[2,2,2,64,512]{4,3,2,1,0:T(8,128)(2,1)S(1)} %copy-done, bf16[2,2,2,64,512]{4,3,2,1,0:T(8,128)(2,1)S(1)} %collective-permute-done.3.refs_0_.refs_2_, ...), custom_call_target="tpu_custom_call" | custom-call | tf_op jit(solution)/shard_map/pallas_call | solution.py:339
  42.3 0.4 collective-permute-done.14.refs_6_
  42.7 0.0 collective-permute-done.13.refs_5_
  42.7 1.3 %shard_map.93 = (bf16[2,2,64,4096]{3,2,1,0:T(8,128)(2,1)}, bf16[1,2,4096]{2,1,0:T(2,128)(2,1)}) custom-call(bf16[128,256]{1,0:T(8,128)(2,1)S(1)} %get-tuple-element.14.refs_0_, bf16[2,2,64,4096]{3,2,1,0:T(8,128)(2,1)} %get-tuple-element.20.refs_1_, bf16[1,2,4096]{2,1,0:T(2,128)(2,1)S(1)} %get-tuple-element.21.refs_2_, ...), custom_call_target="tpu_custom_call", output_to_operand_aliasing={{0}: (1, {})} | custom-call | tf_op jit(solution)/shard_map/pallas_call | solution.py:347
  (9 shorter events, 0.1 us)
Async XLA Ops:
  0.6 21.4 %copy-start.4 = (s32[16]{0:T(128)S(1)}, s32[16]{0:T(128)}, u32[]{:S(2)}) copy-start(s32[16]{0:T(128)} %refs_0_.3) | copy-start | bytes 196
  0.6 21.4 %copy-start.5 = (s32[16]{0:T(128)S(1)}, s32[16]{0:T(128)}, u32[]{:S(2)}) copy-start(s32[16]{0:T(128)} %refs_1_.3) | copy-start | bytes 196
  0.7 21.4 %copy-start.2 = (s32[16,16]{1,0:T(8,128)S(1)}, s32[16,16]{1,0:T(8,128)}, u32[]{:S(2)}) copy-start(s32[16,16]{1,0:T(8,128)} %refs_2_.3) | copy-start | bytes 3076
  0.7 21.4 %copy-start.3 = (s32[16,16]{1,0:T(8,128)S(1)}, s32[16,16]{1,0:T(8,128)}, u32[]{:S(2)}) copy-start(s32[16,16]{1,0:T(8,128)} %refs_3_.3) | copy-start | bytes 3076
  0.7 21.4 %copy-start.1 = (bf16[16,16,64]{2,1,0:T(8,128)(2,1)S(1)}, bf16[16,16,64]{2,1,0:T(8,128)(2,1)}, u32[]{:S(2)}) copy-start(bf16[16,16,64]{2,1,0:T(8,128)(2,1)} %refs_4_.3) | copy-start | bytes 98308
  4.2 11.6 %collective-permute-start = (f32[2,16,512]{2,1,0:T(8,128)}, f32[2,16,512]{2,1,0:T(8,128)S(1)}, u32[]{:S(2)}, u32[]{:S(2)}) collective-permute-start(f32[2,16,512]{2,1,0:T(8,128)} %get-tuple-element.13), channel_id=1, source_target_pairs={{0,8},{8,0},{16,24},{24,16},{1,9},{9,1},{17,25},{25,17},{2,10},{10... | collective-permute-start | bytes 196616 | tf_op jit(solution)/shard_map/ppermute | solution.py:228
  7.3 8.5 %all-to-all-start = ((bf16[8,2,512]{2,1,0:T(2,128)(2,1)}), bf16[8,2,512]{2,1,0:T(2,128)(2,1)S(1)}, u32[]{:S(2)}, u32[]{:S(2)}) async-start(bf16[8,2,512]{2,1,0:T(2,128)(2,1)} %bitcast.5), calls=%async_computation | async-start | bytes 32768 | tf_op jit(solution)/shard_map/all_to_all | solution.py:270
  11.0 15.7 %collective-permute-start.3 = (bf16[2,2,2,64,512]{4,3,2,1,0:T(8,128)(2,1)}, bf16[2,2,2,64,512]{4,3,2,1,0:T(8,128)(2,1)S(1)}, u32[]{:S(2)}, u32[]{:S(2)}) collective-permute-start(bf16[2,2,2,64,512]{4,3,2,1,0:T(8,128)(2,1)} %get-tuple-element.16), channel_id=1, source_target_pairs={{0,2},{1,3},{2,0},{3,1},{4,6},{5,7},{6,4},{7,5},{8,10},{9,11},{10,... | collective-permute-start | bytes 1572872 | tf_op jit(solution)/shard_map/ppermute | solution.py:231
  13.0 23.6 %collective-permute-start.4 = (bf16[2,2,2,64,512]{4,3,2,1,0:T(8,128)(2,1)}, bf16[2,2,2,64,512]{4,3,2,1,0:T(8,128)(2,1)S(1)}, u32[]{:S(2)}, u32[]{:S(2)}) collective-permute-start(bf16[2,2,2,64,512]{4,3,2,1,0:T(8,128)(2,1)} %get-tuple-element.17), channel_id=1, source_target_pairs={{0,4},{1,5},{2,6},{3,7},{4,0},{5,1},{6,2},{7,3},{8,12},{9,13},{10,... | collective-permute-start | bytes 1572872 | tf_op jit(solution)/shard_map/ppermute | solution.py:231
  14.5 23.1 %collective-permute-start.5 = (bf16[2,2,2,64,512]{4,3,2,1,0:T(8,128)(2,1)}, bf16[2,2,2,64,512]{4,3,2,1,0:T(8,128)(2,1)S(1)}, u32[]{:S(2)}, u32[]{:S(2)}) collective-permute-start(bf16[2,2,2,64,512]{4,3,2,1,0:T(8,128)(2,1)} %get-tuple-element.18), channel_id=1, source_target_pairs={{0,6},{1,7},{2,4},{3,5},{4,2},{5,3},{6,0},{7,1},{8,14},{9,15},{10,... | collective-permute-start | bytes 1572872 | tf_op jit(solution)/shard_map/ppermute | solution.py:231
  15.8 4.5 %collective-permute-start.2 = (bf16[4,2,2,512]{3,2,1,0:T(2,128)(2,1)S(1)}, bf16[4,2,2,512]{3,2,1,0:T(2,128)(2,1)S(1)}, u32[]{:S(2)}, u32[]{:S(2)}) collective-permute-start(bf16[4,2,2,512]{3,2,1,0:T(2,128)(2,1)S(1)} %bitcast.13), channel_id=1, source_target_pairs={{0,1},{1,0},{2,3},{3,2},{4,5},{5,4},{6,7},{7,6},{8,9},{9,8},{10,11... | collective-permute-start | bytes 49160 | tf_op jit(solution)/shard_map/ppermute | solution.py:231
  16.7 5.4 %collective-permute-start.1 = (f32[1,16,512]{2,1,0:T(8,128)S(1)}, f32[1,16,512]{2,1,0:T(8,128)S(1)}, u32[]{:S(2)}, u32[]{:S(2)}) collective-permute-start(f32[1,16,512]{2,1,0:T(8,128)S(1)} %get-tuple-element.22), channel_id=1, source_target_pairs={{0,16},{8,24},{16,0},{24,8},{1,17},{9,25},{17,1},{25,9},{2,18},{10... | collective-permute-start | bytes 98312 | tf_op jit(solution)/shard_map/ppermute | solution.py:228
  20.3 20.6 %copy-start = (bf16[2,2,2,64,512]{4,3,2,1,0:T(8,128)(2,1)S(1)}, bf16[2,2,2,64,512]{4,3,2,1,0:T(8,128)(2,1)}, u32[]{:S(2)}) copy-start(bf16[2,2,2,64,512]{4,3,2,1,0:T(8,128)(2,1)} %get-tuple-element.15.refs_1_) | copy-start | bytes 1572868
  20.4 11.5 %collective-permute-start.8 = (bf16[2,2,64,512]{3,2,1,0:T(8,128)(2,1)S(1)}, bf16[2,2,64,512]{3,2,1,0:T(8,128)(2,1)S(1)}, u32[]{:S(2)}, u32[]{:S(2)}) collective-permute-start(bf16[2,2,64,512]{3,2,1,0:T(8,128)(2,1)S(1)} %slice_bitcast_fusion), channel_id=1, source_target_pairs={{0,1},{1,0},{2,3},{3,2},{4,5},{5,4},{6,7},{7,6},{8,9},{9,8},{10,11... | collective-permute-start | bytes 786440 | tf_op jit(solution)/shard_map/ppermute | solution.py:231
  22.9 3.8 %collective-permute-start.6 = (bf16[16,512]{1,0:T(8,128)(2,1)S(1)}, bf16[16,512]{1,0:T(8,128)(2,1)S(1)}, u32[]{:S(2)}, u32[]{:S(2)}) collective-permute-start(bf16[16,512]{1,0:T(8,128)(2,1)S(1)} %get-tuple-element.19), channel_id=1, source_target_pairs={{0,8},{8,0},{16,24},{24,16},{1,9},{9,1},{17,25},{25,17},{2,10},{10... | collective-permute-start | bytes 49160 | tf_op jit(solution)/shard_map/ppermute | solution.py:228
  26.8 5.1 %collective-permute-start.9 = (bf16[1,2,2,64,512]{4,3,2,1,0:T(8,128)(2,1)S(1)}, bf16[1,2,2,64,512]{4,3,2,1,0:T(8,128)(2,1)S(1)}, u32[]{:S(2)}, u32[]{:S(2)}) collective-permute-start(bf16[1,2,2,64,512]{4,3,2,1,0:T(8,128)(2,1)S(1)} %shard_map.88), channel_id=1, source_target_pairs={{0,1},{1,0},{2,3},{3,2},{4,5},{5,4},{6,7},{7,6},{8,9},{9,8},{10,11... | collective-permute-start | bytes 786440 | tf_op jit(solution)/shard_map/ppermute | solution.py:231
  26.9 5.0 %collective-permute-start.7 = (bf16[32,512]{1,0:T(8,128)(2,1)S(1)}, bf16[32,512]{1,0:T(8,128)(2,1)S(1)}, u32[]{:S(2)}, u32[]{:S(2)}) collective-permute-start(bf16[32,512]{1,0:T(8,128)(2,1)S(1)} %constant_dynamic-update-slice_fusion.refs_1_.first_ref), channel_id=1, source_target_pairs={{0,16},{8,24},{16,0},{24,8},{1,17},{9,25},{17,1},{25,9},{2,18},{10... | collective-permute-start | bytes 98312 | tf_op jit(solution)/shard_map/ppermute | solution.py:228
  31.9 5.7 %collective-permute-start.10 = (bf16[64,512]{1,0:T(8,128)(2,1)S(1)}, bf16[64,512]{1,0:T(8,128)(2,1)S(1)}, u32[]{:S(2)}, u32[]{:S(2)}) collective-permute-start(bf16[64,512]{1,0:T(8,128)(2,1)S(1)} %shard_map.89.refs_5_.refs_0_), channel_id=1, source_target_pairs={{0,2},{1,3},{2,0},{3,1},{4,6},{5,7},{6,4},{7,5},{8,10},{9,11},{10,... | collective-permute-start | bytes 196616 | tf_op jit(solution)/shard_map/ppermute | solution.py:231
  33.6 5.6 %collective-permute-start.11 = (bf16[64,512]{1,0:T(8,128)(2,1)S(1)}, bf16[64,512]{1,0:T(8,128)(2,1)S(1)}, u32[]{:S(2)}, u32[]{:S(2)}) collective-permute-start(bf16[64,512]{1,0:T(8,128)(2,1)S(1)} %shard_map.89.refs_5_.refs_0_), channel_id=1, source_target_pairs={{0,4},{1,5},{2,6},{3,7},{4,0},{5,1},{6,2},{7,3},{8,12},{9,13},{10,... | collective-permute-start | bytes 196616 | tf_op jit(solution)/shard_map/ppermute | solution.py:231
  35.1 5.2 %collective-permute-start.12 = (bf16[64,512]{1,0:T(8,128)(2,1)S(1)}, bf16[64,512]{1,0:T(8,128)(2,1)S(1)}, u32[]{:S(2)}, u32[]{:S(2)}) collective-permute-start(bf16[64,512]{1,0:T(8,128)(2,1)S(1)} %shard_map.89.refs_5_.refs_0_), channel_id=1, source_target_pairs={{0,6},{1,7},{2,4},{3,5},{4,2},{5,3},{6,0},{7,1},{8,14},{9,15},{10,... | collective-permute-start | bytes 196616 | tf_op jit(solution)/shard_map/ppermute | solution.py:231
  40.3 2.4 %collective-permute-start.13 = (bf16[2,2,2,64,512]{4,3,2,1,0:T(8,128)(2,1)S(1)}, bf16[2,2,2,64,512]{4,3,2,1,0:T(8,128)(2,1)S(1)}, u32[]{:S(2)}, u32[]{:S(2)}) collective-permute-start(bf16[2,2,2,64,512]{4,3,2,1,0:T(8,128)(2,1)S(1)} %shard_map.91), channel_id=1, source_target_pairs={{0,1},{1,0},{2,3},{3,2},{4,5},{5,4},{6,7},{7,6},{8,9},{9,8},{10,11... | collective-permute-start | bytes 1572872 | tf_op jit(solution)/shard_map/ppermute | solution.py:231
  40.4 2.2 %collective-permute-start.14 = (bf16[4,64,512]{2,1,0:T(8,128)(2,1)S(1)}, bf16[4,64,512]{2,1,0:T(8,128)(2,1)S(1)}, u32[]{:S(2)}, u32[]{:S(2)}) collective-permute-start(bf16[4,64,512]{2,1,0:T(8,128)(2,1)S(1)} %shard_map.92), channel_id=1, source_target_pairs={{0,1},{1,0},{2,3},{3,2},{4,5},{5,4},{6,7},{7,6},{8,9},{9,8},{10,11... | collective-permute-start | bytes 786440 | tf_op jit(solution)/shard_map/ppermute | solution.py:231

commit v14 on v12

--- a/solution.py
+++ b/solution.py
@@ -191,12 +191,12 @@
         put.wait()
 
 
-def adjoint_other(n_pen, chunk, per_owner, table_ref, begun_ref, part_ref, own_ref, near_ref, far_ref, tiles_ref,
+def adjoint_other(n_pen, chunk, per_owner, table_ref, begun_ref, part_ref, near_ref, far_ref, tiles_ref,
                   out_ref, residual_ref, made, out_sems, whole, whole_sem):
     del begun_ref
     chips = n_pen // 2
     whole[...] = part_ref[...]
-    blocks = [own_ref, near_ref.at[0]] + [far_ref.at[i] for i in range(chips - 2)]
+    blocks = [near_ref.at[0], near_ref.at[1]] + [far_ref.at[i] for i in range(chips - 2)]
     tiles = [tiles_ref.at[i] for i in range(chips)]
     puts = adjoint(n_pen, chunk, per_owner, 1, table_ref, blocks, tiles, out_ref, whole, made, out_sems)
     puts.append(pltpu.make_async_copy(whole, residual_ref, whole_sem))
@@ -310,15 +310,14 @@
             compiler_params=pltpu.CompilerParams(vmem_limit_bytes=8 << 20),
         )(*arrived, *after)
 
-    own_swapped = between(outs[0][1], 1)
-    near_swapped = between(take_other(kept[1:2], [held]), 1)
+    near_swapped = between(take_other(kept[:2], [held]), 1)
     held = pl.pallas_call(
         join_tiles,
         out_shape=jax.ShapeDtypeStruct((2 * tiles, columns), BF16),
-        in_specs=[VMEM, VMEM, ANY, ANY],
+        in_specs=[VMEM, VMEM, ANY],
         out_specs=VMEM,
         compiler_params=pltpu.CompilerParams(vmem_limit_bytes=8 << 20),
-    )(held, across(held, step), own_swapped, near_swapped)
+    )(held, across(held, step), near_swapped)
     like = [held] + [between(held, 2 * i) for i in range(1, chips)]
     far_swapped = between(take_other(kept[2:], like[1:]), 1)
     stacked = pl.pallas_call(
@@ -346,12 +345,12 @@
     updated, residual = pl.pallas_call(
         call(adjoint_other, n_pen, chunk, per_owner),
         out_shape=shapes,
-        in_specs=[VMEM, ANY] + [VMEM] * 5,
+        in_specs=[VMEM, ANY] + [VMEM] * 4,
         out_specs=[ANY, ANY],
         scratch_shapes=[*scratch, pltpu.VMEM(measured.shape, BF16), pltpu.SemaphoreType.DMA],
         input_output_aliases={1: 0},
         compiler_params=pltpu.CompilerParams(vmem_limit_bytes=16 << 20),
-    )(table, begun, part, own_swapped, near_swapped, far_swapped, other)
+    )(table, begun, part, near_swapped, far_swapped, other)
     return (updated, residual)
 
 

time: 44.3 us -> 61.7 us (1.39)
  waiting for transfers between devices: 14.4 us -> 24.1 us
  blocking collectives: 0 us -> 8.26 us
    ppermute x11 -> x10, waiting for transfers between devices: 5.17 us -> 18.4 us  [between(): return lax.ppermute(value, 'pen', [(i, i ^ k) for i in range(n_pen)])]
    all_to_all x0 -> x1, blocking collectives: none -> 8.26 us  [body(): lax.all_to_all(sent, 'pen', split_axis=0, concat_axis=0, tiled=True, axis...]
    all_to_all x1 -> x0, starting transfers between devices: 3.72 us -> none  [body(): lax.all_to_all(sent, 'pen', split_axis=0, concat_axis=0, tiled=True, axis...]
    ppermute x4, starting transfers between devices: 7.99 us -> 10.4 us  [across(): return lax.ppermute(value, 'kz', [(i, i ^ k) for i in range(n_kz)])]
    ppermute x4, waiting for transfers between devices: 7.98 us -> 5.74 us  [across(): return lax.ppermute(value, 'kz', [(i, i ^ k) for i in range(n_kz)])]
    all_to_all x1 -> x0, waiting for transfers between devices: 1.3 us -> none  [body(): lax.all_to_all(sent, 'pen', split_axis=0, concat_axis=0, tiled=True, axis...]
    unnamed x13 -> x19, local copies, waits for them, and re-layouts: 0.03 us -> 1.08 us
    squeeze x1 -> x0, local copies, waits for them, and re-layouts: 0.97 us -> none  [body(): own_swapped = between(outs[0][1], 1)]
  transfers between devices with their start and end apart: 16 -> 14, of which waited for: 9 -> 7; matrix products, arithmetic and copies ran while one was open for 4% -> 1% of each run, Pallas kernels for 5% -> 3%
where the time goes in v14:
time: 61.7 us; the launch traced here: 61.4 us
  waiting for transfers between devices  24.1 us (39%)
  starting transfers between devices  19.2 us (31%)
  blocking collectives  8.26 us (13%)
  Pallas kernels  7.08 us (11%)
  local copies, waits for them, and re-layouts  1.08 us (2%)
  other arithmetic  0.85 us (1%)
  between operations  0.81 us (1%)
    ppermute x10, waiting for transfers between devices, between(): return lax.ppermute(value, 'pen', [(i, i ^ k) for i in range(n_pen)])  18.4 us
    ppermute x4, starting transfers between devices, across(): return lax.ppermute(value, 'kz', [(i, i ^ k) for i in range(n_kz)])  10.4 us
    ppermute x10, starting transfers between devices, between(): return lax.ppermute(value, 'pen', [(i, i ^ k) for i in range(n_pen)])  8.8 us
    all_to_all x1, blocking collectives, body(): lax.all_to_all(sent, 'pen', split_axis=0, concat_axis=0, tiled=True, axis...  8.26 us
    ppermute x4, waiting for transfers between devices, across(): return lax.ppermute(value, 'kz', [(i, i ^ k) for i in range(n_kz)])  5.74 us
    pallas_call x1, Pallas kernels, body(): pl.pallas_call(call(order_and_forward, n_pen, n_kz, chunk, per_owner, til...  3.53 us
    pallas_call x1, Pallas kernels, body(): pl.pallas_call(call(adjoint_like, n_pen, chunk, per_owner), out_shape=sha...  1.29 us
    pallas_call x1, Pallas kernels, body(): pl.pallas_call(call(adjoint_other, n_pen, chunk, per_owner), out_shape=sh...  1.29 us
  transfers between devices with their start and end apart: 14, of which 7 were waited for; matrix products, arithmetic and copies ran while one was open for 1% of the time, Pallas kernels for 3%

profile of v14, /device:TPU:0, one launch (start us, length us, event | category | flops | bytes accessed | tf_op | source)
XLA Modules:
  0.0 61.4 jit_solution(2146505329530333424)
XLA Ops:
  0.6 0.0 copy-start.5
  0.6 0.0 copy-start.6
  0.7 0.0 copy-start.3
  0.7 0.0 copy-start.4
  0.7 0.0 copy-start.2
  0.7 0.0 copy-start.7
  0.7 3.5 %shard_map.86 = (bf16[2,2,2,64,512]{4,3,2,1,0:T(8,128)(2,1)}, bf16[2,2,2,64,512]{4,3,2,1,0:T(8,128)(2,1)}, bf16[2,2,2,64,512]{4,3,2,1,0:T(8,128)(2,1)}, bf16[2,2...) custom-call(s32[16]{0:T(128)} %refs_0_.3, s32[16]{0:T(128)} %refs_1_.3, ...), custom_call_target="tpu_custom_call" | custom-call | tf_op jit(solution)/shard_map/pallas_call | solution.py:234
  4.2 0.0 copy-start.8
  4.2 3.1 %collective-permute-start = (f32[2,16,512]{2,1,0:T(8,128)}, f32[2,16,512]{2,1,0:T(8,128)S(1)}, u32[]{:S(2)}, u32[]{:S(2)}) collective-permute-start(f32[2,16,512]{2,1,0:T(8,128)} %get-tuple-element.13), channel_id=1, source_target_pairs={{0,8},{8,0},{16,24},{24,16},{1,9},{9,1},{17,25},{25,17},{2,10},{10... | collective-permute-start | bytes 196616 | tf_op jit(solution)/shard_map/ppermute | solution.py:227
  7.3 1.5 %collective-permute-start.3 = (bf16[2,2,2,64,512]{4,3,2,1,0:T(8,128)(2,1)}, bf16[2,2,2,64,512]{4,3,2,1,0:T(8,128)(2,1)S(1)}, u32[]{:S(2)}, u32[]{:S(2)}) collective-permute-start(bf16[2,2,2,64,512]{4,3,2,1,0:T(8,128)(2,1)} %get-tuple-element.16), channel_id=1, source_target_pairs={{0,2},{1,3},{2,0},{3,1},{4,6},{5,7},{6,4},{7,5},{8,10},{9,11},{10,... | collective-permute-start | bytes 1572872 | tf_op jit(solution)/shard_map/ppermute | solution.py:230
  8.8 1.0 %collective-permute-done = f32[2,16,512]{2,1,0:T(8,128)S(1)} collective-permute-done((f32[2,16,512]{2,1,0:T(8,128)}, f32[2,16,512]{2,1,0:T(8,128)S(1)}, u32[]{:S(2)}, u32[]{:S(2)}) %collective-permute-start) | collective-permute-done | bytes 65568 | tf_op jit(solution)/shard_map/ppermute | solution.py:227
  9.8 0.8 %add_bitcast_fusion = f32[1,2,16,512]{3,2,1,0:T(8,128)S(1)} fusion(f32[2,16,512]{2,1,0:T(8,128)} %get-tuple-element.12, f32[2,16,512]{2,1,0:T(8,128)S(1)} %collective-permute-done), kind=kLoop, calls=%fused_computation | loop fusion | flops 16384 | bytes 196608 | tf_op jit(solution)/shard_map/reshape | solution.py:263
  10.6 3.1 %collective-permute-start.1 = (f32[1,16,512]{2,1,0:T(8,128)S(1)}, f32[1,16,512]{2,1,0:T(8,128)S(1)}, u32[]{:S(2)}, u32[]{:S(2)}) collective-permute-start(f32[1,16,512]{2,1,0:T(8,128)S(1)} %get-tuple-element.22), channel_id=1, source_target_pairs={{0,16},{8,24},{16,0},{24,8},{1,17},{9,25},{17,1},{25,9},{2,18},{10... | collective-permute-start | bytes 98312 | tf_op jit(solution)/shard_map/ppermute | solution.py:227
  13.7 0.0 copy-done.7
  13.8 8.3 %all_to_all.5 = bf16[8,2,512]{2,1,0:T(2,128)(2,1)S(1)} all-to-all(bf16[8,2,512]{2,1,0:T(2,128)(2,1)S(1)} %bitcast.14), channel_id=1, replica_groups={{0,2,4,6},{1,3,5,7},{8,10,12,14},{9,11,13,15},{16,18,20,22},{17,19,21,2..., dimensions={0} | all-to-all | bytes 32768 | tf_op jit(solution)/shard_map/all_to_all | solution.py:269
  22.0 0.0 collective-permute-start.2
  22.0 1.2 %collective-permute-done.2.refs_8_ = bf16[4,2,2,512]{3,2,1,0:T(2,128)(2,1)S(1)} collective-permute-done((bf16[4,2,2,512]{3,2,1,0:T(2,128)(2,1)S(1)}, bf16[4,2,2,512]{3,2,1,0:T(2,128)(2,1)S(1)}, u32[]{:S(2)}, u32[]{:S(2)}) %collective-permute-start.2) | collective-permute-done | bytes 16416 | tf_op jit(solution)/shard_map/ppermute | solution.py:230
  23.2 0.0 collective-permute-done.1
  23.2 0.0 copy-done.5
  23.2 0.0 copy-done.6
  23.2 0.0 copy-done.3
  23.2 0.8 %shard_map.87 = (bf16[16,512]{1,0:T(8,128)(2,1)S(1)}, bf16[128,256]{1,0:T(8,128)(2,1)S(1)}) custom-call(s32[16]{0:T(128)S(1)} %copy-done.5, s32[16]{0:T(128)S(1)} %copy-done.6, s32[16,16]{1,0:T(8,128)S(1)} %copy-done.3, s32[16,16]{1,0:T(8,128)S(1)} %copy-done.4, bf16[16,16,64]{2,1,0:T(8,128)(2,1)S(1)} %copy-done.2, f32[16,512]{1,0:T(8,128)S(1)} %get-tuple-element.23.refs_5_, ...), custom_call_target="tpu_custom_call" | custom-call | tf_op jit(solution)/shard_map/pallas_call | solution.py:272
  24.1 1.6 %collective-permute-start.6 = (bf16[16,512]{1,0:T(8,128)(2,1)S(1)}, bf16[16,512]{1,0:T(8,128)(2,1)S(1)}, u32[]{:S(2)}, u32[]{:S(2)}) collective-permute-start(bf16[16,512]{1,0:T(8,128)(2,1)S(1)} %get-tuple-element.19), channel_id=1, source_target_pairs={{0,8},{8,0},{16,24},{24,16},{1,9},{9,1},{17,25},{25,17},{2,10},{10... | collective-permute-start | bytes 49160 | tf_op jit(solution)/shard_map/ppermute | solution.py:227
  25.7 2.2 %collective-permute-done.6 = bf16[16,512]{1,0:T(8,128)(2,1)S(1)} collective-permute-done((bf16[16,512]{1,0:T(8,128)(2,1)S(1)}, bf16[16,512]{1,0:T(8,128)(2,1)S(1)}, u32[]{:S(2)}, u32[]{:S(2)}) %collective-permute-start.6) | collective-permute-done | bytes 16416 | tf_op jit(solution)/shard_map/ppermute | solution.py:227
  27.9 0.0 collective-permute-done.3.refs_1_.refs_2_
  27.9 1.0 %copy-done = bf16[2,2,2,64,512]{4,3,2,1,0:T(8,128)(2,1)S(1)} copy-done((bf16[2,2,2,64,512]{4,3,2,1,0:T(8,128)(2,1)S(1)}, bf16[2,2,2,64,512]{4,3,2,1,0:T(8,128)(2,1)}, u32[]{:S(2)}) %copy-start) | copy-done | bytes 524312
  28.9 0.1 shard_map.88
  29.0 0.1 collective-permute-start.8
  29.1 0.7 %collective-permute-start.4 = (bf16[2,2,2,64,512]{4,3,2,1,0:T(8,128)(2,1)}, bf16[2,2,2,64,512]{4,3,2,1,0:T(8,128)(2,1)S(1)}, u32[]{:S(2)}, u32[]{:S(2)}) collective-permute-start(bf16[2,2,2,64,512]{4,3,2,1,0:T(8,128)(2,1)} %get-tuple-element.17), channel_id=1, source_target_pairs={{0,4},{1,5},{2,6},{3,7},{4,0},{5,1},{6,2},{7,3},{8,12},{9,13},{10,... | collective-permute-start | bytes 1572872 | tf_op jit(solution)/shard_map/ppermute | solution.py:230
  29.7 2.4 %collective-permute-start.5 = (bf16[2,2,2,64,512]{4,3,2,1,0:T(8,128)(2,1)S(1)}, bf16[2,2,2,64,512]{4,3,2,1,0:T(8,128)(2,1)S(1)}, u32[]{:S(2)}, u32[]{:S(2)}) collective-permute-start(bf16[2,2,2,64,512]{4,3,2,1,0:T(8,128)(2,1)S(1)} %copy-done.8), channel_id=1, source_target_pairs={{0,6},{1,7},{2,4},{3,5},{4,2},{5,3},{6,0},{7,1},{8,14},{9,15},{10,... | collective-permute-start | bytes 1572872 | tf_op jit(solution)/shard_map/ppermute | solution.py:230
  32.1 2.6 %collective-permute-start.7 = (bf16[32,512]{1,0:T(8,128)(2,1)S(1)}, bf16[32,512]{1,0:T(8,128)(2,1)S(1)}, u32[]{:S(2)}, u32[]{:S(2)}) collective-permute-start(bf16[32,512]{1,0:T(8,128)(2,1)S(1)} %constant_dynamic-update-slice_fusion.refs_2_.first_ref), channel_id=1, source_target_pairs={{0,16},{8,24},{16,0},{24,8},{1,17},{9,25},{17,1},{25,9},{2,18},{10... | collective-permute-start | bytes 98312 | tf_op jit(solution)/shard_map/ppermute | solution.py:227
  34.7 2.6 %collective-permute-done.7.second_ref = bf16[32,512]{1,0:T(8,128)(2,1)S(1)} collective-permute-done((bf16[32,512]{1,0:T(8,128)(2,1)S(1)}, bf16[32,512]{1,0:T(8,128)(2,1)S(1)}, u32[]{:S(2)}, u32[]{:S(2)}) %collective-permute-start.7) | collective-permute-done | bytes 32800 | tf_op jit(solution)/shard_map/ppermute | solution.py:227
  37.3 0.0 collective-permute-done.8.rest_0_.refs_3_
  37.3 0.4 collective-permute-start.9
  37.8 0.6 collective-permute-start.10
  38.4 2.5 %collective-permute-start.11 = (bf16[64,512]{1,0:T(8,128)(2,1)S(1)}, bf16[64,512]{1,0:T(8,128)(2,1)S(1)}, u32[]{:S(2)}, u32[]{:S(2)}) collective-permute-start(bf16[64,512]{1,0:T(8,128)(2,1)S(1)} %shard_map.89.refs_5_.refs_0_), channel_id=1, source_target_pairs={{0,6},{1,7},{2,4},{3,5},{4,2},{5,3},{6,0},{7,1},{8,14},{9,15},{10,... | collective-permute-start | bytes 196616 | tf_op jit(solution)/shard_map/ppermute | solution.py:230
  40.9 15.8 %collective-permute-done.4.refs_3_.refs_0_ = bf16[2,2,2,64,512]{4,3,2,1,0:T(8,128)(2,1)S(1)} collective-permute-done((bf16[2,2,2,64,512]{4,3,2,1,0:T(8,128)(2,1)}, bf16[2,2,2,64,512]{4,3,2,1,0:T(8,128)(2,1)S(1)}, u32[]{:S(2)}, u32[]{:S(2)}) %collective-permute-start.4) | collective-permute-done | bytes 524320 | tf_op jit(solution)/shard_map/ppermute | solution.py:230
  56.7 0.0 collective-permute-done.5.refs_4_.refs_1_
  56.7 0.0 collective-permute-done.9.refs_6_.refs_2_.refs_1_
  56.7 0.9 %collective-permute-done.10.refs_7_.refs_3_.refs_2_ = bf16[64,512]{1,0:T(8,128)(2,1)S(1)} collective-permute-done((bf16[64,512]{1,0:T(8,128)(2,1)S(1)}, bf16[64,512]{1,0:T(8,128)(2,1)S(1)}, u32[]{:S(2)}, u32[]{:S(2)}) %collective-permute-start.10) | collective-permute-done | bytes 65568 | tf_op jit(solution)/shard_map/ppermute | solution.py:230
  57.7 0.0 collective-permute-done.11.refs_8_.refs_4_.refs_3_
  57.7 0.1 shard_map.91
  57.7 0.1 collective-permute-start.12
  57.8 0.6 collective-permute-start.13
  58.4 1.3 %shard_map.90 = (bf16[2,2,64,4096]{3,2,1,0:T(8,128)(2,1)}, bf16[1,2,4096]{2,1,0:T(2,128)(2,1)S(1)}) custom-call(bf16[128,256]{1,0:T(8,128)(2,1)S(1)} %get-tuple-element.14.refs_0_, bf16[2,2,2,64,512]{4,3,2,1,0:T(8,128)(2,1)S(1)} %copy-done.1, bf16[2,2,2,64,512]{4,3,2,1,0:T(8,128)(2,1)S(1)} %collective-permute-done.3.refs_1_.refs_2_, ...), custom_call_target="tpu_custom_call" | custom-call | tf_op jit(solution)/shard_map/pallas_call | solution.py:337
  59.7 0.4 collective-permute-done.13.refs_5_
  60.1 0.0 collective-permute-done.12.refs_4_
  60.1 1.3 %shard_map.93 = (bf16[2,2,64,4096]{3,2,1,0:T(8,128)(2,1)}, bf16[1,2,4096]{2,1,0:T(2,128)(2,1)}) custom-call(bf16[128,256]{1,0:T(8,128)(2,1)S(1)} %get-tuple-element.14.refs_0_, bf16[2,2,64,4096]{3,2,1,0:T(8,128)(2,1)} %get-tuple-element.20.refs_1_, bf16[1,2,4096]{2,1,0:T(2,128)(2,1)S(1)} %get-tuple-element.21.refs_2_, ...), custom_call_target="tpu_custom_call", output_to_operand_aliasing={{0}: (1, {})} | custom-call | tf_op jit(solution)/shard_map/pallas_call | solution.py:345
  (11 shorter events, 0.0 us)
Async XLA Ops:
  0.6 22.6 %copy-start.5 = (s32[16]{0:T(128)S(1)}, s32[16]{0:T(128)}, u32[]{:S(2)}) copy-start(s32[16]{0:T(128)} %refs_0_.3) | copy-start | bytes 196
  0.6 22.6 %copy-start.6 = (s32[16]{0:T(128)S(1)}, s32[16]{0:T(128)}, u32[]{:S(2)}) copy-start(s32[16]{0:T(128)} %refs_1_.3) | copy-start | bytes 196
  0.7 22.6 %copy-start.3 = (s32[16,16]{1,0:T(8,128)S(1)}, s32[16,16]{1,0:T(8,128)}, u32[]{:S(2)}) copy-start(s32[16,16]{1,0:T(8,128)} %refs_2_.3) | copy-start | bytes 3076
  0.7 22.6 %copy-start.4 = (s32[16,16]{1,0:T(8,128)S(1)}, s32[16,16]{1,0:T(8,128)}, u32[]{:S(2)}) copy-start(s32[16,16]{1,0:T(8,128)} %refs_3_.3) | copy-start | bytes 3076
  0.7 22.6 %copy-start.2 = (bf16[16,16,64]{2,1,0:T(8,128)(2,1)S(1)}, bf16[16,16,64]{2,1,0:T(8,128)(2,1)}, u32[]{:S(2)}) copy-start(bf16[16,16,64]{2,1,0:T(8,128)(2,1)} %refs_4_.3) | copy-start | bytes 98308
  0.7 13.1 %copy-start.7 = (bf16[1,2,4096]{2,1,0:T(2,128)(2,1)S(1)}, bf16[1,2,4096]{2,1,0:T(2,128)(2,1)}, u32[]{:S(2)}) copy-start(bf16[1,2,4096]{2,1,0:T(2,128)(2,1)} %param.13) | copy-start | bytes 49156
  4.2 25.5 %copy-start.8 = (bf16[2,2,2,64,512]{4,3,2,1,0:T(8,128)(2,1)S(1)}, bf16[2,2,2,64,512]{4,3,2,1,0:T(8,128)(2,1)}, u32[]{:S(2)}) copy-start(bf16[2,2,2,64,512]{4,3,2,1,0:T(8,128)(2,1)} %get-tuple-element.18) | copy-start | bytes 1572868
  4.2 5.5 %collective-permute-start = (f32[2,16,512]{2,1,0:T(8,128)}, f32[2,16,512]{2,1,0:T(8,128)S(1)}, u32[]{:S(2)}, u32[]{:S(2)}) collective-permute-start(f32[2,16,512]{2,1,0:T(8,128)} %get-tuple-element.13), channel_id=1, source_target_pairs={{0,8},{8,0},{16,24},{24,16},{1,9},{9,1},{17,25},{25,17},{2,10},{10... | collective-permute-start | bytes 196616 | tf_op jit(solution)/shard_map/ppermute | solution.py:227
  7.3 20.6 %collective-permute-start.3 = (bf16[2,2,2,64,512]{4,3,2,1,0:T(8,128)(2,1)}, bf16[2,2,2,64,512]{4,3,2,1,0:T(8,128)(2,1)S(1)}, u32[]{:S(2)}, u32[]{:S(2)}) collective-permute-start(bf16[2,2,2,64,512]{4,3,2,1,0:T(8,128)(2,1)} %get-tuple-element.16), channel_id=1, source_target_pairs={{0,2},{1,3},{2,0},{3,1},{4,6},{5,7},{6,4},{7,5},{8,10},{9,11},{10,... | collective-permute-start | bytes 1572872 | tf_op jit(solution)/shard_map/ppermute | solution.py:230
  10.6 12.5 %collective-permute-start.1 = (f32[1,16,512]{2,1,0:T(8,128)S(1)}, f32[1,16,512]{2,1,0:T(8,128)S(1)}, u32[]{:S(2)}, u32[]{:S(2)}) collective-permute-start(f32[1,16,512]{2,1,0:T(8,128)S(1)} %get-tuple-element.22), channel_id=1, source_target_pairs={{0,16},{8,24},{16,0},{24,8},{1,17},{9,25},{17,1},{25,9},{2,18},{10... | collective-permute-start | bytes 98312 | tf_op jit(solution)/shard_map/ppermute | solution.py:227
  22.0 1.2 %collective-permute-start.2 = (bf16[4,2,2,512]{3,2,1,0:T(2,128)(2,1)S(1)}, bf16[4,2,2,512]{3,2,1,0:T(2,128)(2,1)S(1)}, u32[]{:S(2)}, u32[]{:S(2)}) collective-permute-start(bf16[4,2,2,512]{3,2,1,0:T(2,128)(2,1)S(1)} %bitcast.11), channel_id=1, source_target_pairs={{0,1},{1,0},{2,3},{3,2},{4,5},{5,4},{6,7},{7,6},{8,9},{9,8},{10,11... | collective-permute-start | bytes 49160 | tf_op jit(solution)/shard_map/ppermute | solution.py:230
  24.1 3.8 %collective-permute-start.6 = (bf16[16,512]{1,0:T(8,128)(2,1)S(1)}, bf16[16,512]{1,0:T(8,128)(2,1)S(1)}, u32[]{:S(2)}, u32[]{:S(2)}) collective-permute-start(bf16[16,512]{1,0:T(8,128)(2,1)S(1)} %get-tuple-element.19), channel_id=1, source_target_pairs={{0,8},{8,0},{16,24},{24,16},{1,9},{9,1},{17,25},{25,17},{2,10},{10... | collective-permute-start | bytes 49160 | tf_op jit(solution)/shard_map/ppermute | solution.py:227
  27.9 1.0 %copy-start = (bf16[2,2,2,64,512]{4,3,2,1,0:T(8,128)(2,1)S(1)}, bf16[2,2,2,64,512]{4,3,2,1,0:T(8,128)(2,1)}, u32[]{:S(2)}) copy-start(bf16[2,2,2,64,512]{4,3,2,1,0:T(8,128)(2,1)} %get-tuple-element.15.refs_0_.refs_1_) | copy-start | bytes 1572868
  28.9 29.5 %copy-start.1 = (bf16[2,2,2,64,512]{4,3,2,1,0:T(8,128)(2,1)S(1)}, bf16[2,2,2,64,512]{4,3,2,1,0:T(8,128)(2,1)}, u32[]{:S(2)}) copy-start(bf16[2,2,2,64,512]{4,3,2,1,0:T(8,128)(2,1)} %get-tuple-element.15.refs_0_.refs_1_) | copy-start | bytes 1572868
  29.0 8.3 %collective-permute-start.8 = (bf16[2,2,2,64,512]{4,3,2,1,0:T(8,128)(2,1)S(1)}, bf16[2,2,2,64,512]{4,3,2,1,0:T(8,128)(2,1)S(1)}, u32[]{:S(2)}, u32[]{:S(2)}) collective-permute-start(bf16[2,2,2,64,512]{4,3,2,1,0:T(8,128)(2,1)S(1)} %shard_map.88), channel_id=1, source_target_pairs={{0,1},{1,0},{2,3},{3,2},{4,5},{5,4},{6,7},{7,6},{8,9},{9,8},{10,11... | collective-permute-start | bytes 1572872 | tf_op jit(solution)/shard_map/ppermute | solution.py:230
  29.1 27.6 %collective-permute-start.4 = (bf16[2,2,2,64,512]{4,3,2,1,0:T(8,128)(2,1)}, bf16[2,2,2,64,512]{4,3,2,1,0:T(8,128)(2,1)S(1)}, u32[]{:S(2)}, u32[]{:S(2)}) collective-permute-start(bf16[2,2,2,64,512]{4,3,2,1,0:T(8,128)(2,1)} %get-tuple-element.17), channel_id=1, source_target_pairs={{0,4},{1,5},{2,6},{3,7},{4,0},{5,1},{6,2},{7,3},{8,12},{9,13},{10,... | collective-permute-start | bytes 1572872 | tf_op jit(solution)/shard_map/ppermute | solution.py:230
  29.7 27.0 %collective-permute-start.5 = (bf16[2,2,2,64,512]{4,3,2,1,0:T(8,128)(2,1)S(1)}, bf16[2,2,2,64,512]{4,3,2,1,0:T(8,128)(2,1)S(1)}, u32[]{:S(2)}, u32[]{:S(2)}) collective-permute-start(bf16[2,2,2,64,512]{4,3,2,1,0:T(8,128)(2,1)S(1)} %copy-done.8), channel_id=1, source_target_pairs={{0,6},{1,7},{2,4},{3,5},{4,2},{5,3},{6,0},{7,1},{8,14},{9,15},{10,... | collective-permute-start | bytes 1572872 | tf_op jit(solution)/shard_map/ppermute | solution.py:230
  32.1 5.2 %collective-permute-start.7 = (bf16[32,512]{1,0:T(8,128)(2,1)S(1)}, bf16[32,512]{1,0:T(8,128)(2,1)S(1)}, u32[]{:S(2)}, u32[]{:S(2)}) collective-permute-start(bf16[32,512]{1,0:T(8,128)(2,1)S(1)} %constant_dynamic-update-slice_fusion.refs_2_.first_ref), channel_id=1, source_target_pairs={{0,16},{8,24},{16,0},{24,8},{1,17},{9,25},{17,1},{25,9},{2,18},{10... | collective-permute-start | bytes 98312 | tf_op jit(solution)/shard_map/ppermute | solution.py:227
  37.3 19.4 %collective-permute-start.9 = (bf16[64,512]{1,0:T(8,128)(2,1)S(1)}, bf16[64,512]{1,0:T(8,128)(2,1)S(1)}, u32[]{:S(2)}, u32[]{:S(2)}) collective-permute-start(bf16[64,512]{1,0:T(8,128)(2,1)S(1)} %shard_map.89.refs_5_.refs_0_), channel_id=1, source_target_pairs={{0,2},{1,3},{2,0},{3,1},{4,6},{5,7},{6,4},{7,5},{8,10},{9,11},{10,... | collective-permute-start | bytes 196616 | tf_op jit(solution)/shard_map/ppermute | solution.py:230
  37.8 19.9 %collective-permute-start.10 = (bf16[64,512]{1,0:T(8,128)(2,1)S(1)}, bf16[64,512]{1,0:T(8,128)(2,1)S(1)}, u32[]{:S(2)}, u32[]{:S(2)}) collective-permute-start(bf16[64,512]{1,0:T(8,128)(2,1)S(1)} %shard_map.89.refs_5_.refs_0_), channel_id=1, source_target_pairs={{0,4},{1,5},{2,6},{3,7},{4,0},{5,1},{6,2},{7,3},{8,12},{9,13},{10,... | collective-permute-start | bytes 196616 | tf_op jit(solution)/shard_map/ppermute | solution.py:230
  38.4 19.3 %collective-permute-start.11 = (bf16[64,512]{1,0:T(8,128)(2,1)S(1)}, bf16[64,512]{1,0:T(8,128)(2,1)S(1)}, u32[]{:S(2)}, u32[]{:S(2)}) collective-permute-start(bf16[64,512]{1,0:T(8,128)(2,1)S(1)} %shard_map.89.refs_5_.refs_0_), channel_id=1, source_target_pairs={{0,6},{1,7},{2,4},{3,5},{4,2},{5,3},{6,0},{7,1},{8,14},{9,15},{10,... | collective-permute-start | bytes 196616 | tf_op jit(solution)/shard_map/ppermute | solution.py:230
  57.7 2.4 %collective-permute-start.12 = (bf16[2,2,2,64,512]{4,3,2,1,0:T(8,128)(2,1)S(1)}, bf16[2,2,2,64,512]{4,3,2,1,0:T(8,128)(2,1)S(1)}, u32[]{:S(2)}, u32[]{:S(2)}) collective-permute-start(bf16[2,2,2,64,512]{4,3,2,1,0:T(8,128)(2,1)S(1)} %shard_map.91), channel_id=1, source_target_pairs={{0,1},{1,0},{2,3},{3,2},{4,5},{5,4},{6,7},{7,6},{8,9},{9,8},{10,11... | collective-permute-start | bytes 1572872 | tf_op jit(solution)/shard_map/ppermute | solution.py:230
  57.8 2.2 %collective-permute-start.13 = (bf16[4,64,512]{2,1,0:T(8,128)(2,1)S(1)}, bf16[4,64,512]{2,1,0:T(8,128)(2,1)S(1)}, u32[]{:S(2)}, u32[]{:S(2)}) collective-permute-start(bf16[4,64,512]{2,1,0:T(8,128)(2,1)S(1)} %shard_map.92), channel_id=1, source_target_pairs={{0,1},{1,0},{2,3},{3,2},{4,5},{5,4},{6,7},{7,6},{8,9},{9,8},{10,11... | collective-permute-start | bytes 786440 | tf_op jit(solution)/shard_map/ppermute | solution.py:230
